TPU v7x, 32 devices: a whole 2x2x4 slice. The times are simulated.
32 devices in a mesh: ctx: 4 (over x, core), tp: 8 (over z, y).
Axes of the slice: x: 2, y: 2, z: 4, core: 2. Of those that a mesh axis runs over, the one named last changes fastest.
Arguments:
- lin_query: bfloat16 [2048, 8, 128], P('ctx', 'tp'), may hold values from -6 to 6
- lin_key: bfloat16 [2048, 8, 128], P('ctx', 'tp'), may hold values from -6 to 6
- lin_value: bfloat16 [2048, 8, 128], P('ctx', 'tp'), may hold values from -6 to 6
- log_decay: float32 [8, 2048], P('tp', 'ctx'), may hold values from -2 to 0, as said below
- soft_query: bfloat16 [2048, 8, 128], P('ctx', 'tp'), may hold values from -12 to 12
- soft_key: bfloat16 [2048, 8, 128], P('ctx', 'tp'), may hold values from -4 to 4
- soft_value: bfloat16 [2048, 8, 128], P('ctx', 'tp'), may hold values from -6 to 6
Outputs:
- linear_out: bfloat16 [2048, 8, 128], P('ctx', 'tp')
- softmax_out: bfloat16 [2048, 8, 128], P('ctx', 'tp')
Inputs may be any that keep to these rules, and one draw needn't show every extreme that they name: `log_decay`: every entry is negative.
All inputs are finite; a program needn't handle non-finite values.
Results may differ from a plain program's by a relative error of at most 0.0055.
Values may be sent and summed in bfloat16 or wider, within the bound.
No kernel may reach another device: no remote copies, remote signals or barrier semaphores. Data moves between devices by JAX's collectives and lax.ppermute only.
A program may use at most 64 MiB of HBM per device.

v0:
```python
import functools
import math

import jax
import jax.numpy as jnp
from jax import lax
from jax.experimental import pallas as pl
from jax.experimental.pallas import tpu as pltpu
from jax.sharding import PartitionSpec as P

NEG = -1e30
TINY = 1e-6
PAD = 16
F32 = jnp.float32
BF16 = jnp.bfloat16
VMEM = pltpu.VMEM


def dot(a, b):
    return lax.dot_general(a, b, (((1,), (0,)), ((), ())), preferred_element_type=F32)


def three_parts(x):
    high = x.astype(BF16)
    rest = x - high.astype(F32)
    middle = rest.astype(BF16)
    low = (rest - middle.astype(F32)).astype(BF16)
    return high, middle, low


def iota(shape, dim):
    return lax.broadcasted_iota(jnp.int32, shape, dim)


def select_rows(parts, rows, width):
    row = iota((rows, width), 0)
    out = jnp.zeros((rows, width), F32)
    for number, part in enumerate(parts):
        out = jnp.where(row == number, part.astype(F32), out)
    return out.astype(BF16)


def side_by_side(ref, rows, width):
    pieces = [ref[left : left + width, :] for left in range(0, rows, width)]
    return pieces[0] if len(pieces) == 1 else jnp.concatenate(pieces, axis=1)


def state_kernel(
    decay_ref, key_ref, value_ref, soft_value_ref, pack_ref, cum_row_ref, cum_col_ref, value_t_ref
):
    rows, width = key_ref.shape
    parts = select_rows(three_parts(decay_ref[...]), PAD, rows)
    upto = (iota((rows, rows), 0) <= iota((rows, rows), 1)).astype(F32).astype(BF16)
    cum_row = jnp.sum(dot(parts, upto), axis=0, keepdims=True)
    cum_row_ref[...] = cum_row
    cum_col = jnp.transpose(jnp.broadcast_to(cum_row, (width, rows)))
    cum_col_ref[...] = cum_col
    total = cum_col[rows - 1 :, :]
    decayed = (key_ref[...].astype(F32) * jnp.exp(total - cum_col)).astype(BF16)
    value_t = jnp.transpose(value_ref[...])
    value_t_ref[...] = value_t
    state_t = dot(value_t, decayed)
    high = state_t.astype(BF16)
    for left in range(0, rows, width):
        pack_ref[left : left + width, :] = jnp.transpose(soft_value_ref[left : left + width, :])
    pack_ref[rows : rows + width, :] = high
    pack_ref[rows + width : rows + 2 * width, :] = (state_t - high.astype(F32)).astype(BF16)
    pack_ref[rows + 2 * width :, :] = select_rows(three_parts(total), PAD, width)


def local_kernel(
    scale, step,
    lin_q_ref, lin_k_ref, q_ref, k_ref, lin_vt_ref, cum_row_ref, cum_col_ref, pack_ref,
    lin_qt_ref, qt_ref, intra_ref, top_ref, total_ref, summed_ref,
):
    rows, width = lin_q_ref.shape
    lin_qt_ref[...] = jnp.transpose(lin_q_ref[...])
    qt_ref[...] = jnp.transpose(q_ref[...])
    soft_vt = side_by_side(pack_ref, rows, width)
    keep = iota((step, step), 0) <= iota((step, step), 1)
    for start in range(0, rows, step):
        stop = start + step
        scores = dot(k_ref[:stop, :], qt_ref[:, start:stop])
        last = jnp.where(keep, scores[start:, :], NEG)
        scores = jnp.concatenate([scores[:start, :], last], axis=0) if start else last
        top = jnp.max(scores, axis=0, keepdims=True)
        probs = jnp.exp2((scores - top) * scale)
        top_ref[:, start:stop] = top
        total_ref[:, start:stop] = jnp.sum(probs, axis=0, keepdims=True)
        summed_ref[:, start:stop] = dot(soft_vt[:, :stop], probs.astype(BF16))

        scores = dot(lin_k_ref[:stop, :], lin_qt_ref[:, start:stop])
        cum_t = cum_row_ref[:, start:stop]
        cum_s = jnp.concatenate([cum_col_ref[:stop, :]] * (step // width), axis=1)
        diff = cum_t - cum_s
        last = jnp.where(keep, diff[start:, :], NEG)
        diff = jnp.concatenate([diff[:start, :], last], axis=0) if start else last
        weights = (scores * jnp.exp(diff)).astype(BF16)
        intra_ref[:, start:stop] = dot(lin_vt_ref[:, :stop], weights)


def block_numbers(axis, cores, chips):
    position = lax.axis_index(axis)
    if cores == 1:
        return position, [position - apart for apart in range(1, chips)]
    other = lax.rem(position, 2)
    partner = position + 1 - 2 * other
    numbers = [jnp.where(other == 1, position - 1, -1)]
    for apart in range(1, chips):
        numbers += [position - 2 * apart, partner - 2 * apart]
    return position, numbers


def by_chip(position, cores, count, body):
    pl.when(position >= cores)(lambda: body(count))
    pl.when(position < cores)(lambda: body(cores - 1))


def score_kernel(scale, step, axis, cores, chips, qt_ref, top_ref, total_ref, *refs):
    key_refs, (probs_ref, factor_ref, sum_ref) = refs[:-3], refs[-3:]
    rows = qt_ref.shape[1]
    position, numbers = block_numbers(axis, cores, chips)
    away = [jnp.where(number >= 0, 0.0, NEG) for number in numbers]

    def body(count):
        for start in range(0, rows, step):
            mine = slice(start, start + step)
            query = qt_ref[:, mine]
            old = top_ref[:, mine]
            scores = [dot(key_refs[i][...], query) for i in range(count)]
            top = old
            for score, off in zip(scores, away):
                top = jnp.maximum(top, jnp.max(score, axis=0, keepdims=True) + off)
            factor = jnp.exp2((old - top) * scale)
            total = total_ref[:, mine] * factor
            for number, (score, off) in enumerate(zip(scores, away)):
                probs = jnp.exp2((score - (top - off)) * scale)
                total = total + jnp.sum(probs, axis=0, keepdims=True)
                probs_ref[number * rows : (number + 1) * rows, mine] = probs.astype(BF16)
            factor_ref[:, mine] = factor
            sum_ref[:, mine] = total

    by_chip(position, cores, len(key_refs), body)


def finish_kernel(
    step, axis, cores, chips,
    lin_qt_ref, intra_ref, cum_row_ref, summed_ref, probs_ref, factor_ref, sum_ref, *refs,
):
    pack_refs, (linear_ref, softmax_ref) = refs[:-2], refs[-2:]
    width, rows = lin_qt_ref.shape
    position, numbers = block_numbers(axis, cores, chips)

    def body(count):
        totals, states = [], []
        for pack_ref in pack_refs[:count]:
            tail = pack_ref[rows + 2 * width :, :].astype(F32)
            totals.append(tail[0:1] + tail[1:2] + tail[2:3])
            states.append(
                pack_ref[rows : rows + width, :].astype(F32)
                + pack_ref[rows + width : rows + 2 * width, :].astype(F32)
            )
        carried = jnp.zeros((width, width), F32)
        for number, state in zip(numbers, states):
            between = jnp.where(number >= 0, 0.0, NEG)
            for other, total in zip(numbers, totals):
                between = between + jnp.where(other > number, 1.0, 0.0) * total
            carried = carried + jnp.exp(between) * state
        carried = carried.astype(BF16)
        values = [side_by_side(pack_ref, rows, width) for pack_ref in pack_refs[:count]]
        for start in range(0, rows, step):
            mine = slice(start, start + step)
            summed = summed_ref[:, mine] * factor_ref[:, mine]
            for number, value in enumerate(values):
                summed = summed + dot(value, probs_ref[number * rows : (number + 1) * rows, mine])
            softmax_ref[mine, :] = jnp.transpose(summed / sum_ref[:, mine]).astype(BF16)
            inter = dot(carried, lin_qt_ref[:, mine])
            raw = intra_ref[:, mine] + inter * jnp.exp(cum_row_ref[:, mine])
            square = jnp.sum(raw * raw, axis=0, keepdims=True) * (1.0 / width)
            linear_ref[mine, :] = jnp.transpose(raw * lax.rsqrt(square + TINY)).astype(BF16)

    by_chip(position, cores, len(pack_refs), body)


def keep_in_hbm(x):
    return pltpu.with_memory_space_constraint(x, pltpu.HBM)


def keep_in_vmem(x):
    return pltpu.with_memory_space_constraint(x, VMEM)


def kept_in_vmem(x):
    return VMEM(x.shape, x.dtype)


def call(body, given, operands, outs, last=False):
    size = sum(math.prod(x.shape) * x.dtype.itemsize for x in (*given, *operands, *outs))
    operands = [*map(keep_in_hbm, given), *map(keep_in_vmem, operands)]
    if not last:
        outs = [kept_in_vmem(x) for x in outs]
    return pl.pallas_call(
        body,
        out_shape=tuple(outs),
        in_specs=[pl.BlockSpec(memory_space=VMEM)] * len(operands),
        out_specs=tuple(pl.BlockSpec(memory_space=VMEM) for _ in outs),
        cost_estimate=pl.CostEstimate(flops=0, bytes_accessed=size, transcendentals=0),
    )(*operands)


def on_device(axis, lin_query, lin_key, lin_value, log_decay, soft_query, soft_key, soft_value):
    rows, heads, width = lin_query.shape
    count = lax.axis_size(axis)
    cores = 2 if count % 2 == 0 else 1
    chips = count // cores

    def across(x, apart):
        return lax.ppermute(x, axis, [(i, (i + apart * cores) % count) for i in range(count)])

    def swapped(x, after=None):
        if after is not None:
            x, _ = lax.optimization_barrier((x, after))
        return lax.ppermute(x, axis, [(i, i ^ 1) for i in range(count)])

    def spread(x):
        far = [across(x, apart) for apart in range(1, chips)]
        own = [swapped(x)] if cores == 2 else []
        return own, far

    def complete(of, after):
        own, far = of
        out = list(own)
        for block in far:
            out.append(block)
            if cores == 2:
                out.append(swapped(block, after))
        return out

    def one_head(lq, lk, lv, decay, sq, sk, sv):
        step = math.gcd(rows, 256)
        scale = math.log2(math.e) / math.sqrt(width)

        def shape(*dims, dtype=F32):
            return jax.ShapeDtypeStruct(dims, dtype)

        row, flat, flat16 = shape(1, rows), shape(width, rows), shape(width, rows, dtype=BF16)
        keys = spread(sk)
        pack, cum_row, cum_col, lin_vt = call(
            state_kernel,
            (decay, lk, lv, sv),
            (),
            (shape(rows + 2 * width + PAD, width, dtype=BF16), row, shape(rows, width), flat16),
        )
        packs = spread(pack)
        lin_qt, qt, intra, top, total, summed = call(
            functools.partial(local_kernel, scale, step),
            (lq, lk, sq, sk),
            (lin_vt, cum_row, cum_col, pack),
            (flat16, flat16, flat, row, row, flat),
        )
        ring = (axis, cores, chips)
        keys = complete(keys, intra)
        probs, factor, sums = call(
            functools.partial(score_kernel, scale, step, *ring),
            (),
            (qt, top, total, *keys),
            (shape(len(keys) * rows, rows, dtype=BF16), row, row),
        )
        out = shape(rows, width, dtype=BF16)
        packs = complete(packs, factor)
        return call(
            functools.partial(finish_kernel, step, *ring),
            (),
            (lin_qt, intra, cum_row, summed, probs, factor, sums, *packs),
            (out, out),
            last=True,
        )

    outs = [
        one_head(
            *(x[:, head] for x in (lin_query, lin_key, lin_value)),
            log_decay[head : head + 1],
            *(x[:, head] for x in (soft_query, soft_key, soft_value)),
        )
        for head in range(heads)
    ]
    linear = jnp.stack([pair[0] for pair in outs], axis=1)
    softmax = jnp.stack([pair[1] for pair in outs], axis=1)
    return linear, softmax


def solution(mesh):
    block = P("ctx", "tp", None)
    return jax.shard_map(
        functools.partial(on_device, "ctx"),
        mesh=mesh,
        in_specs=(block, block, block, P("tp", "ctx"), block, block, block),
        out_specs=(block, block),
        check_vma=False,
    )
```

profile of v0, /device:TPU:0, one launch (start us, length us, event | category | flops | bytes accessed | tf_op | source)
XLA Modules:
  0.0 22.5 jit_solution(17645956950116202465)
XLA Ops:
  0.6 3.0 %collective-permute-start.1 = (bf16[512,128]{1,0:T(8,128)(2,1)}, bf16[512,128]{1,0:T(8,128)(2,1)S(1)}, u32[]{:S(2)}, u32[]{:S(2)}) collective-permute-start(bf16[512,128]{1,0:T(8,128)(2,1)} %bitcast.14), channel_id=1, source_target_pairs={{0,16},{8,24},{16,0},{24,8},{1,17},{9,25},{17,1},{25,9},{2,18},{10... | collective-permute-start | bytes 393224 | tf_op jit(solution)/shard_map/ppermute | solution.py:218
  3.6 1.6 %shard_map.86 = (bf16[784,128]{1,0:T(8,128)(2,1)S(1)}, f32[1,512]{1,0:T(1,128)S(1)}, f32[512,128]{1,0:T(8,128)S(1)}, bf16[128,512]{1,0:T(8,128)(2,1)S(1)}) custom-call(f32[1,512]{1,0:T(1,128)} %decay_ref.1, bf16[512,128]{1,0:T(8,128)(2,1)} %bitcast.8, bf16[512,128]{1,0:T(8,128)(2,1)} %bitcast.10, bf16[512,128]{1,0:T(8,128)(2,1)} %bitcast.11), custom_call_target="tpu_custom_call" | custom-call | bytes 991232 | tf_op jit(solution)/shard_map/pallas_call | solution.py:202
  5.2 0.1 collective-permute-start.4
  5.3 0.1 collective-permute-start
  5.4 2.4 %shard_map.87 = (bf16[128,512]{1,0:T(8,128)(2,1)S(1)}, bf16[128,512]{1,0:T(8,128)(2,1)S(1)}, f32[128,512]{1,0:T(8,128)S(1)}, f32[1,512]{1,0:T(1,128)S(1)}, f32[1,512]{1,0:T(1,128)S(1)}, /*index=5*/f32[128,512]{1,0:T(8,128)S(1)}) custom-call(bf16[512,128]{1,0:T(8,128)(2,1)} %bitcast.12, bf16[512,128]{1,0:T(8,128)(2,1)} %bitcast.9, bf16[512,128]{1,0:T(8,128)(2,1)} %bitcast.13, ...), custom_call_target="tpu_custom_call" | custom-call | bytes 1910784 | tf_op jit(solution)/shard_map/pallas_call | solution.py:202
  7.8 0.0 copy-start.10
  7.8 0.6 %copy-done.10 = bf16[128,512]{1,0:T(8,128)(2,1)} copy-done((bf16[128,512]{1,0:T(8,128)(2,1)}, bf16[128,512]{1,0:T(8,128)(2,1)S(1)}, u32[]{:S(2)}) %copy-start.10) | copy-done | bytes 131096
  8.5 0.0 collective-permute-done.1.refs_1_
  8.5 0.5 %collective-permute-start.2 = (bf16[512,128]{1,0:T(8,128)(2,1)S(1)}, bf16[512,128]{1,0:T(8,128)(2,1)S(1)}, u32[]{:S(2)}, u32[]{:S(2)}) collective-permute-start(bf16[512,128]{1,0:T(8,128)(2,1)S(1)} %collective-permute-done.1.refs_1_), channel_id=1, source_target_pairs={{0,8},{8,0},{16,24},{24,16},{1,9},{9,1},{17,25},{25,17},{2,10},{10... | collective-permute-start | bytes 393224 | tf_op jit(solution)/shard_map/ppermute | solution.py:223
  9.0 0.0 copy-start.6
  9.0 0.6 %copy-done.6 = bf16[512,128]{1,0:T(8,128)(2,1)} copy-done((bf16[512,128]{1,0:T(8,128)(2,1)}, bf16[512,128]{1,0:T(8,128)(2,1)S(1)}, u32[]{:S(2)}) %copy-start.6) | copy-done | bytes 131096
  9.6 0.0 collective-permute-start.3
  9.6 0.0 collective-permute-done.refs_0_
  9.6 0.0 copy-start.8
  9.6 0.7 %copy-done.8 = bf16[512,128]{1,0:T(8,128)(2,1)} copy-done((bf16[512,128]{1,0:T(8,128)(2,1)}, bf16[512,128]{1,0:T(8,128)(2,1)S(1)}, u32[]{:S(2)}) %copy-start.8) | copy-done | bytes 131096
  10.3 0.0 collective-permute-done.2.refs_2_
  10.3 0.0 copy-start.12
  10.3 0.7 %copy-done.12 = bf16[512,128]{1,0:T(8,128)(2,1)} copy-done((bf16[512,128]{1,0:T(8,128)(2,1)}, bf16[512,128]{1,0:T(8,128)(2,1)S(1)}, u32[]{:S(2)}) %copy-start.12) | copy-done | bytes 131096
  10.9 0.0 copy-start.7
  11.0 0.9 %copy-done.7 = bf16[512,128]{1,0:T(8,128)(2,1)S(1)} copy-done((bf16[512,128]{1,0:T(8,128)(2,1)S(1)}, bf16[512,128]{1,0:T(8,128)(2,1)}, u32[]{:S(2)}) %copy-start.7) | copy-done | bytes 131096
  11.9 0.0 copy-start.9
  11.9 0.9 %copy-done.9 = bf16[512,128]{1,0:T(8,128)(2,1)S(1)} copy-done((bf16[512,128]{1,0:T(8,128)(2,1)S(1)}, bf16[512,128]{1,0:T(8,128)(2,1)}, u32[]{:S(2)}) %copy-start.9) | copy-done | bytes 131096
  12.8 0.0 copy-start.11
  12.8 0.9 %copy-done.11 = bf16[128,512]{1,0:T(8,128)(2,1)S(1)} copy-done((bf16[128,512]{1,0:T(8,128)(2,1)S(1)}, bf16[128,512]{1,0:T(8,128)(2,1)}, u32[]{:S(2)}) %copy-start.11) | copy-done | bytes 131096
  13.7 0.0 copy-start.13
  13.7 0.9 %copy-done.13 = bf16[512,128]{1,0:T(8,128)(2,1)S(1)} copy-done((bf16[512,128]{1,0:T(8,128)(2,1)S(1)}, bf16[512,128]{1,0:T(8,128)(2,1)}, u32[]{:S(2)}) %copy-start.13) | copy-done | bytes 131096
  14.6 0.5 %shard_map.88 = (bf16[1536,512]{1,0:T(8,128)(2,1)S(1)}, f32[1,512]{1,0:T(1,128)S(1)}, f32[1,512]{1,0:T(1,128)S(1)}) custom-call(bf16[128,512]{1,0:T(8,128)(2,1)S(1)} %copy-done.11, f32[1,512]{1,0:T(1,128)S(1)} %get-tuple-element.27.top_ref, f32[1,512]{1,0:T(1,128)S(1)} %get-tuple-element.28.total_ref, bf16[512,128]{1,0:T(8,128)(2,1)S(1)} %copy-done.9, ...), custom_call_target="tpu_custom_call" | custom-call | bytes 2105344 | tf_op jit(solution)/shard_map/pallas_call | solution.py:202
  15.1 0.0 copy-start
  15.1 1.2 %copy-done = bf16[1536,512]{1,0:T(8,128)(2,1)} copy-done((bf16[1536,512]{1,0:T(8,128)(2,1)}, bf16[1536,512]{1,0:T(8,128)(2,1)S(1)}, u32[]{:S(2)}) %copy-start) | copy-done | bytes 1572888
  16.2 0.0 collective-permute-done.4.refs_1_
  16.2 0.5 %collective-permute-start.5 = (bf16[784,128]{1,0:T(8,128)(2,1)S(1)}, bf16[784,128]{1,0:T(8,128)(2,1)S(1)}, u32[]{:S(2)}, u32[]{:S(2)}) collective-permute-start(bf16[784,128]{1,0:T(8,128)(2,1)S(1)} %collective-permute-done.4.refs_1_), channel_id=1, source_target_pairs={{0,8},{8,0},{16,24},{24,16},{1,9},{9,1},{17,25},{25,17},{2,10},{10... | collective-permute-start | bytes 602120 | tf_op jit(solution)/shard_map/ppermute | solution.py:223
  16.7 0.0 copy-start.2
  16.7 0.7 %copy-done.2 = bf16[784,128]{1,0:T(8,128)(2,1)} copy-done((bf16[784,128]{1,0:T(8,128)(2,1)}, bf16[784,128]{1,0:T(8,128)(2,1)S(1)}, u32[]{:S(2)}) %copy-start.2) | copy-done | bytes 200728
  17.4 0.0 collective-permute-done.3.refs_0_
  17.4 0.0 copy-start.4
  17.4 0.7 %copy-done.4 = bf16[784,128]{1,0:T(8,128)(2,1)} copy-done((bf16[784,128]{1,0:T(8,128)(2,1)}, bf16[784,128]{1,0:T(8,128)(2,1)S(1)}, u32[]{:S(2)}) %copy-start.4) | copy-done | bytes 200728
  18.1 0.0 collective-permute-done.5.refs_2_
  18.1 0.0 copy-start.1
  18.1 1.4 %copy-done.1 = bf16[1536,512]{1,0:T(8,128)(2,1)S(1)} copy-done((bf16[1536,512]{1,0:T(8,128)(2,1)S(1)}, bf16[1536,512]{1,0:T(8,128)(2,1)}, u32[]{:S(2)}) %copy-start.1) | copy-done | bytes 1572888
  19.5 0.0 copy-start.3
  19.5 0.9 %copy-done.3 = bf16[784,128]{1,0:T(8,128)(2,1)S(1)} copy-done((bf16[784,128]{1,0:T(8,128)(2,1)S(1)}, bf16[784,128]{1,0:T(8,128)(2,1)}, u32[]{:S(2)}) %copy-start.3) | copy-done | bytes 200728
  20.4 0.0 copy-start.5
  20.4 0.9 %copy-done.5 = bf16[784,128]{1,0:T(8,128)(2,1)S(1)} copy-done((bf16[784,128]{1,0:T(8,128)(2,1)S(1)}, bf16[784,128]{1,0:T(8,128)(2,1)}, u32[]{:S(2)}) %copy-start.5) | copy-done | bytes 200728
  21.4 1.1 %shard_map.89 = (bf16[512,128]{1,0:T(8,128)(2,1)}, bf16[512,128]{1,0:T(8,128)(2,1)}) custom-call(bf16[128,512]{1,0:T(8,128)(2,1)S(1)} %get-tuple-element.23.lin_qt_ref, f32[128,512]{1,0:T(8,128)S(1)} %get-tuple-element.24.intra_ref, f32[1,512]{1,0:T(1,128)S(1)} %get-tuple-element.20.cum_row_ref, f32[128,512]{1,0:T(8,128)S(1)} %get-tuple-element.25.summed_ref, ...), custom_call_target="tpu_custom_call" | custom-call | bytes 3098624 | tf_op jit(solution)/shard_map/pallas_call | solution.py:202
Async XLA Ops:
  0.6 7.8 %collective-permute-start.1 = (bf16[512,128]{1,0:T(8,128)(2,1)}, bf16[512,128]{1,0:T(8,128)(2,1)S(1)}, u32[]{:S(2)}, u32[]{:S(2)}) collective-permute-start(bf16[512,128]{1,0:T(8,128)(2,1)} %bitcast.14), channel_id=1, source_target_pairs={{0,16},{8,24},{16,0},{24,8},{1,17},{9,25},{17,1},{25,9},{2,18},{10... | collective-permute-start | bytes 393224 | tf_op jit(solution)/shard_map/ppermute | solution.py:218
  5.2 11.0 %collective-permute-start.4 = (bf16[784,128]{1,0:T(8,128)(2,1)S(1)}, bf16[784,128]{1,0:T(8,128)(2,1)S(1)}, u32[]{:S(2)}, u32[]{:S(2)}) collective-permute-start(bf16[784,128]{1,0:T(8,128)(2,1)S(1)} %get-tuple-element.22.pack_ref), channel_id=1, source_target_pairs={{0,16},{8,24},{16,0},{24,8},{1,17},{9,25},{17,1},{25,9},{2,18},{10... | collective-permute-start | bytes 602120 | tf_op jit(solution)/shard_map/ppermute | solution.py:218
  5.3 4.3 %collective-permute-start = (bf16[512,128]{1,0:T(8,128)(2,1)}, bf16[512,128]{1,0:T(8,128)(2,1)S(1)}, u32[]{:S(2)}, u32[]{:S(2)}) collective-permute-start(bf16[512,128]{1,0:T(8,128)(2,1)} %bitcast.15), channel_id=1, source_target_pairs={{0,8},{8,0},{16,24},{24,16},{1,9},{9,1},{17,25},{25,17},{2,10},{10... | collective-permute-start | bytes 393224 | tf_op jit(solution)/shard_map/ppermute | solution.py:223
  7.8 0.7 %copy-start.10 = (bf16[128,512]{1,0:T(8,128)(2,1)}, bf16[128,512]{1,0:T(8,128)(2,1)S(1)}, u32[]{:S(2)}) copy-start(bf16[128,512]{1,0:T(8,128)(2,1)S(1)} %get-tuple-element.26.qt_ref) | copy-start | bytes 393220
  8.5 1.8 %collective-permute-start.2 = (bf16[512,128]{1,0:T(8,128)(2,1)S(1)}, bf16[512,128]{1,0:T(8,128)(2,1)S(1)}, u32[]{:S(2)}, u32[]{:S(2)}) collective-permute-start(bf16[512,128]{1,0:T(8,128)(2,1)S(1)} %collective-permute-done.1.refs_1_), channel_id=1, source_target_pairs={{0,8},{8,0},{16,24},{24,16},{1,9},{9,1},{17,25},{25,17},{2,10},{10... | collective-permute-start | bytes 393224 | tf_op jit(solution)/shard_map/ppermute | solution.py:223
  9.0 0.7 %copy-start.6 = (bf16[512,128]{1,0:T(8,128)(2,1)}, bf16[512,128]{1,0:T(8,128)(2,1)S(1)}, u32[]{:S(2)}) copy-start(bf16[512,128]{1,0:T(8,128)(2,1)S(1)} %collective-permute-done.1.refs_1_) | copy-start | bytes 393220
  9.6 7.8 %collective-permute-start.3 = (bf16[784,128]{1,0:T(8,128)(2,1)S(1)}, bf16[784,128]{1,0:T(8,128)(2,1)S(1)}, u32[]{:S(2)}, u32[]{:S(2)}) collective-permute-start(bf16[784,128]{1,0:T(8,128)(2,1)S(1)} %get-tuple-element.22.pack_ref), channel_id=1, source_target_pairs={{0,8},{8,0},{16,24},{24,16},{1,9},{9,1},{17,25},{25,17},{2,10},{10... | collective-permute-start | bytes 602120 | tf_op jit(solution)/shard_map/ppermute | solution.py:223
  9.6 0.7 %copy-start.8 = (bf16[512,128]{1,0:T(8,128)(2,1)}, bf16[512,128]{1,0:T(8,128)(2,1)S(1)}, u32[]{:S(2)}) copy-start(bf16[512,128]{1,0:T(8,128)(2,1)S(1)} %collective-permute-done.refs_0_) | copy-start | bytes 393220
  10.3 0.7 %copy-start.12 = (bf16[512,128]{1,0:T(8,128)(2,1)}, bf16[512,128]{1,0:T(8,128)(2,1)S(1)}, u32[]{:S(2)}) copy-start(bf16[512,128]{1,0:T(8,128)(2,1)S(1)} %collective-permute-done.2.refs_2_) | copy-start | bytes 393220
  10.9 0.9 %copy-start.7 = (bf16[512,128]{1,0:T(8,128)(2,1)S(1)}, bf16[512,128]{1,0:T(8,128)(2,1)}, u32[]{:S(2)}) copy-start(bf16[512,128]{1,0:T(8,128)(2,1)} %copy-done.6) | copy-start | bytes 393220
  11.9 0.9 %copy-start.9 = (bf16[512,128]{1,0:T(8,128)(2,1)S(1)}, bf16[512,128]{1,0:T(8,128)(2,1)}, u32[]{:S(2)}) copy-start(bf16[512,128]{1,0:T(8,128)(2,1)} %copy-done.8) | copy-start | bytes 393220
  12.8 0.9 %copy-start.11 = (bf16[128,512]{1,0:T(8,128)(2,1)S(1)}, bf16[128,512]{1,0:T(8,128)(2,1)}, u32[]{:S(2)}) copy-start(bf16[128,512]{1,0:T(8,128)(2,1)} %copy-done.10) | copy-start | bytes 393220
  13.7 0.9 %copy-start.13 = (bf16[512,128]{1,0:T(8,128)(2,1)S(1)}, bf16[512,128]{1,0:T(8,128)(2,1)}, u32[]{:S(2)}) copy-start(bf16[512,128]{1,0:T(8,128)(2,1)} %copy-done.12) | copy-start | bytes 393220
  15.1 1.2 %copy-start = (bf16[1536,512]{1,0:T(8,128)(2,1)}, bf16[1536,512]{1,0:T(8,128)(2,1)S(1)}, u32[]{:S(2)}) copy-start(bf16[1536,512]{1,0:T(8,128)(2,1)S(1)} %get-tuple-element.30.probs_ref) | copy-start | bytes 4718596
  16.2 1.9 %collective-permute-start.5 = (bf16[784,128]{1,0:T(8,128)(2,1)S(1)}, bf16[784,128]{1,0:T(8,128)(2,1)S(1)}, u32[]{:S(2)}, u32[]{:S(2)}) collective-permute-start(bf16[784,128]{1,0:T(8,128)(2,1)S(1)} %collective-permute-done.4.refs_1_), channel_id=1, source_target_pairs={{0,8},{8,0},{16,24},{24,16},{1,9},{9,1},{17,25},{25,17},{2,10},{10... | collective-permute-start | bytes 602120 | tf_op jit(solution)/shard_map/ppermute | solution.py:223
  16.7 0.7 %copy-start.2 = (bf16[784,128]{1,0:T(8,128)(2,1)}, bf16[784,128]{1,0:T(8,128)(2,1)S(1)}, u32[]{:S(2)}) copy-start(bf16[784,128]{1,0:T(8,128)(2,1)S(1)} %collective-permute-done.4.refs_1_) | copy-start | bytes 602116
  17.4 0.7 %copy-start.4 = (bf16[784,128]{1,0:T(8,128)(2,1)}, bf16[784,128]{1,0:T(8,128)(2,1)S(1)}, u32[]{:S(2)}) copy-start(bf16[784,128]{1,0:T(8,128)(2,1)S(1)} %collective-permute-done.3.refs_0_) | copy-start | bytes 602116
  18.1 1.4 %copy-start.1 = (bf16[1536,512]{1,0:T(8,128)(2,1)S(1)}, bf16[1536,512]{1,0:T(8,128)(2,1)}, u32[]{:S(2)}) copy-start(bf16[1536,512]{1,0:T(8,128)(2,1)} %copy-done) | copy-start | bytes 4718596
  19.5 0.9 %copy-start.3 = (bf16[784,128]{1,0:T(8,128)(2,1)S(1)}, bf16[784,128]{1,0:T(8,128)(2,1)}, u32[]{:S(2)}) copy-start(bf16[784,128]{1,0:T(8,128)(2,1)} %copy-done.2) | copy-start | bytes 602116
  20.4 0.9 %copy-start.5 = (bf16[784,128]{1,0:T(8,128)(2,1)S(1)}, bf16[784,128]{1,0:T(8,128)(2,1)}, u32[]{:S(2)}) copy-start(bf16[784,128]{1,0:T(8,128)(2,1)} %copy-done.4) | copy-start | bytes 602116
where the time goes:
time: 22.8 us; the launch traced here: 22.5 us
  local copies, waits for them, and re-layouts  12 us (53%)
  Pallas kernels  5.57 us (24%)
  starting transfers between devices  4.16 us (18%)
  between operations  0.69 us (3%)
    unnamed x28, local copies, waits for them, and re-layouts  12 us
    pallas_call x4, Pallas kernels, call(): pl.pallas_call(body, out_shape=tuple(outs), in_specs=[pl.BlockSpec(memory...  5.57 us
    ppermute x2, starting transfers between devices, across(): lax.ppermute(x, axis, [(i, (i + apart * cores) % count) for i in range(co...  3.09 us
    ppermute x4, starting transfers between devices, swapped(): return lax.ppermute(x, axis, [(i, i ^ 1) for i in range(count)])  1.07 us
  transfers between devices with their start and end apart: 6, of which 0 were waited for; matrix products, arithmetic and copies ran while one was open for 0% of the time, Pallas kernels for 20%

commit v1 on v0

--- a/solution.py
+++ b/solution.py
@@ -11,6 +11,7 @@
 NEG = -1e30
 TINY = 1e-6
 PAD = 16
+KERNEL_VMEM = 16 * 2**20
 F32 = jnp.float32
 BF16 = jnp.bfloat16
 VMEM = pltpu.VMEM
@@ -205,6 +206,7 @@
         in_specs=[pl.BlockSpec(memory_space=VMEM)] * len(operands),
         out_specs=tuple(pl.BlockSpec(memory_space=VMEM) for _ in outs),
         cost_estimate=pl.CostEstimate(flops=0, bytes_accessed=size, transcendentals=0),
+        compiler_params=pltpu.CompilerParams(vmem_limit_bytes=KERNEL_VMEM),
     )(*operands)
 
 

time: 22.8 us -> 14.4 us (0.63)
  local copies, waits for them, and re-layouts: 12 us -> 0 us
  waiting for transfers between devices: 0.02 us -> 4.26 us
  starting transfers between devices: 4.16 us -> 3.76 us
    unnamed x28 -> x0, local copies, waits for them, and re-layouts: 12 us -> none
    ppermute x4, waiting for transfers between devices: 0.01 us -> 2.35 us  [swapped(): return lax.ppermute(x, axis, [(i, i ^ 1) for i in range(count)])]
    ppermute x2, waiting for transfers between devices: 0.01 us -> 1.91 us  [across(): lax.ppermute(x, axis, [(i, (i + apart * cores) % count) for i in range(co...]
    ppermute x4, starting transfers between devices: 1.07 us -> 0.67 us  [swapped(): return lax.ppermute(x, axis, [(i, i ^ 1) for i in range(count)])]
  transfers between devices with their start and end apart: 6 -> 6, of which waited for: 0 -> 3; matrix products, arithmetic and copies ran while one was open for 0% -> 0% of each run, Pallas kernels for 20% -> 31%
where the time goes in v1:
time: 14.4 us; the launch traced here: 14.3 us
  Pallas kernels  5.58 us (39%)
  waiting for transfers between devices  4.26 us (30%)
  starting transfers between devices  3.76 us (26%)
  between operations  0.66 us (5%)
    pallas_call x4, Pallas kernels, call(): pl.pallas_call(body, out_shape=tuple(outs), in_specs=[pl.BlockSpec(memory...  5.58 us
    ppermute x2, starting transfers between devices, across(): lax.ppermute(x, axis, [(i, (i + apart * cores) % count) for i in range(co...  3.09 us
    ppermute x4, waiting for transfers between devices, swapped(): return lax.ppermute(x, axis, [(i, i ^ 1) for i in range(count)])  2.35 us
    ppermute x2, waiting for transfers between devices, across(): lax.ppermute(x, axis, [(i, (i + apart * cores) % count) for i in range(co...  1.91 us
    ppermute x4, starting transfers between devices, swapped(): return lax.ppermute(x, axis, [(i, i ^ 1) for i in range(count)])  0.67 us
  transfers between devices with their start and end apart: 6, of which 3 were waited for; matrix products, arithmetic and copies ran while one was open for 0% of the time, Pallas kernels for 31%

profile of v1, /device:TPU:0, one launch (start us, length us, event | category | flops | bytes accessed | tf_op | source)
XLA Modules:
  0.0 14.3 jit_solution(2143488299878135337)
XLA Ops:
  0.6 3.0 %collective-permute-start.1 = (bf16[512,128]{1,0:T(8,128)(2,1)}, bf16[512,128]{1,0:T(8,128)(2,1)S(1)}, u32[]{:S(2)}, u32[]{:S(2)}) collective-permute-start(bf16[512,128]{1,0:T(8,128)(2,1)} %bitcast.14), channel_id=1, source_target_pairs={{0,16},{8,24},{16,0},{24,8},{1,17},{9,25},{17,1},{25,9},{2,18},{10... | collective-permute-start | bytes 393224 | tf_op jit(solution)/shard_map/ppermute | solution.py:220
  3.6 1.6 %shard_map.86 = (bf16[784,128]{1,0:T(8,128)(2,1)S(1)}, f32[1,512]{1,0:T(1,128)S(1)}, f32[512,128]{1,0:T(8,128)S(1)}, bf16[128,512]{1,0:T(8,128)(2,1)S(1)}) custom-call(f32[1,512]{1,0:T(1,128)} %decay_ref.1, bf16[512,128]{1,0:T(8,128)(2,1)} %bitcast.8, bf16[512,128]{1,0:T(8,128)(2,1)} %bitcast.10, bf16[512,128]{1,0:T(8,128)(2,1)} %bitcast.11), custom_call_target="tpu_custom_call" | custom-call | bytes 991232 | tf_op jit(solution)/shard_map/pallas_call | solution.py:203
  5.2 0.1 collective-permute-start.4
  5.3 0.1 collective-permute-start
  5.4 2.4 %shard_map.87 = (bf16[128,512]{1,0:T(8,128)(2,1)S(1)}, bf16[128,512]{1,0:T(8,128)(2,1)S(1)}, f32[128,512]{1,0:T(8,128)S(1)}, f32[1,512]{1,0:T(1,128)S(1)}, f32[1,512]{1,0:T(1,128)S(1)}, /*index=5*/f32[128,512]{1,0:T(8,128)S(1)}) custom-call(bf16[512,128]{1,0:T(8,128)(2,1)} %bitcast.12, bf16[512,128]{1,0:T(8,128)(2,1)} %bitcast.9, bf16[512,128]{1,0:T(8,128)(2,1)} %bitcast.13, ...), custom_call_target="tpu_custom_call" | custom-call | bytes 1910784 | tf_op jit(solution)/shard_map/pallas_call | solution.py:203
  7.8 0.0 collective-permute-done.1.refs_1_
  7.9 0.5 %collective-permute-start.2 = (bf16[512,128]{1,0:T(8,128)(2,1)S(1)}, bf16[512,128]{1,0:T(8,128)(2,1)S(1)}, u32[]{:S(2)}, u32[]{:S(2)}) collective-permute-start(bf16[512,128]{1,0:T(8,128)(2,1)S(1)} %collective-permute-done.1.refs_1_), channel_id=1, source_target_pairs={{0,8},{8,0},{16,24},{24,16},{1,9},{9,1},{17,25},{25,17},{2,10},{10... | collective-permute-start | bytes 393224 | tf_op jit(solution)/shard_map/ppermute | solution.py:225
  8.4 0.1 collective-permute-start.3
  8.5 0.0 collective-permute-done.refs_0_
  8.5 0.9 %collective-permute-done.2.refs_2_ = bf16[512,128]{1,0:T(8,128)(2,1)S(1)} collective-permute-done((bf16[512,128]{1,0:T(8,128)(2,1)S(1)}, bf16[512,128]{1,0:T(8,128)(2,1)S(1)}, u32[]{:S(2)}, u32[]{:S(2)}) %collective-permute-start.2) | collective-permute-done | bytes 131104 | tf_op jit(solution)/shard_map/ppermute | solution.py:225
  9.4 0.5 %shard_map.88 = (bf16[1536,512]{1,0:T(8,128)(2,1)S(1)}, f32[1,512]{1,0:T(1,128)S(1)}, f32[1,512]{1,0:T(1,128)S(1)}) custom-call(bf16[128,512]{1,0:T(8,128)(2,1)S(1)} %get-tuple-element.26.qt_ref, f32[1,512]{1,0:T(1,128)S(1)} %get-tuple-element.27.top_ref, f32[1,512]{1,0:T(1,128)S(1)} %get-tuple-element.28.total_ref, ...), custom_call_target="tpu_custom_call" | custom-call | bytes 2105344 | tf_op jit(solution)/shard_map/pallas_call | solution.py:203
  9.9 1.9 %collective-permute-done.4.refs_1_ = bf16[784,128]{1,0:T(8,128)(2,1)S(1)} collective-permute-done((bf16[784,128]{1,0:T(8,128)(2,1)S(1)}, bf16[784,128]{1,0:T(8,128)(2,1)S(1)}, u32[]{:S(2)}, u32[]{:S(2)}) %collective-permute-start.4) | collective-permute-done | bytes 200736 | tf_op jit(solution)/shard_map/ppermute | solution.py:220
  11.7 0.0 collective-permute-start.5
  11.7 0.0 collective-permute-done.3.refs_0_
  11.7 1.4 %collective-permute-done.5.refs_2_ = bf16[784,128]{1,0:T(8,128)(2,1)S(1)} collective-permute-done((bf16[784,128]{1,0:T(8,128)(2,1)S(1)}, bf16[784,128]{1,0:T(8,128)(2,1)S(1)}, u32[]{:S(2)}, u32[]{:S(2)}) %collective-permute-start.5) | collective-permute-done | bytes 200736 | tf_op jit(solution)/shard_map/ppermute | solution.py:225
  13.2 1.1 %shard_map.89 = (bf16[512,128]{1,0:T(8,128)(2,1)}, bf16[512,128]{1,0:T(8,128)(2,1)}) custom-call(bf16[128,512]{1,0:T(8,128)(2,1)S(1)} %get-tuple-element.23.lin_qt_ref, f32[128,512]{1,0:T(8,128)S(1)} %get-tuple-element.24.intra_ref, f32[1,512]{1,0:T(1,128)S(1)} %get-tuple-element.20.cum_row_ref, f32[128,512]{1,0:T(8,128)S(1)} %get-tuple-element.25.summed_ref, ...), custom_call_target="tpu_custom_call" | custom-call | bytes 3098624 | tf_op jit(solution)/shard_map/pallas_call | solution.py:203
Async XLA Ops:
  0.6 7.2 %collective-permute-start.1 = (bf16[512,128]{1,0:T(8,128)(2,1)}, bf16[512,128]{1,0:T(8,128)(2,1)S(1)}, u32[]{:S(2)}, u32[]{:S(2)}) collective-permute-start(bf16[512,128]{1,0:T(8,128)(2,1)} %bitcast.14), channel_id=1, source_target_pairs={{0,16},{8,24},{16,0},{24,8},{1,17},{9,25},{17,1},{25,9},{2,18},{10... | collective-permute-start | bytes 393224 | tf_op jit(solution)/shard_map/ppermute | solution.py:220
  5.2 6.5 %collective-permute-start.4 = (bf16[784,128]{1,0:T(8,128)(2,1)S(1)}, bf16[784,128]{1,0:T(8,128)(2,1)S(1)}, u32[]{:S(2)}, u32[]{:S(2)}) collective-permute-start(bf16[784,128]{1,0:T(8,128)(2,1)S(1)} %get-tuple-element.22.pack_ref), channel_id=1, source_target_pairs={{0,16},{8,24},{16,0},{24,8},{1,17},{9,25},{17,1},{25,9},{2,18},{10... | collective-permute-start | bytes 602120 | tf_op jit(solution)/shard_map/ppermute | solution.py:220
  5.3 3.2 %collective-permute-start = (bf16[512,128]{1,0:T(8,128)(2,1)}, bf16[512,128]{1,0:T(8,128)(2,1)S(1)}, u32[]{:S(2)}, u32[]{:S(2)}) collective-permute-start(bf16[512,128]{1,0:T(8,128)(2,1)} %bitcast.15), channel_id=1, source_target_pairs={{0,8},{8,0},{16,24},{24,16},{1,9},{9,1},{17,25},{25,17},{2,10},{10... | collective-permute-start | bytes 393224 | tf_op jit(solution)/shard_map/ppermute | solution.py:225
  7.9 1.5 %collective-permute-start.2 = (bf16[512,128]{1,0:T(8,128)(2,1)S(1)}, bf16[512,128]{1,0:T(8,128)(2,1)S(1)}, u32[]{:S(2)}, u32[]{:S(2)}) collective-permute-start(bf16[512,128]{1,0:T(8,128)(2,1)S(1)} %collective-permute-done.1.refs_1_), channel_id=1, source_target_pairs={{0,8},{8,0},{16,24},{24,16},{1,9},{9,1},{17,25},{25,17},{2,10},{10... | collective-permute-start | bytes 393224 | tf_op jit(solution)/shard_map/ppermute | solution.py:225
  8.4 3.4 %collective-permute-start.3 = (bf16[784,128]{1,0:T(8,128)(2,1)S(1)}, bf16[784,128]{1,0:T(8,128)(2,1)S(1)}, u32[]{:S(2)}, u32[]{:S(2)}) collective-permute-start(bf16[784,128]{1,0:T(8,128)(2,1)S(1)} %get-tuple-element.22.pack_ref), channel_id=1, source_target_pairs={{0,8},{8,0},{16,24},{24,16},{1,9},{9,1},{17,25},{25,17},{2,10},{10... | collective-permute-start | bytes 602120 | tf_op jit(solution)/shard_map/ppermute | solution.py:225
  11.7 1.4 %collective-permute-start.5 = (bf16[784,128]{1,0:T(8,128)(2,1)S(1)}, bf16[784,128]{1,0:T(8,128)(2,1)S(1)}, u32[]{:S(2)}, u32[]{:S(2)}) collective-permute-start(bf16[784,128]{1,0:T(8,128)(2,1)S(1)} %collective-permute-done.4.refs_1_), channel_id=1, source_target_pairs={{0,8},{8,0},{16,24},{24,16},{1,9},{9,1},{17,25},{25,17},{2,10},{10... | collective-permute-start | bytes 602120 | tf_op jit(solution)/shard_map/ppermute | solution.py:225

commit v2 on v1

--- a/solution.py
+++ b/solution.py
@@ -61,23 +61,16 @@
     value_t = jnp.transpose(value_ref[...])
     value_t_ref[...] = value_t
     state_t = dot(value_t, decayed)
-    high = state_t.astype(BF16)
     for left in range(0, rows, width):
         pack_ref[left : left + width, :] = jnp.transpose(soft_value_ref[left : left + width, :])
-    pack_ref[rows : rows + width, :] = high
-    pack_ref[rows + width : rows + 2 * width, :] = (state_t - high.astype(F32)).astype(BF16)
-    pack_ref[rows + 2 * width :, :] = select_rows(three_parts(total), PAD, width)
-
-
-def local_kernel(
-    scale, step,
-    lin_q_ref, lin_k_ref, q_ref, k_ref, lin_vt_ref, cum_row_ref, cum_col_ref, pack_ref,
-    lin_qt_ref, qt_ref, intra_ref, top_ref, total_ref, summed_ref,
-):
-    rows, width = lin_q_ref.shape
-    lin_qt_ref[...] = jnp.transpose(lin_q_ref[...])
+    pack_ref[rows : rows + width, :] = state_t.astype(BF16)
+    pack_ref[rows + width :, :] = select_rows(three_parts(total), PAD, width)
+
+
+def soft_kernel(scale, step, q_ref, k_ref, pack_ref, qt_ref, top_ref, total_ref, summed_ref):
+    rows, width = q_ref.shape
     qt_ref[...] = jnp.transpose(q_ref[...])
-    soft_vt = side_by_side(pack_ref, rows, width)
+    value_t = side_by_side(pack_ref, rows, width)
     keep = iota((step, step), 0) <= iota((step, step), 1)
     for start in range(0, rows, step):
         stop = start + step
@@ -88,16 +81,23 @@
         probs = jnp.exp2((scores - top) * scale)
         top_ref[:, start:stop] = top
         total_ref[:, start:stop] = jnp.sum(probs, axis=0, keepdims=True)
-        summed_ref[:, start:stop] = dot(soft_vt[:, :stop], probs.astype(BF16))
-
-        scores = dot(lin_k_ref[:stop, :], lin_qt_ref[:, start:stop])
+        summed_ref[:, start:stop] = dot(value_t[:, :stop], probs.astype(BF16))
+
+
+def linear_kernel(step, q_ref, k_ref, value_t_ref, cum_row_ref, cum_col_ref, qt_ref, intra_ref):
+    rows, width = q_ref.shape
+    qt_ref[...] = jnp.transpose(q_ref[...])
+    keep = iota((step, step), 0) <= iota((step, step), 1)
+    for start in range(0, rows, step):
+        stop = start + step
+        scores = dot(k_ref[:stop, :], qt_ref[:, start:stop])
         cum_t = cum_row_ref[:, start:stop]
         cum_s = jnp.concatenate([cum_col_ref[:stop, :]] * (step // width), axis=1)
         diff = cum_t - cum_s
         last = jnp.where(keep, diff[start:, :], NEG)
         diff = jnp.concatenate([diff[:start, :], last], axis=0) if start else last
         weights = (scores * jnp.exp(diff)).astype(BF16)
-        intra_ref[:, start:stop] = dot(lin_vt_ref[:, :stop], weights)
+        intra_ref[:, start:stop] = dot(value_t_ref[:, :stop], weights)
 
 
 def block_numbers(axis, cores, chips):
@@ -144,43 +144,96 @@
     by_chip(position, cores, len(key_refs), body)
 
 
-def finish_kernel(
-    step, axis, cores, chips,
-    lin_qt_ref, intra_ref, cum_row_ref, summed_ref, probs_ref, factor_ref, sum_ref, *refs,
-):
-    pack_refs, (linear_ref, softmax_ref) = refs[:-2], refs[-2:]
+def carried_state(numbers, pack_refs, rows, width):
+    totals, states = [], []
+    for pack_ref in pack_refs:
+        tail = pack_ref[rows + width :, :].astype(F32)
+        totals.append(tail[0:1] + tail[1:2] + tail[2:3])
+        states.append(pack_ref[rows : rows + width, :].astype(F32))
+    carried = jnp.zeros((width, width), F32)
+    for number, state in zip(numbers, states):
+        between = jnp.where(number >= 0, 0.0, NEG)
+        for other, total in zip(numbers, totals):
+            between = between + jnp.where(other > number, 1.0, 0.0) * total
+        carried = carried + jnp.exp(between) * state
+    return carried.astype(BF16)
+
+
+def weighted_values(pack_refs, places, probs_ref, mine, rows, width):
+    out = None
+    for place, pack_ref in zip(places, pack_refs):
+        value_t = side_by_side(pack_ref, rows, width)
+        term = dot(value_t, probs_ref[place * rows : (place + 1) * rows, mine])
+        out = term if out is None else out + term
+    return out
+
+
+def write_out(step, numbers, places, pack_refs, linear_packs, refs, outs, buffers, sems):
+    lin_qt_ref, intra_ref, cum_row_ref, summed_ref, factor_ref, sum_ref, probs_ref = refs
+    width, rows = lin_qt_ref.shape
+    linear_buffer, softmax_buffer = buffers
+    softmax_copy, linear_copy = (
+        pltpu.make_async_copy(buffer, out, sems.at[place])
+        for place, (buffer, out) in enumerate(((softmax_buffer, outs[1]), (linear_buffer, outs[0])))
+    )
+    for start in range(0, rows, step):
+        mine = slice(start, start + step)
+        summed = summed_ref[:, mine]
+        if factor_ref is not None:
+            summed = summed * factor_ref[:, mine]
+        more = weighted_values(pack_refs, places, probs_ref, mine, rows, width)
+        summed = summed if more is None else summed + more
+        softmax_buffer[mine, :] = jnp.transpose((summed / sum_ref[:, mine]).astype(BF16))
+    softmax_copy.start()
+    carried = carried_state(numbers, linear_packs, rows, width)
+    for start in range(0, rows, step):
+        mine = slice(start, start + step)
+        inter = dot(carried, lin_qt_ref[:, mine])
+        raw = intra_ref[:, mine] + inter * jnp.exp(cum_row_ref[:, mine])
+        square = jnp.sum(raw * raw, axis=0, keepdims=True) * (1.0 / width)
+        linear_buffer[mine, :] = jnp.transpose((raw * lax.rsqrt(square + TINY)).astype(BF16))
+    linear_copy.start()
+    softmax_copy.wait()
+    linear_copy.wait()
+
+
+def early_kernel(step, axis, cores, chips, places, *refs):
+    head, refs = refs[:7], refs[7:]
+    packs, (linear_ref, softmax_ref, sofar_ref, *scratch) = refs[: len(places)], refs[len(places) :]
+    lin_qt_ref, intra_ref, cum_row_ref, summed_ref, factor_ref, sum_ref, probs_ref = head
     width, rows = lin_qt_ref.shape
     position, numbers = block_numbers(axis, cores, chips)
 
-    def body(count):
-        totals, states = [], []
-        for pack_ref in pack_refs[:count]:
-            tail = pack_ref[rows + 2 * width :, :].astype(F32)
-            totals.append(tail[0:1] + tail[1:2] + tail[2:3])
-            states.append(
-                pack_ref[rows : rows + width, :].astype(F32)
-                + pack_ref[rows + width : rows + 2 * width, :].astype(F32)
-            )
-        carried = jnp.zeros((width, width), F32)
-        for number, state in zip(numbers, states):
-            between = jnp.where(number >= 0, 0.0, NEG)
-            for other, total in zip(numbers, totals):
-                between = between + jnp.where(other > number, 1.0, 0.0) * total
-            carried = carried + jnp.exp(between) * state
-        carried = carried.astype(BF16)
-        values = [side_by_side(pack_ref, rows, width) for pack_ref in pack_refs[:count]]
+    @pl.when(position >= cores)
+    def _():
         for start in range(0, rows, step):
             mine = slice(start, start + step)
-            summed = summed_ref[:, mine] * factor_ref[:, mine]
-            for number, value in enumerate(values):
-                summed = summed + dot(value, probs_ref[number * rows : (number + 1) * rows, mine])
-            softmax_ref[mine, :] = jnp.transpose(summed / sum_ref[:, mine]).astype(BF16)
-            inter = dot(carried, lin_qt_ref[:, mine])
-            raw = intra_ref[:, mine] + inter * jnp.exp(cum_row_ref[:, mine])
-            square = jnp.sum(raw * raw, axis=0, keepdims=True) * (1.0 / width)
-            linear_ref[mine, :] = jnp.transpose(raw * lax.rsqrt(square + TINY)).astype(BF16)
-
-    by_chip(position, cores, len(pack_refs), body)
+            sofar_ref[:, mine] = summed_ref[:, mine] * factor_ref[:, mine] + weighted_values(
+                packs, places, probs_ref, mine, rows, width
+            )
+
+    @pl.when(position < cores)
+    def _():
+        own = cores - 1
+        write_out(
+            step, numbers[:own], places[:own], packs[:own], packs[:own], head,
+            (linear_ref, softmax_ref), scratch[:2], scratch[2],
+        )
+
+
+def late_kernel(step, axis, cores, chips, early, late, *refs):
+    lin_qt_ref, intra_ref, cum_row_ref, sofar_ref, sum_ref, probs_ref = refs[:6]
+    count = len(early) + len(late)
+    packs, (_, _, linear_ref, softmax_ref, *scratch) = refs[6 : 6 + count], refs[6 + count :]
+    position, numbers = block_numbers(axis, cores, chips)
+
+    @pl.when(position >= cores)
+    def _():
+        write_out(
+            step, numbers, late, [packs[place] for place in late], packs,
+            (lin_qt_ref, intra_ref, cum_row_ref, sofar_ref, None, sum_ref, probs_ref),
+            (linear_ref, softmax_ref), scratch[:2], scratch[2],
+        )
 
 
 def keep_in_hbm(x):
@@ -195,19 +248,25 @@
     return VMEM(x.shape, x.dtype)
 
 
-def call(body, given, operands, outs, last=False):
+def kept_in_hbm(x):
+    return pltpu.HBM(x.shape, x.dtype)
+
+
+def call(body, given, operands, outs, written=(), resumed=()):
     size = sum(math.prod(x.shape) * x.dtype.itemsize for x in (*given, *operands, *outs))
-    operands = [*map(keep_in_hbm, given), *map(keep_in_vmem, operands)]
-    if not last:
-        outs = [kept_in_vmem(x) for x in outs]
+    inside, outside = pl.BlockSpec(memory_space=VMEM), pl.BlockSpec(memory_space=pl.ANY)
+    first = len(given) + len(operands)
+    scratch = [VMEM(x.shape, x.dtype) for x in written]
     return pl.pallas_call(
         body,
-        out_shape=tuple(outs),
-        in_specs=[pl.BlockSpec(memory_space=VMEM)] * len(operands),
-        out_specs=tuple(pl.BlockSpec(memory_space=VMEM) for _ in outs),
+        out_shape=(*map(kept_in_hbm, written), *map(kept_in_vmem, outs)),
+        in_specs=[inside] * first + [outside] * len(resumed),
+        out_specs=(*[outside] * len(written), *[inside] * len(outs)),
+        scratch_shapes=[*scratch, pltpu.SemaphoreType.DMA((2,))] if written else [],
+        input_output_aliases={first + place: place for place in range(len(resumed))},
         cost_estimate=pl.CostEstimate(flops=0, bytes_accessed=size, transcendentals=0),
         compiler_params=pltpu.CompilerParams(vmem_limit_bytes=KERNEL_VMEM),
-    )(*operands)
+    )(*map(keep_in_hbm, given), *map(keep_in_vmem, operands), *map(keep_in_hbm, resumed))
 
 
 def on_device(axis, lin_query, lin_key, lin_value, log_decay, soft_query, soft_key, soft_value):
@@ -251,17 +310,19 @@
             state_kernel,
             (decay, lk, lv, sv),
             (),
-            (shape(rows + 2 * width + PAD, width, dtype=BF16), row, shape(rows, width), flat16),
+            (shape(rows + width + PAD, width, dtype=BF16), row, shape(rows, width), flat16),
         )
         packs = spread(pack)
-        lin_qt, qt, intra, top, total, summed = call(
-            functools.partial(local_kernel, scale, step),
-            (lq, lk, sq, sk),
-            (lin_vt, cum_row, cum_col, pack),
-            (flat16, flat16, flat, row, row, flat),
+        qt, top, total, summed = call(
+            functools.partial(soft_kernel, scale, step), (sq, sk), (pack,), (flat16, row, row, flat)
         )
         ring = (axis, cores, chips)
-        keys = complete(keys, intra)
+        keys = complete(keys, summed)
+        (lq, lk), _ = lax.optimization_barrier(((lq, lk), keys[cores - 1 :: cores]))
+        lin_qt, intra = call(
+            functools.partial(linear_kernel, step), (lq, lk), (lin_vt, cum_row, cum_col), (flat16, flat)
+        )
+        top, _ = lax.optimization_barrier((top, intra))
         probs, factor, sums = call(
             functools.partial(score_kernel, scale, step, *ring),
             (),
@@ -270,12 +331,22 @@
         )
         out = shape(rows, width, dtype=BF16)
         packs = complete(packs, factor)
+        late = tuple(range(cores, len(packs), cores)) if cores == 2 else ()
+        early = tuple(place for place in range(len(packs)) if place not in late)
+        *began, sofar = call(
+            functools.partial(early_kernel, step, *ring, early),
+            (),
+            (lin_qt, intra, cum_row, summed, factor, sums, probs, *(packs[place] for place in early)),
+            (flat,),
+            written=(out, out),
+        )
         return call(
-            functools.partial(finish_kernel, step, *ring),
-            (),
-            (lin_qt, intra, cum_row, summed, probs, factor, sums, *packs),
-            (out, out),
-            last=True,
+            functools.partial(late_kernel, step, *ring, early, late),
+            (),
+            (lin_qt, intra, cum_row, sofar, sums, probs, *packs),
+            (),
+            written=(out, out),
+            resumed=began,
         )
 
     outs = [

time: 14.4 us -> 13.4 us (0.931)
  the two profiles are of different devices: /device:TPU:0 before, /device:TPU:3 now
where the time goes in v2:
time: 13.4 us; the launch traced here: 13.3 us
  Pallas kernels  7.12 us (53%)
  starting transfers between devices  4.75 us (35%)
  waiting for transfers between devices  0.71 us (5%)
  between operations  0.7 us (5%)
    pallas_call x6, Pallas kernels, call(): pl.pallas_call(body, out_shape=(*map(kept_in_hbm, written), *map(kept_in_...  7.12 us
    ppermute x4, starting transfers between devices, swapped(): return lax.ppermute(x, axis, [(i, i ^ 1) for i in range(count)])  3.16 us
    ppermute x2, starting transfers between devices, across(): lax.ppermute(x, axis, [(i, (i + apart * cores) % count) for i in range(co...  1.59 us
    ppermute x4, waiting for transfers between devices, swapped(): return lax.ppermute(x, axis, [(i, i ^ 1) for i in range(count)])  0.7 us
  transfers between devices with their start and end apart: 6, of which 1 were waited for; matrix products, arithmetic and copies ran while one was open for 0% of the time, Pallas kernels for 46%

profile of v2, /device:TPU:3, one launch (start us, length us, event | category | flops | bytes accessed | tf_op | source)
XLA Modules:
  0.0 13.3 jit_solution(9400407607117685740)
XLA Ops:
  0.6 0.1 collective-permute-start
  0.7 1.6 %shard_map.86 = (bf16[656,128]{1,0:T(8,128)(2,1)S(1)}, f32[1,512]{1,0:T(1,128)S(1)}, f32[512,128]{1,0:T(8,128)S(1)}, bf16[128,512]{1,0:T(8,128)(2,1)S(1)}) custom-call(f32[1,512]{1,0:T(1,128)} %decay_ref.1, bf16[512,128]{1,0:T(8,128)(2,1)} %bitcast.8, bf16[512,128]{1,0:T(8,128)(2,1)} %bitcast.10, bf16[512,128]{1,0:T(8,128)(2,1)} %bitcast.11), custom_call_target="tpu_custom_call" | custom-call | bytes 958464 | tf_op jit(solution)/shard_map/pallas_call | solution.py:260
  2.3 1.5 %collective-permute-start.4 = (bf16[656,128]{1,0:T(8,128)(2,1)S(1)}, bf16[656,128]{1,0:T(8,128)(2,1)S(1)}, u32[]{:S(2)}, u32[]{:S(2)}) collective-permute-start(bf16[656,128]{1,0:T(8,128)(2,1)S(1)} %get-tuple-element.32.pack_ref), channel_id=1, source_target_pairs={{0,16},{8,24},{16,0},{24,8},{1,17},{9,25},{17,1},{25,9},{2,18},{10... | collective-permute-start | bytes 503816 | tf_op jit(solution)/shard_map/ppermute | solution.py:279
  3.8 1.2 %collective-permute-start.1 = (bf16[512,128]{1,0:T(8,128)(2,1)}, bf16[512,128]{1,0:T(8,128)(2,1)S(1)}, u32[]{:S(2)}, u32[]{:S(2)}) collective-permute-start(bf16[512,128]{1,0:T(8,128)(2,1)} %bitcast.17), channel_id=1, source_target_pairs={{0,8},{8,0},{16,24},{24,16},{1,9},{9,1},{17,25},{25,17},{2,10},{10... | collective-permute-start | bytes 393224 | tf_op jit(solution)/shard_map/ppermute | solution.py:284
  5.0 1.6 %shard_map.88 = (bf16[128,512]{1,0:T(8,128)(2,1)S(1)}, f32[1,512]{1,0:T(1,128)S(1)}, f32[1,512]{1,0:T(1,128)S(1)}, f32[128,512]{1,0:T(8,128)S(1)}) custom-call(bf16[512,128]{1,0:T(8,128)(2,1)} %bitcast.15, bf16[512,128]{1,0:T(8,128)(2,1)} %bitcast.18, bf16[656,128]{1,0:T(8,128)(2,1)S(1)} %get-tuple-element.32.pack_ref), custom_call_target="tpu_custom_call" | custom-call | bytes 827392 | tf_op jit(solution)/shard_map/pallas_call | solution.py:260
  6.6 0.0 collective-permute-done.refs_1_
  6.6 1.4 %collective-permute-start.2 = (bf16[512,128]{1,0:T(8,128)(2,1)S(1)}, bf16[512,128]{1,0:T(8,128)(2,1)S(1)}, u32[]{:S(2)}, u32[]{:S(2)}) collective-permute-start(bf16[512,128]{1,0:T(8,128)(2,1)S(1)} %collective-permute-done.refs_1_), channel_id=1, source_target_pairs={{0,8},{8,0},{16,24},{24,16},{1,9},{9,1},{17,25},{25,17},{2,10},{10... | collective-permute-start | bytes 393224 | tf_op jit(solution)/shard_map/ppermute | solution.py:284
  8.0 0.0 collective-permute-start.3
  8.0 1.5 %shard_map.87 = (bf16[128,512]{1,0:T(8,128)(2,1)S(1)}, f32[128,512]{1,0:T(8,128)S(1)}) custom-call(bf16[512,128]{1,0:T(8,128)(2,1)} %bitcast.12, bf16[512,128]{1,0:T(8,128)(2,1)} %bitcast.9, bf16[128,512]{1,0:T(8,128)(2,1)S(1)} %get-tuple-element.27.value_t_ref, f32[1,512]{1,0:T(1,128)S(1)} %get-tuple-element.28.cum_row_ref.refs_2_, ...), custom_call_target="tpu_custom_call" | custom-call | bytes 1050624 | tf_op jit(solution)/shard_map/pallas_call | solution.py:260
  9.4 0.0 collective-permute-done.1.refs_0_
  9.5 0.0 collective-permute-done.2.refs_2_
  9.5 1.1 %shard_map.89 = (bf16[1536,512]{1,0:T(8,128)(2,1)S(1)}, f32[1,512]{1,0:T(1,128)S(1)}, f32[1,512]{1,0:T(1,128)S(1)}) custom-call(bf16[128,512]{1,0:T(8,128)(2,1)S(1)} %get-tuple-element.34.qt_ref, f32[1,512]{1,0:T(1,128)S(1)} %get-tuple-element.36.top_ref, f32[1,512]{1,0:T(1,128)S(1)} %get-tuple-element.37.total_ref, ...), custom_call_target="tpu_custom_call" | custom-call | bytes 2105344 | tf_op jit(solution)/shard_map/pallas_call | solution.py:260
  10.6 0.0 collective-permute-done.4.refs_8_.refs_7_
  10.6 0.6 %collective-permute-start.5 = (bf16[656,128]{1,0:T(8,128)(2,1)S(1)}, bf16[656,128]{1,0:T(8,128)(2,1)S(1)}, u32[]{:S(2)}, u32[]{:S(2)}) collective-permute-start(bf16[656,128]{1,0:T(8,128)(2,1)S(1)} %collective-permute-done.4.refs_8_.refs_7_), channel_id=1, source_target_pairs={{0,8},{8,0},{16,24},{24,16},{1,9},{9,1},{17,25},{25,17},{2,10},{10... | collective-permute-start | bytes 503816 | tf_op jit(solution)/shard_map/ppermute | solution.py:284
  11.2 0.0 collective-permute-done.3.refs_7_.refs_6_
  11.2 0.3 %shard_map.90 = (bf16[512,128]{1,0:T(8,128)(2,1)}, bf16[512,128]{1,0:T(8,128)(2,1)}, f32[128,512]{1,0:T(8,128)S(1)}) custom-call(bf16[128,512]{1,0:T(8,128)(2,1)S(1)} %get-tuple-element.30.refs_0_, f32[128,512]{1,0:T(8,128)S(1)} %get-tuple-element.31.refs_1_, f32[1,512]{1,0:T(1,128)S(1)} %get-tuple-element.28.cum_row_ref.refs_2_, ...), custom_call_target="tpu_custom_call" | custom-call | bytes 2832384 | tf_op jit(solution)/shard_map/pallas_call | solution.py:260
  11.5 0.7 %collective-permute-done.5.refs_8_ = bf16[656,128]{1,0:T(8,128)(2,1)S(1)} collective-permute-done((bf16[656,128]{1,0:T(8,128)(2,1)S(1)}, bf16[656,128]{1,0:T(8,128)(2,1)S(1)}, u32[]{:S(2)}, u32[]{:S(2)}) %collective-permute-start.5) | collective-permute-done | bytes 167968 | tf_op jit(solution)/shard_map/ppermute | solution.py:284
  12.2 1.1 %shard_map.91 = (bf16[512,128]{1,0:T(8,128)(2,1)}, bf16[512,128]{1,0:T(8,128)(2,1)}) custom-call(bf16[128,512]{1,0:T(8,128)(2,1)S(1)} %get-tuple-element.30.refs_0_, f32[128,512]{1,0:T(8,128)S(1)} %get-tuple-element.31.refs_1_, f32[1,512]{1,0:T(1,128)S(1)} %get-tuple-element.28.cum_row_ref.refs_2_, ...), custom_call_target="tpu_custom_call", output_to_operand_aliasing={{0}: (9, {}), {1}: (10, {})} | custom-call | bytes 2736128 | tf_op jit(solution)/shard_map/pallas_call | solution.py:260
Async XLA Ops:
  0.6 6.0 %collective-permute-start = (bf16[512,128]{1,0:T(8,128)(2,1)}, bf16[512,128]{1,0:T(8,128)(2,1)S(1)}, u32[]{:S(2)}, u32[]{:S(2)}) collective-permute-start(bf16[512,128]{1,0:T(8,128)(2,1)} %bitcast.16), channel_id=1, source_target_pairs={{0,16},{8,24},{16,0},{24,8},{1,17},{9,25},{17,1},{25,9},{2,18},{10... | collective-permute-start | bytes 393224 | tf_op jit(solution)/shard_map/ppermute | solution.py:279
  2.3 8.3 %collective-permute-start.4 = (bf16[656,128]{1,0:T(8,128)(2,1)S(1)}, bf16[656,128]{1,0:T(8,128)(2,1)S(1)}, u32[]{:S(2)}, u32[]{:S(2)}) collective-permute-start(bf16[656,128]{1,0:T(8,128)(2,1)S(1)} %get-tuple-element.32.pack_ref), channel_id=1, source_target_pairs={{0,16},{8,24},{16,0},{24,8},{1,17},{9,25},{17,1},{25,9},{2,18},{10... | collective-permute-start | bytes 503816 | tf_op jit(solution)/shard_map/ppermute | solution.py:279
  3.8 5.6 %collective-permute-start.1 = (bf16[512,128]{1,0:T(8,128)(2,1)}, bf16[512,128]{1,0:T(8,128)(2,1)S(1)}, u32[]{:S(2)}, u32[]{:S(2)}) collective-permute-start(bf16[512,128]{1,0:T(8,128)(2,1)} %bitcast.17), channel_id=1, source_target_pairs={{0,8},{8,0},{16,24},{24,16},{1,9},{9,1},{17,25},{25,17},{2,10},{10... | collective-permute-start | bytes 393224 | tf_op jit(solution)/shard_map/ppermute | solution.py:284
  6.6 2.8 %collective-permute-start.2 = (bf16[512,128]{1,0:T(8,128)(2,1)S(1)}, bf16[512,128]{1,0:T(8,128)(2,1)S(1)}, u32[]{:S(2)}, u32[]{:S(2)}) collective-permute-start(bf16[512,128]{1,0:T(8,128)(2,1)S(1)} %collective-permute-done.refs_1_), channel_id=1, source_target_pairs={{0,8},{8,0},{16,24},{24,16},{1,9},{9,1},{17,25},{25,17},{2,10},{10... | collective-permute-start | bytes 393224 | tf_op jit(solution)/shard_map/ppermute | solution.py:284
  8.0 3.2 %collective-permute-start.3 = (bf16[656,128]{1,0:T(8,128)(2,1)S(1)}, bf16[656,128]{1,0:T(8,128)(2,1)S(1)}, u32[]{:S(2)}, u32[]{:S(2)}) collective-permute-start(bf16[656,128]{1,0:T(8,128)(2,1)S(1)} %get-tuple-element.32.pack_ref), channel_id=1, source_target_pairs={{0,8},{8,0},{16,24},{24,16},{1,9},{9,1},{17,25},{25,17},{2,10},{10... | collective-permute-start | bytes 503816 | tf_op jit(solution)/shard_map/ppermute | solution.py:284
  10.6 1.6 %collective-permute-start.5 = (bf16[656,128]{1,0:T(8,128)(2,1)S(1)}, bf16[656,128]{1,0:T(8,128)(2,1)S(1)}, u32[]{:S(2)}, u32[]{:S(2)}) collective-permute-start(bf16[656,128]{1,0:T(8,128)(2,1)S(1)} %collective-permute-done.4.refs_8_.refs_7_), channel_id=1, source_target_pairs={{0,8},{8,0},{16,24},{24,16},{1,9},{9,1},{17,25},{25,17},{2,10},{10... | collective-permute-start | bytes 503816 | tf_op jit(solution)/shard_map/ppermute | solution.py:284

commit v3 on v2

--- a/solution.py
+++ b/solution.py
@@ -47,16 +47,37 @@
 
 
 def state_kernel(
-    decay_ref, key_ref, value_ref, soft_value_ref, pack_ref, cum_row_ref, cum_col_ref, value_t_ref
+    decay_hbm, key_hbm, value_hbm, soft_value_hbm, query_hbm, soft_query_hbm, soft_key_hbm,
+    pack_ref, cum_row_ref, cum_col_ref, value_t_ref, key_ref, query_ref, soft_query_ref, soft_key_ref,
+    decay_ref, value_ref, soft_value_ref, sems,
 ):
+    copies = [
+        pltpu.make_async_copy(source, target, sems.at[place])
+        for place, (source, target) in enumerate(
+            (
+                (decay_hbm, decay_ref),
+                (key_hbm, key_ref),
+                (value_hbm, value_ref),
+                (soft_value_hbm, soft_value_ref),
+                (soft_query_hbm, soft_query_ref),
+                (soft_key_hbm, soft_key_ref),
+                (query_hbm, query_ref),
+            )
+        )
+    ]
+    for copy in copies:
+        copy.start()
     rows, width = key_ref.shape
+    upto = (iota((rows, rows), 0) <= iota((rows, rows), 1)).astype(F32).astype(BF16)
+    copies[0].wait()
     parts = select_rows(three_parts(decay_ref[...]), PAD, rows)
-    upto = (iota((rows, rows), 0) <= iota((rows, rows), 1)).astype(F32).astype(BF16)
     cum_row = jnp.sum(dot(parts, upto), axis=0, keepdims=True)
     cum_row_ref[...] = cum_row
     cum_col = jnp.transpose(jnp.broadcast_to(cum_row, (width, rows)))
     cum_col_ref[...] = cum_col
     total = cum_col[rows - 1 :, :]
+    for copy in copies[1:4]:
+        copy.wait()
     decayed = (key_ref[...].astype(F32) * jnp.exp(total - cum_col)).astype(BF16)
     value_t = jnp.transpose(value_ref[...])
     value_t_ref[...] = value_t
@@ -65,6 +86,8 @@
         pack_ref[left : left + width, :] = jnp.transpose(soft_value_ref[left : left + width, :])
     pack_ref[rows : rows + width, :] = state_t.astype(BF16)
     pack_ref[rows + width :, :] = select_rows(three_parts(total), PAD, width)
+    for copy in copies[4:]:
+        copy.wait()
 
 
 def soft_kernel(scale, step, q_ref, k_ref, pack_ref, qt_ref, top_ref, total_ref, summed_ref):
@@ -222,9 +245,10 @@
 
 
 def late_kernel(step, axis, cores, chips, early, late, *refs):
+    refs = refs[2:]
     lin_qt_ref, intra_ref, cum_row_ref, sofar_ref, sum_ref, probs_ref = refs[:6]
     count = len(early) + len(late)
-    packs, (_, _, linear_ref, softmax_ref, *scratch) = refs[6 : 6 + count], refs[6 + count :]
+    packs, (linear_ref, softmax_ref, *scratch) = refs[6 : 6 + count], refs[6 + count :]
     position, numbers = block_numbers(axis, cores, chips)
 
     @pl.when(position >= cores)
@@ -252,21 +276,22 @@
     return pltpu.HBM(x.shape, x.dtype)
 
 
-def call(body, given, operands, outs, written=(), resumed=()):
+def call(body, operands, outs, given=(), written=(), resumed=(), scratch=()):
     size = sum(math.prod(x.shape) * x.dtype.itemsize for x in (*given, *operands, *outs))
     inside, outside = pl.BlockSpec(memory_space=VMEM), pl.BlockSpec(memory_space=pl.ANY)
-    first = len(given) + len(operands)
-    scratch = [VMEM(x.shape, x.dtype) for x in written]
+    hbm = (*given, *resumed)
+    scratch = [VMEM(x.shape, x.dtype) for x in (*scratch, *written)]
+    moved = len(given) + len(written)
     return pl.pallas_call(
         body,
         out_shape=(*map(kept_in_hbm, written), *map(kept_in_vmem, outs)),
-        in_specs=[inside] * first + [outside] * len(resumed),
+        in_specs=[outside] * len(hbm) + [inside] * len(operands),
         out_specs=(*[outside] * len(written), *[inside] * len(outs)),
-        scratch_shapes=[*scratch, pltpu.SemaphoreType.DMA((2,))] if written else [],
-        input_output_aliases={first + place: place for place in range(len(resumed))},
+        scratch_shapes=[*scratch, pltpu.SemaphoreType.DMA((moved,))] if moved else [],
+        input_output_aliases={place: place for place in range(len(resumed))},
         cost_estimate=pl.CostEstimate(flops=0, bytes_accessed=size, transcendentals=0),
         compiler_params=pltpu.CompilerParams(vmem_limit_bytes=KERNEL_VMEM),
-    )(*map(keep_in_hbm, given), *map(keep_in_vmem, operands), *map(keep_in_hbm, resumed))
+    )(*map(keep_in_hbm, hbm), *map(keep_in_vmem, operands))
 
 
 def on_device(axis, lin_query, lin_key, lin_value, log_decay, soft_query, soft_key, soft_value):
@@ -300,52 +325,54 @@
     def one_head(lq, lk, lv, decay, sq, sk, sv):
         step = math.gcd(rows, 256)
         scale = math.log2(math.e) / math.sqrt(width)
+        ring = (axis, cores, chips)
 
         def shape(*dims, dtype=F32):
             return jax.ShapeDtypeStruct(dims, dtype)
 
         row, flat, flat16 = shape(1, rows), shape(width, rows), shape(width, rows, dtype=BF16)
+        block = shape(rows, width, dtype=BF16)
         keys = spread(sk)
-        pack, cum_row, cum_col, lin_vt = call(
+        pack, cum_row, cum_col, lin_vt, lk, lq, sq, sk = call(
             state_kernel,
-            (decay, lk, lv, sv),
             (),
-            (shape(rows + width + PAD, width, dtype=BF16), row, shape(rows, width), flat16),
-        )
+            (
+                shape(rows + width + PAD, width, dtype=BF16), row, shape(rows, width), flat16,
+                block, block, block, block,
+            ),
+            given=(decay, lk, lv, sv, lq, sq, sk),
+            scratch=(row, block, block),
+        )
+        qt, top, total, summed = call(
+            functools.partial(soft_kernel, scale, step), (sq, sk, pack), (flat16, row, row, flat)
+        )
+        (pack, lin_vt), _ = lax.optimization_barrier(((pack, lin_vt), summed))
         packs = spread(pack)
-        qt, top, total, summed = call(
-            functools.partial(soft_kernel, scale, step), (sq, sk), (pack,), (flat16, row, row, flat)
-        )
-        ring = (axis, cores, chips)
         keys = complete(keys, summed)
         (lq, lk), _ = lax.optimization_barrier(((lq, lk), keys[cores - 1 :: cores]))
         lin_qt, intra = call(
-            functools.partial(linear_kernel, step), (lq, lk), (lin_vt, cum_row, cum_col), (flat16, flat)
+            functools.partial(linear_kernel, step), (lq, lk, lin_vt, cum_row, cum_col), (flat16, flat)
         )
         top, _ = lax.optimization_barrier((top, intra))
         probs, factor, sums = call(
             functools.partial(score_kernel, scale, step, *ring),
-            (),
             (qt, top, total, *keys),
             (shape(len(keys) * rows, rows, dtype=BF16), row, row),
         )
-        out = shape(rows, width, dtype=BF16)
         packs = complete(packs, factor)
         late = tuple(range(cores, len(packs), cores)) if cores == 2 else ()
         early = tuple(place for place in range(len(packs)) if place not in late)
         *began, sofar = call(
             functools.partial(early_kernel, step, *ring, early),
-            (),
             (lin_qt, intra, cum_row, summed, factor, sums, probs, *(packs[place] for place in early)),
             (flat,),
-            written=(out, out),
+            written=(block, block),
         )
         return call(
             functools.partial(late_kernel, step, *ring, early, late),
-            (),
             (lin_qt, intra, cum_row, sofar, sums, probs, *packs),
             (),
-            written=(out, out),
+            written=(block, block),
             resumed=began,
         )
 

time: 13.4 us -> 13 us (0.970)
  the two profiles are of different devices: /device:TPU:3 before, /device:TPU:0 now
where the time goes in v3:
time: 13 us; the launch traced here: 12.8 us
  waiting for transfers between devices  4.48 us (34%)
  Pallas kernels  4 us (31%)
  starting transfers between devices  3.67 us (28%)
  between operations  0.68 us (5%)
    pallas_call x6, Pallas kernels, call(): pl.pallas_call(body, out_shape=(*map(kept_in_hbm, written), *map(kept_in_...  4 us
    ppermute x2, waiting for transfers between devices, across(): lax.ppermute(x, axis, [(i, (i + apart * cores) % count) for i in range(co...  3.82 us
    ppermute x2, starting transfers between devices, across(): lax.ppermute(x, axis, [(i, (i + apart * cores) % count) for i in range(co...  3.09 us
    ppermute x4, waiting for transfers between devices, swapped(): return lax.ppermute(x, axis, [(i, i ^ 1) for i in range(count)])  0.66 us
    ppermute x4, starting transfers between devices, swapped(): return lax.ppermute(x, axis, [(i, i ^ 1) for i in range(count)])  0.58 us
  transfers between devices with their start and end apart: 6, of which 4 were waited for; matrix products, arithmetic and copies ran while one was open for 0% of the time, Pallas kernels for 31%

profile of v3, /device:TPU:0, one launch (start us, length us, event | category | flops | bytes accessed | tf_op | source)
XLA Modules:
  0.0 12.8 jit_solution(14431274660658289075)
XLA Ops:
  0.6 3.0 %collective-permute-start = (bf16[512,128]{1,0:T(8,128)(2,1)}, bf16[512,128]{1,0:T(8,128)(2,1)S(1)}, u32[]{:S(2)}, u32[]{:S(2)}) collective-permute-start(bf16[512,128]{1,0:T(8,128)(2,1)} %bitcast.15), channel_id=1, source_target_pairs={{0,16},{8,24},{16,0},{24,8},{1,17},{9,25},{17,1},{25,9},{2,18},{10... | collective-permute-start | bytes 393224 | tf_op jit(solution)/shard_map/ppermute | solution.py:304
  3.6 1.3 %shard_map.86 = (bf16[656,128]{1,0:T(8,128)(2,1)S(1)}, f32[1,512]{1,0:T(1,128)S(1)}, f32[512,128]{1,0:T(8,128)S(1)}, bf16[128,512]{1,0:T(8,128)(2,1)S(1)}, bf16[...) custom-call(f32[1,512]{1,0:T(1,128)} %decay_hbm.1, ...), custom_call_target="tpu_custom_call" | custom-call | bytes 1875968 | tf_op jit(solution)/shard_map/pallas_call | solution.py:285
  5.0 0.6 %shard_map.87 = (bf16[128,512]{1,0:T(8,128)(2,1)S(1)}, f32[1,512]{1,0:T(1,128)S(1)}, f32[1,512]{1,0:T(1,128)S(1)}, f32[128,512]{1,0:T(8,128)S(1)}) custom-call(bf16[512,128]{1,0:T(8,128)(2,1)S(1)} %get-tuple-element.37.q_ref, bf16[512,128]{1,0:T(8,128)(2,1)S(1)} %get-tuple-element.38.k_ref, bf16[656,128]{1,0:T(8,128)(2,1)S(1)} %get-tuple-element.53.pack_ref), custom_call_target="tpu_custom_call" | custom-call | bytes 827392 | tf_op jit(solution)/shard_map/pallas_call | solution.py:285
  5.6 0.1 collective-permute-start.4
  5.7 0.1 collective-permute-start.1
  5.7 2.0 %collective-permute-done.refs_1_ = bf16[512,128]{1,0:T(8,128)(2,1)S(1)} collective-permute-done((bf16[512,128]{1,0:T(8,128)(2,1)}, bf16[512,128]{1,0:T(8,128)(2,1)S(1)}, u32[]{:S(2)}, u32[]{:S(2)}) %collective-permute-start) | collective-permute-done | bytes 131104 | tf_op jit(solution)/shard_map/ppermute | solution.py:304
  7.7 0.0 collective-permute-start.2
  7.7 0.5 %collective-permute-start.3 = (bf16[656,128]{1,0:T(8,128)(2,1)S(1)}, bf16[656,128]{1,0:T(8,128)(2,1)S(1)}, u32[]{:S(2)}, u32[]{:S(2)}) collective-permute-start(bf16[656,128]{1,0:T(8,128)(2,1)S(1)} %get-tuple-element.53.pack_ref), channel_id=1, source_target_pairs={{0,8},{8,0},{16,24},{24,16},{1,9},{9,1},{17,25},{25,17},{2,10},{10... | collective-permute-start | bytes 503816 | tf_op jit(solution)/shard_map/ppermute | solution.py:309
  8.2 0.5 %shard_map.88 = (bf16[128,512]{1,0:T(8,128)(2,1)S(1)}, f32[128,512]{1,0:T(8,128)S(1)}) custom-call(bf16[512,128]{1,0:T(8,128)(2,1)S(1)} %get-tuple-element.33.q_ref, bf16[512,128]{1,0:T(8,128)(2,1)S(1)} %get-tuple-element.34.k_ref, bf16[128,512]{1,0:T(8,128)(2,1)S(1)} %get-tuple-element.40.value_t_ref, ...), custom_call_target="tpu_custom_call" | custom-call | bytes 1050624 | tf_op jit(solution)/shard_map/pallas_call | solution.py:285
  8.7 0.0 collective-permute-done.1.refs_0_
  8.8 0.3 %collective-permute-done.2.refs_2_ = bf16[512,128]{1,0:T(8,128)(2,1)S(1)} collective-permute-done((bf16[512,128]{1,0:T(8,128)(2,1)S(1)}, bf16[512,128]{1,0:T(8,128)(2,1)S(1)}, u32[]{:S(2)}, u32[]{:S(2)}) %collective-permute-start.2) | collective-permute-done | bytes 131104 | tf_op jit(solution)/shard_map/ppermute | solution.py:309
  9.1 0.5 %shard_map.89 = (bf16[1536,512]{1,0:T(8,128)(2,1)S(1)}, f32[1,512]{1,0:T(1,128)S(1)}, f32[1,512]{1,0:T(1,128)S(1)}) custom-call(bf16[128,512]{1,0:T(8,128)(2,1)S(1)} %get-tuple-element.45.qt_ref, f32[1,512]{1,0:T(1,128)S(1)} %get-tuple-element.47.top_ref, f32[1,512]{1,0:T(1,128)S(1)} %get-tuple-element.48.total_ref, ...), custom_call_target="tpu_custom_call" | custom-call | bytes 2105344 | tf_op jit(solution)/shard_map/pallas_call | solution.py:285
  9.6 1.8 %collective-permute-done.4.refs_8_.refs_9_ = bf16[656,128]{1,0:T(8,128)(2,1)S(1)} collective-permute-done((bf16[656,128]{1,0:T(8,128)(2,1)S(1)}, bf16[656,128]{1,0:T(8,128)(2,1)S(1)}, u32[]{:S(2)}, u32[]{:S(2)}) %collective-permute-start.4) | collective-permute-done | bytes 167968 | tf_op jit(solution)/shard_map/ppermute | solution.py:304
  11.4 0.0 collective-permute-start.5
  11.4 0.0 collective-permute-done.3.refs_7_.refs_8_
  11.4 1.1 %shard_map.90 = (bf16[512,128]{1,0:T(8,128)(2,1)}, bf16[512,128]{1,0:T(8,128)(2,1)}, f32[128,512]{1,0:T(8,128)S(1)}) custom-call(bf16[128,512]{1,0:T(8,128)(2,1)S(1)} %get-tuple-element.43.refs_0_.refs_2_, f32[128,512]{1,0:T(8,128)S(1)} %get-tuple-element.44.refs_1_.refs_3_, f32[1,512]{1,0:T(1,128)S(1)} %get-tuple-element.41.cum_row_ref.refs_2_.refs_4_, ...), custom_call_target="tpu_custom_call" | custom-call | bytes 2832384 | tf_op jit(solution)/shard_map/pallas_call | solution.py:285
  12.5 0.3 %collective-permute-done.5.refs_10_ = bf16[656,128]{1,0:T(8,128)(2,1)S(1)} collective-permute-done((bf16[656,128]{1,0:T(8,128)(2,1)S(1)}, bf16[656,128]{1,0:T(8,128)(2,1)S(1)}, u32[]{:S(2)}, u32[]{:S(2)}) %collective-permute-start.5) | collective-permute-done | bytes 167968 | tf_op jit(solution)/shard_map/ppermute | solution.py:309
  (1 shorter events, 0.0 us)
Async XLA Ops:
  0.6 7.1 %collective-permute-start = (bf16[512,128]{1,0:T(8,128)(2,1)}, bf16[512,128]{1,0:T(8,128)(2,1)S(1)}, u32[]{:S(2)}, u32[]{:S(2)}) collective-permute-start(bf16[512,128]{1,0:T(8,128)(2,1)} %bitcast.15), channel_id=1, source_target_pairs={{0,16},{8,24},{16,0},{24,8},{1,17},{9,25},{17,1},{25,9},{2,18},{10... | collective-permute-start | bytes 393224 | tf_op jit(solution)/shard_map/ppermute | solution.py:304
  5.6 5.8 %collective-permute-start.4 = (bf16[656,128]{1,0:T(8,128)(2,1)S(1)}, bf16[656,128]{1,0:T(8,128)(2,1)S(1)}, u32[]{:S(2)}, u32[]{:S(2)}) collective-permute-start(bf16[656,128]{1,0:T(8,128)(2,1)S(1)} %get-tuple-element.53.pack_ref), channel_id=1, source_target_pairs={{0,16},{8,24},{16,0},{24,8},{1,17},{9,25},{17,1},{25,9},{2,18},{10... | collective-permute-start | bytes 503816 | tf_op jit(solution)/shard_map/ppermute | solution.py:304
  5.7 3.1 %collective-permute-start.1 = (bf16[512,128]{1,0:T(8,128)(2,1)}, bf16[512,128]{1,0:T(8,128)(2,1)S(1)}, u32[]{:S(2)}, u32[]{:S(2)}) collective-permute-start(bf16[512,128]{1,0:T(8,128)(2,1)} %bitcast.17), channel_id=1, source_target_pairs={{0,8},{8,0},{16,24},{24,16},{1,9},{9,1},{17,25},{25,17},{2,10},{10... | collective-permute-start | bytes 393224 | tf_op jit(solution)/shard_map/ppermute | solution.py:309
  7.7 1.3 %collective-permute-start.2 = (bf16[512,128]{1,0:T(8,128)(2,1)S(1)}, bf16[512,128]{1,0:T(8,128)(2,1)S(1)}, u32[]{:S(2)}, u32[]{:S(2)}) collective-permute-start(bf16[512,128]{1,0:T(8,128)(2,1)S(1)} %collective-permute-done.refs_1_), channel_id=1, source_target_pairs={{0,8},{8,0},{16,24},{24,16},{1,9},{9,1},{17,25},{25,17},{2,10},{10... | collective-permute-start | bytes 393224 | tf_op jit(solution)/shard_map/ppermute | solution.py:309
  7.7 3.7 %collective-permute-start.3 = (bf16[656,128]{1,0:T(8,128)(2,1)S(1)}, bf16[656,128]{1,0:T(8,128)(2,1)S(1)}, u32[]{:S(2)}, u32[]{:S(2)}) collective-permute-start(bf16[656,128]{1,0:T(8,128)(2,1)S(1)} %get-tuple-element.53.pack_ref), channel_id=1, source_target_pairs={{0,8},{8,0},{16,24},{24,16},{1,9},{9,1},{17,25},{25,17},{2,10},{10... | collective-permute-start | bytes 503816 | tf_op jit(solution)/shard_map/ppermute | solution.py:309
  11.4 1.4 %collective-permute-start.5 = (bf16[656,128]{1,0:T(8,128)(2,1)S(1)}, bf16[656,128]{1,0:T(8,128)(2,1)S(1)}, u32[]{:S(2)}, u32[]{:S(2)}) collective-permute-start(bf16[656,128]{1,0:T(8,128)(2,1)S(1)} %collective-permute-done.4.refs_8_.refs_9_), channel_id=1, source_target_pairs={{0,8},{8,0},{16,24},{24,16},{1,9},{9,1},{17,25},{25,17},{2,10},{10... | collective-permute-start | bytes 503816 | tf_op jit(solution)/shard_map/ppermute | solution.py:309

commit v4 on v3

v4 whole, which is shorter than its diff:
```python
import functools
import math

import jax
import jax.numpy as jnp
from jax import lax
from jax.experimental import pallas as pl
from jax.experimental.pallas import tpu as pltpu
from jax.sharding import PartitionSpec as P

NEG = -1e30
TINY = 1e-6
PAD = 16
KERNEL_VMEM = 16 * 2**20
F32 = jnp.float32
BF16 = jnp.bfloat16
VMEM = pltpu.VMEM


def dot(a, b):
    return lax.dot_general(a, b, (((1,), (0,)), ((), ())), preferred_element_type=F32)


def three_parts(x):
    high = x.astype(BF16)
    rest = x - high.astype(F32)
    middle = rest.astype(BF16)
    low = (rest - middle.astype(F32)).astype(BF16)
    return high, middle, low


def iota(shape, dim):
    return lax.broadcasted_iota(jnp.int32, shape, dim)


def select_rows(parts, rows, width):
    row = iota((rows, width), 0)
    out = jnp.zeros((rows, width), F32)
    for number, part in enumerate(parts):
        out = jnp.where(row == number, part.astype(F32), out)
    return out.astype(BF16)


def side_by_side(ref, rows, width):
    pieces = [ref[left : left + width, :] for left in range(0, rows, width)]
    return pieces[0] if len(pieces) == 1 else jnp.concatenate(pieces, axis=1)


def state_kernel(
    decay_hbm, key_hbm, value_hbm, soft_value_hbm, query_hbm, soft_query_hbm, soft_key_hbm,
    pack_ref, cum_row_ref, cum_col_ref, value_t_ref, key_ref, query_ref, soft_query_ref, soft_key_ref,
    decay_ref, value_ref, soft_value_ref, sems,
):
    rows, width = key_ref.shape
    copies = [
        pltpu.make_async_copy(source, target, sems.at[place])
        for place, (source, target) in enumerate(
            (
                (decay_hbm, decay_ref),
                (key_hbm, key_ref),
                (value_hbm, value_ref),
                (soft_value_hbm, soft_value_ref),
                (soft_query_hbm, soft_query_ref),
                (soft_key_hbm, soft_key_ref),
                (query_hbm, query_ref),
            )
        )
    ]
    for copy in copies:
        copy.start()
    upto = (iota((rows, rows), 0) <= iota((rows, rows), 1)).astype(F32).astype(BF16)
    copies[0].wait()
    parts = select_rows(three_parts(decay_ref[...]), PAD, rows)
    cum_row = jnp.sum(dot(parts, upto), axis=0, keepdims=True)
    cum_row_ref[...] = cum_row
    cum_col = jnp.transpose(jnp.broadcast_to(cum_row, (width, rows)))
    cum_col_ref[...] = cum_col
    total = cum_col[rows - 1 :, :]
    for copy in copies[1:4]:
        copy.wait()
    decayed = (key_ref[...].astype(F32) * jnp.exp(total - cum_col)).astype(BF16)
    value_t = jnp.transpose(value_ref[...])
    value_t_ref[...] = value_t
    pack_ref[rows : rows + width, :] = dot(value_t, decayed).astype(BF16)
    pack_ref[rows + width :, :] = select_rows(three_parts(total), PAD, width)
    for left in range(0, rows, width):
        pack_ref[left : left + width, :] = jnp.transpose(soft_value_ref[left : left + width, :])
    for copy in copies[4:]:
        copy.wait()


def soft_kernel(scale, step, q_ref, k_ref, pack_ref, qt_ref, top_ref, total_ref, summed_ref):
    rows, width = q_ref.shape
    qt_ref[...] = jnp.transpose(q_ref[...])
    value_t = side_by_side(pack_ref, rows, width)
    keep = iota((step, step), 0) <= iota((step, step), 1)
    for start in range(0, rows, step):
        stop = start + step
        scores = dot(k_ref[:stop, :], qt_ref[:, start:stop])
        last = jnp.where(keep, scores[start:, :], NEG)
        scores = jnp.concatenate([scores[:start, :], last], axis=0) if start else last
        top = jnp.max(scores, axis=0, keepdims=True)
        probs = jnp.exp2((scores - top) * scale)
        top_ref[:, start:stop] = top
        total_ref[:, start:stop] = jnp.sum(probs, axis=0, keepdims=True)
        summed_ref[:, start:stop] = dot(value_t[:, :stop], probs.astype(BF16))


def linear_kernel(step, q_ref, k_ref, value_t_ref, cum_row_ref, cum_col_ref, qt_ref, intra_ref):
    rows, width = q_ref.shape
    qt_ref[...] = jnp.transpose(q_ref[...])
    keep = iota((step, step), 0) <= iota((step, step), 1)
    for start in range(0, rows, step):
        stop = start + step
        scores = dot(k_ref[:stop, :], qt_ref[:, start:stop])
        cum_t = cum_row_ref[:, start:stop]
        cum_s = jnp.concatenate([cum_col_ref[:stop, :]] * (step // width), axis=1)
        diff = cum_t - cum_s
        last = jnp.where(keep, diff[start:, :], NEG)
        diff = jnp.concatenate([diff[:start, :], last], axis=0) if start else last
        weights = (scores * jnp.exp(diff)).astype(BF16)
        intra_ref[:, start:stop] = dot(value_t_ref[:, :stop], weights)


def block_numbers(axis, cores, chips):
    position = lax.axis_index(axis)
    if cores == 1:
        return position, [position - apart for apart in range(1, chips)]
    other = lax.rem(position, 2)
    partner = position + 1 - 2 * other
    numbers = [jnp.where(other == 1, position - 1, -1)]
    for apart in range(1, chips):
        numbers += [position - 2 * apart, partner - 2 * apart]
    return position, numbers


def normalized(raw):
    square = jnp.sum(raw * raw, axis=0, keepdims=True) * (1.0 / raw.shape[0])
    return jnp.transpose((raw * lax.rsqrt(square + TINY)).astype(BF16))


def put_linear(step, carried, qt_ref, intra_ref, cum_row_ref, buffer):
    for start in range(0, qt_ref.shape[1], step):
        mine = slice(start, start + step)
        inter = dot(carried, qt_ref[:, mine])
        buffer[mine, :] = normalized(intra_ref[:, mine] + inter * jnp.exp(cum_row_ref[:, mine]))


def score_kernel(scale, step, axis, cores, chips, *refs):
    qt_ref, top_ref, total_ref, summed_ref, lin_qt_ref, intra_ref, cum_row_ref = refs[:7]
    near_packs, refs = refs[7 : 6 + cores], refs[6 + cores :]
    *key_refs, linear_ref, softmax_ref, probs_ref, factor_ref, sum_ref = refs[:-3]
    linear_buffer, softmax_buffer, sems = refs[-3:]
    width, rows = qt_ref.shape
    position, numbers = block_numbers(axis, cores, chips)
    away = [jnp.where(number >= 0, 0.0, NEG) for number in numbers]

    def weights(mine, keys):
        query = qt_ref[:, mine]
        old = top_ref[:, mine]
        scores = [dot(key, query) for key in keys]
        top = old
        for score, off in zip(scores, away):
            top = jnp.maximum(top, jnp.max(score, axis=0, keepdims=True) + off)
        factor = jnp.exp2((old - top) * scale)
        total = total_ref[:, mine] * factor
        probs = []
        for score, off in zip(scores, away):
            prob = jnp.exp2((score - (top - off)) * scale)
            total = total + jnp.sum(prob, axis=0, keepdims=True)
            probs.append(prob.astype(BF16))
        return probs, factor, total

    keys = [key_ref[...] for key_ref in key_refs]

    @pl.when(position >= cores)
    def _():
        for start in range(0, rows, step):
            mine = slice(start, start + step)
            probs, factor, total = weights(mine, keys)
            for place, prob in enumerate(probs):
                probs_ref[place * rows : (place + 1) * rows, mine] = prob
            factor_ref[:, mine] = factor
            sum_ref[:, mine] = total

    @pl.when(position < cores)
    def _():
        linear_copy = pltpu.make_async_copy(linear_buffer, linear_ref, sems.at[0])
        softmax_copy = pltpu.make_async_copy(softmax_buffer, softmax_ref, sems.at[1])
        for start in range(0, rows, step):
            mine = slice(start, start + step)
            probs, factor, total = weights(mine, keys[: cores - 1])
            summed = summed_ref[:, mine] * factor
            for pack_ref, prob in zip(near_packs, probs):
                summed = summed + dot(side_by_side(pack_ref, rows, width), prob)
            softmax_buffer[mine, :] = jnp.transpose((summed / total).astype(BF16))
        softmax_copy.start()
        carried = jnp.zeros((width, width), F32)
        for pack_ref in near_packs:
            carried = jnp.where(position == 1, pack_ref[rows : rows + width, :].astype(F32), carried)
        put_linear(step, carried.astype(BF16), lin_qt_ref, intra_ref, cum_row_ref, linear_buffer)
        linear_copy.start()
        softmax_copy.wait()
        linear_copy.wait()


def weighted_values(refs, places, probs_ref, mine, rows, width):
    out = None
    for place, ref in zip(places, refs):
        term = dot(side_by_side(ref, rows, width), probs_ref[place * rows : (place + 1) * rows, mine])
        out = term if out is None else out + term
    return out


def early_kernel(step, axis, cores, places, *refs):
    summed_ref, factor_ref, probs_ref, *packs, sofar_ref = refs
    width, rows = summed_ref.shape

    @pl.when(lax.axis_index(axis) >= cores)
    def _():
        for start in range(0, rows, step):
            mine = slice(start, start + step)
            sofar_ref[:, mine] = summed_ref[:, mine] * factor_ref[:, mine] + weighted_values(
                packs, places, probs_ref, mine, rows, width
            )


def carried_state(numbers, packs, rows, width):
    totals, states = [], []
    for pack_ref in packs:
        tail = pack_ref[rows + width : rows + width + PAD, :].astype(F32)
        totals.append(tail[0:1] + tail[1:2] + tail[2:3])
        states.append(pack_ref[rows : rows + width, :].astype(F32))
    carried = jnp.zeros((width, width), F32)
    for number, state in zip(numbers, states):
        between = jnp.where(number >= 0, 0.0, NEG)
        for other, total in zip(numbers, totals):
            between = between + jnp.where(other > number, 1.0, 0.0) * total
        carried = carried + jnp.exp(between) * state
    return carried.astype(BF16)


def late_kernel(step, axis, cores, chips, late, *refs):
    lin_qt_ref, intra_ref, cum_row_ref, sofar_ref, sum_ref, probs_ref = refs[2:8]
    *blocks, linear_ref, softmax_ref, linear_buffer, softmax_buffer, sems = refs[8:]
    width, rows = lin_qt_ref.shape
    position, numbers = block_numbers(axis, cores, chips)

    @pl.when(position >= cores)
    def _():
        linear_copy = pltpu.make_async_copy(linear_buffer, linear_ref, sems.at[0])
        softmax_copy = pltpu.make_async_copy(softmax_buffer, softmax_ref, sems.at[1])
        for start in range(0, rows, step):
            mine = slice(start, start + step)
            summed = sofar_ref[:, mine]
            if late:
                last = [blocks[place] for place in late]
                summed = summed + weighted_values(last, late, probs_ref, mine, rows, width)
            softmax_buffer[mine, :] = jnp.transpose((summed / sum_ref[:, mine]).astype(BF16))
        softmax_copy.start()
        carried = carried_state(numbers, blocks, rows, width)
        put_linear(step, carried, lin_qt_ref, intra_ref, cum_row_ref, linear_buffer)
        linear_copy.start()
        softmax_copy.wait()
        linear_copy.wait()


def keep_in_hbm(x):
    return pltpu.with_memory_space_constraint(x, pltpu.HBM)


def keep_in_vmem(x):
    return pltpu.with_memory_space_constraint(x, VMEM)


def kept_in_vmem(x):
    return VMEM(x.shape, x.dtype)


def kept_in_hbm(x):
    return pltpu.HBM(x.shape, x.dtype)


def call(body, operands, outs, given=(), written=(), resumed=(), scratch=()):
    size = sum(math.prod(x.shape) * x.dtype.itemsize for x in (*given, *operands, *outs))
    inside, outside = pl.BlockSpec(memory_space=VMEM), pl.BlockSpec(memory_space=pl.ANY)
    hbm = (*given, *resumed)
    scratch = [VMEM(x.shape, x.dtype) for x in (*scratch, *written)]
    moved = len(given) + len(written)
    return pl.pallas_call(
        body,
        out_shape=(*map(kept_in_hbm, written), *map(kept_in_vmem, outs)),
        in_specs=[outside] * len(hbm) + [inside] * len(operands),
        out_specs=(*[outside] * len(written), *[inside] * len(outs)),
        scratch_shapes=[*scratch, pltpu.SemaphoreType.DMA((moved,))] if moved else [],
        input_output_aliases={place: place for place in range(len(resumed))},
        cost_estimate=pl.CostEstimate(flops=0, bytes_accessed=size, transcendentals=0),
        compiler_params=pltpu.CompilerParams(vmem_limit_bytes=KERNEL_VMEM),
    )(*map(keep_in_hbm, hbm), *map(keep_in_vmem, operands))


def on_device(axis, lin_query, lin_key, lin_value, log_decay, soft_query, soft_key, soft_value):
    rows, heads, width = lin_query.shape
    count = lax.axis_size(axis)
    cores = 2 if count % 2 == 0 else 1
    chips = count // cores

    def across(x, apart):
        return lax.ppermute(x, axis, [(i, (i + apart * cores) % count) for i in range(count)])

    def swapped(x, apart=0, after=None):
        if after is not None:
            x, _ = lax.optimization_barrier((x, after))
        return lax.ppermute(x, axis, [(i, i ^ 1 if i >= apart * cores else i) for i in range(count)])

    def near(x):
        return [swapped(x)] if cores == 2 else []

    def far(x):
        return [across(x, apart) for apart in range(1, chips)]

    def completed(blocks, after):
        out = []
        for apart, block in enumerate(blocks, 1):
            out.append(block)
            if cores == 2:
                out.append(swapped(block, apart, after))
        return out

    def one_head(lq, lk, lv, decay, sq, sk, sv):
        step = math.gcd(rows, 256)
        scale = math.log2(math.e) / math.sqrt(width)
        ring = (axis, cores, chips)

        def shape(*dims, dtype=F32):
            return jax.ShapeDtypeStruct(dims, dtype)

        def half(*dims):
            return shape(*dims, dtype=BF16)

        row, flat, flat16, block = shape(1, rows), shape(width, rows), half(width, rows), half(rows, width)
        keys = far(sk)
        pack, cum_row, cum_col, lin_vt, lk, lq, sq, own_keys = call(
            state_kernel,
            (),
            (half(rows + width + PAD, width), row, shape(rows, width), flat16, block, block, block, block),
            given=(decay, lk, lv, sv, lq, sq, sk),
            scratch=(row, block, block),
        )
        qt, top, total, summed = call(
            functools.partial(soft_kernel, scale, step), (sq, own_keys, pack), (flat16, row, row, flat)
        )
        (pack, lin_vt), _ = lax.optimization_barrier(((pack, lin_vt), summed))
        packs, near_packs = far(pack), near(pack)
        (lq, lk), _ = lax.optimization_barrier(((lq, lk), keys))
        keys = [*near(sk), *completed(keys, summed)]
        lin_qt, intra = call(
            functools.partial(linear_kernel, step), (lq, lk, lin_vt, cum_row, cum_col), (flat16, flat)
        )
        top, _ = lax.optimization_barrier((top, intra))
        *began, probs, factor, sums = call(
            functools.partial(score_kernel, scale, step, *ring),
            (qt, top, total, summed, lin_qt, intra, cum_row, *near_packs, *keys),
            (half(len(keys) * rows, rows), row, row),
            written=(block, block),
        )
        blocks = [*near_packs, *completed(packs, factor)]
        late = tuple(range(cores, len(blocks), cores)) if cores == 2 else ()
        early = tuple(place for place in range(len(blocks)) if place not in late)
        (sofar,) = call(
            functools.partial(early_kernel, step, axis, cores, early),
            (summed, factor, probs, *(blocks[place] for place in early)),
            (flat,),
        )
        return call(
            functools.partial(late_kernel, step, *ring, late),
            (lin_qt, intra, cum_row, sofar, sums, probs, *blocks),
            (),
            written=(block, block),
            resumed=began,
        )

    outs = [
        one_head(
            *(x[:, head] for x in (lin_query, lin_key, lin_value)),
            log_decay[head : head + 1],
            *(x[:, head] for x in (soft_query, soft_key, soft_value)),
        )
        for head in range(heads)
    ]
    linear = jnp.stack([pair[0] for pair in outs], axis=1)
    softmax = jnp.stack([pair[1] for pair in outs], axis=1)
    return linear, softmax


def solution(mesh):
    block = P("ctx", "tp", None)
    return jax.shard_map(
        functools.partial(on_device, "ctx"),
        mesh=mesh,
        in_specs=(block, block, block, P("tp", "ctx"), block, block, block),
        out_specs=(block, block),
        check_vma=False,
    )
```

time: 13 us -> 15.5 us (1.19)
  the two profiles are of different devices: /device:TPU:0 before, /device:TPU:7 now
where the time goes in v4:
time: 15.5 us; the launch traced here: 15.3 us
  starting transfers between devices  8.39 us (54%)
  Pallas kernels  5.1 us (33%)
  waiting for transfers between devices  1.14 us (7%)
  between operations  0.7 us (5%)
    ppermute x4, starting transfers between devices, swapped(): lax.ppermute(x, axis, [(i, i ^ 1 if i >= apart * cores else i) for i in r...  6.85 us
    pallas_call x6, Pallas kernels, call(): pl.pallas_call(body, out_shape=(*map(kept_in_hbm, written), *map(kept_in_...  5.1 us
    ppermute x2, starting transfers between devices, across(): lax.ppermute(x, axis, [(i, (i + apart * cores) % count) for i in range(co...  1.54 us
    ppermute x4, waiting for transfers between devices, swapped(): lax.ppermute(x, axis, [(i, i ^ 1 if i >= apart * cores else i) for i in r...  1.13 us
  transfers between devices with their start and end apart: 6, of which 2 were waited for; matrix products, arithmetic and copies ran while one was open for 0% of the time, Pallas kernels for 26%

profile of v4, /device:TPU:7, one launch (start us, length us, event | category | flops | bytes accessed | tf_op | source)
XLA Modules:
  0.0 15.3 jit_solution(8868862797510044829)
XLA Ops:
  0.6 0.3 %collective-permute-start = (bf16[512,128]{1,0:T(8,128)(2,1)}, bf16[512,128]{1,0:T(8,128)(2,1)S(1)}, u32[]{:S(2)}, u32[]{:S(2)}) collective-permute-start(bf16[512,128]{1,0:T(8,128)(2,1)} %bitcast.15), channel_id=1, source_target_pairs={{0,16},{8,24},{16,0},{24,8},{1,17},{9,25},{17,1},{25,9},{2,18},{10... | collective-permute-start | bytes 393224 | tf_op jit(solution)/shard_map/ppermute | solution.py:309
  1.0 1.3 %shard_map.86 = (bf16[656,128]{1,0:T(8,128)(2,1)S(1)}, f32[1,512]{1,0:T(1,128)S(1)}, f32[512,128]{1,0:T(8,128)S(1)}, bf16[128,512]{1,0:T(8,128)(2,1)S(1)}, bf16[...) custom-call(f32[1,512]{1,0:T(1,128)} %decay_hbm.1, ...), custom_call_target="tpu_custom_call" | custom-call | bytes 1875968 | tf_op jit(solution)/shard_map/pallas_call | solution.py:290
  2.3 0.6 %shard_map.87 = (bf16[128,512]{1,0:T(8,128)(2,1)S(1)}, f32[1,512]{1,0:T(1,128)S(1)}, f32[1,512]{1,0:T(1,128)S(1)}, f32[128,512]{1,0:T(8,128)S(1)}) custom-call(bf16[512,128]{1,0:T(8,128)(2,1)S(1)} %get-tuple-element.30.q_ref, bf16[512,128]{1,0:T(8,128)(2,1)S(1)} %get-tuple-element.31.k_ref, bf16[656,128]{1,0:T(8,128)(2,1)S(1)} %get-tuple-element.48.pack_ref), custom_call_target="tpu_custom_call" | custom-call | bytes 827392 | tf_op jit(solution)/shard_map/pallas_call | solution.py:290
  2.9 1.0 %collective-permute-start.1 = (bf16[656,128]{1,0:T(8,128)(2,1)S(1)}, bf16[656,128]{1,0:T(8,128)(2,1)S(1)}, u32[]{:S(2)}, u32[]{:S(2)}) collective-permute-start(bf16[656,128]{1,0:T(8,128)(2,1)S(1)} %get-tuple-element.48.pack_ref), channel_id=1, source_target_pairs={{0,8},{8,0},{16,24},{24,16},{1,9},{9,1},{17,25},{25,17},{2,10},{10... | collective-permute-start | bytes 503816 | tf_op jit(solution)/shard_map/ppermute | solution.py:314
  3.9 1.2 %collective-permute-start.4 = (bf16[656,128]{1,0:T(8,128)(2,1)S(1)}, bf16[656,128]{1,0:T(8,128)(2,1)S(1)}, u32[]{:S(2)}, u32[]{:S(2)}) collective-permute-start(bf16[656,128]{1,0:T(8,128)(2,1)S(1)} %get-tuple-element.48.pack_ref), channel_id=1, source_target_pairs={{0,16},{8,24},{16,0},{24,8},{1,17},{9,25},{17,1},{25,9},{2,18},{10... | collective-permute-start | bytes 503816 | tf_op jit(solution)/shard_map/ppermute | solution.py:309
  5.2 0.3 %collective-permute-start.2 = (bf16[512,128]{1,0:T(8,128)(2,1)}, bf16[512,128]{1,0:T(8,128)(2,1)S(1)}, u32[]{:S(2)}, u32[]{:S(2)}) collective-permute-start(bf16[512,128]{1,0:T(8,128)(2,1)} %bitcast.17), channel_id=1, source_target_pairs={{0,8},{8,0},{16,24},{24,16},{1,9},{9,1},{17,25},{25,17},{2,10},{10... | collective-permute-start | bytes 393224 | tf_op jit(solution)/shard_map/ppermute | solution.py:314
  5.5 0.0 collective-permute-done.refs_9_
  5.5 3.2 %collective-permute-start.3 = (bf16[512,128]{1,0:T(8,128)(2,1)S(1)}, bf16[512,128]{1,0:T(8,128)(2,1)S(1)}, u32[]{:S(2)}, u32[]{:S(2)}) collective-permute-start(bf16[512,128]{1,0:T(8,128)(2,1)S(1)} %collective-permute-done.refs_9_), channel_id=1, source_target_pairs={{0,0},{8,8},{16,24},{24,16},{1,1},{9,9},{17,25},{25,17},{2,2},{10,... | collective-permute-start | bytes 393224 | tf_op jit(solution)/shard_map/ppermute | solution.py:314
  8.7 0.5 %shard_map.88 = (bf16[128,512]{1,0:T(8,128)(2,1)S(1)}, f32[128,512]{1,0:T(8,128)S(1)}) custom-call(bf16[512,128]{1,0:T(8,128)(2,1)S(1)} %get-tuple-element.37.q_ref, bf16[512,128]{1,0:T(8,128)(2,1)S(1)} %get-tuple-element.38.k_ref, bf16[128,512]{1,0:T(8,128)(2,1)S(1)} %get-tuple-element.41.value_t_ref, ...), custom_call_target="tpu_custom_call" | custom-call | bytes 1050624 | tf_op jit(solution)/shard_map/pallas_call | solution.py:290
  9.2 0.0 collective-permute-done.2.refs_8_
  9.2 0.0 collective-permute-done.1.refs_7_.refs_3_.refs_8_
  9.2 0.4 %collective-permute-done.3.refs_10_ = bf16[512,128]{1,0:T(8,128)(2,1)S(1)} collective-permute-done((bf16[512,128]{1,0:T(8,128)(2,1)S(1)}, bf16[512,128]{1,0:T(8,128)(2,1)S(1)}, u32[]{:S(2)}, u32[]{:S(2)}) %collective-permute-start.3) | collective-permute-done | bytes 131104 | tf_op jit(solution)/shard_map/ppermute | solution.py:314
  9.7 1.3 %shard_map.89 = (bf16[512,128]{1,0:T(8,128)(2,1)}, bf16[512,128]{1,0:T(8,128)(2,1)}, bf16[1536,512]{1,0:T(8,128)(2,1)S(1)}, f32[1,512]{1,0:T(1,128)S(1)}, f32[1,512]{1,0:T(1,128)S(1)}) custom-call(bf16[128,512]{1,0:T(8,128)(2,1)S(1)} %get-tuple-element.33.refs_0_, f32[1,512]{1,0:T(1,128)S(1)} %get-tuple-element.45.refs_1_, ...), custom_call_target="tpu_custom_call" | custom-call | bytes 2930688 | tf_op jit(solution)/shard_map/pallas_call | solution.py:290
  11.0 0.0 collective-permute-done.4.refs_4_.refs_9_
  11.0 2.3 %collective-permute-start.5 = (bf16[656,128]{1,0:T(8,128)(2,1)S(1)}, bf16[656,128]{1,0:T(8,128)(2,1)S(1)}, u32[]{:S(2)}, u32[]{:S(2)}) collective-permute-start(bf16[656,128]{1,0:T(8,128)(2,1)S(1)} %collective-permute-done.4.refs_4_.refs_9_), channel_id=1, source_target_pairs={{0,0},{8,8},{16,24},{24,16},{1,1},{9,9},{17,25},{25,17},{2,2},{10,... | collective-permute-start | bytes 503816 | tf_op jit(solution)/shard_map/ppermute | solution.py:314
  13.3 0.3 %shard_map.90.refs_5_ = f32[128,512]{1,0:T(8,128)S(1)} custom-call(f32[128,512]{1,0:T(8,128)S(1)} %get-tuple-element.40.refs_3_.refs_0_, f32[1,512]{1,0:T(1,128)S(1)} %get-tuple-element.52.refs_1_, bf16[1536,512]{1,0:T(8,128)(2,1)S(1)} %get-tuple-element.53.refs_2_.refs_7_, bf16[656,128]{1,0:T(8,128)(2,1)S(1)} %collective-permute-done.1.refs_7_.refs_3_.refs_8_, ...), custom_call_target="tpu_custom_call" | custom-call | bytes 2435072 | tf_op jit(solution)/shard_map/pallas_call | solution.py:290
  13.6 0.7 %collective-permute-done.5.refs_10_ = bf16[656,128]{1,0:T(8,128)(2,1)S(1)} collective-permute-done((bf16[656,128]{1,0:T(8,128)(2,1)S(1)}, bf16[656,128]{1,0:T(8,128)(2,1)S(1)}, u32[]{:S(2)}, u32[]{:S(2)}) %collective-permute-start.5) | collective-permute-done | bytes 167968 | tf_op jit(solution)/shard_map/ppermute | solution.py:314
  14.3 1.1 %shard_map.91 = (bf16[512,128]{1,0:T(8,128)(2,1)}, bf16[512,128]{1,0:T(8,128)(2,1)}) custom-call(bf16[512,128]{1,0:T(8,128)(2,1)} %get-tuple-element.50.refs_0_, bf16[512,128]{1,0:T(8,128)(2,1)} %get-tuple-element.51.refs_1_, bf16[128,512]{1,0:T(8,128)(2,1)S(1)} %get-tuple-element.47.refs_4_.refs_2_, ...), custom_call_target="tpu_custom_call", output_to_operand_aliasing={{0}: (0, {}), {1}: (1, {})} | custom-call | bytes 2736128 | tf_op jit(solution)/shard_map/pallas_call | solution.py:290
Async XLA Ops:
  0.6 4.9 %collective-permute-start = (bf16[512,128]{1,0:T(8,128)(2,1)}, bf16[512,128]{1,0:T(8,128)(2,1)S(1)}, u32[]{:S(2)}, u32[]{:S(2)}) collective-permute-start(bf16[512,128]{1,0:T(8,128)(2,1)} %bitcast.15), channel_id=1, source_target_pairs={{0,16},{8,24},{16,0},{24,8},{1,17},{9,25},{17,1},{25,9},{2,18},{10... | collective-permute-start | bytes 393224 | tf_op jit(solution)/shard_map/ppermute | solution.py:309
  2.9 6.3 %collective-permute-start.1 = (bf16[656,128]{1,0:T(8,128)(2,1)S(1)}, bf16[656,128]{1,0:T(8,128)(2,1)S(1)}, u32[]{:S(2)}, u32[]{:S(2)}) collective-permute-start(bf16[656,128]{1,0:T(8,128)(2,1)S(1)} %get-tuple-element.48.pack_ref), channel_id=1, source_target_pairs={{0,8},{8,0},{16,24},{24,16},{1,9},{9,1},{17,25},{25,17},{2,10},{10... | collective-permute-start | bytes 503816 | tf_op jit(solution)/shard_map/ppermute | solution.py:314
  3.9 7.0 %collective-permute-start.4 = (bf16[656,128]{1,0:T(8,128)(2,1)S(1)}, bf16[656,128]{1,0:T(8,128)(2,1)S(1)}, u32[]{:S(2)}, u32[]{:S(2)}) collective-permute-start(bf16[656,128]{1,0:T(8,128)(2,1)S(1)} %get-tuple-element.48.pack_ref), channel_id=1, source_target_pairs={{0,16},{8,24},{16,0},{24,8},{1,17},{9,25},{17,1},{25,9},{2,18},{10... | collective-permute-start | bytes 503816 | tf_op jit(solution)/shard_map/ppermute | solution.py:309
  5.2 4.1 %collective-permute-start.2 = (bf16[512,128]{1,0:T(8,128)(2,1)}, bf16[512,128]{1,0:T(8,128)(2,1)S(1)}, u32[]{:S(2)}, u32[]{:S(2)}) collective-permute-start(bf16[512,128]{1,0:T(8,128)(2,1)} %bitcast.17), channel_id=1, source_target_pairs={{0,8},{8,0},{16,24},{24,16},{1,9},{9,1},{17,25},{25,17},{2,10},{10... | collective-permute-start | bytes 393224 | tf_op jit(solution)/shard_map/ppermute | solution.py:314
  5.5 4.2 %collective-permute-start.3 = (bf16[512,128]{1,0:T(8,128)(2,1)S(1)}, bf16[512,128]{1,0:T(8,128)(2,1)S(1)}, u32[]{:S(2)}, u32[]{:S(2)}) collective-permute-start(bf16[512,128]{1,0:T(8,128)(2,1)S(1)} %collective-permute-done.refs_9_), channel_id=1, source_target_pairs={{0,0},{8,8},{16,24},{24,16},{1,1},{9,9},{17,25},{25,17},{2,2},{10,... | collective-permute-start | bytes 393224 | tf_op jit(solution)/shard_map/ppermute | solution.py:314
  11.0 3.3 %collective-permute-start.5 = (bf16[656,128]{1,0:T(8,128)(2,1)S(1)}, bf16[656,128]{1,0:T(8,128)(2,1)S(1)}, u32[]{:S(2)}, u32[]{:S(2)}) collective-permute-start(bf16[656,128]{1,0:T(8,128)(2,1)S(1)} %collective-permute-done.4.refs_4_.refs_9_), channel_id=1, source_target_pairs={{0,0},{8,8},{16,24},{24,16},{1,1},{9,9},{17,25},{25,17},{2,2},{10,... | collective-permute-start | bytes 503816 | tf_op jit(solution)/shard_map/ppermute | solution.py:314

commit v5 on v4

--- a/solution.py
+++ b/solution.py
@@ -308,10 +308,10 @@
     def across(x, apart):
         return lax.ppermute(x, axis, [(i, (i + apart * cores) % count) for i in range(count)])
 
-    def swapped(x, apart=0, after=None):
+    def swapped(x, after=None):
         if after is not None:
             x, _ = lax.optimization_barrier((x, after))
-        return lax.ppermute(x, axis, [(i, i ^ 1 if i >= apart * cores else i) for i in range(count)])
+        return lax.ppermute(x, axis, [(i, i ^ 1) for i in range(count)])
 
     def near(x):
         return [swapped(x)] if cores == 2 else []
@@ -321,10 +321,10 @@
 
     def completed(blocks, after):
         out = []
-        for apart, block in enumerate(blocks, 1):
+        for block in blocks:
             out.append(block)
             if cores == 2:
-                out.append(swapped(block, apart, after))
+                out.append(swapped(block, after))
         return out
 
     def one_head(lq, lk, lv, decay, sq, sk, sv):

time: 15.5 us -> 14 us (0.903)
  the two profiles are of different devices: /device:TPU:7 before, /device:TPU:0 now
where the time goes in v5:
time: 14 us; the launch traced here: 13.8 us
  waiting for transfers between devices  5.26 us (38%)
  Pallas kernels  4.27 us (30%)
  starting transfers between devices  3.58 us (26%)
  between operations  0.68 us (5%)
    pallas_call x6, Pallas kernels, call(): pl.pallas_call(body, out_shape=(*map(kept_in_hbm, written), *map(kept_in_...  4.27 us
    ppermute x2, starting transfers between devices, across(): lax.ppermute(x, axis, [(i, (i + apart * cores) % count) for i in range(co...  3.09 us
    ppermute x2, waiting for transfers between devices, across(): lax.ppermute(x, axis, [(i, (i + apart * cores) % count) for i in range(co...  3.04 us
    ppermute x4, waiting for transfers between devices, swapped(): return lax.ppermute(x, axis, [(i, i ^ 1) for i in range(count)])  2.22 us
    ppermute x4, starting transfers between devices, swapped(): return lax.ppermute(x, axis, [(i, i ^ 1) for i in range(count)])  0.49 us
  transfers between devices with their start and end apart: 6, of which 4 were waited for; matrix products, arithmetic and copies ran while one was open for 0% of the time, Pallas kernels for 31%

profile of v5, /device:TPU:0, one launch (start us, length us, event | category | flops | bytes accessed | tf_op | source)
XLA Modules:
  0.0 13.8 jit_solution(1191365657373840958)
XLA Ops:
  0.6 3.0 %collective-permute-start = (bf16[512,128]{1,0:T(8,128)(2,1)}, bf16[512,128]{1,0:T(8,128)(2,1)S(1)}, u32[]{:S(2)}, u32[]{:S(2)}) collective-permute-start(bf16[512,128]{1,0:T(8,128)(2,1)} %bitcast.15), channel_id=1, source_target_pairs={{0,16},{8,24},{16,0},{24,8},{1,17},{9,25},{17,1},{25,9},{2,18},{10... | collective-permute-start | bytes 393224 | tf_op jit(solution)/shard_map/ppermute | solution.py:309
  3.6 1.3 %shard_map.86 = (bf16[656,128]{1,0:T(8,128)(2,1)S(1)}, f32[1,512]{1,0:T(1,128)S(1)}, f32[512,128]{1,0:T(8,128)S(1)}, bf16[128,512]{1,0:T(8,128)(2,1)S(1)}, bf16[...) custom-call(f32[1,512]{1,0:T(1,128)} %decay_hbm.1, ...), custom_call_target="tpu_custom_call" | custom-call | bytes 1875968 | tf_op jit(solution)/shard_map/pallas_call | solution.py:290
  5.0 0.6 %shard_map.87 = (bf16[128,512]{1,0:T(8,128)(2,1)S(1)}, f32[1,512]{1,0:T(1,128)S(1)}, f32[1,512]{1,0:T(1,128)S(1)}, f32[128,512]{1,0:T(8,128)S(1)}) custom-call(bf16[512,128]{1,0:T(8,128)(2,1)S(1)} %get-tuple-element.30.q_ref, bf16[512,128]{1,0:T(8,128)(2,1)S(1)} %get-tuple-element.31.k_ref, bf16[656,128]{1,0:T(8,128)(2,1)S(1)} %get-tuple-element.48.pack_ref), custom_call_target="tpu_custom_call" | custom-call | bytes 827392 | tf_op jit(solution)/shard_map/pallas_call | solution.py:290
  5.6 0.1 collective-permute-start.1
  5.7 0.1 collective-permute-start.4
  5.8 0.4 %collective-permute-start.2 = (bf16[512,128]{1,0:T(8,128)(2,1)}, bf16[512,128]{1,0:T(8,128)(2,1)S(1)}, u32[]{:S(2)}, u32[]{:S(2)}) collective-permute-start(bf16[512,128]{1,0:T(8,128)(2,1)} %bitcast.17), channel_id=1, source_target_pairs={{0,8},{8,0},{16,24},{24,16},{1,9},{9,1},{17,25},{25,17},{2,10},{10... | collective-permute-start | bytes 393224 | tf_op jit(solution)/shard_map/ppermute | solution.py:314
  6.2 1.2 %collective-permute-done.refs_9_ = bf16[512,128]{1,0:T(8,128)(2,1)S(1)} collective-permute-done((bf16[512,128]{1,0:T(8,128)(2,1)}, bf16[512,128]{1,0:T(8,128)(2,1)S(1)}, u32[]{:S(2)}, u32[]{:S(2)}) %collective-permute-start) | collective-permute-done | bytes 131104 | tf_op jit(solution)/shard_map/ppermute | solution.py:309
  7.3 0.0 collective-permute-start.3
  7.3 0.5 %shard_map.88 = (bf16[128,512]{1,0:T(8,128)(2,1)S(1)}, f32[128,512]{1,0:T(8,128)S(1)}) custom-call(bf16[512,128]{1,0:T(8,128)(2,1)S(1)} %get-tuple-element.37.q_ref, bf16[512,128]{1,0:T(8,128)(2,1)S(1)} %get-tuple-element.38.k_ref, bf16[128,512]{1,0:T(8,128)(2,1)S(1)} %get-tuple-element.41.value_t_ref, ...), custom_call_target="tpu_custom_call" | custom-call | bytes 1050624 | tf_op jit(solution)/shard_map/pallas_call | solution.py:290
  7.9 0.0 collective-permute-done.2.refs_8_
  7.9 0.0 collective-permute-done.1.refs_7_.refs_3_.refs_8_
  7.9 0.8 %collective-permute-done.3.refs_10_ = bf16[512,128]{1,0:T(8,128)(2,1)S(1)} collective-permute-done((bf16[512,128]{1,0:T(8,128)(2,1)S(1)}, bf16[512,128]{1,0:T(8,128)(2,1)S(1)}, u32[]{:S(2)}, u32[]{:S(2)}) %collective-permute-start.3) | collective-permute-done | bytes 131104 | tf_op jit(solution)/shard_map/ppermute | solution.py:314
  8.7 1.8 %shard_map.89 = (bf16[512,128]{1,0:T(8,128)(2,1)}, bf16[512,128]{1,0:T(8,128)(2,1)}, bf16[1536,512]{1,0:T(8,128)(2,1)S(1)}, f32[1,512]{1,0:T(1,128)S(1)}, f32[1,512]{1,0:T(1,128)S(1)}) custom-call(bf16[128,512]{1,0:T(8,128)(2,1)S(1)} %get-tuple-element.33.refs_0_, f32[1,512]{1,0:T(1,128)S(1)} %get-tuple-element.45.refs_1_, ...), custom_call_target="tpu_custom_call" | custom-call | bytes 2930688 | tf_op jit(solution)/shard_map/pallas_call | solution.py:290
  10.5 1.9 %collective-permute-done.4.refs_4_.refs_9_ = bf16[656,128]{1,0:T(8,128)(2,1)S(1)} collective-permute-done((bf16[656,128]{1,0:T(8,128)(2,1)S(1)}, bf16[656,128]{1,0:T(8,128)(2,1)S(1)}, u32[]{:S(2)}, u32[]{:S(2)}) %collective-permute-start.4) | collective-permute-done | bytes 167968 | tf_op jit(solution)/shard_map/ppermute | solution.py:309
  12.4 0.0 collective-permute-start.5
  12.4 1.4 %collective-permute-done.5.refs_10_ = bf16[656,128]{1,0:T(8,128)(2,1)S(1)} collective-permute-done((bf16[656,128]{1,0:T(8,128)(2,1)S(1)}, bf16[656,128]{1,0:T(8,128)(2,1)S(1)}, u32[]{:S(2)}, u32[]{:S(2)}) %collective-permute-start.5) | collective-permute-done | bytes 167968 | tf_op jit(solution)/shard_map/ppermute | solution.py:314
  (2 shorter events, 0.0 us)
Async XLA Ops:
  0.6 6.7 %collective-permute-start = (bf16[512,128]{1,0:T(8,128)(2,1)}, bf16[512,128]{1,0:T(8,128)(2,1)S(1)}, u32[]{:S(2)}, u32[]{:S(2)}) collective-permute-start(bf16[512,128]{1,0:T(8,128)(2,1)} %bitcast.15), channel_id=1, source_target_pairs={{0,16},{8,24},{16,0},{24,8},{1,17},{9,25},{17,1},{25,9},{2,18},{10... | collective-permute-start | bytes 393224 | tf_op jit(solution)/shard_map/ppermute | solution.py:309
  5.6 2.3 %collective-permute-start.1 = (bf16[656,128]{1,0:T(8,128)(2,1)S(1)}, bf16[656,128]{1,0:T(8,128)(2,1)S(1)}, u32[]{:S(2)}, u32[]{:S(2)}) collective-permute-start(bf16[656,128]{1,0:T(8,128)(2,1)S(1)} %get-tuple-element.48.pack_ref), channel_id=1, source_target_pairs={{0,8},{8,0},{16,24},{24,16},{1,9},{9,1},{17,25},{25,17},{2,10},{10... | collective-permute-start | bytes 503816 | tf_op jit(solution)/shard_map/ppermute | solution.py:314
  5.7 6.7 %collective-permute-start.4 = (bf16[656,128]{1,0:T(8,128)(2,1)S(1)}, bf16[656,128]{1,0:T(8,128)(2,1)S(1)}, u32[]{:S(2)}, u32[]{:S(2)}) collective-permute-start(bf16[656,128]{1,0:T(8,128)(2,1)S(1)} %get-tuple-element.48.pack_ref), channel_id=1, source_target_pairs={{0,16},{8,24},{16,0},{24,8},{1,17},{9,25},{17,1},{25,9},{2,18},{10... | collective-permute-start | bytes 503816 | tf_op jit(solution)/shard_map/ppermute | solution.py:309
  5.8 2.1 %collective-permute-start.2 = (bf16[512,128]{1,0:T(8,128)(2,1)}, bf16[512,128]{1,0:T(8,128)(2,1)S(1)}, u32[]{:S(2)}, u32[]{:S(2)}) collective-permute-start(bf16[512,128]{1,0:T(8,128)(2,1)} %bitcast.17), channel_id=1, source_target_pairs={{0,8},{8,0},{16,24},{24,16},{1,9},{9,1},{17,25},{25,17},{2,10},{10... | collective-permute-start | bytes 393224 | tf_op jit(solution)/shard_map/ppermute | solution.py:314
  7.3 1.3 %collective-permute-start.3 = (bf16[512,128]{1,0:T(8,128)(2,1)S(1)}, bf16[512,128]{1,0:T(8,128)(2,1)S(1)}, u32[]{:S(2)}, u32[]{:S(2)}) collective-permute-start(bf16[512,128]{1,0:T(8,128)(2,1)S(1)} %collective-permute-done.refs_9_), channel_id=1, source_target_pairs={{0,8},{8,0},{16,24},{24,16},{1,9},{9,1},{17,25},{25,17},{2,10},{10... | collective-permute-start | bytes 393224 | tf_op jit(solution)/shard_map/ppermute | solution.py:314
  12.4 1.4 %collective-permute-start.5 = (bf16[656,128]{1,0:T(8,128)(2,1)S(1)}, bf16[656,128]{1,0:T(8,128)(2,1)S(1)}, u32[]{:S(2)}, u32[]{:S(2)}) collective-permute-start(bf16[656,128]{1,0:T(8,128)(2,1)S(1)} %collective-permute-done.4.refs_4_.refs_9_), channel_id=1, source_target_pairs={{0,8},{8,0},{16,24},{24,16},{1,9},{9,1},{17,25},{25,17},{2,10},{10... | collective-permute-start | bytes 503816 | tf_op jit(solution)/shard_map/ppermute | solution.py:314

commit v6 on v3

--- a/solution.py
+++ b/solution.py
@@ -303,13 +303,16 @@
     def across(x, apart):
         return lax.ppermute(x, axis, [(i, (i + apart * cores) % count) for i in range(count)])
 
+    def onward(x, apart):
+        return lax.ppermute(x, axis, [(i, i + apart * cores) for i in range(count - apart * cores)])
+
     def swapped(x, after=None):
         if after is not None:
             x, _ = lax.optimization_barrier((x, after))
         return lax.ppermute(x, axis, [(i, i ^ 1) for i in range(count)])
 
-    def spread(x):
-        far = [across(x, apart) for apart in range(1, chips)]
+    def spread(x, send):
+        far = [send(x, apart) for apart in range(1, chips)]
         own = [swapped(x)] if cores == 2 else []
         return own, far
 
@@ -332,7 +335,7 @@
 
         row, flat, flat16 = shape(1, rows), shape(width, rows), shape(width, rows, dtype=BF16)
         block = shape(rows, width, dtype=BF16)
-        keys = spread(sk)
+        keys = spread(sk, across)
         pack, cum_row, cum_col, lin_vt, lk, lq, sq, sk = call(
             state_kernel,
             (),
@@ -346,8 +349,7 @@
         qt, top, total, summed = call(
             functools.partial(soft_kernel, scale, step), (sq, sk, pack), (flat16, row, row, flat)
         )
-        (pack, lin_vt), _ = lax.optimization_barrier(((pack, lin_vt), summed))
-        packs = spread(pack)
+        packs = spread(pack, onward)
         keys = complete(keys, summed)
         (lq, lk), _ = lax.optimization_barrier(((lq, lk), keys[cores - 1 :: cores]))
         lin_qt, intra = call(

time: 13 us -> 13.2 us (1.015)
  the two profiles are of different devices: /device:TPU:0 before, /device:TPU:27 now
where the time goes in v6:
time: 13.2 us; the launch traced here: 13 us
  starting transfers between devices  6.05 us (46%)
  Pallas kernels  4.95 us (38%)
  waiting for transfers between devices  1.32 us (10%)
  between operations  0.68 us (5%)
    pallas_call x6, Pallas kernels, call(): pl.pallas_call(body, out_shape=(*map(kept_in_hbm, written), *map(kept_in_...  4.95 us
    ppermute x4, starting transfers between devices, swapped(): return lax.ppermute(x, axis, [(i, i ^ 1) for i in range(count)])  4.43 us
    ppermute x1, starting transfers between devices, onward(): lax.ppermute(x, axis, [(i, i + apart * cores) for i in range(count - apar...  1.29 us
    ppermute x4, waiting for transfers between devices, swapped(): return lax.ppermute(x, axis, [(i, i ^ 1) for i in range(count)])  1.17 us
    ppermute x1, starting transfers between devices, across(): lax.ppermute(x, axis, [(i, (i + apart * cores) % count) for i in range(co...  0.32 us
  transfers between devices with their start and end apart: 6, of which 3 were waited for; matrix products, arithmetic and copies ran while one was open for 0% of the time, Pallas kernels for 30%

profile of v6, /device:TPU:27, one launch (start us, length us, event | category | flops | bytes accessed | tf_op | source)
XLA Modules:
  0.0 13.0 jit_solution(15049763724599373559)
XLA Ops:
  0.6 0.3 %collective-permute-start = (bf16[512,128]{1,0:T(8,128)(2,1)}, bf16[512,128]{1,0:T(8,128)(2,1)S(1)}, u32[]{:S(2)}, u32[]{:S(2)}) collective-permute-start(bf16[512,128]{1,0:T(8,128)(2,1)} %bitcast.15), channel_id=1, source_target_pairs={{0,16},{8,24},{16,0},{24,8},{1,17},{9,25},{17,1},{25,9},{2,18},{10... | collective-permute-start | bytes 393224 | tf_op jit(solution)/shard_map/ppermute | solution.py:304
  1.0 1.3 %shard_map.86 = (bf16[656,128]{1,0:T(8,128)(2,1)S(1)}, f32[1,512]{1,0:T(1,128)S(1)}, f32[512,128]{1,0:T(8,128)S(1)}, bf16[128,512]{1,0:T(8,128)(2,1)S(1)}, bf16[...) custom-call(f32[1,512]{1,0:T(1,128)} %decay_hbm.1, ...), custom_call_target="tpu_custom_call" | custom-call | bytes 1875968 | tf_op jit(solution)/shard_map/pallas_call | solution.py:285
  2.3 1.3 %collective-permute-start.4 = (bf16[656,128]{1,0:T(8,128)(2,1)S(1)}, bf16[656,128]{1,0:T(8,128)(2,1)S(1)}, u32[]{:S(2)}, u32[]{:S(2)}) collective-permute-start(bf16[656,128]{1,0:T(8,128)(2,1)S(1)} %get-tuple-element.40.pack_ref), channel_id=1, source_target_pairs={{0,16},{8,24},{1,17},{9,25},{2,18},{10,26},{3,19},{11,27},{4,20},{... | collective-permute-start | bytes 503816 | tf_op jit(solution)/shard_map/ppermute | solution.py:307
  3.6 1.0 %collective-permute-start.1 = (bf16[512,128]{1,0:T(8,128)(2,1)}, bf16[512,128]{1,0:T(8,128)(2,1)S(1)}, u32[]{:S(2)}, u32[]{:S(2)}) collective-permute-start(bf16[512,128]{1,0:T(8,128)(2,1)} %bitcast.17), channel_id=1, source_target_pairs={{0,8},{8,0},{16,24},{24,16},{1,9},{9,1},{17,25},{25,17},{2,10},{10... | collective-permute-start | bytes 393224 | tf_op jit(solution)/shard_map/ppermute | solution.py:312
  4.6 0.6 %shard_map.88 = (bf16[128,512]{1,0:T(8,128)(2,1)S(1)}, f32[1,512]{1,0:T(1,128)S(1)}, f32[1,512]{1,0:T(1,128)S(1)}, f32[128,512]{1,0:T(8,128)S(1)}) custom-call(bf16[512,128]{1,0:T(8,128)(2,1)S(1)} %get-tuple-element.38.q_ref, bf16[512,128]{1,0:T(8,128)(2,1)S(1)} %get-tuple-element.39.k_ref, bf16[656,128]{1,0:T(8,128)(2,1)S(1)} %get-tuple-element.40.pack_ref), custom_call_target="tpu_custom_call" | custom-call | bytes 827392 | tf_op jit(solution)/shard_map/pallas_call | solution.py:285
  5.2 0.0 collective-permute-done.refs_1_
  5.3 1.5 %collective-permute-start.2 = (bf16[512,128]{1,0:T(8,128)(2,1)S(1)}, bf16[512,128]{1,0:T(8,128)(2,1)S(1)}, u32[]{:S(2)}, u32[]{:S(2)}) collective-permute-start(bf16[512,128]{1,0:T(8,128)(2,1)S(1)} %collective-permute-done.refs_1_), channel_id=1, source_target_pairs={{0,8},{8,0},{16,24},{24,16},{1,9},{9,1},{17,25},{25,17},{2,10},{10... | collective-permute-start | bytes 393224 | tf_op jit(solution)/shard_map/ppermute | solution.py:312
  6.8 0.0 collective-permute-start.3
  6.8 0.5 %shard_map.87 = (bf16[128,512]{1,0:T(8,128)(2,1)S(1)}, f32[128,512]{1,0:T(8,128)S(1)}) custom-call(bf16[512,128]{1,0:T(8,128)(2,1)S(1)} %get-tuple-element.31.q_ref, bf16[512,128]{1,0:T(8,128)(2,1)S(1)} %get-tuple-element.32.k_ref, bf16[128,512]{1,0:T(8,128)(2,1)S(1)} %get-tuple-element.33.value_t_ref, ...), custom_call_target="tpu_custom_call" | custom-call | bytes 1050624 | tf_op jit(solution)/shard_map/pallas_call | solution.py:285
  7.3 0.0 collective-permute-done.1.refs_0_
  7.3 0.5 %collective-permute-done.2.refs_2_ = bf16[512,128]{1,0:T(8,128)(2,1)S(1)} collective-permute-done((bf16[512,128]{1,0:T(8,128)(2,1)S(1)}, bf16[512,128]{1,0:T(8,128)(2,1)S(1)}, u32[]{:S(2)}, u32[]{:S(2)}) %collective-permute-start.2) | collective-permute-done | bytes 131104 | tf_op jit(solution)/shard_map/ppermute | solution.py:312
  7.8 1.1 %shard_map.89 = (bf16[1536,512]{1,0:T(8,128)(2,1)S(1)}, f32[1,512]{1,0:T(1,128)S(1)}, f32[1,512]{1,0:T(1,128)S(1)}) custom-call(bf16[128,512]{1,0:T(8,128)(2,1)S(1)} %get-tuple-element.42.qt_ref, f32[1,512]{1,0:T(1,128)S(1)} %get-tuple-element.44.top_ref, f32[1,512]{1,0:T(1,128)S(1)} %get-tuple-element.45.total_ref, ...), custom_call_target="tpu_custom_call" | custom-call | bytes 2105344 | tf_op jit(solution)/shard_map/pallas_call | solution.py:285
  8.9 0.1 collective-permute-done.4.refs_8_.refs_9_
  9.0 1.9 %collective-permute-start.5 = (bf16[656,128]{1,0:T(8,128)(2,1)S(1)}, bf16[656,128]{1,0:T(8,128)(2,1)S(1)}, u32[]{:S(2)}, u32[]{:S(2)}) collective-permute-start(bf16[656,128]{1,0:T(8,128)(2,1)S(1)} %collective-permute-done.4.refs_8_.refs_9_), channel_id=1, source_target_pairs={{0,8},{8,0},{16,24},{24,16},{1,9},{9,1},{17,25},{25,17},{2,10},{10... | collective-permute-start | bytes 503816 | tf_op jit(solution)/shard_map/ppermute | solution.py:312
  10.9 0.0 collective-permute-done.3.refs_7_.refs_8_
  10.9 0.3 %shard_map.90 = (bf16[512,128]{1,0:T(8,128)(2,1)}, bf16[512,128]{1,0:T(8,128)(2,1)}, f32[128,512]{1,0:T(8,128)S(1)}) custom-call(bf16[128,512]{1,0:T(8,128)(2,1)S(1)} %get-tuple-element.36.refs_0_.refs_2_, f32[128,512]{1,0:T(8,128)S(1)} %get-tuple-element.37.refs_1_.refs_3_, f32[1,512]{1,0:T(1,128)S(1)} %get-tuple-element.34.cum_row_ref.refs_2_.refs_4_, ...), custom_call_target="tpu_custom_call" | custom-call | bytes 2832384 | tf_op jit(solution)/shard_map/pallas_call | solution.py:285
  11.2 0.7 %collective-permute-done.5.refs_10_ = bf16[656,128]{1,0:T(8,128)(2,1)S(1)} collective-permute-done((bf16[656,128]{1,0:T(8,128)(2,1)S(1)}, bf16[656,128]{1,0:T(8,128)(2,1)S(1)}, u32[]{:S(2)}, u32[]{:S(2)}) %collective-permute-start.5) | collective-permute-done | bytes 167968 | tf_op jit(solution)/shard_map/ppermute | solution.py:312
  11.9 1.1 %shard_map.91 = (bf16[512,128]{1,0:T(8,128)(2,1)}, bf16[512,128]{1,0:T(8,128)(2,1)}) custom-call(bf16[512,128]{1,0:T(8,128)(2,1)} %get-tuple-element.50.refs_0_, bf16[512,128]{1,0:T(8,128)(2,1)} %get-tuple-element.51.refs_1_, bf16[128,512]{1,0:T(8,128)(2,1)S(1)} %get-tuple-element.36.refs_0_.refs_2_, ...), custom_call_target="tpu_custom_call", output_to_operand_aliasing={{0}: (0, {}), {1}: (1, {})} | custom-call | bytes 2736128 | tf_op jit(solution)/shard_map/pallas_call | solution.py:285
Async XLA Ops:
  0.6 4.6 %collective-permute-start = (bf16[512,128]{1,0:T(8,128)(2,1)}, bf16[512,128]{1,0:T(8,128)(2,1)S(1)}, u32[]{:S(2)}, u32[]{:S(2)}) collective-permute-start(bf16[512,128]{1,0:T(8,128)(2,1)} %bitcast.15), channel_id=1, source_target_pairs={{0,16},{8,24},{16,0},{24,8},{1,17},{9,25},{17,1},{25,9},{2,18},{10... | collective-permute-start | bytes 393224 | tf_op jit(solution)/shard_map/ppermute | solution.py:304
  2.3 6.7 %collective-permute-start.4 = (bf16[656,128]{1,0:T(8,128)(2,1)S(1)}, bf16[656,128]{1,0:T(8,128)(2,1)S(1)}, u32[]{:S(2)}, u32[]{:S(2)}) collective-permute-start(bf16[656,128]{1,0:T(8,128)(2,1)S(1)} %get-tuple-element.40.pack_ref), channel_id=1, source_target_pairs={{0,16},{8,24},{1,17},{9,25},{2,18},{10,26},{3,19},{11,27},{4,20},{... | collective-permute-start | bytes 503816 | tf_op jit(solution)/shard_map/ppermute | solution.py:307
  3.6 3.7 %collective-permute-start.1 = (bf16[512,128]{1,0:T(8,128)(2,1)}, bf16[512,128]{1,0:T(8,128)(2,1)S(1)}, u32[]{:S(2)}, u32[]{:S(2)}) collective-permute-start(bf16[512,128]{1,0:T(8,128)(2,1)} %bitcast.17), channel_id=1, source_target_pairs={{0,8},{8,0},{16,24},{24,16},{1,9},{9,1},{17,25},{25,17},{2,10},{10... | collective-permute-start | bytes 393224 | tf_op jit(solution)/shard_map/ppermute | solution.py:312
  5.3 2.5 %collective-permute-start.2 = (bf16[512,128]{1,0:T(8,128)(2,1)S(1)}, bf16[512,128]{1,0:T(8,128)(2,1)S(1)}, u32[]{:S(2)}, u32[]{:S(2)}) collective-permute-start(bf16[512,128]{1,0:T(8,128)(2,1)S(1)} %collective-permute-done.refs_1_), channel_id=1, source_target_pairs={{0,8},{8,0},{16,24},{24,16},{1,9},{9,1},{17,25},{25,17},{2,10},{10... | collective-permute-start | bytes 393224 | tf_op jit(solution)/shard_map/ppermute | solution.py:312
  6.8 4.1 %collective-permute-start.3 = (bf16[656,128]{1,0:T(8,128)(2,1)S(1)}, bf16[656,128]{1,0:T(8,128)(2,1)S(1)}, u32[]{:S(2)}, u32[]{:S(2)}) collective-permute-start(bf16[656,128]{1,0:T(8,128)(2,1)S(1)} %get-tuple-element.40.pack_ref), channel_id=1, source_target_pairs={{0,8},{8,0},{16,24},{24,16},{1,9},{9,1},{17,25},{25,17},{2,10},{10... | collective-permute-start | bytes 503816 | tf_op jit(solution)/shard_map/ppermute | solution.py:312
  9.0 2.9 %collective-permute-start.5 = (bf16[656,128]{1,0:T(8,128)(2,1)S(1)}, bf16[656,128]{1,0:T(8,128)(2,1)S(1)}, u32[]{:S(2)}, u32[]{:S(2)}) collective-permute-start(bf16[656,128]{1,0:T(8,128)(2,1)S(1)} %collective-permute-done.4.refs_8_.refs_9_), channel_id=1, source_target_pairs={{0,8},{8,0},{16,24},{24,16},{1,9},{9,1},{17,25},{25,17},{2,10},{10... | collective-permute-start | bytes 503816 | tf_op jit(solution)/shard_map/ppermute | solution.py:312

commit v7 on v3

--- a/solution.py
+++ b/solution.py
@@ -48,7 +48,7 @@
 
 def state_kernel(
     decay_hbm, key_hbm, value_hbm, soft_value_hbm, query_hbm, soft_query_hbm, soft_key_hbm,
-    pack_ref, cum_row_ref, cum_col_ref, value_t_ref, key_ref, query_ref, soft_query_ref, soft_key_ref,
+    soft_vt_ref, state_ref, cum_row_ref, cum_col_ref, value_t_ref, key_ref, query_ref, soft_query_ref, soft_key_ref,
     decay_ref, value_ref, soft_value_ref, sems,
 ):
     copies = [
@@ -81,13 +81,36 @@
     decayed = (key_ref[...].astype(F32) * jnp.exp(total - cum_col)).astype(BF16)
     value_t = jnp.transpose(value_ref[...])
     value_t_ref[...] = value_t
-    state_t = dot(value_t, decayed)
+    state_ref[:width, :] = dot(value_t, decayed).astype(BF16)
+    state_ref[width:, :] = select_rows(three_parts(total), PAD, width)
     for left in range(0, rows, width):
-        pack_ref[left : left + width, :] = jnp.transpose(soft_value_ref[left : left + width, :])
-    pack_ref[rows : rows + width, :] = state_t.astype(BF16)
-    pack_ref[rows + width :, :] = select_rows(three_parts(total), PAD, width)
+        soft_vt_ref[left : left + width, :] = jnp.transpose(soft_value_ref[left : left + width, :])
     for copy in copies[4:]:
         copy.wait()
+
+
+def sum_of_parts(tail):
+    tail = tail.astype(F32)
+    return tail[0:1] + tail[1:2] + tail[2:3]
+
+
+def combine_kernel(axis, cores, *refs):
+    *state_refs, soft_vt_ref, pack_ref = refs
+    rows, width = soft_vt_ref.shape
+    share = width // cores
+    pack_ref[:rows, :] = soft_vt_ref[...]
+    states = [ref[:width, :].astype(F32) for ref in state_refs]
+    totals = [sum_of_parts(ref[width:, :]) for ref in state_refs]
+    state, total = states[0], totals[0]
+    if cores == 2:
+        upper = lax.rem(lax.axis_index(axis), 2) == 1
+        first, second = jnp.where(upper, states[1], state), jnp.where(upper, state, states[1])
+        state = jnp.exp(jnp.where(upper, total, totals[1])) * first + second
+        state = jnp.where(upper, state[share:], state[:share])
+        total = total + totals[1]
+    pack_ref[rows : rows + share, :] = state.astype(BF16)
+    if pack_ref.shape[0] > rows + share:
+        pack_ref[rows + share :, :] = select_rows(three_parts(total), PAD, width)
 
 
 def soft_kernel(scale, step, q_ref, k_ref, pack_ref, qt_ref, top_ref, total_ref, summed_ref):
@@ -167,18 +190,24 @@
     by_chip(position, cores, len(key_refs), body)
 
 
-def carried_state(numbers, pack_refs, rows, width):
-    totals, states = [], []
-    for pack_ref in pack_refs:
-        tail = pack_ref[rows + width :, :].astype(F32)
-        totals.append(tail[0:1] + tail[1:2] + tail[2:3])
-        states.append(pack_ref[rows : rows + width, :].astype(F32))
+def carried_state(position, cores, states, packs, rows, width):
+    share = width // cores
+    upper = lax.rem(position, 2) == 1
+    chip = position // cores
     carried = jnp.zeros((width, width), F32)
-    for number, state in zip(numbers, states):
-        between = jnp.where(number >= 0, 0.0, NEG)
-        for other, total in zip(numbers, totals):
-            between = between + jnp.where(other > number, 1.0, 0.0) * total
-        carried = carried + jnp.exp(between) * state
+    between = jnp.zeros((1, width), F32)
+    for apart in range(1, len(packs) // cores + 1):
+        parts = packs[(apart - 1) * cores : apart * cores]
+        state = [part[rows : rows + share, :].astype(F32) for part in parts]
+        if cores == 2:
+            halves = jnp.where(upper, state[1], state[0]), jnp.where(upper, state[0], state[1])
+            state = [jnp.concatenate(halves, axis=0)]
+        carried = carried + jnp.exp(between + jnp.where(chip >= apart, 0.0, NEG)) * state[0]
+        if apart * cores < len(packs):
+            between = between + sum_of_parts(parts[0][rows + share :, :])
+    for ref in states:
+        passed = jnp.exp(sum_of_parts(ref[width:, :])) * carried + ref[:width, :].astype(F32)
+        carried = jnp.where(upper, passed, carried)
     return carried.astype(BF16)
 
 
@@ -191,7 +220,7 @@
     return out
 
 
-def write_out(step, numbers, places, pack_refs, linear_packs, refs, outs, buffers, sems):
+def write_out(step, carried, places, pack_refs, refs, outs, buffers, sems):
     lin_qt_ref, intra_ref, cum_row_ref, summed_ref, factor_ref, sum_ref, probs_ref = refs
     width, rows = lin_qt_ref.shape
     linear_buffer, softmax_buffer = buffers
@@ -208,7 +237,7 @@
         summed = summed if more is None else summed + more
         softmax_buffer[mine, :] = jnp.transpose((summed / sum_ref[:, mine]).astype(BF16))
     softmax_copy.start()
-    carried = carried_state(numbers, linear_packs, rows, width)
+    carried = carried()
     for start in range(0, rows, step):
         mine = slice(start, start + step)
         inter = dot(carried, lin_qt_ref[:, mine])
@@ -220,43 +249,46 @@
     linear_copy.wait()
 
 
-def early_kernel(step, axis, cores, chips, places, *refs):
+def early_kernel(step, axis, cores, places, *refs):
     head, refs = refs[:7], refs[7:]
-    packs, (linear_ref, softmax_ref, sofar_ref, *scratch) = refs[: len(places)], refs[len(places) :]
+    states, refs = refs[: cores - 1], refs[cores - 1 :]
+    values, (linear_ref, softmax_ref, sofar_ref, *scratch) = refs[: len(places)], refs[len(places) :]
     lin_qt_ref, intra_ref, cum_row_ref, summed_ref, factor_ref, sum_ref, probs_ref = head
     width, rows = lin_qt_ref.shape
-    position, numbers = block_numbers(axis, cores, chips)
+    position = lax.axis_index(axis)
 
     @pl.when(position >= cores)
     def _():
         for start in range(0, rows, step):
             mine = slice(start, start + step)
             sofar_ref[:, mine] = summed_ref[:, mine] * factor_ref[:, mine] + weighted_values(
-                packs, places, probs_ref, mine, rows, width
+                values, places, probs_ref, mine, rows, width
             )
 
     @pl.when(position < cores)
     def _():
         own = cores - 1
         write_out(
-            step, numbers[:own], places[:own], packs[:own], packs[:own], head,
-            (linear_ref, softmax_ref), scratch[:2], scratch[2],
-        )
-
-
-def late_kernel(step, axis, cores, chips, early, late, *refs):
+            step, lambda: carried_state(position, cores, states, (), rows, width),
+            places[:own], values[:own], head, (linear_ref, softmax_ref), scratch[:2], scratch[2],
+        )
+
+
+def late_kernel(step, axis, cores, late, *refs):
     refs = refs[2:]
     lin_qt_ref, intra_ref, cum_row_ref, sofar_ref, sum_ref, probs_ref = refs[:6]
-    count = len(early) + len(late)
-    packs, (linear_ref, softmax_ref, *scratch) = refs[6 : 6 + count], refs[6 + count :]
-    position, numbers = block_numbers(axis, cores, chips)
+    states, refs = refs[6 : 5 + cores], refs[5 + cores :]
+    *packs, linear_ref, softmax_ref, linear_buffer, softmax_buffer, sems = refs
+    width, rows = lin_qt_ref.shape
+    position = lax.axis_index(axis)
 
     @pl.when(position >= cores)
     def _():
         write_out(
-            step, numbers, late, [packs[place] for place in late], packs,
+            step, lambda: carried_state(position, cores, states, packs, rows, width),
+            late, packs[1::cores] if late else (),
             (lin_qt_ref, intra_ref, cum_row_ref, sofar_ref, None, sum_ref, probs_ref),
-            (linear_ref, softmax_ref), scratch[:2], scratch[2],
+            (linear_ref, softmax_ref), (linear_buffer, softmax_buffer), sems,
         )
 
 
@@ -308,15 +340,15 @@
             x, _ = lax.optimization_barrier((x, after))
         return lax.ppermute(x, axis, [(i, i ^ 1) for i in range(count)])
 
-    def spread(x):
-        far = [across(x, apart) for apart in range(1, chips)]
-        own = [swapped(x)] if cores == 2 else []
-        return own, far
-
-    def complete(of, after):
-        own, far = of
-        out = list(own)
-        for block in far:
+    def near(x):
+        return [swapped(x)] if cores == 2 else []
+
+    def far(x):
+        return [across(x, apart) for apart in range(1, chips)]
+
+    def completed(blocks, after):
+        out = []
+        for block in blocks:
             out.append(block)
             if cores == 2:
                 out.append(swapped(block, after))
@@ -330,47 +362,55 @@
         def shape(*dims, dtype=F32):
             return jax.ShapeDtypeStruct(dims, dtype)
 
-        row, flat, flat16 = shape(1, rows), shape(width, rows), shape(width, rows, dtype=BF16)
-        block = shape(rows, width, dtype=BF16)
-        keys = spread(sk)
-        pack, cum_row, cum_col, lin_vt, lk, lq, sq, sk = call(
+        def half(*dims):
+            return shape(*dims, dtype=BF16)
+
+        row, flat, flat16, block = shape(1, rows), shape(width, rows), half(width, rows), half(rows, width)
+        packed = half(rows + width // cores + (PAD if chips > 2 else 0), width)
+        keys = far(sk)
+        soft_vt, state, cum_row, cum_col, lin_vt, lk, lq, sq, own_keys = call(
             state_kernel,
             (),
-            (
-                shape(rows + width + PAD, width, dtype=BF16), row, shape(rows, width), flat16,
-                block, block, block, block,
-            ),
+            (block, half(width + PAD, width), row, shape(rows, width), flat16, block, block, block, block),
             given=(decay, lk, lv, sv, lq, sq, sk),
             scratch=(row, block, block),
         )
+        states = near(state)
         qt, top, total, summed = call(
-            functools.partial(soft_kernel, scale, step), (sq, sk, pack), (flat16, row, row, flat)
-        )
-        (pack, lin_vt), _ = lax.optimization_barrier(((pack, lin_vt), summed))
-        packs = spread(pack)
-        keys = complete(keys, summed)
-        (lq, lk), _ = lax.optimization_barrier(((lq, lk), keys[cores - 1 :: cores]))
+            functools.partial(soft_kernel, scale, step), (sq, own_keys, soft_vt), (flat16, row, row, flat)
+        )
+        (states, lin_vt), _ = lax.optimization_barrier(((states, lin_vt), summed))
+        (pack,) = call(
+            functools.partial(combine_kernel, axis, cores), (state, *states, soft_vt), (packed,)
+        )
+        packs = far(pack)
+        (lq, lk), _ = lax.optimization_barrier(((lq, lk), keys))
+        keys, near_values = [*near(sk), *completed(keys, summed)], near(soft_vt)
         lin_qt, intra = call(
             functools.partial(linear_kernel, step), (lq, lk, lin_vt, cum_row, cum_col), (flat16, flat)
         )
-        top, _ = lax.optimization_barrier((top, intra))
+        top, _ = lax.optimization_barrier((top, (intra, near_values)))
         probs, factor, sums = call(
             functools.partial(score_kernel, scale, step, *ring),
             (qt, top, total, *keys),
-            (shape(len(keys) * rows, rows, dtype=BF16), row, row),
-        )
-        packs = complete(packs, factor)
-        late = tuple(range(cores, len(packs), cores)) if cores == 2 else ()
-        early = tuple(place for place in range(len(packs)) if place not in late)
+            (half(len(keys) * rows, rows), row, row),
+        )
+        packs = completed(packs, factor)
+        blocks = [*near_values, *packs]
+        late = tuple(range(cores, len(blocks), cores)) if cores == 2 else ()
+        early = tuple(place for place in range(len(blocks)) if place not in late)
         *began, sofar = call(
-            functools.partial(early_kernel, step, *ring, early),
-            (lin_qt, intra, cum_row, summed, factor, sums, probs, *(packs[place] for place in early)),
+            functools.partial(early_kernel, step, axis, cores, early),
+            (
+                lin_qt, intra, cum_row, summed, factor, sums, probs,
+                *states, *(blocks[place] for place in early),
+            ),
             (flat,),
             written=(block, block),
         )
         return call(
-            functools.partial(late_kernel, step, *ring, early, late),
-            (lin_qt, intra, cum_row, sofar, sums, probs, *packs),
+            functools.partial(late_kernel, step, axis, cores, late),
+            (lin_qt, intra, cum_row, sofar, sums, probs, *states, *packs),
             (),
             written=(block, block),
             resumed=began,

time: 13 us -> 13.8 us (1.062)
  waiting for transfers between devices: 4.48 us -> 5.21 us
    ppermute x4 -> x5, waiting for transfers between devices: 0.66 us -> 1.73 us  [swapped(): return lax.ppermute(x, axis, [(i, i ^ 1) for i in range(count)])]
    ppermute x2, waiting for transfers between devices: 3.82 us -> 3.48 us  [across(): lax.ppermute(x, axis, [(i, (i + apart * cores) % count) for i in range(co...]
    ppermute x4 -> x5, starting transfers between devices: 0.58 us -> 0.65 us  [swapped(): return lax.ppermute(x, axis, [(i, i ^ 1) for i in range(count)])]
    pallas_call x6 -> x7, Pallas kernels: 4 us -> 4.04 us  [call(): pl.pallas_call(body, out_shape=(*map(kept_in_hbm, written), *map(kept_in_...]
  transfers between devices with their start and end apart: 6 -> 7, of which waited for: 4 -> 6; matrix products, arithmetic and copies ran while one was open for 0% -> 0% of each run, Pallas kernels for 31% -> 29%
where the time goes in v7:
time: 13.8 us; the launch traced here: 13.7 us
  waiting for transfers between devices  5.21 us (38%)
  Pallas kernels  4.04 us (29%)
  starting transfers between devices  3.73 us (27%)
  between operations  0.68 us (5%)
    pallas_call x7, Pallas kernels, call(): pl.pallas_call(body, out_shape=(*map(kept_in_hbm, written), *map(kept_in_...  4.04 us
    ppermute x2, waiting for transfers between devices, across(): lax.ppermute(x, axis, [(i, (i + apart * cores) % count) for i in range(co...  3.48 us
    ppermute x2, starting transfers between devices, across(): lax.ppermute(x, axis, [(i, (i + apart * cores) % count) for i in range(co...  3.09 us
    ppermute x5, waiting for transfers between devices, swapped(): return lax.ppermute(x, axis, [(i, i ^ 1) for i in range(count)])  1.73 us
    ppermute x5, starting transfers between devices, swapped(): return lax.ppermute(x, axis, [(i, i ^ 1) for i in range(count)])  0.65 us
  transfers between devices with their start and end apart: 7, of which 6 were waited for; matrix products, arithmetic and copies ran while one was open for 0% of the time, Pallas kernels for 29%

profile of v7, /device:TPU:0, one launch (start us, length us, event | category | flops | bytes accessed | tf_op | source)
XLA Modules:
  0.0 13.7 jit_solution(8025545568305845781)
XLA Ops:
  0.6 3.0 %collective-permute-start = (bf16[512,128]{1,0:T(8,128)(2,1)}, bf16[512,128]{1,0:T(8,128)(2,1)S(1)}, u32[]{:S(2)}, u32[]{:S(2)}) collective-permute-start(bf16[512,128]{1,0:T(8,128)(2,1)} %bitcast.15), channel_id=1, source_target_pairs={{0,16},{8,24},{16,0},{24,8},{1,17},{9,25},{17,1},{25,9},{2,18},{10... | collective-permute-start | bytes 393224 | tf_op jit(solution)/shard_map/ppermute | solution.py:336
  3.6 1.3 %shard_map.86 = (bf16[512,128]{1,0:T(8,128)(2,1)S(1)}, bf16[144,128]{1,0:T(8,128)(2,1)S(1)}, f32[1,512]{1,0:T(1,128)S(1)}, f32[512,128]{1,0:T(8,128)S(1)}, bf16[...) custom-call(f32[1,512]{1,0:T(1,128)} %decay_hbm.1, ...), custom_call_target="tpu_custom_call" | custom-call | bytes 1875968 | tf_op jit(solution)/shard_map/pallas_call | solution.py:317
  5.0 0.1 collective-permute-start.1
  5.1 0.6 %shard_map.87 = (bf16[128,512]{1,0:T(8,128)(2,1)S(1)}, f32[1,512]{1,0:T(1,128)S(1)}, f32[1,512]{1,0:T(1,128)S(1)}, f32[128,512]{1,0:T(8,128)S(1)}) custom-call(bf16[512,128]{1,0:T(8,128)(2,1)S(1)} %get-tuple-element.38.q_ref, bf16[512,128]{1,0:T(8,128)(2,1)S(1)} %get-tuple-element.39.k_ref, bf16[512,128]{1,0:T(8,128)(2,1)S(1)} %get-tuple-element.40.pack_ref.refs_2_), custom_call_target="tpu_custom_call" | custom-call | bytes 790528 | tf_op jit(solution)/shard_map/pallas_call | solution.py:317
  5.7 0.6 %collective-permute-done.1.refs_1_.refs_7_.refs_8_ = bf16[144,128]{1,0:T(8,128)(2,1)S(1)} collective-permute-done((bf16[144,128]{1,0:T(8,128)(2,1)S(1)}, bf16[144,128]{1,0:T(8,128)(2,1)S(1)}, u32[]{:S(2)}, u32[]{:S(2)}) %collective-permute-start.1) | collective-permute-done | bytes 36896 | tf_op jit(solution)/shard_map/ppermute | solution.py:341
  6.3 0.1 collective-permute-start.5
  6.4 0.2 %collective-permute-start.2 = (bf16[512,128]{1,0:T(8,128)(2,1)S(1)}, bf16[512,128]{1,0:T(8,128)(2,1)S(1)}, u32[]{:S(2)}, u32[]{:S(2)}) collective-permute-start(bf16[512,128]{1,0:T(8,128)(2,1)S(1)} %get-tuple-element.40.pack_ref.refs_2_), channel_id=1, source_target_pairs={{0,8},{8,0},{16,24},{24,16},{1,9},{9,1},{17,25},{25,17},{2,10},{10... | collective-permute-start | bytes 393224 | tf_op jit(solution)/shard_map/ppermute | solution.py:341
  6.6 0.3 %collective-permute-start.3 = (bf16[512,128]{1,0:T(8,128)(2,1)}, bf16[512,128]{1,0:T(8,128)(2,1)S(1)}, u32[]{:S(2)}, u32[]{:S(2)}) collective-permute-start(bf16[512,128]{1,0:T(8,128)(2,1)} %bitcast.17), channel_id=1, source_target_pairs={{0,8},{8,0},{16,24},{24,16},{1,9},{9,1},{17,25},{25,17},{2,10},{10... | collective-permute-start | bytes 393224 | tf_op jit(solution)/shard_map/ppermute | solution.py:341
  7.0 0.4 %collective-permute-done.refs_1_ = bf16[512,128]{1,0:T(8,128)(2,1)S(1)} collective-permute-done((bf16[512,128]{1,0:T(8,128)(2,1)}, bf16[512,128]{1,0:T(8,128)(2,1)S(1)}, u32[]{:S(2)}, u32[]{:S(2)}) %collective-permute-start) | collective-permute-done | bytes 131104 | tf_op jit(solution)/shard_map/ppermute | solution.py:336
  7.3 0.0 collective-permute-start.4
  7.3 0.5 %shard_map.88 = (bf16[128,512]{1,0:T(8,128)(2,1)S(1)}, f32[128,512]{1,0:T(8,128)S(1)}) custom-call(bf16[512,128]{1,0:T(8,128)(2,1)S(1)} %get-tuple-element.34.q_ref, bf16[512,128]{1,0:T(8,128)(2,1)S(1)} %get-tuple-element.35.k_ref, bf16[128,512]{1,0:T(8,128)(2,1)S(1)} %get-tuple-element.42.value_t_ref, ...), custom_call_target="tpu_custom_call" | custom-call | bytes 1050624 | tf_op jit(solution)/shard_map/pallas_call | solution.py:317
  7.9 0.0 collective-permute-done.2.refs_8_
  7.9 0.3 %collective-permute-done.3.refs_0_ = bf16[512,128]{1,0:T(8,128)(2,1)S(1)} collective-permute-done((bf16[512,128]{1,0:T(8,128)(2,1)}, bf16[512,128]{1,0:T(8,128)(2,1)S(1)}, u32[]{:S(2)}, u32[]{:S(2)}) %collective-permute-start.3) | collective-permute-done | bytes 131104 | tf_op jit(solution)/shard_map/ppermute | solution.py:341
  8.2 0.5 %collective-permute-done.4.refs_2_ = bf16[512,128]{1,0:T(8,128)(2,1)S(1)} collective-permute-done((bf16[512,128]{1,0:T(8,128)(2,1)S(1)}, bf16[512,128]{1,0:T(8,128)(2,1)S(1)}, u32[]{:S(2)}, u32[]{:S(2)}) %collective-permute-start.4) | collective-permute-done | bytes 131104 | tf_op jit(solution)/shard_map/ppermute | solution.py:341
  8.7 0.5 %shard_map.89 = (bf16[1536,512]{1,0:T(8,128)(2,1)S(1)}, f32[1,512]{1,0:T(1,128)S(1)}, f32[1,512]{1,0:T(1,128)S(1)}) custom-call(bf16[128,512]{1,0:T(8,128)(2,1)S(1)} %get-tuple-element.47.qt_ref, f32[1,512]{1,0:T(1,128)S(1)} %get-tuple-element.49.top_ref, f32[1,512]{1,0:T(1,128)S(1)} %get-tuple-element.50.total_ref, ...), custom_call_target="tpu_custom_call" | custom-call | bytes 2105344 | tf_op jit(solution)/shard_map/pallas_call | solution.py:317
  9.2 3.1 %collective-permute-done.5.refs_9_ = bf16[576,128]{1,0:T(8,128)(2,1)S(1)} collective-permute-done((bf16[576,128]{1,0:T(8,128)(2,1)S(1)}, bf16[576,128]{1,0:T(8,128)(2,1)S(1)}, u32[]{:S(2)}, u32[]{:S(2)}) %collective-permute-start.5) | collective-permute-done | bytes 147488 | tf_op jit(solution)/shard_map/ppermute | solution.py:336
  12.3 0.0 collective-permute-start.6
  12.3 1.1 %shard_map.91 = (bf16[512,128]{1,0:T(8,128)(2,1)}, bf16[512,128]{1,0:T(8,128)(2,1)}, f32[128,512]{1,0:T(8,128)S(1)}) custom-call(bf16[128,512]{1,0:T(8,128)(2,1)S(1)} %get-tuple-element.45.refs_0_.refs_2_, f32[128,512]{1,0:T(8,128)S(1)} %get-tuple-element.46.refs_1_.refs_3_, f32[1,512]{1,0:T(1,128)S(1)} %get-tuple-element.43.cum_row_ref.refs_2_.refs_4_, ...), custom_call_target="tpu_custom_call" | custom-call | bytes 2811904 | tf_op jit(solution)/shard_map/pallas_call | solution.py:317
  13.3 0.3 %collective-permute-done.6.refs_10_ = bf16[576,128]{1,0:T(8,128)(2,1)S(1)} collective-permute-done((bf16[576,128]{1,0:T(8,128)(2,1)S(1)}, bf16[576,128]{1,0:T(8,128)(2,1)S(1)}, u32[]{:S(2)}, u32[]{:S(2)}) %collective-permute-start.6) | collective-permute-done | bytes 147488 | tf_op jit(solution)/shard_map/ppermute | solution.py:341
  (2 shorter events, 0.1 us)
Async XLA Ops:
  0.6 6.7 %collective-permute-start = (bf16[512,128]{1,0:T(8,128)(2,1)}, bf16[512,128]{1,0:T(8,128)(2,1)S(1)}, u32[]{:S(2)}, u32[]{:S(2)}) collective-permute-start(bf16[512,128]{1,0:T(8,128)(2,1)} %bitcast.15), channel_id=1, source_target_pairs={{0,16},{8,24},{16,0},{24,8},{1,17},{9,25},{17,1},{25,9},{2,18},{10... | collective-permute-start | bytes 393224 | tf_op jit(solution)/shard_map/ppermute | solution.py:336
  5.0 1.3 %collective-permute-start.1 = (bf16[144,128]{1,0:T(8,128)(2,1)S(1)}, bf16[144,128]{1,0:T(8,128)(2,1)S(1)}, u32[]{:S(2)}, u32[]{:S(2)}) collective-permute-start(bf16[144,128]{1,0:T(8,128)(2,1)S(1)} %get-tuple-element.36.refs_0_), channel_id=1, source_target_pairs={{0,8},{8,0},{16,24},{24,16},{1,9},{9,1},{17,25},{25,17},{2,10},{10... | collective-permute-start | bytes 110600 | tf_op jit(solution)/shard_map/ppermute | solution.py:341
  6.3 6.0 %collective-permute-start.5 = (bf16[576,128]{1,0:T(8,128)(2,1)S(1)}, bf16[576,128]{1,0:T(8,128)(2,1)S(1)}, u32[]{:S(2)}, u32[]{:S(2)}) collective-permute-start(bf16[576,128]{1,0:T(8,128)(2,1)S(1)} %shard_map.90), channel_id=1, source_target_pairs={{0,16},{8,24},{16,0},{24,8},{1,17},{9,25},{17,1},{25,9},{2,18},{10... | collective-permute-start | bytes 442376 | tf_op jit(solution)/shard_map/ppermute | solution.py:336
  6.4 1.5 %collective-permute-start.2 = (bf16[512,128]{1,0:T(8,128)(2,1)S(1)}, bf16[512,128]{1,0:T(8,128)(2,1)S(1)}, u32[]{:S(2)}, u32[]{:S(2)}) collective-permute-start(bf16[512,128]{1,0:T(8,128)(2,1)S(1)} %get-tuple-element.40.pack_ref.refs_2_), channel_id=1, source_target_pairs={{0,8},{8,0},{16,24},{24,16},{1,9},{9,1},{17,25},{25,17},{2,10},{10... | collective-permute-start | bytes 393224 | tf_op jit(solution)/shard_map/ppermute | solution.py:341
  6.6 1.6 %collective-permute-start.3 = (bf16[512,128]{1,0:T(8,128)(2,1)}, bf16[512,128]{1,0:T(8,128)(2,1)S(1)}, u32[]{:S(2)}, u32[]{:S(2)}) collective-permute-start(bf16[512,128]{1,0:T(8,128)(2,1)} %bitcast.17), channel_id=1, source_target_pairs={{0,8},{8,0},{16,24},{24,16},{1,9},{9,1},{17,25},{25,17},{2,10},{10... | collective-permute-start | bytes 393224 | tf_op jit(solution)/shard_map/ppermute | solution.py:341
  7.3 1.3 %collective-permute-start.4 = (bf16[512,128]{1,0:T(8,128)(2,1)S(1)}, bf16[512,128]{1,0:T(8,128)(2,1)S(1)}, u32[]{:S(2)}, u32[]{:S(2)}) collective-permute-start(bf16[512,128]{1,0:T(8,128)(2,1)S(1)} %collective-permute-done.refs_1_), channel_id=1, source_target_pairs={{0,8},{8,0},{16,24},{24,16},{1,9},{9,1},{17,25},{25,17},{2,10},{10... | collective-permute-start | bytes 393224 | tf_op jit(solution)/shard_map/ppermute | solution.py:341
  12.3 1.4 %collective-permute-start.6 = (bf16[576,128]{1,0:T(8,128)(2,1)S(1)}, bf16[576,128]{1,0:T(8,128)(2,1)S(1)}, u32[]{:S(2)}, u32[]{:S(2)}) collective-permute-start(bf16[576,128]{1,0:T(8,128)(2,1)S(1)} %collective-permute-done.5.refs_9_), channel_id=1, source_target_pairs={{0,8},{8,0},{16,24},{24,16},{1,9},{9,1},{17,25},{25,17},{2,10},{10... | collective-permute-start | bytes 442376 | tf_op jit(solution)/shard_map/ppermute | solution.py:341

commit v8 on v3

--- a/solution.py
+++ b/solution.py
@@ -48,9 +48,10 @@
 
 def state_kernel(
     decay_hbm, key_hbm, value_hbm, soft_value_hbm, query_hbm, soft_query_hbm, soft_key_hbm,
-    pack_ref, cum_row_ref, cum_col_ref, value_t_ref, key_ref, query_ref, soft_query_ref, soft_key_ref,
+    pack_ref, state_ref, cum_row_ref, cum_col_ref, value_t_ref, key_ref, query_ref, soft_query_ref, soft_key_ref,
     decay_ref, value_ref, soft_value_ref, sems,
 ):
+    rows, width = key_ref.shape
     copies = [
         pltpu.make_async_copy(source, target, sems.at[place])
         for place, (source, target) in enumerate(
@@ -67,7 +68,6 @@
     ]
     for copy in copies:
         copy.start()
-    rows, width = key_ref.shape
     upto = (iota((rows, rows), 0) <= iota((rows, rows), 1)).astype(F32).astype(BF16)
     copies[0].wait()
     parts = select_rows(three_parts(decay_ref[...]), PAD, rows)
@@ -81,11 +81,14 @@
     decayed = (key_ref[...].astype(F32) * jnp.exp(total - cum_col)).astype(BF16)
     value_t = jnp.transpose(value_ref[...])
     value_t_ref[...] = value_t
-    state_t = dot(value_t, decayed)
+    state_t = dot(value_t, decayed).astype(BF16)
+    tail = select_rows(three_parts(total), PAD, width)
+    state_ref[:width, :] = state_t
+    state_ref[width:, :] = tail
     for left in range(0, rows, width):
         pack_ref[left : left + width, :] = jnp.transpose(soft_value_ref[left : left + width, :])
-    pack_ref[rows : rows + width, :] = state_t.astype(BF16)
-    pack_ref[rows + width :, :] = select_rows(three_parts(total), PAD, width)
+    pack_ref[rows : rows + width, :] = state_t
+    pack_ref[rows + width :, :] = tail
     for copy in copies[4:]:
         copy.wait()
 
@@ -141,7 +144,7 @@
 
 
 def score_kernel(scale, step, axis, cores, chips, qt_ref, top_ref, total_ref, *refs):
-    key_refs, (probs_ref, factor_ref, sum_ref) = refs[:-3], refs[-3:]
+    *key_refs, probs_ref, factor_ref, sum_ref = refs
     rows = qt_ref.shape[1]
     position, numbers = block_numbers(axis, cores, chips)
     away = [jnp.where(number >= 0, 0.0, NEG) for number in numbers]
@@ -151,7 +154,7 @@
             mine = slice(start, start + step)
             query = qt_ref[:, mine]
             old = top_ref[:, mine]
-            scores = [dot(key_refs[i][...], query) for i in range(count)]
+            scores = [dot(key_ref[...], query) for key_ref in key_refs[:count]]
             top = old
             for score, off in zip(scores, away):
                 top = jnp.maximum(top, jnp.max(score, axis=0, keepdims=True) + off)
@@ -167,12 +170,12 @@
     by_chip(position, cores, len(key_refs), body)
 
 
-def carried_state(numbers, pack_refs, rows, width):
+def carried_state(numbers, parts, width):
     totals, states = [], []
-    for pack_ref in pack_refs:
-        tail = pack_ref[rows + width :, :].astype(F32)
+    for part in parts:
+        tail = part[width:, :].astype(F32)
         totals.append(tail[0:1] + tail[1:2] + tail[2:3])
-        states.append(pack_ref[rows : rows + width, :].astype(F32))
+        states.append(part[:width, :].astype(F32))
     carried = jnp.zeros((width, width), F32)
     for number, state in zip(numbers, states):
         between = jnp.where(number >= 0, 0.0, NEG)
@@ -182,82 +185,53 @@
     return carried.astype(BF16)
 
 
-def weighted_values(pack_refs, places, probs_ref, mine, rows, width):
-    out = None
-    for place, pack_ref in zip(places, pack_refs):
-        value_t = side_by_side(pack_ref, rows, width)
-        term = dot(value_t, probs_ref[place * rows : (place + 1) * rows, mine])
-        out = term if out is None else out + term
-    return out
-
-
-def write_out(step, numbers, places, pack_refs, linear_packs, refs, outs, buffers, sems):
-    lin_qt_ref, intra_ref, cum_row_ref, summed_ref, factor_ref, sum_ref, probs_ref = refs
-    width, rows = lin_qt_ref.shape
-    linear_buffer, softmax_buffer = buffers
-    softmax_copy, linear_copy = (
-        pltpu.make_async_copy(buffer, out, sems.at[place])
-        for place, (buffer, out) in enumerate(((softmax_buffer, outs[1]), (linear_buffer, outs[0])))
-    )
+def put_linear(step, carried, qt_ref, intra_ref, cum_row_ref, buffer):
+    width, rows = qt_ref.shape
     for start in range(0, rows, step):
         mine = slice(start, start + step)
-        summed = summed_ref[:, mine]
-        if factor_ref is not None:
-            summed = summed * factor_ref[:, mine]
-        more = weighted_values(pack_refs, places, probs_ref, mine, rows, width)
-        summed = summed if more is None else summed + more
-        softmax_buffer[mine, :] = jnp.transpose((summed / sum_ref[:, mine]).astype(BF16))
-    softmax_copy.start()
-    carried = carried_state(numbers, linear_packs, rows, width)
+        inter = dot(carried, qt_ref[:, mine])
+        raw = intra_ref[:, mine] + inter * jnp.exp(cum_row_ref[:, mine])
+        square = jnp.sum(raw * raw, axis=0, keepdims=True) * (1.0 / width)
+        buffer[mine, :] = jnp.transpose((raw * lax.rsqrt(square + TINY)).astype(BF16))
+
+
+def put_softmax(step, sofar, values_t, places, probs_ref, sum_ref, buffer):
+    rows = sum_ref.shape[1]
     for start in range(0, rows, step):
         mine = slice(start, start + step)
-        inter = dot(carried, lin_qt_ref[:, mine])
-        raw = intra_ref[:, mine] + inter * jnp.exp(cum_row_ref[:, mine])
-        square = jnp.sum(raw * raw, axis=0, keepdims=True) * (1.0 / width)
-        linear_buffer[mine, :] = jnp.transpose((raw * lax.rsqrt(square + TINY)).astype(BF16))
-    linear_copy.start()
-    softmax_copy.wait()
-    linear_copy.wait()
-
-
-def early_kernel(step, axis, cores, chips, places, *refs):
-    head, refs = refs[:7], refs[7:]
-    packs, (linear_ref, softmax_ref, sofar_ref, *scratch) = refs[: len(places)], refs[len(places) :]
-    lin_qt_ref, intra_ref, cum_row_ref, summed_ref, factor_ref, sum_ref, probs_ref = head
+        summed = sofar(mine)
+        for place, value_t in zip(places, values_t):
+            summed = summed + dot(value_t, probs_ref[place * rows : (place + 1) * rows, mine])
+        buffer[mine, :] = jnp.transpose((summed / sum_ref[:, mine]).astype(BF16))
+
+
+def finish_kernel(step, axis, cores, chips, *refs):
+    lin_qt_ref, intra_ref, cum_row_ref, summed_ref, factor_ref, sum_ref, probs_ref = refs[:7]
+    *received, linear_ref, softmax_ref, linear_buffer, softmax_buffer, sems = refs[7:]
+    near, received = received[: cores - 1], received[cores - 1 :]
+    states, values = received[: len(received) // 2], received[len(received) // 2 :]
     width, rows = lin_qt_ref.shape
     position, numbers = block_numbers(axis, cores, chips)
-
-    @pl.when(position >= cores)
-    def _():
-        for start in range(0, rows, step):
-            mine = slice(start, start + step)
-            sofar_ref[:, mine] = summed_ref[:, mine] * factor_ref[:, mine] + weighted_values(
-                packs, places, probs_ref, mine, rows, width
-            )
-
-    @pl.when(position < cores)
-    def _():
-        own = cores - 1
-        write_out(
-            step, numbers[:own], places[:own], packs[:own], packs[:own], head,
-            (linear_ref, softmax_ref), scratch[:2], scratch[2],
-        )
-
-
-def late_kernel(step, axis, cores, chips, early, late, *refs):
-    refs = refs[2:]
-    lin_qt_ref, intra_ref, cum_row_ref, sofar_ref, sum_ref, probs_ref = refs[:6]
-    count = len(early) + len(late)
-    packs, (linear_ref, softmax_ref, *scratch) = refs[6 : 6 + count], refs[6 + count :]
-    position, numbers = block_numbers(axis, cores, chips)
-
-    @pl.when(position >= cores)
-    def _():
-        write_out(
-            step, numbers, late, [packs[place] for place in late], packs,
-            (lin_qt_ref, intra_ref, cum_row_ref, sofar_ref, None, sum_ref, probs_ref),
-            (linear_ref, softmax_ref), scratch[:2], scratch[2],
-        )
+    linear_copy = pltpu.make_async_copy(linear_buffer, linear_ref, sems.at[0])
+    softmax_copy = pltpu.make_async_copy(softmax_buffer, softmax_ref, sems.at[1])
+
+    def body(count):
+        parts = [ref[rows:, :] for ref in near] + [ref[...] for ref in states]
+        put_linear(
+            step, carried_state(numbers, parts[:count], width), lin_qt_ref, intra_ref, cum_row_ref, linear_buffer
+        )
+        linear_copy.start()
+        values_t = [side_by_side(ref, rows, width) for ref in near]
+        values_t += [jnp.transpose(ref[...]) for ref in values[: count - len(near)]]
+        put_softmax(
+            step, lambda mine: summed_ref[:, mine] * factor_ref[:, mine],
+            values_t, range(count), probs_ref, sum_ref, softmax_buffer,
+        )
+        softmax_copy.start()
+        linear_copy.wait()
+        softmax_copy.wait()
+
+    by_chip(position, cores, len(near) + len(values), body)
 
 
 def keep_in_hbm(x):
@@ -303,23 +277,23 @@
     def across(x, apart):
         return lax.ppermute(x, axis, [(i, (i + apart * cores) % count) for i in range(count)])
 
-    def swapped(x, after=None):
-        if after is not None:
-            x, _ = lax.optimization_barrier((x, after))
+    def swapped(x):
         return lax.ppermute(x, axis, [(i, i ^ 1) for i in range(count)])
 
-    def spread(x):
-        far = [across(x, apart) for apart in range(1, chips)]
-        own = [swapped(x)] if cores == 2 else []
-        return own, far
-
-    def complete(of, after):
-        own, far = of
-        out = list(own)
-        for block in far:
+    def near(x):
+        return [swapped(x)] if cores == 2 else []
+
+    def far(x):
+        return [across(x, apart) for apart in range(1, chips)]
+
+    def completed(blocks, after=None):
+        out = []
+        for block in blocks:
             out.append(block)
             if cores == 2:
-                out.append(swapped(block, after))
+                if after is not None:
+                    block, _ = lax.optimization_barrier((block, after))
+                out.append(swapped(block))
         return out
 
     def one_head(lq, lk, lv, decay, sq, sk, sv):
@@ -330,50 +304,41 @@
         def shape(*dims, dtype=F32):
             return jax.ShapeDtypeStruct(dims, dtype)
 
-        row, flat, flat16 = shape(1, rows), shape(width, rows), shape(width, rows, dtype=BF16)
-        block = shape(rows, width, dtype=BF16)
-        keys = spread(sk)
-        pack, cum_row, cum_col, lin_vt, lk, lq, sq, sk = call(
+        def half(*dims):
+            return shape(*dims, dtype=BF16)
+
+        row, flat, flat16, block = shape(1, rows), shape(width, rows), half(width, rows), half(rows, width)
+        keys, values = far(sk), far(sv)
+        pack, state, cum_row, cum_col, lin_vt, lk, lq, sq, own_keys = call(
             state_kernel,
             (),
             (
-                shape(rows + width + PAD, width, dtype=BF16), row, shape(rows, width), flat16,
-                block, block, block, block,
+                half(rows + width + PAD, width), half(width + PAD, width),
+                row, shape(rows, width), flat16, block, block, block, block,
             ),
             given=(decay, lk, lv, sv, lq, sq, sk),
             scratch=(row, block, block),
         )
+        states, near_packs = far(state), near(pack)
         qt, top, total, summed = call(
-            functools.partial(soft_kernel, scale, step), (sq, sk, pack), (flat16, row, row, flat)
-        )
-        (pack, lin_vt), _ = lax.optimization_barrier(((pack, lin_vt), summed))
-        packs = spread(pack)
-        keys = complete(keys, summed)
-        (lq, lk), _ = lax.optimization_barrier(((lq, lk), keys[cores - 1 :: cores]))
+            functools.partial(soft_kernel, scale, step), (sq, own_keys, pack), (flat16, row, row, flat)
+        )
         lin_qt, intra = call(
             functools.partial(linear_kernel, step), (lq, lk, lin_vt, cum_row, cum_col), (flat16, flat)
         )
-        top, _ = lax.optimization_barrier((top, intra))
+        sent, _ = lax.optimization_barrier((sk, summed))
+        keys = [*near(sent), *completed(keys, (summed, intra))]
+        values, states = completed(values, (summed, intra, states)), completed(states, (summed, intra))
         probs, factor, sums = call(
             functools.partial(score_kernel, scale, step, *ring),
             (qt, top, total, *keys),
-            (shape(len(keys) * rows, rows, dtype=BF16), row, row),
-        )
-        packs = complete(packs, factor)
-        late = tuple(range(cores, len(packs), cores)) if cores == 2 else ()
-        early = tuple(place for place in range(len(packs)) if place not in late)
-        *began, sofar = call(
-            functools.partial(early_kernel, step, *ring, early),
-            (lin_qt, intra, cum_row, summed, factor, sums, probs, *(packs[place] for place in early)),
-            (flat,),
-            written=(block, block),
+            (half(len(keys) * rows, rows), row, row),
         )
         return call(
-            functools.partial(late_kernel, step, *ring, early, late),
-            (lin_qt, intra, cum_row, sofar, sums, probs, *packs),
+            functools.partial(finish_kernel, step, *ring),
+            (lin_qt, intra, cum_row, summed, factor, sums, probs, *near_packs, *states, *values),
             (),
             written=(block, block),
-            resumed=began,
         )
 
     outs = [

time: 13 us -> 13.5 us (1.038)
  starting transfers between devices: 3.67 us -> 6.27 us
  waiting for transfers between devices: 4.48 us -> 2.5 us
    ppermute x2 -> x3, starting transfers between devices: 3.09 us -> 5.09 us  [across(): lax.ppermute(x, axis, [(i, (i + apart * cores) % count) for i in range(co...]
    ppermute x2 -> x3, waiting for transfers between devices: 3.82 us -> 2.09 us  [across(): lax.ppermute(x, axis, [(i, (i + apart * cores) % count) for i in range(co...]
    ppermute x4 -> x5, starting transfers between devices: 0.58 us -> 1.17 us  [swapped(): return lax.ppermute(x, axis, [(i, i ^ 1) for i in range(count)])]
    ppermute x4 -> x5, waiting for transfers between devices: 0.66 us -> 0.41 us  [swapped(): return lax.ppermute(x, axis, [(i, i ^ 1) for i in range(count)])]
    pallas_call x6 -> x5, Pallas kernels: 4 us -> 3.94 us  [call(): pl.pallas_call(body, out_shape=(*map(kept_in_hbm, written), *map(kept_in_...]
  transfers between devices with their start and end apart: 6 -> 8, of which waited for: 4 -> 2; matrix products, arithmetic and copies ran while one was open for 0% -> 0% of each run, Pallas kernels for 31% -> 22%
where the time goes in v8:
time: 13.5 us; the launch traced here: 13.4 us
  starting transfers between devices  6.27 us (46%)
  Pallas kernels  3.94 us (29%)
  waiting for transfers between devices  2.5 us (19%)
  between operations  0.67 us (5%)
    ppermute x3, starting transfers between devices, across(): lax.ppermute(x, axis, [(i, (i + apart * cores) % count) for i in range(co...  5.09 us
    pallas_call x5, Pallas kernels, call(): pl.pallas_call(body, out_shape=(*map(kept_in_hbm, written), *map(kept_in_...  3.94 us
    ppermute x3, waiting for transfers between devices, across(): lax.ppermute(x, axis, [(i, (i + apart * cores) % count) for i in range(co...  2.09 us
    ppermute x5, starting transfers between devices, swapped(): return lax.ppermute(x, axis, [(i, i ^ 1) for i in range(count)])  1.17 us
    ppermute x5, waiting for transfers between devices, swapped(): return lax.ppermute(x, axis, [(i, i ^ 1) for i in range(count)])  0.41 us
  transfers between devices with their start and end apart: 8, of which 2 were waited for; matrix products, arithmetic and copies ran while one was open for 0% of the time, Pallas kernels for 22%

profile of v8, /device:TPU:0, one launch (start us, length us, event | category | flops | bytes accessed | tf_op | source)
XLA Modules:
  0.0 13.4 jit_solution(11834862466373431653)
XLA Ops:
  0.6 3.0 %collective-permute-start.1 = (bf16[512,128]{1,0:T(8,128)(2,1)}, bf16[512,128]{1,0:T(8,128)(2,1)S(1)}, u32[]{:S(2)}, u32[]{:S(2)}) collective-permute-start(bf16[512,128]{1,0:T(8,128)(2,1)} %bitcast.14), channel_id=1, source_target_pairs={{0,16},{8,24},{16,0},{24,8},{1,17},{9,25},{17,1},{25,9},{2,18},{10... | collective-permute-start | bytes 393224 | tf_op jit(solution)/shard_map/ppermute | solution.py:278
  3.6 0.1 collective-permute-start.6
  3.7 1.3 %shard_map.86 = (bf16[656,128]{1,0:T(8,128)(2,1)S(1)}, bf16[144,128]{1,0:T(8,128)(2,1)S(1)}, f32[1,512]{1,0:T(1,128)S(1)}, f32[512,128]{1,0:T(8,128)S(1)}, bf16[...) custom-call(f32[1,512]{1,0:T(1,128)} %decay_hbm.1, ...), custom_call_target="tpu_custom_call" | custom-call | bytes 1912832 | tf_op jit(solution)/shard_map/pallas_call | solution.py:259
  5.1 2.0 %collective-permute-start.4 = (bf16[144,128]{1,0:T(8,128)(2,1)S(1)}, bf16[144,128]{1,0:T(8,128)(2,1)S(1)}, u32[]{:S(2)}, u32[]{:S(2)}) collective-permute-start(bf16[144,128]{1,0:T(8,128)(2,1)S(1)} %get-tuple-element.45), channel_id=1, source_target_pairs={{0,16},{8,24},{16,0},{24,8},{1,17},{9,25},{17,1},{25,9},{2,18},{10... | collective-permute-start | bytes 110600 | tf_op jit(solution)/shard_map/ppermute | solution.py:278
  7.1 0.0 collective-permute-start.3
  7.1 0.6 %shard_map.88 = (bf16[128,512]{1,0:T(8,128)(2,1)S(1)}, f32[1,512]{1,0:T(1,128)S(1)}, f32[1,512]{1,0:T(1,128)S(1)}, f32[128,512]{1,0:T(8,128)S(1)}) custom-call(bf16[512,128]{1,0:T(8,128)(2,1)S(1)} %get-tuple-element.33.q_ref, bf16[512,128]{1,0:T(8,128)(2,1)S(1)} %get-tuple-element.34.k_ref, bf16[656,128]{1,0:T(8,128)(2,1)S(1)} %get-tuple-element.35.pack_ref), custom_call_target="tpu_custom_call" | custom-call | bytes 827392 | tf_op jit(solution)/shard_map/pallas_call | solution.py:259
  7.7 0.6 %collective-permute-start = (bf16[512,128]{1,0:T(8,128)(2,1)}, bf16[512,128]{1,0:T(8,128)(2,1)S(1)}, u32[]{:S(2)}, u32[]{:S(2)}) collective-permute-start(bf16[512,128]{1,0:T(8,128)(2,1)} %bitcast.16), channel_id=1, source_target_pairs={{0,8},{8,0},{16,24},{24,16},{1,9},{9,1},{17,25},{25,17},{2,10},{10... | collective-permute-start | bytes 393224 | tf_op jit(solution)/shard_map/ppermute | solution.py:281
  8.3 0.5 %shard_map.87 = (bf16[128,512]{1,0:T(8,128)(2,1)S(1)}, f32[128,512]{1,0:T(8,128)S(1)}) custom-call(bf16[512,128]{1,0:T(8,128)(2,1)S(1)} %get-tuple-element.26.q_ref, bf16[512,128]{1,0:T(8,128)(2,1)S(1)} %get-tuple-element.27.k_ref, bf16[128,512]{1,0:T(8,128)(2,1)S(1)} %get-tuple-element.28.value_t_ref, f32[1,512]{1,0:T(1,128)S(1)} %get-tuple-element.29.cum_row_ref.refs_2_, ...), custom_call_target="tpu_custom_call" | custom-call | bytes 1050624 | tf_op jit(solution)/shard_map/pallas_call | solution.py:259
  8.8 0.0 collective-permute-done.1.refs_1_
  8.8 0.1 collective-permute-start.2
  8.9 2.1 %collective-permute-done.4.refs_8_ = bf16[144,128]{1,0:T(8,128)(2,1)S(1)} collective-permute-done((bf16[144,128]{1,0:T(8,128)(2,1)S(1)}, bf16[144,128]{1,0:T(8,128)(2,1)S(1)}, u32[]{:S(2)}, u32[]{:S(2)}) %collective-permute-start.4) | collective-permute-done | bytes 36896 | tf_op jit(solution)/shard_map/ppermute | solution.py:278
  10.9 0.0 collective-permute-done.6.refs_10_
  10.9 0.0 collective-permute-start.7
  10.9 0.5 %collective-permute-start.5 = (bf16[144,128]{1,0:T(8,128)(2,1)S(1)}, bf16[144,128]{1,0:T(8,128)(2,1)S(1)}, u32[]{:S(2)}, u32[]{:S(2)}) collective-permute-start(bf16[144,128]{1,0:T(8,128)(2,1)S(1)} %collective-permute-done.4.refs_8_), channel_id=1, source_target_pairs={{0,8},{8,0},{16,24},{24,16},{1,9},{9,1},{17,25},{25,17},{2,10},{10... | collective-permute-start | bytes 110600 | tf_op jit(solution)/shard_map/ppermute | solution.py:281
  11.5 0.0 collective-permute-done.refs_0_
  11.5 0.0 collective-permute-done.2.refs_2_
  11.5 0.5 %shard_map.89 = (bf16[1536,512]{1,0:T(8,128)(2,1)S(1)}, f32[1,512]{1,0:T(1,128)S(1)}, f32[1,512]{1,0:T(1,128)S(1)}) custom-call(bf16[128,512]{1,0:T(8,128)(2,1)S(1)} %get-tuple-element.37.qt_ref, f32[1,512]{1,0:T(1,128)S(1)} %get-tuple-element.38.top_ref, f32[1,512]{1,0:T(1,128)S(1)} %get-tuple-element.39.total_ref, ...), custom_call_target="tpu_custom_call" | custom-call | bytes 2105344 | tf_op jit(solution)/shard_map/pallas_call | solution.py:259
  12.0 0.4 %collective-permute-done.5.refs_9_ = bf16[144,128]{1,0:T(8,128)(2,1)S(1)} collective-permute-done((bf16[144,128]{1,0:T(8,128)(2,1)S(1)}, bf16[144,128]{1,0:T(8,128)(2,1)S(1)}, u32[]{:S(2)}, u32[]{:S(2)}) %collective-permute-start.5) | collective-permute-done | bytes 36896 | tf_op jit(solution)/shard_map/ppermute | solution.py:281
  12.3 0.0 collective-permute-done.3.refs_7_
  12.4 0.0 collective-permute-done.7.refs_11_
  12.4 1.0 %shard_map.90 = (bf16[512,128]{1,0:T(8,128)(2,1)}, bf16[512,128]{1,0:T(8,128)(2,1)}) custom-call(bf16[128,512]{1,0:T(8,128)(2,1)S(1)} %get-tuple-element.31.refs_0_, f32[128,512]{1,0:T(8,128)S(1)} %get-tuple-element.32.refs_1_, f32[1,512]{1,0:T(1,128)S(1)} %get-tuple-element.29.cum_row_ref.refs_2_, f32[128,512]{1,0:T(8,128)S(1)} %get-tuple-element.36.refs_3_, ...), custom_call_target="tpu_custom_call" | custom-call | bytes 2738176 | tf_op jit(solution)/shard_map/pallas_call | solution.py:259
Async XLA Ops:
  0.6 8.1 %collective-permute-start.1 = (bf16[512,128]{1,0:T(8,128)(2,1)}, bf16[512,128]{1,0:T(8,128)(2,1)S(1)}, u32[]{:S(2)}, u32[]{:S(2)}) collective-permute-start(bf16[512,128]{1,0:T(8,128)(2,1)} %bitcast.14), channel_id=1, source_target_pairs={{0,16},{8,24},{16,0},{24,8},{1,17},{9,25},{17,1},{25,9},{2,18},{10... | collective-permute-start | bytes 393224 | tf_op jit(solution)/shard_map/ppermute | solution.py:278
  3.6 7.3 %collective-permute-start.6 = (bf16[512,128]{1,0:T(8,128)(2,1)}, bf16[512,128]{1,0:T(8,128)(2,1)S(1)}, u32[]{:S(2)}, u32[]{:S(2)}) collective-permute-start(bf16[512,128]{1,0:T(8,128)(2,1)} %bitcast.12), channel_id=1, source_target_pairs={{0,16},{8,24},{16,0},{24,8},{1,17},{9,25},{17,1},{25,9},{2,18},{10... | collective-permute-start | bytes 393224 | tf_op jit(solution)/shard_map/ppermute | solution.py:278
  5.1 5.9 %collective-permute-start.4 = (bf16[144,128]{1,0:T(8,128)(2,1)S(1)}, bf16[144,128]{1,0:T(8,128)(2,1)S(1)}, u32[]{:S(2)}, u32[]{:S(2)}) collective-permute-start(bf16[144,128]{1,0:T(8,128)(2,1)S(1)} %get-tuple-element.45), channel_id=1, source_target_pairs={{0,16},{8,24},{16,0},{24,8},{1,17},{9,25},{17,1},{25,9},{2,18},{10... | collective-permute-start | bytes 110600 | tf_op jit(solution)/shard_map/ppermute | solution.py:278
  7.1 5.3 %collective-permute-start.3 = (bf16[656,128]{1,0:T(8,128)(2,1)S(1)}, bf16[656,128]{1,0:T(8,128)(2,1)S(1)}, u32[]{:S(2)}, u32[]{:S(2)}) collective-permute-start(bf16[656,128]{1,0:T(8,128)(2,1)S(1)} %get-tuple-element.35.pack_ref), channel_id=1, source_target_pairs={{0,8},{8,0},{16,24},{24,16},{1,9},{9,1},{17,25},{25,17},{2,10},{10... | collective-permute-start | bytes 503816 | tf_op jit(solution)/shard_map/ppermute | solution.py:281
  7.7 3.8 %collective-permute-start = (bf16[512,128]{1,0:T(8,128)(2,1)}, bf16[512,128]{1,0:T(8,128)(2,1)S(1)}, u32[]{:S(2)}, u32[]{:S(2)}) collective-permute-start(bf16[512,128]{1,0:T(8,128)(2,1)} %bitcast.16), channel_id=1, source_target_pairs={{0,8},{8,0},{16,24},{24,16},{1,9},{9,1},{17,25},{25,17},{2,10},{10... | collective-permute-start | bytes 393224 | tf_op jit(solution)/shard_map/ppermute | solution.py:281
  8.8 2.7 %collective-permute-start.2 = (bf16[512,128]{1,0:T(8,128)(2,1)S(1)}, bf16[512,128]{1,0:T(8,128)(2,1)S(1)}, u32[]{:S(2)}, u32[]{:S(2)}) collective-permute-start(bf16[512,128]{1,0:T(8,128)(2,1)S(1)} %collective-permute-done.1.refs_1_), channel_id=1, source_target_pairs={{0,8},{8,0},{16,24},{24,16},{1,9},{9,1},{17,25},{25,17},{2,10},{10... | collective-permute-start | bytes 393224 | tf_op jit(solution)/shard_map/ppermute | solution.py:281
  10.9 1.4 %collective-permute-start.7 = (bf16[512,128]{1,0:T(8,128)(2,1)S(1)}, bf16[512,128]{1,0:T(8,128)(2,1)S(1)}, u32[]{:S(2)}, u32[]{:S(2)}) collective-permute-start(bf16[512,128]{1,0:T(8,128)(2,1)S(1)} %collective-permute-done.6.refs_10_), channel_id=1, source_target_pairs={{0,8},{8,0},{16,24},{24,16},{1,9},{9,1},{17,25},{25,17},{2,10},{10... | collective-permute-start | bytes 393224 | tf_op jit(solution)/shard_map/ppermute | solution.py:281
  10.9 1.4 %collective-permute-start.5 = (bf16[144,128]{1,0:T(8,128)(2,1)S(1)}, bf16[144,128]{1,0:T(8,128)(2,1)S(1)}, u32[]{:S(2)}, u32[]{:S(2)}) collective-permute-start(bf16[144,128]{1,0:T(8,128)(2,1)S(1)} %collective-permute-done.4.refs_8_), channel_id=1, source_target_pairs={{0,8},{8,0},{16,24},{24,16},{1,9},{9,1},{17,25},{25,17},{2,10},{10... | collective-permute-start | bytes 110600 | tf_op jit(solution)/shard_map/ppermute | solution.py:281

commit v9 on v8

--- a/solution.py
+++ b/solution.py
@@ -48,10 +48,9 @@
 
 def state_kernel(
     decay_hbm, key_hbm, value_hbm, soft_value_hbm, query_hbm, soft_query_hbm, soft_key_hbm,
-    pack_ref, state_ref, cum_row_ref, cum_col_ref, value_t_ref, key_ref, query_ref, soft_query_ref, soft_key_ref,
+    soft_vt_ref, state_ref, cum_row_ref, cum_col_ref, value_t_ref, key_ref, query_ref, soft_query_ref, soft_key_ref,
     decay_ref, value_ref, soft_value_ref, sems,
 ):
-    rows, width = key_ref.shape
     copies = [
         pltpu.make_async_copy(source, target, sems.at[place])
         for place, (source, target) in enumerate(
@@ -68,6 +67,7 @@
     ]
     for copy in copies:
         copy.start()
+    rows, width = key_ref.shape
     upto = (iota((rows, rows), 0) <= iota((rows, rows), 1)).astype(F32).astype(BF16)
     copies[0].wait()
     parts = select_rows(three_parts(decay_ref[...]), PAD, rows)
@@ -81,16 +81,57 @@
     decayed = (key_ref[...].astype(F32) * jnp.exp(total - cum_col)).astype(BF16)
     value_t = jnp.transpose(value_ref[...])
     value_t_ref[...] = value_t
-    state_t = dot(value_t, decayed).astype(BF16)
-    tail = select_rows(three_parts(total), PAD, width)
-    state_ref[:width, :] = state_t
-    state_ref[width:, :] = tail
+    state_ref[:width, :] = dot(value_t, decayed).astype(BF16)
+    state_ref[width:, :] = select_rows(three_parts(total), PAD, width)
     for left in range(0, rows, width):
-        pack_ref[left : left + width, :] = jnp.transpose(soft_value_ref[left : left + width, :])
-    pack_ref[rows : rows + width, :] = state_t
-    pack_ref[rows + width :, :] = tail
+        soft_vt_ref[left : left + width, :] = jnp.transpose(soft_value_ref[left : left + width, :])
     for copy in copies[4:]:
         copy.wait()
+
+
+def sum_of_parts(tail):
+    tail = tail.astype(F32)
+    return tail[0:1] + tail[1:2] + tail[2:3]
+
+
+def combine_kernel(axis, cores, *refs):
+    *state_refs, soft_vt_ref, pack_ref = refs
+    rows, width = soft_vt_ref.shape
+    share = width // cores
+    pack_ref[:rows, :] = soft_vt_ref[...]
+    states = [ref[:width, :].astype(F32) for ref in state_refs]
+    totals = [sum_of_parts(ref[width:, :]) for ref in state_refs]
+    state, total = states[0], totals[0]
+    if cores == 2:
+        upper = lax.rem(lax.axis_index(axis), 2) == 1
+        first, second = jnp.where(upper, states[1], state), jnp.where(upper, state, states[1])
+        state = jnp.exp(jnp.where(upper, total, totals[1])) * first + second
+        state = jnp.where(upper, state[share:], state[:share])
+        total = total + totals[1]
+    pack_ref[rows : rows + share, :] = state.astype(BF16)
+    if pack_ref.shape[0] > rows + share:
+        pack_ref[rows + share :, :] = select_rows(three_parts(total), PAD, width)
+
+
+def sum_of_parts(tail):
+    tail = tail.astype(F32)
+    return tail[0:1] + tail[1:2] + tail[2:3]
+
+
+def combine_kernel(axis, cores, *refs):
+    *state_refs, share_ref = refs
+    width = share_ref.shape[1]
+    states = [ref[:width, :].astype(F32) for ref in state_refs]
+    totals = [sum_of_parts(ref[width:, :]) for ref in state_refs]
+    state, total = states[0], totals[0]
+    if cores == 2:
+        upper = lax.rem(lax.axis_index(axis), 2) == 1
+        first, second = jnp.where(upper, states[1], state), jnp.where(upper, state, states[1])
+        state = jnp.exp(jnp.where(upper, total, totals[1])) * first + second
+        total = total + totals[1]
+    share_ref[:width, :] = state.astype(BF16)
+    if share_ref.shape[0] > width:
+        share_ref[width:, :] = select_rows(three_parts(total), PAD, width)
 
 
 def soft_kernel(scale, step, q_ref, k_ref, pack_ref, qt_ref, top_ref, total_ref, summed_ref):
@@ -126,28 +167,19 @@
         intra_ref[:, start:stop] = dot(value_t_ref[:, :stop], weights)
 
 
-def block_numbers(axis, cores, chips):
-    position = lax.axis_index(axis)
-    if cores == 1:
-        return position, [position - apart for apart in range(1, chips)]
-    other = lax.rem(position, 2)
-    partner = position + 1 - 2 * other
-    numbers = [jnp.where(other == 1, position - 1, -1)]
-    for apart in range(1, chips):
-        numbers += [position - 2 * apart, partner - 2 * apart]
-    return position, numbers
-
-
 def by_chip(position, cores, count, body):
     pl.when(position >= cores)(lambda: body(count))
     pl.when(position < cores)(lambda: body(cores - 1))
 
 
-def score_kernel(scale, step, axis, cores, chips, qt_ref, top_ref, total_ref, *refs):
-    *key_refs, probs_ref, factor_ref, sum_ref = refs
+def score_kernel(scale, step, axis, cores, offsets, qt_ref, top_ref, total_ref, *refs):
+    key_refs, (probs_ref, new_top_ref, factor_ref, sum_ref) = refs[:-4], refs[-4:]
     rows = qt_ref.shape[1]
-    position, numbers = block_numbers(axis, cores, chips)
-    away = [jnp.where(number >= 0, 0.0, NEG) for number in numbers]
+    position = lax.axis_index(axis)
+    chip = position // cores
+    away = [
+        jnp.where(position - chip * cores >= 1 if apart == 0 else chip >= apart, 0.0, NEG) for apart in offsets
+    ]
 
     def body(count):
         for start in range(0, rows, step):
@@ -160,28 +192,29 @@
                 top = jnp.maximum(top, jnp.max(score, axis=0, keepdims=True) + off)
             factor = jnp.exp2((old - top) * scale)
             total = total_ref[:, mine] * factor
-            for number, (score, off) in enumerate(zip(scores, away)):
+            for place, (score, off) in enumerate(zip(scores, away)):
                 probs = jnp.exp2((score - (top - off)) * scale)
                 total = total + jnp.sum(probs, axis=0, keepdims=True)
-                probs_ref[number * rows : (number + 1) * rows, mine] = probs.astype(BF16)
+                probs_ref[place * rows : (place + 1) * rows, mine] = probs.astype(BF16)
+            new_top_ref[:, mine] = top
             factor_ref[:, mine] = factor
             sum_ref[:, mine] = total
 
-    by_chip(position, cores, len(key_refs), body)
-
-
-def carried_state(numbers, parts, width):
-    totals, states = [], []
-    for part in parts:
-        tail = part[width:, :].astype(F32)
-        totals.append(tail[0:1] + tail[1:2] + tail[2:3])
-        states.append(part[:width, :].astype(F32))
+    pl.when(chip >= 1)(lambda: body(len(offsets)))
+    pl.when(chip < 1)(lambda: body(offsets.count(0)))
+
+
+def carried_state(position, cores, near, shares, width):
+    chip = position // cores
     carried = jnp.zeros((width, width), F32)
-    for number, state in zip(numbers, states):
-        between = jnp.where(number >= 0, 0.0, NEG)
-        for other, total in zip(numbers, totals):
-            between = between + jnp.where(other > number, 1.0, 0.0) * total
-        carried = carried + jnp.exp(between) * state
+    between = jnp.zeros((1, width), F32)
+    for apart, ref in enumerate(shares, 1):
+        carried = carried + jnp.exp(between + jnp.where(chip >= apart, 0.0, NEG)) * ref[:width, :].astype(F32)
+        if ref.shape[0] > width:
+            between = between + sum_of_parts(ref[width:, :])
+    for ref in near:
+        passed = jnp.exp(sum_of_parts(ref[width:, :])) * carried + ref[:width, :].astype(F32)
+        carried = jnp.where(position - chip * cores == 1, passed, carried)
     return carried.astype(BF16)
 
 
@@ -195,43 +228,67 @@
         buffer[mine, :] = jnp.transpose((raw * lax.rsqrt(square + TINY)).astype(BF16))
 
 
-def put_softmax(step, sofar, values_t, places, probs_ref, sum_ref, buffer):
-    rows = sum_ref.shape[1]
-    for start in range(0, rows, step):
-        mine = slice(start, start + step)
-        summed = sofar(mine)
-        for place, value_t in zip(places, values_t):
-            summed = summed + dot(value_t, probs_ref[place * rows : (place + 1) * rows, mine])
-        buffer[mine, :] = jnp.transpose((summed / sum_ref[:, mine]).astype(BF16))
-
-
-def finish_kernel(step, axis, cores, chips, *refs):
-    lin_qt_ref, intra_ref, cum_row_ref, summed_ref, factor_ref, sum_ref, probs_ref = refs[:7]
-    *received, linear_ref, softmax_ref, linear_buffer, softmax_buffer, sems = refs[7:]
-    near, received = received[: cores - 1], received[cores - 1 :]
-    states, values = received[: len(received) // 2], received[len(received) // 2 :]
+def value_sum(values_t, probs_ref, mine):
+    rows = values_t[0].shape[1]
+    terms = [
+        dot(value_t, probs_ref[place * rows : (place + 1) * rows, mine]) for place, value_t in enumerate(values_t)
+    ]
+    return functools.reduce(jnp.add, terms)
+
+
+def early_kernel(step, axis, cores, counts, *refs):
+    lin_qt_ref, intra_ref, cum_row_ref, summed_ref, factor_ref, sum_ref, probs_ref, late_factor_ref = refs[:8]
+    linear_ref, softmax_ref, sofar_ref, linear_buffer, softmax_buffer, sems = refs[-6:]
+    received, groups = list(refs[8:-6]), []
+    for count in counts:
+        groups.append(received[:count])
+        received = received[count:]
+    near_states, shares, near_values, values = groups
     width, rows = lin_qt_ref.shape
-    position, numbers = block_numbers(axis, cores, chips)
+    position = lax.axis_index(axis)
     linear_copy = pltpu.make_async_copy(linear_buffer, linear_ref, sems.at[0])
     softmax_copy = pltpu.make_async_copy(softmax_buffer, softmax_ref, sems.at[1])
 
     def body(count):
-        parts = [ref[rows:, :] for ref in near] + [ref[...] for ref in states]
-        put_linear(
-            step, carried_state(numbers, parts[:count], width), lin_qt_ref, intra_ref, cum_row_ref, linear_buffer
-        )
+        first = count == len(near_values)
+        carried = carried_state(position, cores, near_states, () if first else shares, width)
+        put_linear(step, carried, lin_qt_ref, intra_ref, cum_row_ref, linear_buffer)
         linear_copy.start()
-        values_t = [side_by_side(ref, rows, width) for ref in near]
-        values_t += [jnp.transpose(ref[...]) for ref in values[: count - len(near)]]
-        put_softmax(
-            step, lambda mine: summed_ref[:, mine] * factor_ref[:, mine],
-            values_t, range(count), probs_ref, sum_ref, softmax_buffer,
-        )
+        values_t = [side_by_side(ref, rows, width) for ref in near_values]
+        values_t += [jnp.transpose(ref[...]) for ref in values[: count - len(near_values)]]
+        for start in range(0, rows, step):
+            mine = slice(start, start + step)
+            summed = summed_ref[:, mine] * factor_ref[:, mine]
+            if values_t:
+                summed = summed + value_sum(values_t, probs_ref, mine)
+            if first:
+                softmax_buffer[mine, :] = jnp.transpose((summed / sum_ref[:, mine]).astype(BF16))
+            else:
+                sofar_ref[:, mine] = summed * late_factor_ref[:, mine]
+        if first:
+            softmax_copy.start()
+            softmax_copy.wait()
+        linear_copy.wait()
+
+    by_chip(position, cores, len(near_values) + len(values), body)
+
+
+def late_kernel(step, axis, cores, *refs):
+    sofar_ref, sum_ref, probs_ref, *values, softmax_ref, softmax_buffer, sems = refs[1:]
+    rows = sum_ref.shape[1]
+
+    @pl.when(lax.axis_index(axis) >= cores)
+    def _():
+        softmax_copy = pltpu.make_async_copy(softmax_buffer, softmax_ref, sems.at[0])
+        values_t = [jnp.transpose(ref[...]) for ref in values]
+        for start in range(0, rows, step):
+            mine = slice(start, start + step)
+            summed = sofar_ref[:, mine]
+            if values_t:
+                summed = summed + value_sum(values_t, probs_ref, mine)
+            softmax_buffer[mine, :] = jnp.transpose((summed / sum_ref[:, mine]).astype(BF16))
         softmax_copy.start()
-        linear_copy.wait()
         softmax_copy.wait()
-
-    by_chip(position, cores, len(near) + len(values), body)
 
 
 def keep_in_hbm(x):
@@ -280,26 +337,18 @@
     def swapped(x):
         return lax.ppermute(x, axis, [(i, i ^ 1) for i in range(count)])
 
-    def near(x):
-        return [swapped(x)] if cores == 2 else []
+    def near(blocks):
+        return [swapped(block) for block in blocks] if cores == 2 else []
 
     def far(x):
         return [across(x, apart) for apart in range(1, chips)]
 
-    def completed(blocks, after=None):
-        out = []
-        for block in blocks:
-            out.append(block)
-            if cores == 2:
-                if after is not None:
-                    block, _ = lax.optimization_barrier((block, after))
-                out.append(swapped(block))
-        return out
+    def passed(blocks, after):
+        return near(lax.optimization_barrier((block, after))[0] for block in blocks)
 
     def one_head(lq, lk, lv, decay, sq, sk, sv):
         step = math.gcd(rows, 256)
         scale = math.log2(math.e) / math.sqrt(width)
-        ring = (axis, cores, chips)
 
         def shape(*dims, dtype=F32):
             return jax.ShapeDtypeStruct(dims, dtype)
@@ -309,37 +358,62 @@
 
         row, flat, flat16, block = shape(1, rows), shape(width, rows), half(width, rows), half(rows, width)
         keys, values = far(sk), far(sv)
-        pack, state, cum_row, cum_col, lin_vt, lk, lq, sq, own_keys = call(
+        soft_vt, state, cum_row, cum_col, lin_vt, lk, lq, sq, own_keys = call(
             state_kernel,
             (),
-            (
-                half(rows + width + PAD, width), half(width + PAD, width),
-                row, shape(rows, width), flat16, block, block, block, block,
-            ),
+            (block, half(width + PAD, width), row, shape(rows, width), flat16, block, block, block, block),
             given=(decay, lk, lv, sv, lq, sq, sk),
             scratch=(row, block, block),
         )
-        states, near_packs = far(state), near(pack)
+        near_states, near_values = near([state]), near([soft_vt])
         qt, top, total, summed = call(
-            functools.partial(soft_kernel, scale, step), (sq, own_keys, pack), (flat16, row, row, flat)
-        )
+            functools.partial(soft_kernel, scale, step), (sq, own_keys, soft_vt), (flat16, row, row, flat)
+        )
+        near_states, _ = lax.optimization_barrier((near_states, summed))
+        (share,) = call(
+            functools.partial(combine_kernel, axis, cores),
+            (state, *near_states),
+            (half(width + (PAD if chips > 2 else 0), width),),
+        )
+        shares = far(share)
         lin_qt, intra = call(
             functools.partial(linear_kernel, step), (lq, lk, lin_vt, cum_row, cum_col), (flat16, flat)
         )
-        sent, _ = lax.optimization_barrier((sk, summed))
-        keys = [*near(sent), *completed(keys, (summed, intra))]
-        values, states = completed(values, (summed, intra, states)), completed(states, (summed, intra))
-        probs, factor, sums = call(
-            functools.partial(score_kernel, scale, step, *ring),
-            (qt, top, total, *keys),
-            (half(len(keys) * rows, rows), row, row),
-        )
-        return call(
-            functools.partial(finish_kernel, step, *ring),
-            (lin_qt, intra, cum_row, summed, factor, sums, probs, *near_packs, *states, *values),
+
+        def scored(top, total, blocks, offsets):
+            return call(
+                functools.partial(score_kernel, scale, step, axis, cores, offsets),
+                (qt, top, total, *blocks),
+                (half(len(blocks) * rows, rows), row, row, row),
+            )
+
+        apart = tuple(range(1, chips))
+        late_keys = passed(keys, (summed, intra))
+        probs, top, factor, sums = scored(top, total, [*near([sk]), *keys], (0,) * (cores - 1) + apart)
+        late_values = passed(values, (factor, shares))
+        late_keys, _ = lax.optimization_barrier((late_keys, values))
+        late_factor, late_sums = jnp.ones_like(factor), sums
+        if late_keys:
+            late_probs, _, late_factor, late_sums = scored(top, sums, late_keys, apart)
+        linear, softmax, sofar = call(
+            functools.partial(
+                early_kernel, step, axis, cores, [len(x) for x in (near_states, shares, near_values, values)]
+            ),
+            (
+                lin_qt, intra, cum_row, summed, factor, sums, probs, late_factor,
+                *near_states, *shares, *near_values, *values,
+            ),
+            (flat,),
+            written=(block, block),
+        )
+        (softmax,) = call(
+            functools.partial(late_kernel, step, axis, cores),
+            (sofar, late_sums, late_probs if late_keys else probs, *late_values),
             (),
-            written=(block, block),
-        )
+            written=(block,),
+            resumed=(softmax,),
+        )
+        return linear, softmax
 
     outs = [
         one_head(

time: 13.5 us -> 13.6 us (level)
  the two profiles are of different devices: /device:TPU:0 before, /device:TPU:27 now
where the time goes in v9:
time: 13.6 us; the launch traced here: 13.4 us
  Pallas kernels  6.3 us (46%)
  starting transfers between devices  5.54 us (41%)
  waiting for transfers between devices  0.9 us (7%)
  between operations  0.69 us (5%)
    pallas_call x8, Pallas kernels, call(): pl.pallas_call(body, out_shape=(*map(kept_in_hbm, written), *map(kept_in_...  6.3 us
    ppermute x5, starting transfers between devices, swapped(): return lax.ppermute(x, axis, [(i, i ^ 1) for i in range(count)])  3.69 us
    ppermute x3, starting transfers between devices, across(): lax.ppermute(x, axis, [(i, (i + apart * cores) % count) for i in range(co...  1.85 us
    ppermute x3, waiting for transfers between devices, across(): lax.ppermute(x, axis, [(i, (i + apart * cores) % count) for i in range(co...  0.56 us
    ppermute x5, waiting for transfers between devices, swapped(): return lax.ppermute(x, axis, [(i, i ^ 1) for i in range(count)])  0.34 us
  transfers between devices with their start and end apart: 8, of which 2 were waited for; matrix products, arithmetic and copies ran while one was open for 0% of the time, Pallas kernels for 40%

profile of v9, /device:TPU:27, one launch (start us, length us, event | category | flops | bytes accessed | tf_op | source)
XLA Modules:
  0.0 13.4 jit_solution(9943369115758023307)
XLA Ops:
  0.6 0.3 %collective-permute-start.1 = (bf16[512,128]{1,0:T(8,128)(2,1)}, bf16[512,128]{1,0:T(8,128)(2,1)S(1)}, u32[]{:S(2)}, u32[]{:S(2)}) collective-permute-start(bf16[512,128]{1,0:T(8,128)(2,1)} %bitcast.13), channel_id=1, source_target_pairs={{0,16},{8,24},{16,0},{24,8},{1,17},{9,25},{17,1},{25,9},{2,18},{10... | collective-permute-start | bytes 393224 | tf_op jit(solution)/shard_map/ppermute | solution.py:335
  1.0 1.0 %collective-permute-start = (bf16[512,128]{1,0:T(8,128)(2,1)}, bf16[512,128]{1,0:T(8,128)(2,1)S(1)}, u32[]{:S(2)}, u32[]{:S(2)}) collective-permute-start(bf16[512,128]{1,0:T(8,128)(2,1)} %bitcast.14), channel_id=1, source_target_pairs={{0,8},{8,0},{16,24},{24,16},{1,9},{9,1},{17,25},{25,17},{2,10},{10... | collective-permute-start | bytes 393224 | tf_op jit(solution)/shard_map/ppermute | solution.py:338
  1.9 1.2 %collective-permute-start.3 = (bf16[512,128]{1,0:T(8,128)(2,1)}, bf16[512,128]{1,0:T(8,128)(2,1)S(1)}, u32[]{:S(2)}, u32[]{:S(2)}) collective-permute-start(bf16[512,128]{1,0:T(8,128)(2,1)} %bitcast.16), channel_id=1, source_target_pairs={{0,16},{8,24},{16,0},{24,8},{1,17},{9,25},{17,1},{25,9},{2,18},{10... | collective-permute-start | bytes 393224 | tf_op jit(solution)/shard_map/ppermute | solution.py:335
  3.1 1.3 %shard_map.86 = (bf16[512,128]{1,0:T(8,128)(2,1)S(1)}, bf16[144,128]{1,0:T(8,128)(2,1)S(1)}, f32[1,512]{1,0:T(1,128)S(1)}, f32[512,128]{1,0:T(8,128)S(1)}, bf16[...) custom-call(f32[1,512]{1,0:T(1,128)} %decay_hbm.1, ...), custom_call_target="tpu_custom_call" | custom-call | bytes 1875968 | tf_op jit(solution)/shard_map/pallas_call | solution.py:316
  4.5 0.3 %collective-permute-start.4 = (bf16[144,128]{1,0:T(8,128)(2,1)S(1)}, bf16[144,128]{1,0:T(8,128)(2,1)S(1)}, u32[]{:S(2)}, u32[]{:S(2)}) collective-permute-start(bf16[144,128]{1,0:T(8,128)(2,1)S(1)} %get-tuple-element.52.refs_0_), channel_id=1, source_target_pairs={{0,8},{8,0},{16,24},{24,16},{1,9},{9,1},{17,25},{25,17},{2,10},{10... | collective-permute-start | bytes 110600 | tf_op jit(solution)/shard_map/ppermute | solution.py:338
  4.8 0.6 %shard_map.88 = (bf16[128,512]{1,0:T(8,128)(2,1)S(1)}, f32[1,512]{1,0:T(1,128)S(1)}, f32[1,512]{1,0:T(1,128)S(1)}, f32[128,512]{1,0:T(8,128)S(1)}) custom-call(bf16[512,128]{1,0:T(8,128)(2,1)S(1)} %get-tuple-element.38.q_ref, bf16[512,128]{1,0:T(8,128)(2,1)S(1)} %get-tuple-element.39.k_ref, bf16[512,128]{1,0:T(8,128)(2,1)S(1)} %get-tuple-element.40.pack_ref), custom_call_target="tpu_custom_call" | custom-call | bytes 790528 | tf_op jit(solution)/shard_map/pallas_call | solution.py:316
  5.4 0.3 %collective-permute-done.4.refs_1_.refs_8_ = bf16[144,128]{1,0:T(8,128)(2,1)S(1)} collective-permute-done((bf16[144,128]{1,0:T(8,128)(2,1)S(1)}, bf16[144,128]{1,0:T(8,128)(2,1)S(1)}, u32[]{:S(2)}, u32[]{:S(2)}) %collective-permute-start.4) | collective-permute-done | bytes 36896 | tf_op jit(solution)/shard_map/ppermute | solution.py:338
  5.8 0.3 %collective-permute-start.5 = (bf16[128,128]{1,0:T(8,128)(2,1)S(1)}, bf16[128,128]{1,0:T(8,128)(2,1)S(1)}, u32[]{:S(2)}, u32[]{:S(2)}) collective-permute-start(bf16[128,128]{1,0:T(8,128)(2,1)S(1)} %shard_map.91), channel_id=1, source_target_pairs={{0,16},{8,24},{16,0},{24,8},{1,17},{9,25},{17,1},{25,9},{2,18},{10... | collective-permute-start | bytes 98312 | tf_op jit(solution)/shard_map/ppermute | solution.py:335
  6.1 0.6 %collective-permute-start.6 = (bf16[512,128]{1,0:T(8,128)(2,1)S(1)}, bf16[512,128]{1,0:T(8,128)(2,1)S(1)}, u32[]{:S(2)}, u32[]{:S(2)}) collective-permute-start(bf16[512,128]{1,0:T(8,128)(2,1)S(1)} %get-tuple-element.40.pack_ref), channel_id=1, source_target_pairs={{0,8},{8,0},{16,24},{24,16},{1,9},{9,1},{17,25},{25,17},{2,10},{10... | collective-permute-start | bytes 393224 | tf_op jit(solution)/shard_map/ppermute | solution.py:338
  6.7 0.5 %shard_map.87 = (bf16[128,512]{1,0:T(8,128)(2,1)S(1)}, f32[128,512]{1,0:T(8,128)S(1)}) custom-call(bf16[512,128]{1,0:T(8,128)(2,1)S(1)} %get-tuple-element.31.q_ref, bf16[512,128]{1,0:T(8,128)(2,1)S(1)} %get-tuple-element.32.k_ref, bf16[128,512]{1,0:T(8,128)(2,1)S(1)} %get-tuple-element.33.value_t_ref, f32[1,512]{1,0:T(1,128)S(1)} %get-tuple-element.34.cum_row_ref.refs_2_, ...), custom_call_target="tpu_custom_call" | custom-call | bytes 1050624 | tf_op jit(solution)/shard_map/pallas_call | solution.py:316
  7.2 0.0 collective-permute-done.1.refs_1_
  7.2 0.8 %collective-permute-start.2 = (bf16[512,128]{1,0:T(8,128)(2,1)S(1)}, bf16[512,128]{1,0:T(8,128)(2,1)S(1)}, u32[]{:S(2)}, u32[]{:S(2)}) collective-permute-start(bf16[512,128]{1,0:T(8,128)(2,1)S(1)} %collective-permute-done.1.refs_1_), channel_id=1, source_target_pairs={{0,8},{8,0},{16,24},{24,16},{1,9},{9,1},{17,25},{25,17},{2,10},{10... | collective-permute-start | bytes 393224 | tf_op jit(solution)/shard_map/ppermute | solution.py:338
  8.0 0.0 collective-permute-done.refs_0_
  8.0 0.8 %shard_map.89 = (bf16[1024,512]{1,0:T(8,128)(2,1)S(1)}, f32[1,512]{1,0:T(1,128)S(1)}, f32[1,512]{1,0:T(1,128)S(1)}, f32[1,512]{1,0:T(1,128)S(1)}) custom-call(bf16[128,512]{1,0:T(8,128)(2,1)S(1)} %get-tuple-element.42.qt_ref, f32[1,512]{1,0:T(1,128)S(1)} %get-tuple-element.43.top_ref, f32[1,512]{1,0:T(1,128)S(1)} %get-tuple-element.44.total_ref, ...), custom_call_target="tpu_custom_call" | custom-call | bytes 1452032 | tf_op jit(solution)/shard_map/pallas_call | solution.py:316
  8.8 0.6 %collective-permute-done.5.refs_9_ = bf16[128,128]{1,0:T(8,128)(2,1)S(1)} collective-permute-done((bf16[128,128]{1,0:T(8,128)(2,1)S(1)}, bf16[128,128]{1,0:T(8,128)(2,1)S(1)}, u32[]{:S(2)}, u32[]{:S(2)}) %collective-permute-start.5) | collective-permute-done | bytes 32800 | tf_op jit(solution)/shard_map/ppermute | solution.py:335
  9.3 0.0 collective-permute-done.3.refs_11_
  9.3 1.0 %collective-permute-start.7 = (bf16[512,128]{1,0:T(8,128)(2,1)S(1)}, bf16[512,128]{1,0:T(8,128)(2,1)S(1)}, u32[]{:S(2)}, u32[]{:S(2)}) collective-permute-start(bf16[512,128]{1,0:T(8,128)(2,1)S(1)} %collective-permute-done.3.refs_11_), channel_id=1, source_target_pairs={{0,8},{8,0},{16,24},{24,16},{1,9},{9,1},{17,25},{25,17},{2,10},{10... | collective-permute-start | bytes 393224 | tf_op jit(solution)/shard_map/ppermute | solution.py:338
  10.3 0.0 collective-permute-done.2.refs_0_
  10.3 1.1 %shard_map.90 = (bf16[512,512]{1,0:T(8,128)(2,1)S(1)}, f32[1,512]{1,0:T(1,128)}, f32[1,512]{1,0:T(1,128)S(1)}, f32[1,512]{1,0:T(1,128)S(1)}) custom-call(bf16[128,512]{1,0:T(8,128)(2,1)S(1)} %get-tuple-element.42.qt_ref, f32[1,512]{1,0:T(1,128)S(1)} %get-tuple-element.48.top_ref, f32[1,512]{1,0:T(1,128)S(1)} %get-tuple-element.46.total_ref.refs_5_, ...), custom_call_target="tpu_custom_call" | custom-call | bytes 796672 | tf_op jit(solution)/shard_map/pallas_call | solution.py:316
  11.4 0.0 collective-permute-done.6.refs_10_
  11.4 1.0 %shard_map.92 = (bf16[512,128]{1,0:T(8,128)(2,1)}, bf16[512,128]{1,0:T(8,128)(2,1)}, f32[128,512]{1,0:T(8,128)S(1)}) custom-call(bf16[128,512]{1,0:T(8,128)(2,1)S(1)} %get-tuple-element.36.refs_0_, f32[128,512]{1,0:T(8,128)S(1)} %get-tuple-element.37.refs_1_, f32[1,512]{1,0:T(1,128)S(1)} %get-tuple-element.34.cum_row_ref.refs_2_, ...), custom_call_target="tpu_custom_call" | custom-call | bytes 2306048 | tf_op jit(solution)/shard_map/pallas_call | solution.py:316
  12.4 0.0 collective-permute-done.7.refs_4_
  12.4 1.0 %shard_map.93 = bf16[512,128]{1,0:T(8,128)(2,1)} custom-call(bf16[512,128]{1,0:T(8,128)(2,1)} %get-tuple-element.55.refs_0_, f32[128,512]{1,0:T(8,128)S(1)} %get-tuple-element.56.refs_1_, f32[1,512]{1,0:T(1,128)S(1)} %get-tuple-element.57.refs_2_, bf16[512,512]{1,0:T(8,128)(2,1)S(1)} %get-tuple-element.58.refs_3_, ...), custom_call_target="tpu_custom_call", output_to_operand_aliasing={{}: (0, {})} | custom-call | bytes 919552 | tf_op jit(solution)/shard_map/pallas_call | solution.py:316
  (1 shorter events, 0.0 us)
Async XLA Ops:
  0.6 6.5 %collective-permute-start.1 = (bf16[512,128]{1,0:T(8,128)(2,1)}, bf16[512,128]{1,0:T(8,128)(2,1)S(1)}, u32[]{:S(2)}, u32[]{:S(2)}) collective-permute-start(bf16[512,128]{1,0:T(8,128)(2,1)} %bitcast.13), channel_id=1, source_target_pairs={{0,16},{8,24},{16,0},{24,8},{1,17},{9,25},{17,1},{25,9},{2,18},{10... | collective-permute-start | bytes 393224 | tf_op jit(solution)/shard_map/ppermute | solution.py:335
  1.0 7.0 %collective-permute-start = (bf16[512,128]{1,0:T(8,128)(2,1)}, bf16[512,128]{1,0:T(8,128)(2,1)S(1)}, u32[]{:S(2)}, u32[]{:S(2)}) collective-permute-start(bf16[512,128]{1,0:T(8,128)(2,1)} %bitcast.14), channel_id=1, source_target_pairs={{0,8},{8,0},{16,24},{24,16},{1,9},{9,1},{17,25},{25,17},{2,10},{10... | collective-permute-start | bytes 393224 | tf_op jit(solution)/shard_map/ppermute | solution.py:338
  1.9 7.4 %collective-permute-start.3 = (bf16[512,128]{1,0:T(8,128)(2,1)}, bf16[512,128]{1,0:T(8,128)(2,1)S(1)}, u32[]{:S(2)}, u32[]{:S(2)}) collective-permute-start(bf16[512,128]{1,0:T(8,128)(2,1)} %bitcast.16), channel_id=1, source_target_pairs={{0,16},{8,24},{16,0},{24,8},{1,17},{9,25},{17,1},{25,9},{2,18},{10... | collective-permute-start | bytes 393224 | tf_op jit(solution)/shard_map/ppermute | solution.py:335
  4.5 1.3 %collective-permute-start.4 = (bf16[144,128]{1,0:T(8,128)(2,1)S(1)}, bf16[144,128]{1,0:T(8,128)(2,1)S(1)}, u32[]{:S(2)}, u32[]{:S(2)}) collective-permute-start(bf16[144,128]{1,0:T(8,128)(2,1)S(1)} %get-tuple-element.52.refs_0_), channel_id=1, source_target_pairs={{0,8},{8,0},{16,24},{24,16},{1,9},{9,1},{17,25},{25,17},{2,10},{10... | collective-permute-start | bytes 110600 | tf_op jit(solution)/shard_map/ppermute | solution.py:338
  5.8 3.5 %collective-permute-start.5 = (bf16[128,128]{1,0:T(8,128)(2,1)S(1)}, bf16[128,128]{1,0:T(8,128)(2,1)S(1)}, u32[]{:S(2)}, u32[]{:S(2)}) collective-permute-start(bf16[128,128]{1,0:T(8,128)(2,1)S(1)} %shard_map.91), channel_id=1, source_target_pairs={{0,16},{8,24},{16,0},{24,8},{1,17},{9,25},{17,1},{25,9},{2,18},{10... | collective-permute-start | bytes 98312 | tf_op jit(solution)/shard_map/ppermute | solution.py:335
  6.1 5.3 %collective-permute-start.6 = (bf16[512,128]{1,0:T(8,128)(2,1)S(1)}, bf16[512,128]{1,0:T(8,128)(2,1)S(1)}, u32[]{:S(2)}, u32[]{:S(2)}) collective-permute-start(bf16[512,128]{1,0:T(8,128)(2,1)S(1)} %get-tuple-element.40.pack_ref), channel_id=1, source_target_pairs={{0,8},{8,0},{16,24},{24,16},{1,9},{9,1},{17,25},{25,17},{2,10},{10... | collective-permute-start | bytes 393224 | tf_op jit(solution)/shard_map/ppermute | solution.py:338
  7.2 3.2 %collective-permute-start.2 = (bf16[512,128]{1,0:T(8,128)(2,1)S(1)}, bf16[512,128]{1,0:T(8,128)(2,1)S(1)}, u32[]{:S(2)}, u32[]{:S(2)}) collective-permute-start(bf16[512,128]{1,0:T(8,128)(2,1)S(1)} %collective-permute-done.1.refs_1_), channel_id=1, source_target_pairs={{0,8},{8,0},{16,24},{24,16},{1,9},{9,1},{17,25},{25,17},{2,10},{10... | collective-permute-start | bytes 393224 | tf_op jit(solution)/shard_map/ppermute | solution.py:338
  9.3 3.1 %collective-permute-start.7 = (bf16[512,128]{1,0:T(8,128)(2,1)S(1)}, bf16[512,128]{1,0:T(8,128)(2,1)S(1)}, u32[]{:S(2)}, u32[]{:S(2)}) collective-permute-start(bf16[512,128]{1,0:T(8,128)(2,1)S(1)} %collective-permute-done.3.refs_11_), channel_id=1, source_target_pairs={{0,8},{8,0},{16,24},{24,16},{1,9},{9,1},{17,25},{25,17},{2,10},{10... | collective-permute-start | bytes 393224 | tf_op jit(solution)/shard_map/ppermute | solution.py:338

commit v10 on v9

--- a/solution.py
+++ b/solution.py
@@ -173,7 +173,7 @@
 
 
 def score_kernel(scale, step, axis, cores, offsets, qt_ref, top_ref, total_ref, *refs):
-    key_refs, (probs_ref, new_top_ref, factor_ref, sum_ref) = refs[:-4], refs[-4:]
+    key_refs, (probs_ref, factor_ref, sum_ref, *new_top_ref) = refs[: len(offsets)], refs[len(offsets) :]
     rows = qt_ref.shape[1]
     position = lax.axis_index(axis)
     chip = position // cores
@@ -196,7 +196,8 @@
                 probs = jnp.exp2((score - (top - off)) * scale)
                 total = total + jnp.sum(probs, axis=0, keepdims=True)
                 probs_ref[place * rows : (place + 1) * rows, mine] = probs.astype(BF16)
-            new_top_ref[:, mine] = top
+            for ref in new_top_ref:
+                ref[:, mine] = top
             factor_ref[:, mine] = factor
             sum_ref[:, mine] = total
 
@@ -254,8 +255,7 @@
         carried = carried_state(position, cores, near_states, () if first else shares, width)
         put_linear(step, carried, lin_qt_ref, intra_ref, cum_row_ref, linear_buffer)
         linear_copy.start()
-        values_t = [side_by_side(ref, rows, width) for ref in near_values]
-        values_t += [jnp.transpose(ref[...]) for ref in values[: count - len(near_values)]]
+        values_t = [side_by_side(ref, rows, width) for ref in (*near_values, *values)[:count]]
         for start in range(0, rows, step):
             mine = slice(start, start + step)
             summed = summed_ref[:, mine] * factor_ref[:, mine]
@@ -280,7 +280,7 @@
     @pl.when(lax.axis_index(axis) >= cores)
     def _():
         softmax_copy = pltpu.make_async_copy(softmax_buffer, softmax_ref, sems.at[0])
-        values_t = [jnp.transpose(ref[...]) for ref in values]
+        values_t = [side_by_side(ref, rows, sofar_ref.shape[0]) for ref in values]
         for start in range(0, rows, step):
             mine = slice(start, start + step)
             summed = sofar_ref[:, mine]
@@ -357,7 +357,7 @@
             return shape(*dims, dtype=BF16)
 
         row, flat, flat16, block = shape(1, rows), shape(width, rows), half(width, rows), half(rows, width)
-        keys, values = far(sk), far(sv)
+        keys = far(sk)
         soft_vt, state, cum_row, cum_col, lin_vt, lk, lq, sq, own_keys = call(
             state_kernel,
             (),
@@ -365,7 +365,7 @@
             given=(decay, lk, lv, sv, lq, sq, sk),
             scratch=(row, block, block),
         )
-        near_states, near_values = near([state]), near([soft_vt])
+        values, near_states, near_values = far(soft_vt), near([state]), near([soft_vt])
         qt, top, total, summed = call(
             functools.partial(soft_kernel, scale, step), (sq, own_keys, soft_vt), (flat16, row, row, flat)
         )
@@ -380,21 +380,23 @@
             functools.partial(linear_kernel, step), (lq, lk, lin_vt, cum_row, cum_col), (flat16, flat)
         )
 
-        def scored(top, total, blocks, offsets):
+        def scored(top, total, blocks, offsets, more):
             return call(
                 functools.partial(score_kernel, scale, step, axis, cores, offsets),
                 (qt, top, total, *blocks),
-                (half(len(blocks) * rows, rows), row, row, row),
+                (half(len(blocks) * rows, rows), *[row] * (2 + more)),
             )
 
         apart = tuple(range(1, chips))
         late_keys = passed(keys, (summed, intra))
-        probs, top, factor, sums = scored(top, total, [*near([sk]), *keys], (0,) * (cores - 1) + apart)
+        probs, factor, sums, *top = scored(
+            top, total, [*near([own_keys]), *keys], (0,) * (cores - 1) + apart, len(late_keys) > 0
+        )
         late_values = passed(values, (factor, shares))
         late_keys, _ = lax.optimization_barrier((late_keys, values))
         late_factor, late_sums = jnp.ones_like(factor), sums
         if late_keys:
-            late_probs, _, late_factor, late_sums = scored(top, sums, late_keys, apart)
+            late_probs, late_factor, late_sums = scored(*top, sums, late_keys, apart, False)
         linear, softmax, sofar = call(
             functools.partial(
                 early_kernel, step, axis, cores, [len(x) for x in (near_states, shares, near_values, values)]

time: 13.6 us -> 13.2 us (0.971)
  the two profiles are of different devices: /device:TPU:27 before, /device:TPU:0 now
where the time goes in v10:
time: 13.2 us; the launch traced here: 13 us
  starting transfers between devices  6.14 us (47%)
  Pallas kernels  4.03 us (31%)
  waiting for transfers between devices  2.17 us (16%)
  between operations  0.7 us (5%)
    ppermute x3, starting transfers between devices, across(): lax.ppermute(x, axis, [(i, (i + apart * cores) % count) for i in range(co...  5.07 us
    pallas_call x8, Pallas kernels, call(): pl.pallas_call(body, out_shape=(*map(kept_in_hbm, written), *map(kept_in_...  4.03 us
    ppermute x3, waiting for transfers between devices, across(): lax.ppermute(x, axis, [(i, (i + apart * cores) % count) for i in range(co...  1.63 us
    ppermute x5, starting transfers between devices, swapped(): return lax.ppermute(x, axis, [(i, i ^ 1) for i in range(count)])  1.07 us
    ppermute x5, waiting for transfers between devices, swapped(): return lax.ppermute(x, axis, [(i, i ^ 1) for i in range(count)])  0.54 us
  transfers between devices with their start and end apart: 8, of which 3 were waited for; matrix products, arithmetic and copies ran while one was open for 0% of the time, Pallas kernels for 31%

profile of v10, /device:TPU:0, one launch (start us, length us, event | category | flops | bytes accessed | tf_op | source)
XLA Modules:
  0.0 13.0 jit_solution(11087720348127787949)
XLA Ops:
  0.6 3.0 %collective-permute-start.1 = (bf16[512,128]{1,0:T(8,128)(2,1)}, bf16[512,128]{1,0:T(8,128)(2,1)S(1)}, u32[]{:S(2)}, u32[]{:S(2)}) collective-permute-start(bf16[512,128]{1,0:T(8,128)(2,1)} %bitcast.14), channel_id=1, source_target_pairs={{0,16},{8,24},{16,0},{24,8},{1,17},{9,25},{17,1},{25,9},{2,18},{10... | collective-permute-start | bytes 393224 | tf_op jit(solution)/shard_map/ppermute | solution.py:335
  3.6 1.3 %shard_map.86 = (bf16[512,128]{1,0:T(8,128)(2,1)S(1)}, bf16[144,128]{1,0:T(8,128)(2,1)S(1)}, f32[1,512]{1,0:T(1,128)S(1)}, f32[512,128]{1,0:T(8,128)S(1)}, bf16[...) custom-call(f32[1,512]{1,0:T(1,128)} %decay_hbm.1, ...), custom_call_target="tpu_custom_call" | custom-call | bytes 1875968 | tf_op jit(solution)/shard_map/pallas_call | solution.py:316
  5.0 0.1 collective-permute-start
  5.1 0.1 collective-permute-start.3
  5.1 0.4 %collective-permute-start.4 = (bf16[144,128]{1,0:T(8,128)(2,1)S(1)}, bf16[144,128]{1,0:T(8,128)(2,1)S(1)}, u32[]{:S(2)}, u32[]{:S(2)}) collective-permute-start(bf16[144,128]{1,0:T(8,128)(2,1)S(1)} %get-tuple-element.52.refs_0_), channel_id=1, source_target_pairs={{0,8},{8,0},{16,24},{24,16},{1,9},{9,1},{17,25},{25,17},{2,10},{10... | collective-permute-start | bytes 110600 | tf_op jit(solution)/shard_map/ppermute | solution.py:338
  5.6 0.6 %shard_map.88 = (bf16[128,512]{1,0:T(8,128)(2,1)S(1)}, f32[1,512]{1,0:T(1,128)S(1)}, f32[1,512]{1,0:T(1,128)S(1)}, f32[128,512]{1,0:T(8,128)S(1)}) custom-call(bf16[512,128]{1,0:T(8,128)(2,1)S(1)} %get-tuple-element.38.q_ref, bf16[512,128]{1,0:T(8,128)(2,1)S(1)} %get-tuple-element.39.k_ref, bf16[512,128]{1,0:T(8,128)(2,1)S(1)} %get-tuple-element.40.pack_ref), custom_call_target="tpu_custom_call" | custom-call | bytes 790528 | tf_op jit(solution)/shard_map/pallas_call | solution.py:316
  6.2 0.3 %collective-permute-done.4.refs_1_.refs_8_ = bf16[144,128]{1,0:T(8,128)(2,1)S(1)} collective-permute-done((bf16[144,128]{1,0:T(8,128)(2,1)S(1)}, bf16[144,128]{1,0:T(8,128)(2,1)S(1)}, u32[]{:S(2)}, u32[]{:S(2)}) %collective-permute-start.4) | collective-permute-done | bytes 36896 | tf_op jit(solution)/shard_map/ppermute | solution.py:338
  6.5 2.0 %collective-permute-start.5 = (bf16[128,128]{1,0:T(8,128)(2,1)S(1)}, bf16[128,128]{1,0:T(8,128)(2,1)S(1)}, u32[]{:S(2)}, u32[]{:S(2)}) collective-permute-start(bf16[128,128]{1,0:T(8,128)(2,1)S(1)} %shard_map.91), channel_id=1, source_target_pairs={{0,16},{8,24},{16,0},{24,8},{1,17},{9,25},{17,1},{25,9},{2,18},{10... | collective-permute-start | bytes 98312 | tf_op jit(solution)/shard_map/ppermute | solution.py:335
  8.5 0.0 collective-permute-start.6
  8.5 0.5 %shard_map.87 = (bf16[128,512]{1,0:T(8,128)(2,1)S(1)}, f32[128,512]{1,0:T(8,128)S(1)}) custom-call(bf16[512,128]{1,0:T(8,128)(2,1)S(1)} %get-tuple-element.31.q_ref, bf16[512,128]{1,0:T(8,128)(2,1)S(1)} %get-tuple-element.32.k_ref, bf16[128,512]{1,0:T(8,128)(2,1)S(1)} %get-tuple-element.33.value_t_ref, f32[1,512]{1,0:T(1,128)S(1)} %get-tuple-element.34.cum_row_ref.refs_2_, ...), custom_call_target="tpu_custom_call" | custom-call | bytes 1050624 | tf_op jit(solution)/shard_map/pallas_call | solution.py:316
  9.0 0.0 collective-permute-done.1.refs_1_
  9.0 0.6 %collective-permute-start.2 = (bf16[512,128]{1,0:T(8,128)(2,1)S(1)}, bf16[512,128]{1,0:T(8,128)(2,1)S(1)}, u32[]{:S(2)}, u32[]{:S(2)}) collective-permute-start(bf16[512,128]{1,0:T(8,128)(2,1)S(1)} %collective-permute-done.1.refs_1_), channel_id=1, source_target_pairs={{0,8},{8,0},{16,24},{24,16},{1,9},{9,1},{17,25},{25,17},{2,10},{10... | collective-permute-start | bytes 393224 | tf_op jit(solution)/shard_map/ppermute | solution.py:338
  9.5 0.0 collective-permute-done.refs_0_
  9.6 0.5 %shard_map.89 = (bf16[1024,512]{1,0:T(8,128)(2,1)S(1)}, f32[1,512]{1,0:T(1,128)S(1)}, f32[1,512]{1,0:T(1,128)S(1)}, f32[1,512]{1,0:T(1,128)S(1)}) custom-call(bf16[128,512]{1,0:T(8,128)(2,1)S(1)} %get-tuple-element.42.qt_ref, f32[1,512]{1,0:T(1,128)S(1)} %get-tuple-element.43.top_ref, f32[1,512]{1,0:T(1,128)S(1)} %get-tuple-element.44.total_ref, ...), custom_call_target="tpu_custom_call" | custom-call | bytes 1452032 | tf_op jit(solution)/shard_map/pallas_call | solution.py:316
  10.1 1.6 %collective-permute-done.5.refs_9_ = bf16[128,128]{1,0:T(8,128)(2,1)S(1)} collective-permute-done((bf16[128,128]{1,0:T(8,128)(2,1)S(1)}, bf16[128,128]{1,0:T(8,128)(2,1)S(1)}, u32[]{:S(2)}, u32[]{:S(2)}) %collective-permute-start.5) | collective-permute-done | bytes 32800 | tf_op jit(solution)/shard_map/ppermute | solution.py:335
  11.7 0.0 collective-permute-done.3.refs_11_
  11.7 0.0 collective-permute-start.7
  11.7 0.0 collective-permute-done.2.refs_0_
  11.7 0.0 collective-permute-done.6.refs_10_
  11.7 1.0 %shard_map.92 = (bf16[512,128]{1,0:T(8,128)(2,1)}, bf16[512,128]{1,0:T(8,128)(2,1)}, f32[128,512]{1,0:T(8,128)S(1)}) custom-call(bf16[128,512]{1,0:T(8,128)(2,1)S(1)} %get-tuple-element.36.refs_0_, f32[128,512]{1,0:T(8,128)S(1)} %get-tuple-element.37.refs_1_, f32[1,512]{1,0:T(1,128)S(1)} %get-tuple-element.34.cum_row_ref.refs_2_, ...), custom_call_target="tpu_custom_call" | custom-call | bytes 2306048 | tf_op jit(solution)/shard_map/pallas_call | solution.py:316
  12.8 0.2 %collective-permute-done.7.refs_4_ = bf16[512,128]{1,0:T(8,128)(2,1)S(1)} collective-permute-done((bf16[512,128]{1,0:T(8,128)(2,1)S(1)}, bf16[512,128]{1,0:T(8,128)(2,1)S(1)}, u32[]{:S(2)}, u32[]{:S(2)}) %collective-permute-start.7) | collective-permute-done | bytes 131104 | tf_op jit(solution)/shard_map/ppermute | solution.py:338
  (3 shorter events, 0.1 us)
Async XLA Ops:
  0.6 8.3 %collective-permute-start.1 = (bf16[512,128]{1,0:T(8,128)(2,1)}, bf16[512,128]{1,0:T(8,128)(2,1)S(1)}, u32[]{:S(2)}, u32[]{:S(2)}) collective-permute-start(bf16[512,128]{1,0:T(8,128)(2,1)} %bitcast.14), channel_id=1, source_target_pairs={{0,16},{8,24},{16,0},{24,8},{1,17},{9,25},{17,1},{25,9},{2,18},{10... | collective-permute-start | bytes 393224 | tf_op jit(solution)/shard_map/ppermute | solution.py:335
  5.0 4.6 %collective-permute-start = (bf16[512,128]{1,0:T(8,128)(2,1)S(1)}, bf16[512,128]{1,0:T(8,128)(2,1)S(1)}, u32[]{:S(2)}, u32[]{:S(2)}) collective-permute-start(bf16[512,128]{1,0:T(8,128)(2,1)S(1)} %get-tuple-element.39.k_ref), channel_id=1, source_target_pairs={{0,8},{8,0},{16,24},{24,16},{1,9},{9,1},{17,25},{25,17},{2,10},{10... | collective-permute-start | bytes 393224 | tf_op jit(solution)/shard_map/ppermute | solution.py:338
  5.1 6.6 %collective-permute-start.3 = (bf16[512,128]{1,0:T(8,128)(2,1)S(1)}, bf16[512,128]{1,0:T(8,128)(2,1)S(1)}, u32[]{:S(2)}, u32[]{:S(2)}) collective-permute-start(bf16[512,128]{1,0:T(8,128)(2,1)S(1)} %get-tuple-element.40.pack_ref), channel_id=1, source_target_pairs={{0,16},{8,24},{16,0},{24,8},{1,17},{9,25},{17,1},{25,9},{2,18},{10... | collective-permute-start | bytes 393224 | tf_op jit(solution)/shard_map/ppermute | solution.py:335
  5.1 1.3 %collective-permute-start.4 = (bf16[144,128]{1,0:T(8,128)(2,1)S(1)}, bf16[144,128]{1,0:T(8,128)(2,1)S(1)}, u32[]{:S(2)}, u32[]{:S(2)}) collective-permute-start(bf16[144,128]{1,0:T(8,128)(2,1)S(1)} %get-tuple-element.52.refs_0_), channel_id=1, source_target_pairs={{0,8},{8,0},{16,24},{24,16},{1,9},{9,1},{17,25},{25,17},{2,10},{10... | collective-permute-start | bytes 110600 | tf_op jit(solution)/shard_map/ppermute | solution.py:338
  6.5 5.2 %collective-permute-start.5 = (bf16[128,128]{1,0:T(8,128)(2,1)S(1)}, bf16[128,128]{1,0:T(8,128)(2,1)S(1)}, u32[]{:S(2)}, u32[]{:S(2)}) collective-permute-start(bf16[128,128]{1,0:T(8,128)(2,1)S(1)} %shard_map.91), channel_id=1, source_target_pairs={{0,16},{8,24},{16,0},{24,8},{1,17},{9,25},{17,1},{25,9},{2,18},{10... | collective-permute-start | bytes 98312 | tf_op jit(solution)/shard_map/ppermute | solution.py:335
  8.5 3.3 %collective-permute-start.6 = (bf16[512,128]{1,0:T(8,128)(2,1)S(1)}, bf16[512,128]{1,0:T(8,128)(2,1)S(1)}, u32[]{:S(2)}, u32[]{:S(2)}) collective-permute-start(bf16[512,128]{1,0:T(8,128)(2,1)S(1)} %get-tuple-element.40.pack_ref), channel_id=1, source_target_pairs={{0,8},{8,0},{16,24},{24,16},{1,9},{9,1},{17,25},{25,17},{2,10},{10... | collective-permute-start | bytes 393224 | tf_op jit(solution)/shard_map/ppermute | solution.py:338
  9.0 2.7 %collective-permute-start.2 = (bf16[512,128]{1,0:T(8,128)(2,1)S(1)}, bf16[512,128]{1,0:T(8,128)(2,1)S(1)}, u32[]{:S(2)}, u32[]{:S(2)}) collective-permute-start(bf16[512,128]{1,0:T(8,128)(2,1)S(1)} %collective-permute-done.1.refs_1_), channel_id=1, source_target_pairs={{0,8},{8,0},{16,24},{24,16},{1,9},{9,1},{17,25},{25,17},{2,10},{10... | collective-permute-start | bytes 393224 | tf_op jit(solution)/shard_map/ppermute | solution.py:338
  11.7 1.3 %collective-permute-start.7 = (bf16[512,128]{1,0:T(8,128)(2,1)S(1)}, bf16[512,128]{1,0:T(8,128)(2,1)S(1)}, u32[]{:S(2)}, u32[]{:S(2)}) collective-permute-start(bf16[512,128]{1,0:T(8,128)(2,1)S(1)} %collective-permute-done.3.refs_11_), channel_id=1, source_target_pairs={{0,8},{8,0},{16,24},{24,16},{1,9},{9,1},{17,25},{25,17},{2,10},{10... | collective-permute-start | bytes 393224 | tf_op jit(solution)/shard_map/ppermute | solution.py:338

commit v11 on v10

--- a/solution.py
+++ b/solution.py
@@ -95,10 +95,9 @@
 
 
 def combine_kernel(axis, cores, *refs):
-    *state_refs, soft_vt_ref, pack_ref = refs
-    rows, width = soft_vt_ref.shape
+    *state_refs, share_ref = refs
+    width = share_ref.shape[1]
     share = width // cores
-    pack_ref[:rows, :] = soft_vt_ref[...]
     states = [ref[:width, :].astype(F32) for ref in state_refs]
     totals = [sum_of_parts(ref[width:, :]) for ref in state_refs]
     state, total = states[0], totals[0]
@@ -108,30 +107,9 @@
         state = jnp.exp(jnp.where(upper, total, totals[1])) * first + second
         state = jnp.where(upper, state[share:], state[:share])
         total = total + totals[1]
-    pack_ref[rows : rows + share, :] = state.astype(BF16)
-    if pack_ref.shape[0] > rows + share:
-        pack_ref[rows + share :, :] = select_rows(three_parts(total), PAD, width)
-
-
-def sum_of_parts(tail):
-    tail = tail.astype(F32)
-    return tail[0:1] + tail[1:2] + tail[2:3]
-
-
-def combine_kernel(axis, cores, *refs):
-    *state_refs, share_ref = refs
-    width = share_ref.shape[1]
-    states = [ref[:width, :].astype(F32) for ref in state_refs]
-    totals = [sum_of_parts(ref[width:, :]) for ref in state_refs]
-    state, total = states[0], totals[0]
-    if cores == 2:
-        upper = lax.rem(lax.axis_index(axis), 2) == 1
-        first, second = jnp.where(upper, states[1], state), jnp.where(upper, state, states[1])
-        state = jnp.exp(jnp.where(upper, total, totals[1])) * first + second
-        total = total + totals[1]
-    share_ref[:width, :] = state.astype(BF16)
-    if share_ref.shape[0] > width:
-        share_ref[width:, :] = select_rows(three_parts(total), PAD, width)
+    share_ref[:share, :] = state.astype(BF16)
+    if share_ref.shape[0] > share:
+        share_ref[share:, :] = select_rows(three_parts(total), PAD, width)
 
 
 def soft_kernel(scale, step, q_ref, k_ref, pack_ref, qt_ref, top_ref, total_ref, summed_ref):
@@ -206,16 +184,23 @@
 
 
 def carried_state(position, cores, near, shares, width):
+    share = width // cores
     chip = position // cores
+    upper = position - chip * cores == 1
     carried = jnp.zeros((width, width), F32)
     between = jnp.zeros((1, width), F32)
-    for apart, ref in enumerate(shares, 1):
-        carried = carried + jnp.exp(between + jnp.where(chip >= apart, 0.0, NEG)) * ref[:width, :].astype(F32)
-        if ref.shape[0] > width:
-            between = between + sum_of_parts(ref[width:, :])
+    for apart in range(1, len(shares) // cores + 1):
+        parts = shares[(apart - 1) * cores : apart * cores]
+        state = [ref[:share, :].astype(F32) for ref in parts]
+        if cores == 2:
+            halves = jnp.where(upper, state[1], state[0]), jnp.where(upper, state[0], state[1])
+            state = [jnp.concatenate(halves, axis=0)]
+        carried = carried + jnp.exp(between + jnp.where(chip >= apart, 0.0, NEG)) * state[0]
+        if parts[0].shape[0] > share:
+            between = between + sum_of_parts(parts[0][share:, :])
     for ref in near:
         passed = jnp.exp(sum_of_parts(ref[width:, :])) * carried + ref[:width, :].astype(F32)
-        carried = jnp.where(position - chip * cores == 1, passed, carried)
+        carried = jnp.where(upper, passed, carried)
     return carried.astype(BF16)
 
 
@@ -237,58 +222,69 @@
     return functools.reduce(jnp.add, terms)
 
 
-def early_kernel(step, axis, cores, counts, *refs):
+def write_out(step, sofar, values_t, probs_ref, sum_ref, carried, linear_refs, outs, buffers, sems):
+    lin_qt_ref, intra_ref, cum_row_ref = linear_refs
+    linear_buffer, softmax_buffer = buffers
+    rows = sum_ref.shape[1]
+    linear_copy = pltpu.make_async_copy(linear_buffer, outs[0], sems.at[0])
+    softmax_copy = pltpu.make_async_copy(softmax_buffer, outs[1], sems.at[1])
+    for start in range(0, rows, step):
+        mine = slice(start, start + step)
+        summed = sofar(mine)
+        if values_t:
+            summed = summed + value_sum(values_t, probs_ref, mine)
+        softmax_buffer[mine, :] = jnp.transpose((summed / sum_ref[:, mine]).astype(BF16))
+    softmax_copy.start()
+    put_linear(step, carried(), lin_qt_ref, intra_ref, cum_row_ref, linear_buffer)
+    linear_copy.start()
+    softmax_copy.wait()
+    linear_copy.wait()
+
+
+def early_kernel(step, axis, cores, near_count, *refs):
     lin_qt_ref, intra_ref, cum_row_ref, summed_ref, factor_ref, sum_ref, probs_ref, late_factor_ref = refs[:8]
-    linear_ref, softmax_ref, sofar_ref, linear_buffer, softmax_buffer, sems = refs[-6:]
-    received, groups = list(refs[8:-6]), []
-    for count in counts:
-        groups.append(received[:count])
-        received = received[count:]
-    near_states, shares, near_values, values = groups
+    linear_ref, softmax_ref, sofar_ref, *scratch, sems = refs[-6:]
+    near_states, values = refs[8 : 8 + near_count], refs[8 + near_count : -6]
     width, rows = lin_qt_ref.shape
     position = lax.axis_index(axis)
-    linear_copy = pltpu.make_async_copy(linear_buffer, linear_ref, sems.at[0])
-    softmax_copy = pltpu.make_async_copy(softmax_buffer, softmax_ref, sems.at[1])
-
-    def body(count):
-        first = count == len(near_values)
-        carried = carried_state(position, cores, near_states, () if first else shares, width)
-        put_linear(step, carried, lin_qt_ref, intra_ref, cum_row_ref, linear_buffer)
-        linear_copy.start()
-        values_t = [side_by_side(ref, rows, width) for ref in (*near_values, *values)[:count]]
+
+    def scaled(mine):
+        return summed_ref[:, mine] * factor_ref[:, mine]
+
+    @pl.when(position >= cores)
+    def _():
+        values_t = [side_by_side(ref, rows, width) for ref in values]
         for start in range(0, rows, step):
             mine = slice(start, start + step)
-            summed = summed_ref[:, mine] * factor_ref[:, mine]
-            if values_t:
-                summed = summed + value_sum(values_t, probs_ref, mine)
-            if first:
-                softmax_buffer[mine, :] = jnp.transpose((summed / sum_ref[:, mine]).astype(BF16))
-            else:
-                sofar_ref[:, mine] = summed * late_factor_ref[:, mine]
-        if first:
-            softmax_copy.start()
-            softmax_copy.wait()
-        linear_copy.wait()
-
-    by_chip(position, cores, len(near_values) + len(values), body)
-
-
-def late_kernel(step, axis, cores, *refs):
-    sofar_ref, sum_ref, probs_ref, *values, softmax_ref, softmax_buffer, sems = refs[1:]
-    rows = sum_ref.shape[1]
-
-    @pl.when(lax.axis_index(axis) >= cores)
+            summed = scaled(mine) + value_sum(values_t, probs_ref, mine)
+            sofar_ref[:, mine] = summed * late_factor_ref[:, mine]
+
+    @pl.when(position < cores)
     def _():
-        softmax_copy = pltpu.make_async_copy(softmax_buffer, softmax_ref, sems.at[0])
-        values_t = [side_by_side(ref, rows, sofar_ref.shape[0]) for ref in values]
-        for start in range(0, rows, step):
-            mine = slice(start, start + step)
-            summed = sofar_ref[:, mine]
-            if values_t:
-                summed = summed + value_sum(values_t, probs_ref, mine)
-            softmax_buffer[mine, :] = jnp.transpose((summed / sum_ref[:, mine]).astype(BF16))
-        softmax_copy.start()
-        softmax_copy.wait()
+        write_out(
+            step, scaled, [side_by_side(ref, rows, width) for ref in values[:near_count]], probs_ref, sum_ref,
+            lambda: carried_state(position, cores, near_states, (), width),
+            (lin_qt_ref, intra_ref, cum_row_ref), (linear_ref, softmax_ref), scratch, sems,
+        )
+
+
+def late_kernel(step, axis, cores, counts, *refs):
+    refs = refs[2:]
+    lin_qt_ref, intra_ref, cum_row_ref, sofar_ref, sum_ref, probs_ref = refs[:6]
+    linear_ref, softmax_ref, *scratch, sems = refs[-5:]
+    near_states = refs[6 : 6 + counts[0]]
+    shares = refs[6 + counts[0] : 6 + counts[0] + counts[1]]
+    values = refs[6 + counts[0] + counts[1] : -5]
+    width, rows = lin_qt_ref.shape
+    position = lax.axis_index(axis)
+
+    @pl.when(position >= cores)
+    def _():
+        write_out(
+            step, lambda mine: sofar_ref[:, mine], [side_by_side(ref, rows, width) for ref in values],
+            probs_ref, sum_ref, lambda: carried_state(position, cores, near_states, shares, width),
+            (lin_qt_ref, intra_ref, cum_row_ref), (linear_ref, softmax_ref), scratch, sems,
+        )
 
 
 def keep_in_hbm(x):
@@ -373,7 +369,7 @@
         (share,) = call(
             functools.partial(combine_kernel, axis, cores),
             (state, *near_states),
-            (half(width + (PAD if chips > 2 else 0), width),),
+            (half(width // cores + (PAD if chips > 2 else 0), width),),
         )
         shares = far(share)
         lin_qt, intra = call(
@@ -397,25 +393,28 @@
         late_factor, late_sums = jnp.ones_like(factor), sums
         if late_keys:
             late_probs, late_factor, late_sums = scored(*top, sums, late_keys, apart, False)
-        linear, softmax, sofar = call(
-            functools.partial(
-                early_kernel, step, axis, cores, [len(x) for x in (near_states, shares, near_values, values)]
-            ),
+        late_shares = passed(shares, values)
+        if cores == 2:
+            shares = [part for pair in zip(shares, late_shares) for part in pair]
+        *began, sofar = call(
+            functools.partial(early_kernel, step, axis, cores, len(near_states)),
             (
                 lin_qt, intra, cum_row, summed, factor, sums, probs, late_factor,
-                *near_states, *shares, *near_values, *values,
+                *near_states, *near_values, *values,
             ),
             (flat,),
             written=(block, block),
         )
-        (softmax,) = call(
-            functools.partial(late_kernel, step, axis, cores),
-            (sofar, late_sums, late_probs if late_keys else probs, *late_values),
+        return call(
+            functools.partial(late_kernel, step, axis, cores, (len(near_states), len(shares))),
+            (
+                lin_qt, intra, cum_row, sofar, late_sums, late_probs if late_keys else probs,
+                *near_states, *shares, *late_values,
+            ),
             (),
-            written=(block,),
-            resumed=(softmax,),
-        )
-        return linear, softmax
+            written=(block, block),
+            resumed=began,
+        )
 
     outs = [
         one_head(

time: 13.2 us -> 13.2 us (level)
  waiting for transfers between devices: 2.17 us -> 1.58 us
  starting transfers between devices: 6.14 us -> 6.64 us
    ppermute x5 -> x6, starting transfers between devices: 1.07 us -> 1.57 us  [swapped(): return lax.ppermute(x, axis, [(i, i ^ 1) for i in range(count)])]
    ppermute x3, waiting for transfers between devices: 1.63 us -> 1.28 us  [across(): lax.ppermute(x, axis, [(i, (i + apart * cores) % count) for i in range(co...]
    ppermute x5 -> x6, waiting for transfers between devices: 0.54 us -> 0.3 us  [swapped(): return lax.ppermute(x, axis, [(i, i ^ 1) for i in range(count)])]
  transfers between devices with their start and end apart: 8 -> 9, of which waited for: 3 -> 2; matrix products, arithmetic and copies ran while one was open for 0% -> 0% of each run, Pallas kernels for 31% -> 31%
where the time goes in v11:
time: 13.2 us; the launch traced here: 13 us
  starting transfers between devices  6.64 us (50%)
  Pallas kernels  4.08 us (31%)
  waiting for transfers between devices  1.58 us (12%)
  between operations  0.72 us (5%)
    ppermute x3, starting transfers between devices, across(): lax.ppermute(x, axis, [(i, (i + apart * cores) % count) for i in range(co...  5.07 us
    pallas_call x8, Pallas kernels, call(): pl.pallas_call(body, out_shape=(*map(kept_in_hbm, written), *map(kept_in_...  4.08 us
    ppermute x6, starting transfers between devices, swapped(): return lax.ppermute(x, axis, [(i, i ^ 1) for i in range(count)])  1.57 us
    ppermute x3, waiting for transfers between devices, across(): lax.ppermute(x, axis, [(i, (i + apart * cores) % count) for i in range(co...  1.28 us
    ppermute x6, waiting for transfers between devices, swapped(): return lax.ppermute(x, axis, [(i, i ^ 1) for i in range(count)])  0.3 us
  transfers between devices with their start and end apart: 9, of which 2 were waited for; matrix products, arithmetic and copies ran while one was open for 0% of the time, Pallas kernels for 31%

profile of v11, /device:TPU:0, one launch (start us, length us, event | category | flops | bytes accessed | tf_op | source)
XLA Modules:
  0.0 13.0 jit_solution(9274361322598340226)
XLA Ops:
  0.6 3.0 %collective-permute-start.1 = (bf16[512,128]{1,0:T(8,128)(2,1)}, bf16[512,128]{1,0:T(8,128)(2,1)S(1)}, u32[]{:S(2)}, u32[]{:S(2)}) collective-permute-start(bf16[512,128]{1,0:T(8,128)(2,1)} %bitcast.15), channel_id=1, source_target_pairs={{0,16},{8,24},{16,0},{24,8},{1,17},{9,25},{17,1},{25,9},{2,18},{10... | collective-permute-start | bytes 393224 | tf_op jit(solution)/shard_map/ppermute | solution.py:331
  3.6 1.3 %shard_map.86 = (bf16[512,128]{1,0:T(8,128)(2,1)S(1)}, bf16[144,128]{1,0:T(8,128)(2,1)S(1)}, f32[1,512]{1,0:T(1,128)S(1)}, f32[512,128]{1,0:T(8,128)S(1)}, bf16[...) custom-call(f32[1,512]{1,0:T(1,128)} %decay_hbm.1, ...), custom_call_target="tpu_custom_call" | custom-call | bytes 1875968 | tf_op jit(solution)/shard_map/pallas_call | solution.py:312
  5.0 0.1 collective-permute-start
  5.1 0.1 collective-permute-start.3
  5.1 0.4 %collective-permute-start.4 = (bf16[144,128]{1,0:T(8,128)(2,1)S(1)}, bf16[144,128]{1,0:T(8,128)(2,1)S(1)}, u32[]{:S(2)}, u32[]{:S(2)}) collective-permute-start(bf16[144,128]{1,0:T(8,128)(2,1)S(1)} %get-tuple-element.55.refs_0_), channel_id=1, source_target_pairs={{0,8},{8,0},{16,24},{24,16},{1,9},{9,1},{17,25},{25,17},{2,10},{10... | collective-permute-start | bytes 110600 | tf_op jit(solution)/shard_map/ppermute | solution.py:334
  5.6 0.6 %shard_map.88 = (bf16[128,512]{1,0:T(8,128)(2,1)S(1)}, f32[1,512]{1,0:T(1,128)S(1)}, f32[1,512]{1,0:T(1,128)S(1)}, f32[128,512]{1,0:T(8,128)S(1)}) custom-call(bf16[512,128]{1,0:T(8,128)(2,1)S(1)} %get-tuple-element.41.q_ref, bf16[512,128]{1,0:T(8,128)(2,1)S(1)} %get-tuple-element.42.k_ref, bf16[512,128]{1,0:T(8,128)(2,1)S(1)} %get-tuple-element.43.pack_ref), custom_call_target="tpu_custom_call" | custom-call | bytes 790528 | tf_op jit(solution)/shard_map/pallas_call | solution.py:312
  6.2 0.3 %collective-permute-done.4.refs_8_.refs_1_ = bf16[144,128]{1,0:T(8,128)(2,1)S(1)} collective-permute-done((bf16[144,128]{1,0:T(8,128)(2,1)S(1)}, bf16[144,128]{1,0:T(8,128)(2,1)S(1)}, u32[]{:S(2)}, u32[]{:S(2)}) %collective-permute-start.4) | collective-permute-done | bytes 36896 | tf_op jit(solution)/shard_map/ppermute | solution.py:334
  6.5 2.0 %collective-permute-start.6 = (bf16[64,128]{1,0:T(8,128)(2,1)S(1)}, bf16[64,128]{1,0:T(8,128)(2,1)S(1)}, u32[]{:S(2)}, u32[]{:S(2)}) collective-permute-start(bf16[64,128]{1,0:T(8,128)(2,1)S(1)} %shard_map.92), channel_id=1, source_target_pairs={{0,16},{8,24},{16,0},{24,8},{1,17},{9,25},{17,1},{25,9},{2,18},{10... | collective-permute-start | bytes 49160 | tf_op jit(solution)/shard_map/ppermute | solution.py:331
  8.5 0.5 %shard_map.87 = (bf16[128,512]{1,0:T(8,128)(2,1)S(1)}, f32[128,512]{1,0:T(8,128)S(1)}) custom-call(bf16[512,128]{1,0:T(8,128)(2,1)S(1)} %get-tuple-element.34.q_ref, bf16[512,128]{1,0:T(8,128)(2,1)S(1)} %get-tuple-element.35.k_ref, bf16[128,512]{1,0:T(8,128)(2,1)S(1)} %get-tuple-element.36.value_t_ref, ...), custom_call_target="tpu_custom_call" | custom-call | bytes 1050624 | tf_op jit(solution)/shard_map/pallas_call | solution.py:312
  9.0 0.0 collective-permute-done.1.refs_1_
  9.0 0.1 collective-permute-start.2
  9.1 0.5 %collective-permute-start.5 = (bf16[512,128]{1,0:T(8,128)(2,1)S(1)}, bf16[512,128]{1,0:T(8,128)(2,1)S(1)}, u32[]{:S(2)}, u32[]{:S(2)}) collective-permute-start(bf16[512,128]{1,0:T(8,128)(2,1)S(1)} %get-tuple-element.43.pack_ref), channel_id=1, source_target_pairs={{0,8},{8,0},{16,24},{24,16},{1,9},{9,1},{17,25},{25,17},{2,10},{10... | collective-permute-start | bytes 393224 | tf_op jit(solution)/shard_map/ppermute | solution.py:334
  9.5 0.0 collective-permute-done.refs_0_
  9.6 0.5 %shard_map.89 = (bf16[1024,512]{1,0:T(8,128)(2,1)S(1)}, f32[1,512]{1,0:T(1,128)S(1)}, f32[1,512]{1,0:T(1,128)S(1)}, f32[1,512]{1,0:T(1,128)S(1)}) custom-call(bf16[128,512]{1,0:T(8,128)(2,1)S(1)} %get-tuple-element.45.qt_ref, f32[1,512]{1,0:T(1,128)S(1)} %get-tuple-element.46.top_ref, f32[1,512]{1,0:T(1,128)S(1)} %get-tuple-element.47.total_ref, ...), custom_call_target="tpu_custom_call" | custom-call | bytes 1452032 | tf_op jit(solution)/shard_map/pallas_call | solution.py:312
  10.1 1.3 %collective-permute-done.6.refs_9_ = bf16[64,128]{1,0:T(8,128)(2,1)S(1)} collective-permute-done((bf16[64,128]{1,0:T(8,128)(2,1)S(1)}, bf16[64,128]{1,0:T(8,128)(2,1)S(1)}, u32[]{:S(2)}, u32[]{:S(2)}) %collective-permute-start.6) | collective-permute-done | bytes 16416 | tf_op jit(solution)/shard_map/ppermute | solution.py:331
  11.3 0.0 collective-permute-done.3.refs_10_
  11.3 0.0 collective-permute-start.8
  11.3 0.5 %collective-permute-start.7 = (bf16[64,128]{1,0:T(8,128)(2,1)S(1)}, bf16[64,128]{1,0:T(8,128)(2,1)S(1)}, u32[]{:S(2)}, u32[]{:S(2)}) collective-permute-start(bf16[64,128]{1,0:T(8,128)(2,1)S(1)} %collective-permute-done.6.refs_9_), channel_id=1, source_target_pairs={{0,8},{8,0},{16,24},{24,16},{1,9},{9,1},{17,25},{25,17},{2,10},{10... | collective-permute-start | bytes 49160 | tf_op jit(solution)/shard_map/ppermute | solution.py:334
  11.8 0.0 collective-permute-done.2.refs_0_
  11.9 0.0 collective-permute-done.5.refs_9_
  11.9 1.1 %shard_map.91 = (bf16[512,128]{1,0:T(8,128)(2,1)}, bf16[512,128]{1,0:T(8,128)(2,1)}, f32[128,512]{1,0:T(8,128)S(1)}) custom-call(bf16[128,512]{1,0:T(8,128)(2,1)S(1)} %get-tuple-element.39.refs_0_.refs_2_, f32[128,512]{1,0:T(8,128)S(1)} %get-tuple-element.40.refs_1_.refs_3_, f32[1,512]{1,0:T(1,128)S(1)} %get-tuple-element.37.cum_row_ref.refs_2_.refs_4_, ...), custom_call_target="tpu_custom_call" | custom-call | bytes 2273280 | tf_op jit(solution)/shard_map/pallas_call | solution.py:312
  12.9 0.0 collective-permute-done.7.refs_10_
  13.0 0.0 collective-permute-done.8.refs_11_
  (3 shorter events, 0.1 us)
Async XLA Ops:
  0.6 8.3 %collective-permute-start.1 = (bf16[512,128]{1,0:T(8,128)(2,1)}, bf16[512,128]{1,0:T(8,128)(2,1)S(1)}, u32[]{:S(2)}, u32[]{:S(2)}) collective-permute-start(bf16[512,128]{1,0:T(8,128)(2,1)} %bitcast.15), channel_id=1, source_target_pairs={{0,16},{8,24},{16,0},{24,8},{1,17},{9,25},{17,1},{25,9},{2,18},{10... | collective-permute-start | bytes 393224 | tf_op jit(solution)/shard_map/ppermute | solution.py:331
  5.0 4.6 %collective-permute-start = (bf16[512,128]{1,0:T(8,128)(2,1)S(1)}, bf16[512,128]{1,0:T(8,128)(2,1)S(1)}, u32[]{:S(2)}, u32[]{:S(2)}) collective-permute-start(bf16[512,128]{1,0:T(8,128)(2,1)S(1)} %get-tuple-element.42.k_ref), channel_id=1, source_target_pairs={{0,8},{8,0},{16,24},{24,16},{1,9},{9,1},{17,25},{25,17},{2,10},{10... | collective-permute-start | bytes 393224 | tf_op jit(solution)/shard_map/ppermute | solution.py:334
  5.1 6.3 %collective-permute-start.3 = (bf16[512,128]{1,0:T(8,128)(2,1)S(1)}, bf16[512,128]{1,0:T(8,128)(2,1)S(1)}, u32[]{:S(2)}, u32[]{:S(2)}) collective-permute-start(bf16[512,128]{1,0:T(8,128)(2,1)S(1)} %get-tuple-element.43.pack_ref), channel_id=1, source_target_pairs={{0,16},{8,24},{16,0},{24,8},{1,17},{9,25},{17,1},{25,9},{2,18},{10... | collective-permute-start | bytes 393224 | tf_op jit(solution)/shard_map/ppermute | solution.py:331
  5.1 1.3 %collective-permute-start.4 = (bf16[144,128]{1,0:T(8,128)(2,1)S(1)}, bf16[144,128]{1,0:T(8,128)(2,1)S(1)}, u32[]{:S(2)}, u32[]{:S(2)}) collective-permute-start(bf16[144,128]{1,0:T(8,128)(2,1)S(1)} %get-tuple-element.55.refs_0_), channel_id=1, source_target_pairs={{0,8},{8,0},{16,24},{24,16},{1,9},{9,1},{17,25},{25,17},{2,10},{10... | collective-permute-start | bytes 110600 | tf_op jit(solution)/shard_map/ppermute | solution.py:334
  6.5 4.8 %collective-permute-start.6 = (bf16[64,128]{1,0:T(8,128)(2,1)S(1)}, bf16[64,128]{1,0:T(8,128)(2,1)S(1)}, u32[]{:S(2)}, u32[]{:S(2)}) collective-permute-start(bf16[64,128]{1,0:T(8,128)(2,1)S(1)} %shard_map.92), channel_id=1, source_target_pairs={{0,16},{8,24},{16,0},{24,8},{1,17},{9,25},{17,1},{25,9},{2,18},{10... | collective-permute-start | bytes 49160 | tf_op jit(solution)/shard_map/ppermute | solution.py:331
  9.0 2.9 %collective-permute-start.2 = (bf16[512,128]{1,0:T(8,128)(2,1)S(1)}, bf16[512,128]{1,0:T(8,128)(2,1)S(1)}, u32[]{:S(2)}, u32[]{:S(2)}) collective-permute-start(bf16[512,128]{1,0:T(8,128)(2,1)S(1)} %collective-permute-done.1.refs_1_), channel_id=1, source_target_pairs={{0,8},{8,0},{16,24},{24,16},{1,9},{9,1},{17,25},{25,17},{2,10},{10... | collective-permute-start | bytes 393224 | tf_op jit(solution)/shard_map/ppermute | solution.py:334
  9.1 2.8 %collective-permute-start.5 = (bf16[512,128]{1,0:T(8,128)(2,1)S(1)}, bf16[512,128]{1,0:T(8,128)(2,1)S(1)}, u32[]{:S(2)}, u32[]{:S(2)}) collective-permute-start(bf16[512,128]{1,0:T(8,128)(2,1)S(1)} %get-tuple-element.43.pack_ref), channel_id=1, source_target_pairs={{0,8},{8,0},{16,24},{24,16},{1,9},{9,1},{17,25},{25,17},{2,10},{10... | collective-permute-start | bytes 393224 | tf_op jit(solution)/shard_map/ppermute | solution.py:334
  11.3 1.6 %collective-permute-start.8 = (bf16[512,128]{1,0:T(8,128)(2,1)S(1)}, bf16[512,128]{1,0:T(8,128)(2,1)S(1)}, u32[]{:S(2)}, u32[]{:S(2)}) collective-permute-start(bf16[512,128]{1,0:T(8,128)(2,1)S(1)} %collective-permute-done.3.refs_10_), channel_id=1, source_target_pairs={{0,8},{8,0},{16,24},{24,16},{1,9},{9,1},{17,25},{25,17},{2,10},{10... | collective-permute-start | bytes 393224 | tf_op jit(solution)/shard_map/ppermute | solution.py:334
  11.3 1.6 %collective-permute-start.7 = (bf16[64,128]{1,0:T(8,128)(2,1)S(1)}, bf16[64,128]{1,0:T(8,128)(2,1)S(1)}, u32[]{:S(2)}, u32[]{:S(2)}) collective-permute-start(bf16[64,128]{1,0:T(8,128)(2,1)S(1)} %collective-permute-done.6.refs_9_), channel_id=1, source_target_pairs={{0,8},{8,0},{16,24},{24,16},{1,9},{9,1},{17,25},{25,17},{2,10},{10... | collective-permute-start | bytes 49160 | tf_op jit(solution)/shard_map/ppermute | solution.py:334

commit v12 on v11

--- a/solution.py
+++ b/solution.py
@@ -234,38 +234,41 @@
         if values_t:
             summed = summed + value_sum(values_t, probs_ref, mine)
         softmax_buffer[mine, :] = jnp.transpose((summed / sum_ref[:, mine]).astype(BF16))
+    put_linear(step, carried(), lin_qt_ref, intra_ref, cum_row_ref, linear_buffer)
     softmax_copy.start()
-    put_linear(step, carried(), lin_qt_ref, intra_ref, cum_row_ref, linear_buffer)
     linear_copy.start()
     softmax_copy.wait()
     linear_copy.wait()
 
 
-def early_kernel(step, axis, cores, near_count, *refs):
-    lin_qt_ref, intra_ref, cum_row_ref, summed_ref, factor_ref, sum_ref, probs_ref, late_factor_ref = refs[:8]
-    linear_ref, softmax_ref, sofar_ref, *scratch, sems = refs[-6:]
-    near_states, values = refs[8 : 8 + near_count], refs[8 + near_count : -6]
+def first_kernel(step, axis, cores, *refs):
+    lin_qt_ref, intra_ref, cum_row_ref, summed_ref, factor_ref, sum_ref, probs_ref = refs[:7]
+    linear_ref, softmax_ref, *scratch, sems = refs[-5:]
+    near_states, near_values = refs[7 : 6 + cores], refs[6 + cores : -5]
     width, rows = lin_qt_ref.shape
     position = lax.axis_index(axis)
 
-    def scaled(mine):
-        return summed_ref[:, mine] * factor_ref[:, mine]
-
-    @pl.when(position >= cores)
+    @pl.when(position < cores)
+    def _():
+        write_out(
+            step, lambda mine: summed_ref[:, mine] * factor_ref[:, mine],
+            [side_by_side(ref, rows, width) for ref in near_values], probs_ref, sum_ref,
+            lambda: carried_state(position, cores, near_states, (), width),
+            (lin_qt_ref, intra_ref, cum_row_ref), (linear_ref, softmax_ref), scratch, sems,
+        )
+
+
+def early_kernel(step, axis, cores, *refs):
+    summed_ref, factor_ref, probs_ref, late_factor_ref, *values, sofar_ref = refs
+    width, rows = summed_ref.shape
+
+    @pl.when(lax.axis_index(axis) >= cores)
     def _():
         values_t = [side_by_side(ref, rows, width) for ref in values]
         for start in range(0, rows, step):
             mine = slice(start, start + step)
-            summed = scaled(mine) + value_sum(values_t, probs_ref, mine)
+            summed = summed_ref[:, mine] * factor_ref[:, mine] + value_sum(values_t, probs_ref, mine)
             sofar_ref[:, mine] = summed * late_factor_ref[:, mine]
-
-    @pl.when(position < cores)
-    def _():
-        write_out(
-            step, scaled, [side_by_side(ref, rows, width) for ref in values[:near_count]], probs_ref, sum_ref,
-            lambda: carried_state(position, cores, near_states, (), width),
-            (lin_qt_ref, intra_ref, cum_row_ref), (linear_ref, softmax_ref), scratch, sems,
-        )
 
 
 def late_kernel(step, axis, cores, counts, *refs):
@@ -388,7 +391,13 @@
         probs, factor, sums, *top = scored(
             top, total, [*near([own_keys]), *keys], (0,) * (cores - 1) + apart, len(late_keys) > 0
         )
-        late_values = passed(values, (factor, shares))
+        began = call(
+            functools.partial(first_kernel, step, axis, cores),
+            (lin_qt, intra, cum_row, summed, factor, sums, probs, *near_states, *near_values),
+            (),
+            written=(block, block),
+        )
+        late_values = passed(values, (began, shares))
         late_keys, _ = lax.optimization_barrier((late_keys, values))
         late_factor, late_sums = jnp.ones_like(factor), sums
         if late_keys:
@@ -396,14 +405,10 @@
         late_shares = passed(shares, values)
         if cores == 2:
             shares = [part for pair in zip(shares, late_shares) for part in pair]
-        *began, sofar = call(
-            functools.partial(early_kernel, step, axis, cores, len(near_states)),
-            (
-                lin_qt, intra, cum_row, summed, factor, sums, probs, late_factor,
-                *near_states, *near_values, *values,
-            ),
+        (sofar,) = call(
+            functools.partial(early_kernel, step, axis, cores),
+            (summed, factor, probs, late_factor, *near_values, *values),
             (flat,),
-            written=(block, block),
         )
         return call(
             functools.partial(late_kernel, step, axis, cores, (len(near_states), len(shares))),

time: 13.2 us -> 13 us (0.985)
  starting transfers between devices: 6.64 us -> 6.31 us
  waiting for transfers between devices: 1.58 us -> 1.76 us
    ppermute x6, waiting for transfers between devices: 0.3 us -> 1.46 us  [swapped(): return lax.ppermute(x, axis, [(i, i ^ 1) for i in range(count)])]
    ppermute x3, waiting for transfers between devices: 1.28 us -> 0.3 us  [across(): lax.ppermute(x, axis, [(i, (i + apart * cores) % count) for i in range(co...]
    ppermute x6, starting transfers between devices: 1.57 us -> 1.22 us  [swapped(): return lax.ppermute(x, axis, [(i, i ^ 1) for i in range(count)])]
    pallas_call x8 -> x9, Pallas kernels: 4.08 us -> 4.08 us  [call(): pl.pallas_call(body, out_shape=(*map(kept_in_hbm, written), *map(kept_in_...]
  transfers between devices with their start and end apart: 9 -> 9, of which waited for: 2 -> 3; matrix products, arithmetic and copies ran while one was open for 0% -> 0% of each run, Pallas kernels for 31% -> 32%
where the time goes in v12:
time: 13 us; the launch traced here: 12.9 us
  starting transfers between devices  6.31 us (49%)
  Pallas kernels  4.08 us (31%)
  waiting for transfers between devices  1.76 us (14%)
  between operations  0.72 us (6%)
    ppermute x3, starting transfers between devices, across(): lax.ppermute(x, axis, [(i, (i + apart * cores) % count) for i in range(co...  5.09 us
    pallas_call x9, Pallas kernels, call(): pl.pallas_call(body, out_shape=(*map(kept_in_hbm, written), *map(kept_in_...  4.08 us
    ppermute x6, waiting for transfers between devices, swapped(): return lax.ppermute(x, axis, [(i, i ^ 1) for i in range(count)])  1.46 us
    ppermute x6, starting transfers between devices, swapped(): return lax.ppermute(x, axis, [(i, i ^ 1) for i in range(count)])  1.22 us
    ppermute x3, waiting for transfers between devices, across(): lax.ppermute(x, axis, [(i, (i + apart * cores) % count) for i in range(co...  0.3 us
  transfers between devices with their start and end apart: 9, of which 3 were waited for; matrix products, arithmetic and copies ran while one was open for 0% of the time, Pallas kernels for 32%

profile of v12, /device:TPU:0, one launch (start us, length us, event | category | flops | bytes accessed | tf_op | source)
XLA Modules:
  0.0 12.9 jit_solution(3115042477804023096)
XLA Ops:
  0.6 3.0 %collective-permute-start.1 = (bf16[512,128]{1,0:T(8,128)(2,1)}, bf16[512,128]{1,0:T(8,128)(2,1)S(1)}, u32[]{:S(2)}, u32[]{:S(2)}) collective-permute-start(bf16[512,128]{1,0:T(8,128)(2,1)} %bitcast.15), channel_id=1, source_target_pairs={{0,16},{8,24},{16,0},{24,8},{1,17},{9,25},{17,1},{25,9},{2,18},{10... | collective-permute-start | bytes 393224 | tf_op jit(solution)/shard_map/ppermute | solution.py:334
  3.6 1.3 %shard_map.86 = (bf16[512,128]{1,0:T(8,128)(2,1)S(1)}, bf16[144,128]{1,0:T(8,128)(2,1)S(1)}, f32[1,512]{1,0:T(1,128)S(1)}, f32[512,128]{1,0:T(8,128)S(1)}, bf16[...) custom-call(f32[1,512]{1,0:T(1,128)} %decay_hbm.1, ...), custom_call_target="tpu_custom_call" | custom-call | bytes 1875968 | tf_op jit(solution)/shard_map/pallas_call | solution.py:315
  5.0 0.1 collective-permute-start
  5.1 0.5 %collective-permute-start.3 = (bf16[512,128]{1,0:T(8,128)(2,1)S(1)}, bf16[512,128]{1,0:T(8,128)(2,1)S(1)}, u32[]{:S(2)}, u32[]{:S(2)}) collective-permute-start(bf16[512,128]{1,0:T(8,128)(2,1)S(1)} %get-tuple-element.42.pack_ref), channel_id=1, source_target_pairs={{0,8},{8,0},{16,24},{24,16},{1,9},{9,1},{17,25},{25,17},{2,10},{10... | collective-permute-start | bytes 393224 | tf_op jit(solution)/shard_map/ppermute | solution.py:337
  5.6 0.0 collective-permute-start.5
  5.6 0.1 collective-permute-start.2
  5.6 0.6 %shard_map.88 = (bf16[128,512]{1,0:T(8,128)(2,1)S(1)}, f32[1,512]{1,0:T(1,128)S(1)}, f32[1,512]{1,0:T(1,128)S(1)}, f32[128,512]{1,0:T(8,128)S(1)}) custom-call(bf16[512,128]{1,0:T(8,128)(2,1)S(1)} %get-tuple-element.40.q_ref, bf16[512,128]{1,0:T(8,128)(2,1)S(1)} %get-tuple-element.41.k_ref, bf16[512,128]{1,0:T(8,128)(2,1)S(1)} %get-tuple-element.42.pack_ref), custom_call_target="tpu_custom_call" | custom-call | bytes 790528 | tf_op jit(solution)/shard_map/pallas_call | solution.py:315
  6.2 0.5 %collective-permute-done.2.refs_7_.refs_1_.refs_8_ = bf16[144,128]{1,0:T(8,128)(2,1)S(1)} collective-permute-done((bf16[144,128]{1,0:T(8,128)(2,1)S(1)}, bf16[144,128]{1,0:T(8,128)(2,1)S(1)}, u32[]{:S(2)}, u32[]{:S(2)}) %collective-permute-start.2) | collective-permute-done | bytes 36896 | tf_op jit(solution)/shard_map/ppermute | solution.py:337
  6.8 2.1 %collective-permute-start.6 = (bf16[64,128]{1,0:T(8,128)(2,1)S(1)}, bf16[64,128]{1,0:T(8,128)(2,1)S(1)}, u32[]{:S(2)}, u32[]{:S(2)}) collective-permute-start(bf16[64,128]{1,0:T(8,128)(2,1)S(1)} %shard_map.93), channel_id=1, source_target_pairs={{0,16},{8,24},{16,0},{24,8},{1,17},{9,25},{17,1},{25,9},{2,18},{10... | collective-permute-start | bytes 49160 | tf_op jit(solution)/shard_map/ppermute | solution.py:334
  8.9 0.5 %shard_map.87 = (bf16[128,512]{1,0:T(8,128)(2,1)S(1)}, f32[128,512]{1,0:T(8,128)S(1)}) custom-call(bf16[512,128]{1,0:T(8,128)(2,1)S(1)} %get-tuple-element.33.q_ref, bf16[512,128]{1,0:T(8,128)(2,1)S(1)} %get-tuple-element.34.k_ref, bf16[128,512]{1,0:T(8,128)(2,1)S(1)} %get-tuple-element.35.value_t_ref, ...), custom_call_target="tpu_custom_call" | custom-call | bytes 1050624 | tf_op jit(solution)/shard_map/pallas_call | solution.py:315
  9.4 0.0 collective-permute-done.1.refs_1_
  9.4 0.1 collective-permute-start.4
  9.5 0.0 collective-permute-done.refs_0_
  9.5 0.5 %shard_map.89 = (bf16[1024,512]{1,0:T(8,128)(2,1)S(1)}, f32[1,512]{1,0:T(1,128)S(1)}, f32[1,512]{1,0:T(1,128)S(1)}, f32[1,512]{1,0:T(1,128)S(1)}) custom-call(bf16[128,512]{1,0:T(8,128)(2,1)S(1)} %get-tuple-element.44.qt_ref, f32[1,512]{1,0:T(1,128)S(1)} %get-tuple-element.45.top_ref, f32[1,512]{1,0:T(1,128)S(1)} %get-tuple-element.46.total_ref, ...), custom_call_target="tpu_custom_call" | custom-call | bytes 1452032 | tf_op jit(solution)/shard_map/pallas_call | solution.py:315
  10.0 0.0 collective-permute-done.3.refs_8_.refs_4_
  10.0 1.1 %shard_map.90 = (bf16[512,128]{1,0:T(8,128)(2,1)}, bf16[512,128]{1,0:T(8,128)(2,1)}) custom-call(bf16[128,512]{1,0:T(8,128)(2,1)S(1)} %get-tuple-element.38.refs_0_.refs_2_, f32[128,512]{1,0:T(8,128)S(1)} %get-tuple-element.39.refs_1_.refs_3_, f32[1,512]{1,0:T(1,128)S(1)} %get-tuple-element.36.cum_row_ref.refs_2_.refs_4_, ...), custom_call_target="tpu_custom_call" | custom-call | bytes 1878016 | tf_op jit(solution)/shard_map/pallas_call | solution.py:315
  11.1 0.3 %collective-permute-done.6.refs_9_ = bf16[64,128]{1,0:T(8,128)(2,1)S(1)} collective-permute-done((bf16[64,128]{1,0:T(8,128)(2,1)S(1)}, bf16[64,128]{1,0:T(8,128)(2,1)S(1)}, u32[]{:S(2)}, u32[]{:S(2)}) %collective-permute-start.6) | collective-permute-done | bytes 16416 | tf_op jit(solution)/shard_map/ppermute | solution.py:334
  11.4 0.0 collective-permute-done.5.refs_5_
  11.4 0.3 %collective-permute-start.8 = (bf16[512,128]{1,0:T(8,128)(2,1)S(1)}, bf16[512,128]{1,0:T(8,128)(2,1)S(1)}, u32[]{:S(2)}, u32[]{:S(2)}) collective-permute-start(bf16[512,128]{1,0:T(8,128)(2,1)S(1)} %collective-permute-done.5.refs_5_), channel_id=1, source_target_pairs={{0,8},{8,0},{16,24},{24,16},{1,9},{9,1},{17,25},{25,17},{2,10},{10... | collective-permute-start | bytes 393224 | tf_op jit(solution)/shard_map/ppermute | solution.py:337
  11.7 0.2 %collective-permute-start.7 = (bf16[64,128]{1,0:T(8,128)(2,1)S(1)}, bf16[64,128]{1,0:T(8,128)(2,1)S(1)}, u32[]{:S(2)}, u32[]{:S(2)}) collective-permute-start(bf16[64,128]{1,0:T(8,128)(2,1)S(1)} %collective-permute-done.6.refs_9_), channel_id=1, source_target_pairs={{0,8},{8,0},{16,24},{24,16},{1,9},{9,1},{17,25},{25,17},{2,10},{10... | collective-permute-start | bytes 49160 | tf_op jit(solution)/shard_map/ppermute | solution.py:337
  11.9 0.0 collective-permute-done.4.refs_0_
  11.9 0.9 %collective-permute-done.7.refs_10_ = bf16[64,128]{1,0:T(8,128)(2,1)S(1)} collective-permute-done((bf16[64,128]{1,0:T(8,128)(2,1)S(1)}, bf16[64,128]{1,0:T(8,128)(2,1)S(1)}, u32[]{:S(2)}, u32[]{:S(2)}) %collective-permute-start.7) | collective-permute-done | bytes 16416 | tf_op jit(solution)/shard_map/ppermute | solution.py:337
  12.8 0.0 collective-permute-done.8.refs_11_
  (4 shorter events, 0.1 us)
Async XLA Ops:
  0.6 8.8 %collective-permute-start.1 = (bf16[512,128]{1,0:T(8,128)(2,1)}, bf16[512,128]{1,0:T(8,128)(2,1)S(1)}, u32[]{:S(2)}, u32[]{:S(2)}) collective-permute-start(bf16[512,128]{1,0:T(8,128)(2,1)} %bitcast.15), channel_id=1, source_target_pairs={{0,16},{8,24},{16,0},{24,8},{1,17},{9,25},{17,1},{25,9},{2,18},{10... | collective-permute-start | bytes 393224 | tf_op jit(solution)/shard_map/ppermute | solution.py:334
  5.0 4.5 %collective-permute-start = (bf16[512,128]{1,0:T(8,128)(2,1)S(1)}, bf16[512,128]{1,0:T(8,128)(2,1)S(1)}, u32[]{:S(2)}, u32[]{:S(2)}) collective-permute-start(bf16[512,128]{1,0:T(8,128)(2,1)S(1)} %get-tuple-element.41.k_ref), channel_id=1, source_target_pairs={{0,8},{8,0},{16,24},{24,16},{1,9},{9,1},{17,25},{25,17},{2,10},{10... | collective-permute-start | bytes 393224 | tf_op jit(solution)/shard_map/ppermute | solution.py:337
  5.1 5.0 %collective-permute-start.3 = (bf16[512,128]{1,0:T(8,128)(2,1)S(1)}, bf16[512,128]{1,0:T(8,128)(2,1)S(1)}, u32[]{:S(2)}, u32[]{:S(2)}) collective-permute-start(bf16[512,128]{1,0:T(8,128)(2,1)S(1)} %get-tuple-element.42.pack_ref), channel_id=1, source_target_pairs={{0,8},{8,0},{16,24},{24,16},{1,9},{9,1},{17,25},{25,17},{2,10},{10... | collective-permute-start | bytes 393224 | tf_op jit(solution)/shard_map/ppermute | solution.py:337
  5.6 5.8 %collective-permute-start.5 = (bf16[512,128]{1,0:T(8,128)(2,1)S(1)}, bf16[512,128]{1,0:T(8,128)(2,1)S(1)}, u32[]{:S(2)}, u32[]{:S(2)}) collective-permute-start(bf16[512,128]{1,0:T(8,128)(2,1)S(1)} %get-tuple-element.42.pack_ref), channel_id=1, source_target_pairs={{0,16},{8,24},{16,0},{24,8},{1,17},{9,25},{17,1},{25,9},{2,18},{10... | collective-permute-start | bytes 393224 | tf_op jit(solution)/shard_map/ppermute | solution.py:334
  5.6 1.2 %collective-permute-start.2 = (bf16[144,128]{1,0:T(8,128)(2,1)S(1)}, bf16[144,128]{1,0:T(8,128)(2,1)S(1)}, u32[]{:S(2)}, u32[]{:S(2)}) collective-permute-start(bf16[144,128]{1,0:T(8,128)(2,1)S(1)} %get-tuple-element.50.refs_0_), channel_id=1, source_target_pairs={{0,8},{8,0},{16,24},{24,16},{1,9},{9,1},{17,25},{25,17},{2,10},{10... | collective-permute-start | bytes 110600 | tf_op jit(solution)/shard_map/ppermute | solution.py:337
  6.8 4.6 %collective-permute-start.6 = (bf16[64,128]{1,0:T(8,128)(2,1)S(1)}, bf16[64,128]{1,0:T(8,128)(2,1)S(1)}, u32[]{:S(2)}, u32[]{:S(2)}) collective-permute-start(bf16[64,128]{1,0:T(8,128)(2,1)S(1)} %shard_map.93), channel_id=1, source_target_pairs={{0,16},{8,24},{16,0},{24,8},{1,17},{9,25},{17,1},{25,9},{2,18},{10... | collective-permute-start | bytes 49160 | tf_op jit(solution)/shard_map/ppermute | solution.py:334
  9.4 2.5 %collective-permute-start.4 = (bf16[512,128]{1,0:T(8,128)(2,1)S(1)}, bf16[512,128]{1,0:T(8,128)(2,1)S(1)}, u32[]{:S(2)}, u32[]{:S(2)}) collective-permute-start(bf16[512,128]{1,0:T(8,128)(2,1)S(1)} %collective-permute-done.1.refs_1_), channel_id=1, source_target_pairs={{0,8},{8,0},{16,24},{24,16},{1,9},{9,1},{17,25},{25,17},{2,10},{10... | collective-permute-start | bytes 393224 | tf_op jit(solution)/shard_map/ppermute | solution.py:337
  11.4 1.5 %collective-permute-start.8 = (bf16[512,128]{1,0:T(8,128)(2,1)S(1)}, bf16[512,128]{1,0:T(8,128)(2,1)S(1)}, u32[]{:S(2)}, u32[]{:S(2)}) collective-permute-start(bf16[512,128]{1,0:T(8,128)(2,1)S(1)} %collective-permute-done.5.refs_5_), channel_id=1, source_target_pairs={{0,8},{8,0},{16,24},{24,16},{1,9},{9,1},{17,25},{25,17},{2,10},{10... | collective-permute-start | bytes 393224 | tf_op jit(solution)/shard_map/ppermute | solution.py:337
  11.7 1.2 %collective-permute-start.7 = (bf16[64,128]{1,0:T(8,128)(2,1)S(1)}, bf16[64,128]{1,0:T(8,128)(2,1)S(1)}, u32[]{:S(2)}, u32[]{:S(2)}) collective-permute-start(bf16[64,128]{1,0:T(8,128)(2,1)S(1)} %collective-permute-done.6.refs_9_), channel_id=1, source_target_pairs={{0,8},{8,0},{16,24},{24,16},{1,9},{9,1},{17,25},{25,17},{2,10},{10... | collective-permute-start | bytes 49160 | tf_op jit(solution)/shard_map/ppermute | solution.py:337

commit v13 on v12

--- a/solution.py
+++ b/solution.py
@@ -252,7 +252,7 @@
     def _():
         write_out(
             step, lambda mine: summed_ref[:, mine] * factor_ref[:, mine],
-            [side_by_side(ref, rows, width) for ref in near_values], probs_ref, sum_ref,
+            [jnp.transpose(ref[...]) for ref in near_values], probs_ref, sum_ref,
             lambda: carried_state(position, cores, near_states, (), width),
             (lin_qt_ref, intra_ref, cum_row_ref), (linear_ref, softmax_ref), scratch, sems,
         )
@@ -264,7 +264,7 @@
 
     @pl.when(lax.axis_index(axis) >= cores)
     def _():
-        values_t = [side_by_side(ref, rows, width) for ref in values]
+        values_t = [jnp.transpose(ref[...]) for ref in values]
         for start in range(0, rows, step):
             mine = slice(start, start + step)
             summed = summed_ref[:, mine] * factor_ref[:, mine] + value_sum(values_t, probs_ref, mine)
@@ -284,7 +284,7 @@
     @pl.when(position >= cores)
     def _():
         write_out(
-            step, lambda mine: sofar_ref[:, mine], [side_by_side(ref, rows, width) for ref in values],
+            step, lambda mine: sofar_ref[:, mine], [jnp.transpose(ref[...]) for ref in values],
             probs_ref, sum_ref, lambda: carried_state(position, cores, near_states, shares, width),
             (lin_qt_ref, intra_ref, cum_row_ref), (linear_ref, softmax_ref), scratch, sems,
         )
@@ -356,7 +356,7 @@
             return shape(*dims, dtype=BF16)
 
         row, flat, flat16, block = shape(1, rows), shape(width, rows), half(width, rows), half(rows, width)
-        keys = far(sk)
+        keys, values = far(sk), far(sv)
         soft_vt, state, cum_row, cum_col, lin_vt, lk, lq, sq, own_keys = call(
             state_kernel,
             (),
@@ -364,7 +364,7 @@
             given=(decay, lk, lv, sv, lq, sq, sk),
             scratch=(row, block, block),
         )
-        values, near_states, near_values = far(soft_vt), near([state]), near([soft_vt])
+        near_states, near_values = near([state]), near([sv])
         qt, top, total, summed = call(
             functools.partial(soft_kernel, scale, step), (sq, own_keys, soft_vt), (flat16, row, row, flat)
         )
@@ -389,7 +389,7 @@
         apart = tuple(range(1, chips))
         late_keys = passed(keys, (summed, intra))
         probs, factor, sums, *top = scored(
-            top, total, [*near([own_keys]), *keys], (0,) * (cores - 1) + apart, len(late_keys) > 0
+            top, total, [*near([sk]), *keys], (0,) * (cores - 1) + apart, len(late_keys) > 0
         )
         began = call(
             functools.partial(first_kernel, step, axis, cores),

time: 13 us -> 13 us (level)
    ppermute x3, waiting for transfers between devices: 0.3 us -> 0.01 us  [across(): lax.ppermute(x, axis, [(i, (i + apart * cores) % count) for i in range(co...]
    ppermute x6, waiting for transfers between devices: 1.46 us -> 1.67 us  [swapped(): return lax.ppermute(x, axis, [(i, i ^ 1) for i in range(count)])]
  transfers between devices with their start and end apart: 9 -> 9, of which waited for: 3 -> 2; matrix products, arithmetic and copies ran while one was open for 0% -> 0% of each run, Pallas kernels for 32% -> 32%
where the time goes in v13:
time: 13 us; the launch traced here: 12.9 us
  starting transfers between devices  6.35 us (49%)
  Pallas kernels  4.11 us (32%)
  waiting for transfers between devices  1.68 us (13%)
  between operations  0.73 us (6%)
    ppermute x3, starting transfers between devices, across(): lax.ppermute(x, axis, [(i, (i + apart * cores) % count) for i in range(co...  5.09 us
    pallas_call x9, Pallas kernels, call(): pl.pallas_call(body, out_shape=(*map(kept_in_hbm, written), *map(kept_in_...  4.11 us
    ppermute x6, waiting for transfers between devices, swapped(): return lax.ppermute(x, axis, [(i, i ^ 1) for i in range(count)])  1.67 us
    ppermute x6, starting transfers between devices, swapped(): return lax.ppermute(x, axis, [(i, i ^ 1) for i in range(count)])  1.25 us
  transfers between devices with their start and end apart: 9, of which 2 were waited for; matrix products, arithmetic and copies ran while one was open for 0% of the time, Pallas kernels for 32%

profile of v13, /device:TPU:0, one launch (start us, length us, event | category | flops | bytes accessed | tf_op | source)
XLA Modules:
  0.0 12.9 jit_solution(3919592449777732865)
XLA Ops:
  0.6 3.0 %collective-permute-start.1 = (bf16[512,128]{1,0:T(8,128)(2,1)}, bf16[512,128]{1,0:T(8,128)(2,1)S(1)}, u32[]{:S(2)}, u32[]{:S(2)}) collective-permute-start(bf16[512,128]{1,0:T(8,128)(2,1)} %bitcast.14), channel_id=1, source_target_pairs={{0,16},{8,24},{16,0},{24,8},{1,17},{9,25},{17,1},{25,9},{2,18},{10... | collective-permute-start | bytes 393224 | tf_op jit(solution)/shard_map/ppermute | solution.py:334
  3.6 0.0 collective-permute-start
  3.6 0.5 %collective-permute-start.3 = (bf16[512,128]{1,0:T(8,128)(2,1)}, bf16[512,128]{1,0:T(8,128)(2,1)S(1)}, u32[]{:S(2)}, u32[]{:S(2)}) collective-permute-start(bf16[512,128]{1,0:T(8,128)(2,1)} %bitcast.17), channel_id=1, source_target_pairs={{0,8},{8,0},{16,24},{24,16},{1,9},{9,1},{17,25},{25,17},{2,10},{10... | collective-permute-start | bytes 393224 | tf_op jit(solution)/shard_map/ppermute | solution.py:337
  4.1 0.1 collective-permute-start.5
  4.2 1.3 %shard_map.86 = (bf16[512,128]{1,0:T(8,128)(2,1)S(1)}, bf16[144,128]{1,0:T(8,128)(2,1)S(1)}, f32[1,512]{1,0:T(1,128)S(1)}, f32[512,128]{1,0:T(8,128)S(1)}, bf16[...) custom-call(f32[1,512]{1,0:T(1,128)} %decay_hbm.1, ...), custom_call_target="tpu_custom_call" | custom-call | bytes 1875968 | tf_op jit(solution)/shard_map/pallas_call | solution.py:315
  5.6 0.1 collective-permute-start.2
  5.7 0.6 %shard_map.88 = (bf16[128,512]{1,0:T(8,128)(2,1)S(1)}, f32[1,512]{1,0:T(1,128)S(1)}, f32[1,512]{1,0:T(1,128)S(1)}, f32[128,512]{1,0:T(8,128)S(1)}) custom-call(bf16[512,128]{1,0:T(8,128)(2,1)S(1)} %get-tuple-element.40.q_ref, bf16[512,128]{1,0:T(8,128)(2,1)S(1)} %get-tuple-element.41.k_ref, bf16[512,128]{1,0:T(8,128)(2,1)S(1)} %get-tuple-element.42.pack_ref), custom_call_target="tpu_custom_call" | custom-call | bytes 790528 | tf_op jit(solution)/shard_map/pallas_call | solution.py:315
  6.3 0.6 %collective-permute-done.2.refs_7_.refs_1_.refs_8_ = bf16[144,128]{1,0:T(8,128)(2,1)S(1)} collective-permute-done((bf16[144,128]{1,0:T(8,128)(2,1)S(1)}, bf16[144,128]{1,0:T(8,128)(2,1)S(1)}, u32[]{:S(2)}, u32[]{:S(2)}) %collective-permute-start.2) | collective-permute-done | bytes 36896 | tf_op jit(solution)/shard_map/ppermute | solution.py:337
  6.9 2.0 %collective-permute-start.6 = (bf16[64,128]{1,0:T(8,128)(2,1)S(1)}, bf16[64,128]{1,0:T(8,128)(2,1)S(1)}, u32[]{:S(2)}, u32[]{:S(2)}) collective-permute-start(bf16[64,128]{1,0:T(8,128)(2,1)S(1)} %shard_map.93), channel_id=1, source_target_pairs={{0,16},{8,24},{16,0},{24,8},{1,17},{9,25},{17,1},{25,9},{2,18},{10... | collective-permute-start | bytes 49160 | tf_op jit(solution)/shard_map/ppermute | solution.py:334
  8.9 0.5 %shard_map.87 = (bf16[128,512]{1,0:T(8,128)(2,1)S(1)}, f32[128,512]{1,0:T(8,128)S(1)}) custom-call(bf16[512,128]{1,0:T(8,128)(2,1)S(1)} %get-tuple-element.33.q_ref, bf16[512,128]{1,0:T(8,128)(2,1)S(1)} %get-tuple-element.34.k_ref, bf16[128,512]{1,0:T(8,128)(2,1)S(1)} %get-tuple-element.35.value_t_ref, ...), custom_call_target="tpu_custom_call" | custom-call | bytes 1050624 | tf_op jit(solution)/shard_map/pallas_call | solution.py:315
  9.4 0.0 collective-permute-done.1.refs_1_
  9.4 0.1 collective-permute-start.4
  9.5 0.0 collective-permute-done.refs_0_
  9.5 0.5 %shard_map.89 = (bf16[1024,512]{1,0:T(8,128)(2,1)S(1)}, f32[1,512]{1,0:T(1,128)S(1)}, f32[1,512]{1,0:T(1,128)S(1)}, f32[1,512]{1,0:T(1,128)S(1)}) custom-call(bf16[128,512]{1,0:T(8,128)(2,1)S(1)} %get-tuple-element.44.qt_ref, f32[1,512]{1,0:T(1,128)S(1)} %get-tuple-element.45.top_ref, f32[1,512]{1,0:T(1,128)S(1)} %get-tuple-element.46.total_ref, ...), custom_call_target="tpu_custom_call" | custom-call | bytes 1452032 | tf_op jit(solution)/shard_map/pallas_call | solution.py:315
  10.0 0.0 collective-permute-done.3.refs_8_.refs_4_
  10.0 1.1 %shard_map.90 = (bf16[512,128]{1,0:T(8,128)(2,1)}, bf16[512,128]{1,0:T(8,128)(2,1)}) custom-call(bf16[128,512]{1,0:T(8,128)(2,1)S(1)} %get-tuple-element.38.refs_0_.refs_2_, f32[128,512]{1,0:T(8,128)S(1)} %get-tuple-element.39.refs_1_.refs_3_, f32[1,512]{1,0:T(1,128)S(1)} %get-tuple-element.36.cum_row_ref.refs_2_.refs_4_, ...), custom_call_target="tpu_custom_call" | custom-call | bytes 1878016 | tf_op jit(solution)/shard_map/pallas_call | solution.py:315
  11.1 0.0 collective-permute-done.6.refs_9_
  11.1 0.0 collective-permute-done.5.refs_5_
  11.1 0.5 %collective-permute-start.8 = (bf16[512,128]{1,0:T(8,128)(2,1)S(1)}, bf16[512,128]{1,0:T(8,128)(2,1)S(1)}, u32[]{:S(2)}, u32[]{:S(2)}) collective-permute-start(bf16[512,128]{1,0:T(8,128)(2,1)S(1)} %collective-permute-done.5.refs_5_), channel_id=1, source_target_pairs={{0,8},{8,0},{16,24},{24,16},{1,9},{9,1},{17,25},{25,17},{2,10},{10... | collective-permute-start | bytes 393224 | tf_op jit(solution)/shard_map/ppermute | solution.py:337
  11.7 0.1 collective-permute-start.7
  11.7 0.0 collective-permute-done.4.refs_0_
  11.8 1.1 %collective-permute-done.7.refs_10_ = bf16[64,128]{1,0:T(8,128)(2,1)S(1)} collective-permute-done((bf16[64,128]{1,0:T(8,128)(2,1)S(1)}, bf16[64,128]{1,0:T(8,128)(2,1)S(1)}, u32[]{:S(2)}, u32[]{:S(2)}) %collective-permute-start.7) | collective-permute-done | bytes 16416 | tf_op jit(solution)/shard_map/ppermute | solution.py:337
  12.9 0.0 collective-permute-done.8.refs_11_
  (4 shorter events, 0.1 us)
Async XLA Ops:
  0.6 8.8 %collective-permute-start.1 = (bf16[512,128]{1,0:T(8,128)(2,1)}, bf16[512,128]{1,0:T(8,128)(2,1)S(1)}, u32[]{:S(2)}, u32[]{:S(2)}) collective-permute-start(bf16[512,128]{1,0:T(8,128)(2,1)} %bitcast.14), channel_id=1, source_target_pairs={{0,16},{8,24},{16,0},{24,8},{1,17},{9,25},{17,1},{25,9},{2,18},{10... | collective-permute-start | bytes 393224 | tf_op jit(solution)/shard_map/ppermute | solution.py:334
  3.6 5.8 %collective-permute-start = (bf16[512,128]{1,0:T(8,128)(2,1)}, bf16[512,128]{1,0:T(8,128)(2,1)S(1)}, u32[]{:S(2)}, u32[]{:S(2)}) collective-permute-start(bf16[512,128]{1,0:T(8,128)(2,1)} %bitcast.15), channel_id=1, source_target_pairs={{0,8},{8,0},{16,24},{24,16},{1,9},{9,1},{17,25},{25,17},{2,10},{10... | collective-permute-start | bytes 393224 | tf_op jit(solution)/shard_map/ppermute | solution.py:337
  3.6 6.4 %collective-permute-start.3 = (bf16[512,128]{1,0:T(8,128)(2,1)}, bf16[512,128]{1,0:T(8,128)(2,1)S(1)}, u32[]{:S(2)}, u32[]{:S(2)}) collective-permute-start(bf16[512,128]{1,0:T(8,128)(2,1)} %bitcast.17), channel_id=1, source_target_pairs={{0,8},{8,0},{16,24},{24,16},{1,9},{9,1},{17,25},{25,17},{2,10},{10... | collective-permute-start | bytes 393224 | tf_op jit(solution)/shard_map/ppermute | solution.py:337
  4.1 7.0 %collective-permute-start.5 = (bf16[512,128]{1,0:T(8,128)(2,1)}, bf16[512,128]{1,0:T(8,128)(2,1)S(1)}, u32[]{:S(2)}, u32[]{:S(2)}) collective-permute-start(bf16[512,128]{1,0:T(8,128)(2,1)} %bitcast.18), channel_id=1, source_target_pairs={{0,16},{8,24},{16,0},{24,8},{1,17},{9,25},{17,1},{25,9},{2,18},{10... | collective-permute-start | bytes 393224 | tf_op jit(solution)/shard_map/ppermute | solution.py:334
  5.6 1.3 %collective-permute-start.2 = (bf16[144,128]{1,0:T(8,128)(2,1)S(1)}, bf16[144,128]{1,0:T(8,128)(2,1)S(1)}, u32[]{:S(2)}, u32[]{:S(2)}) collective-permute-start(bf16[144,128]{1,0:T(8,128)(2,1)S(1)} %get-tuple-element.50.refs_0_), channel_id=1, source_target_pairs={{0,8},{8,0},{16,24},{24,16},{1,9},{9,1},{17,25},{25,17},{2,10},{10... | collective-permute-start | bytes 110600 | tf_op jit(solution)/shard_map/ppermute | solution.py:337
  6.9 4.2 %collective-permute-start.6 = (bf16[64,128]{1,0:T(8,128)(2,1)S(1)}, bf16[64,128]{1,0:T(8,128)(2,1)S(1)}, u32[]{:S(2)}, u32[]{:S(2)}) collective-permute-start(bf16[64,128]{1,0:T(8,128)(2,1)S(1)} %shard_map.93), channel_id=1, source_target_pairs={{0,16},{8,24},{16,0},{24,8},{1,17},{9,25},{17,1},{25,9},{2,18},{10... | collective-permute-start | bytes 49160 | tf_op jit(solution)/shard_map/ppermute | solution.py:334
  9.4 2.3 %collective-permute-start.4 = (bf16[512,128]{1,0:T(8,128)(2,1)S(1)}, bf16[512,128]{1,0:T(8,128)(2,1)S(1)}, u32[]{:S(2)}, u32[]{:S(2)}) collective-permute-start(bf16[512,128]{1,0:T(8,128)(2,1)S(1)} %collective-permute-done.1.refs_1_), channel_id=1, source_target_pairs={{0,8},{8,0},{16,24},{24,16},{1,9},{9,1},{17,25},{25,17},{2,10},{10... | collective-permute-start | bytes 393224 | tf_op jit(solution)/shard_map/ppermute | solution.py:337
  11.1 1.7 %collective-permute-start.8 = (bf16[512,128]{1,0:T(8,128)(2,1)S(1)}, bf16[512,128]{1,0:T(8,128)(2,1)S(1)}, u32[]{:S(2)}, u32[]{:S(2)}) collective-permute-start(bf16[512,128]{1,0:T(8,128)(2,1)S(1)} %collective-permute-done.5.refs_5_), channel_id=1, source_target_pairs={{0,8},{8,0},{16,24},{24,16},{1,9},{9,1},{17,25},{25,17},{2,10},{10... | collective-permute-start | bytes 393224 | tf_op jit(solution)/shard_map/ppermute | solution.py:337
  11.7 1.2 %collective-permute-start.7 = (bf16[64,128]{1,0:T(8,128)(2,1)S(1)}, bf16[64,128]{1,0:T(8,128)(2,1)S(1)}, u32[]{:S(2)}, u32[]{:S(2)}) collective-permute-start(bf16[64,128]{1,0:T(8,128)(2,1)S(1)} %collective-permute-done.6.refs_9_), channel_id=1, source_target_pairs={{0,8},{8,0},{16,24},{24,16},{1,9},{9,1},{17,25},{25,17},{2,10},{10... | collective-permute-start | bytes 49160 | tf_op jit(solution)/shard_map/ppermute | solution.py:337

commit v14 on v11

--- a/solution.py
+++ b/solution.py
@@ -253,7 +253,8 @@
 
     @pl.when(position >= cores)
     def _():
-        values_t = [side_by_side(ref, rows, width) for ref in values]
+        values_t = [side_by_side(ref, rows, width) for ref in values[:near_count]]
+        values_t += [jnp.transpose(ref[...]) for ref in values[near_count:]]
         for start in range(0, rows, step):
             mine = slice(start, start + step)
             summed = scaled(mine) + value_sum(values_t, probs_ref, mine)
@@ -281,7 +282,7 @@
     @pl.when(position >= cores)
     def _():
         write_out(
-            step, lambda mine: sofar_ref[:, mine], [side_by_side(ref, rows, width) for ref in values],
+            step, lambda mine: sofar_ref[:, mine], [jnp.transpose(ref[...]) for ref in values],
             probs_ref, sum_ref, lambda: carried_state(position, cores, near_states, shares, width),
             (lin_qt_ref, intra_ref, cum_row_ref), (linear_ref, softmax_ref), scratch, sems,
         )
@@ -353,7 +354,7 @@
             return shape(*dims, dtype=BF16)
 
         row, flat, flat16, block = shape(1, rows), shape(width, rows), half(width, rows), half(rows, width)
-        keys = far(sk)
+        keys, values = far(sk), far(sv)
         soft_vt, state, cum_row, cum_col, lin_vt, lk, lq, sq, own_keys = call(
             state_kernel,
             (),
@@ -361,11 +362,10 @@
             given=(decay, lk, lv, sv, lq, sq, sk),
             scratch=(row, block, block),
         )
-        values, near_states, near_values = far(soft_vt), near([state]), near([soft_vt])
+        near_states, near_values = near([state]), near([soft_vt])
         qt, top, total, summed = call(
             functools.partial(soft_kernel, scale, step), (sq, own_keys, soft_vt), (flat16, row, row, flat)
         )
-        near_states, _ = lax.optimization_barrier((near_states, summed))
         (share,) = call(
             functools.partial(combine_kernel, axis, cores),
             (state, *near_states),
@@ -386,7 +386,7 @@
         apart = tuple(range(1, chips))
         late_keys = passed(keys, (summed, intra))
         probs, factor, sums, *top = scored(
-            top, total, [*near([own_keys]), *keys], (0,) * (cores - 1) + apart, len(late_keys) > 0
+            top, total, [*near([sk]), *keys], (0,) * (cores - 1) + apart, len(late_keys) > 0
         )
         late_values = passed(values, (factor, shares))
         late_keys, _ = lax.optimization_barrier((late_keys, values))

time: 13.2 us -> 12.5 us (0.947)
  waiting for transfers between devices: 1.58 us -> 0.89 us
    ppermute x3, waiting for transfers between devices: 1.28 us -> 0.01 us  [across(): lax.ppermute(x, axis, [(i, (i + apart * cores) % count) for i in range(co...]
    ppermute x6, waiting for transfers between devices: 0.3 us -> 0.88 us  [swapped(): return lax.ppermute(x, axis, [(i, i ^ 1) for i in range(count)])]
  transfers between devices with their start and end apart: 9 -> 9, of which waited for: 2 -> 1; matrix products, arithmetic and copies ran while one was open for 0% -> 0% of each run, Pallas kernels for 31% -> 33%
where the time goes in v14:
time: 12.5 us; the launch traced here: 12.4 us
  starting transfers between devices  6.65 us (53%)
  Pallas kernels  4.09 us (33%)
  waiting for transfers between devices  0.89 us (7%)
  between operations  0.72 us (6%)
    ppermute x3, starting transfers between devices, across(): lax.ppermute(x, axis, [(i, (i + apart * cores) % count) for i in range(co...  5.09 us
    pallas_call x8, Pallas kernels, call(): pl.pallas_call(body, out_shape=(*map(kept_in_hbm, written), *map(kept_in_...  4.09 us
    ppermute x6, starting transfers between devices, swapped(): return lax.ppermute(x, axis, [(i, i ^ 1) for i in range(count)])  1.57 us
    ppermute x6, waiting for transfers between devices, swapped(): return lax.ppermute(x, axis, [(i, i ^ 1) for i in range(count)])  0.88 us
  transfers between devices with their start and end apart: 9, of which 1 were waited for; matrix products, arithmetic and copies ran while one was open for 0% of the time, Pallas kernels for 33%

profile of v14, /device:TPU:0, one launch (start us, length us, event | category | flops | bytes accessed | tf_op | source)
XLA Modules:
  0.0 12.4 jit_solution(11643355859377142714)
XLA Ops:
  0.6 3.0 %collective-permute-start.1 = (bf16[512,128]{1,0:T(8,128)(2,1)}, bf16[512,128]{1,0:T(8,128)(2,1)S(1)}, u32[]{:S(2)}, u32[]{:S(2)}) collective-permute-start(bf16[512,128]{1,0:T(8,128)(2,1)} %bitcast.14), channel_id=1, source_target_pairs={{0,16},{8,24},{16,0},{24,8},{1,17},{9,25},{17,1},{25,9},{2,18},{10... | collective-permute-start | bytes 393224 | tf_op jit(solution)/shard_map/ppermute | solution.py:332
  3.6 0.0 collective-permute-start
  3.6 0.2 %collective-permute-start.3 = (bf16[512,128]{1,0:T(8,128)(2,1)}, bf16[512,128]{1,0:T(8,128)(2,1)S(1)}, u32[]{:S(2)}, u32[]{:S(2)}) collective-permute-start(bf16[512,128]{1,0:T(8,128)(2,1)} %bitcast.17), channel_id=1, source_target_pairs={{0,16},{8,24},{16,0},{24,8},{1,17},{9,25},{17,1},{25,9},{2,18},{10... | collective-permute-start | bytes 393224 | tf_op jit(solution)/shard_map/ppermute | solution.py:332
  3.8 1.3 %shard_map.86 = (bf16[512,128]{1,0:T(8,128)(2,1)S(1)}, bf16[144,128]{1,0:T(8,128)(2,1)S(1)}, f32[1,512]{1,0:T(1,128)S(1)}, f32[512,128]{1,0:T(8,128)S(1)}, bf16[...) custom-call(f32[1,512]{1,0:T(1,128)} %decay_hbm.1, ...), custom_call_target="tpu_custom_call" | custom-call | bytes 1875968 | tf_op jit(solution)/shard_map/pallas_call | solution.py:313
  5.1 0.4 %collective-permute-start.4 = (bf16[144,128]{1,0:T(8,128)(2,1)S(1)}, bf16[144,128]{1,0:T(8,128)(2,1)S(1)}, u32[]{:S(2)}, u32[]{:S(2)}) collective-permute-start(bf16[144,128]{1,0:T(8,128)(2,1)S(1)} %get-tuple-element.54.refs_0_), channel_id=1, source_target_pairs={{0,8},{8,0},{16,24},{24,16},{1,9},{9,1},{17,25},{25,17},{2,10},{10... | collective-permute-start | bytes 110600 | tf_op jit(solution)/shard_map/ppermute | solution.py:335
  5.6 0.9 %collective-permute-done.4.refs_8_.refs_1_ = bf16[144,128]{1,0:T(8,128)(2,1)S(1)} collective-permute-done((bf16[144,128]{1,0:T(8,128)(2,1)S(1)}, bf16[144,128]{1,0:T(8,128)(2,1)S(1)}, u32[]{:S(2)}, u32[]{:S(2)}) %collective-permute-start.4) | collective-permute-done | bytes 36896 | tf_op jit(solution)/shard_map/ppermute | solution.py:335
  6.5 1.9 %collective-permute-start.6 = (bf16[64,128]{1,0:T(8,128)(2,1)S(1)}, bf16[64,128]{1,0:T(8,128)(2,1)S(1)}, u32[]{:S(2)}, u32[]{:S(2)}) collective-permute-start(bf16[64,128]{1,0:T(8,128)(2,1)S(1)} %shard_map.92), channel_id=1, source_target_pairs={{0,16},{8,24},{16,0},{24,8},{1,17},{9,25},{17,1},{25,9},{2,18},{10... | collective-permute-start | bytes 49160 | tf_op jit(solution)/shard_map/ppermute | solution.py:332
  8.4 0.6 %shard_map.88 = (bf16[128,512]{1,0:T(8,128)(2,1)S(1)}, f32[1,512]{1,0:T(1,128)S(1)}, f32[1,512]{1,0:T(1,128)S(1)}, f32[128,512]{1,0:T(8,128)S(1)}) custom-call(bf16[512,128]{1,0:T(8,128)(2,1)S(1)} %get-tuple-element.40.q_ref, bf16[512,128]{1,0:T(8,128)(2,1)S(1)} %get-tuple-element.41.k_ref, bf16[512,128]{1,0:T(8,128)(2,1)S(1)} %get-tuple-element.42.pack_ref), custom_call_target="tpu_custom_call" | custom-call | bytes 790528 | tf_op jit(solution)/shard_map/pallas_call | solution.py:313
  9.0 0.5 %shard_map.87 = (bf16[128,512]{1,0:T(8,128)(2,1)S(1)}, f32[128,512]{1,0:T(8,128)S(1)}) custom-call(bf16[512,128]{1,0:T(8,128)(2,1)S(1)} %get-tuple-element.33.q_ref, bf16[512,128]{1,0:T(8,128)(2,1)S(1)} %get-tuple-element.34.k_ref, bf16[128,512]{1,0:T(8,128)(2,1)S(1)} %get-tuple-element.35.value_t_ref, ...), custom_call_target="tpu_custom_call" | custom-call | bytes 1050624 | tf_op jit(solution)/shard_map/pallas_call | solution.py:313
  9.5 0.0 collective-permute-done.1.refs_1_
  9.5 0.1 collective-permute-start.2
  9.6 0.5 %collective-permute-start.5 = (bf16[512,128]{1,0:T(8,128)(2,1)S(1)}, bf16[512,128]{1,0:T(8,128)(2,1)S(1)}, u32[]{:S(2)}, u32[]{:S(2)}) collective-permute-start(bf16[512,128]{1,0:T(8,128)(2,1)S(1)} %get-tuple-element.42.pack_ref), channel_id=1, source_target_pairs={{0,8},{8,0},{16,24},{24,16},{1,9},{9,1},{17,25},{25,17},{2,10},{10... | collective-permute-start | bytes 393224 | tf_op jit(solution)/shard_map/ppermute | solution.py:335
  10.1 0.0 collective-permute-done.refs_0_
  10.1 0.5 %shard_map.89 = (bf16[1024,512]{1,0:T(8,128)(2,1)S(1)}, f32[1,512]{1,0:T(1,128)S(1)}, f32[1,512]{1,0:T(1,128)S(1)}, f32[1,512]{1,0:T(1,128)S(1)}) custom-call(bf16[128,512]{1,0:T(8,128)(2,1)S(1)} %get-tuple-element.44.qt_ref, f32[1,512]{1,0:T(1,128)S(1)} %get-tuple-element.45.top_ref, f32[1,512]{1,0:T(1,128)S(1)} %get-tuple-element.46.total_ref, ...), custom_call_target="tpu_custom_call" | custom-call | bytes 1452032 | tf_op jit(solution)/shard_map/pallas_call | solution.py:313
  10.6 0.0 collective-permute-done.6.refs_9_
  10.6 0.0 collective-permute-done.3.refs_10_
  10.6 0.1 %collective-permute-start.8 = (bf16[512,128]{1,0:T(8,128)(2,1)S(1)}, bf16[512,128]{1,0:T(8,128)(2,1)S(1)}, u32[]{:S(2)}, u32[]{:S(2)}) collective-permute-start(bf16[512,128]{1,0:T(8,128)(2,1)S(1)} %collective-permute-done.3.refs_10_), channel_id=1, source_target_pairs={{0,8},{8,0},{16,24},{24,16},{1,9},{9,1},{17,25},{25,17},{2,10},{10... | collective-permute-start | bytes 393224 | tf_op jit(solution)/shard_map/ppermute | solution.py:335
  10.7 0.4 %collective-permute-start.7 = (bf16[64,128]{1,0:T(8,128)(2,1)S(1)}, bf16[64,128]{1,0:T(8,128)(2,1)S(1)}, u32[]{:S(2)}, u32[]{:S(2)}) collective-permute-start(bf16[64,128]{1,0:T(8,128)(2,1)S(1)} %collective-permute-done.6.refs_9_), channel_id=1, source_target_pairs={{0,8},{8,0},{16,24},{24,16},{1,9},{9,1},{17,25},{25,17},{2,10},{10... | collective-permute-start | bytes 49160 | tf_op jit(solution)/shard_map/ppermute | solution.py:335
  11.2 0.0 collective-permute-done.2.refs_0_
  11.2 0.0 collective-permute-done.5.refs_9_
  11.2 1.1 %shard_map.91 = (bf16[512,128]{1,0:T(8,128)(2,1)}, bf16[512,128]{1,0:T(8,128)(2,1)}, f32[128,512]{1,0:T(8,128)S(1)}) custom-call(bf16[128,512]{1,0:T(8,128)(2,1)S(1)} %get-tuple-element.38.refs_0_.refs_2_, f32[128,512]{1,0:T(8,128)S(1)} %get-tuple-element.39.refs_1_.refs_3_, f32[1,512]{1,0:T(1,128)S(1)} %get-tuple-element.36.cum_row_ref.refs_2_.refs_4_, ...), custom_call_target="tpu_custom_call" | custom-call | bytes 2273280 | tf_op jit(solution)/shard_map/pallas_call | solution.py:313
  12.3 0.0 collective-permute-done.7.refs_10_
  12.3 0.0 collective-permute-done.8.refs_11_
  (3 shorter events, 0.1 us)
Async XLA Ops:
  0.6 8.9 %collective-permute-start.1 = (bf16[512,128]{1,0:T(8,128)(2,1)}, bf16[512,128]{1,0:T(8,128)(2,1)S(1)}, u32[]{:S(2)}, u32[]{:S(2)}) collective-permute-start(bf16[512,128]{1,0:T(8,128)(2,1)} %bitcast.14), channel_id=1, source_target_pairs={{0,16},{8,24},{16,0},{24,8},{1,17},{9,25},{17,1},{25,9},{2,18},{10... | collective-permute-start | bytes 393224 | tf_op jit(solution)/shard_map/ppermute | solution.py:332
  3.6 6.4 %collective-permute-start = (bf16[512,128]{1,0:T(8,128)(2,1)}, bf16[512,128]{1,0:T(8,128)(2,1)S(1)}, u32[]{:S(2)}, u32[]{:S(2)}) collective-permute-start(bf16[512,128]{1,0:T(8,128)(2,1)} %bitcast.15), channel_id=1, source_target_pairs={{0,8},{8,0},{16,24},{24,16},{1,9},{9,1},{17,25},{25,17},{2,10},{10... | collective-permute-start | bytes 393224 | tf_op jit(solution)/shard_map/ppermute | solution.py:335
  3.6 7.0 %collective-permute-start.3 = (bf16[512,128]{1,0:T(8,128)(2,1)}, bf16[512,128]{1,0:T(8,128)(2,1)S(1)}, u32[]{:S(2)}, u32[]{:S(2)}) collective-permute-start(bf16[512,128]{1,0:T(8,128)(2,1)} %bitcast.17), channel_id=1, source_target_pairs={{0,16},{8,24},{16,0},{24,8},{1,17},{9,25},{17,1},{25,9},{2,18},{10... | collective-permute-start | bytes 393224 | tf_op jit(solution)/shard_map/ppermute | solution.py:332
  5.1 1.3 %collective-permute-start.4 = (bf16[144,128]{1,0:T(8,128)(2,1)S(1)}, bf16[144,128]{1,0:T(8,128)(2,1)S(1)}, u32[]{:S(2)}, u32[]{:S(2)}) collective-permute-start(bf16[144,128]{1,0:T(8,128)(2,1)S(1)} %get-tuple-element.54.refs_0_), channel_id=1, source_target_pairs={{0,8},{8,0},{16,24},{24,16},{1,9},{9,1},{17,25},{25,17},{2,10},{10... | collective-permute-start | bytes 110600 | tf_op jit(solution)/shard_map/ppermute | solution.py:335
  6.5 4.1 %collective-permute-start.6 = (bf16[64,128]{1,0:T(8,128)(2,1)S(1)}, bf16[64,128]{1,0:T(8,128)(2,1)S(1)}, u32[]{:S(2)}, u32[]{:S(2)}) collective-permute-start(bf16[64,128]{1,0:T(8,128)(2,1)S(1)} %shard_map.92), channel_id=1, source_target_pairs={{0,16},{8,24},{16,0},{24,8},{1,17},{9,25},{17,1},{25,9},{2,18},{10... | collective-permute-start | bytes 49160 | tf_op jit(solution)/shard_map/ppermute | solution.py:332
  9.5 1.7 %collective-permute-start.2 = (bf16[512,128]{1,0:T(8,128)(2,1)S(1)}, bf16[512,128]{1,0:T(8,128)(2,1)S(1)}, u32[]{:S(2)}, u32[]{:S(2)}) collective-permute-start(bf16[512,128]{1,0:T(8,128)(2,1)S(1)} %collective-permute-done.1.refs_1_), channel_id=1, source_target_pairs={{0,8},{8,0},{16,24},{24,16},{1,9},{9,1},{17,25},{25,17},{2,10},{10... | collective-permute-start | bytes 393224 | tf_op jit(solution)/shard_map/ppermute | solution.py:335
  9.6 1.6 %collective-permute-start.5 = (bf16[512,128]{1,0:T(8,128)(2,1)S(1)}, bf16[512,128]{1,0:T(8,128)(2,1)S(1)}, u32[]{:S(2)}, u32[]{:S(2)}) collective-permute-start(bf16[512,128]{1,0:T(8,128)(2,1)S(1)} %get-tuple-element.42.pack_ref), channel_id=1, source_target_pairs={{0,8},{8,0},{16,24},{24,16},{1,9},{9,1},{17,25},{25,17},{2,10},{10... | collective-permute-start | bytes 393224 | tf_op jit(solution)/shard_map/ppermute | solution.py:335
  10.6 1.7 %collective-permute-start.8 = (bf16[512,128]{1,0:T(8,128)(2,1)S(1)}, bf16[512,128]{1,0:T(8,128)(2,1)S(1)}, u32[]{:S(2)}, u32[]{:S(2)}) collective-permute-start(bf16[512,128]{1,0:T(8,128)(2,1)S(1)} %collective-permute-done.3.refs_10_), channel_id=1, source_target_pairs={{0,8},{8,0},{16,24},{24,16},{1,9},{9,1},{17,25},{25,17},{2,10},{10... | collective-permute-start | bytes 393224 | tf_op jit(solution)/shard_map/ppermute | solution.py:335
  10.7 1.6 %collective-permute-start.7 = (bf16[64,128]{1,0:T(8,128)(2,1)S(1)}, bf16[64,128]{1,0:T(8,128)(2,1)S(1)}, u32[]{:S(2)}, u32[]{:S(2)}) collective-permute-start(bf16[64,128]{1,0:T(8,128)(2,1)S(1)} %collective-permute-done.6.refs_9_), channel_id=1, source_target_pairs={{0,8},{8,0},{16,24},{24,16},{1,9},{9,1},{17,25},{25,17},{2,10},{10... | collective-permute-start | bytes 49160 | tf_op jit(solution)/shard_map/ppermute | solution.py:335

commit v15 on v14

--- a/solution.py
+++ b/solution.py
@@ -11,6 +11,7 @@
 NEG = -1e30
 TINY = 1e-6
 PAD = 16
+STEP = 256
 KERNEL_VMEM = 16 * 2**20
 F32 = jnp.float32
 BF16 = jnp.bfloat16
@@ -204,16 +205,6 @@
     return carried.astype(BF16)
 
 
-def put_linear(step, carried, qt_ref, intra_ref, cum_row_ref, buffer):
-    width, rows = qt_ref.shape
-    for start in range(0, rows, step):
-        mine = slice(start, start + step)
-        inter = dot(carried, qt_ref[:, mine])
-        raw = intra_ref[:, mine] + inter * jnp.exp(cum_row_ref[:, mine])
-        square = jnp.sum(raw * raw, axis=0, keepdims=True) * (1.0 / width)
-        buffer[mine, :] = jnp.transpose((raw * lax.rsqrt(square + TINY)).astype(BF16))
-
-
 def value_sum(values_t, probs_ref, mine):
     rows = values_t[0].shape[1]
     terms = [
@@ -224,21 +215,28 @@
 
 def write_out(step, sofar, values_t, probs_ref, sum_ref, carried, linear_refs, outs, buffers, sems):
     lin_qt_ref, intra_ref, cum_row_ref = linear_refs
-    linear_buffer, softmax_buffer = buffers
-    rows = sum_ref.shape[1]
-    linear_copy = pltpu.make_async_copy(linear_buffer, outs[0], sems.at[0])
-    softmax_copy = pltpu.make_async_copy(softmax_buffer, outs[1], sems.at[1])
+    width, rows = lin_qt_ref.shape
+    copies = []
+
+    def put(place, mine, block):
+        buffers[place][mine, :] = jnp.transpose(block.astype(BF16))
+        span = pl.ds(mine.start, step)
+        copy = pltpu.make_async_copy(buffers[place].at[span], outs[place].at[span], sems.at[len(copies)])
+        copy.start()
+        copies.append(copy)
+
     for start in range(0, rows, step):
         mine = slice(start, start + step)
+        inter = dot(carried, lin_qt_ref[:, mine])
         summed = sofar(mine)
         if values_t:
             summed = summed + value_sum(values_t, probs_ref, mine)
-        softmax_buffer[mine, :] = jnp.transpose((summed / sum_ref[:, mine]).astype(BF16))
-    softmax_copy.start()
-    put_linear(step, carried(), lin_qt_ref, intra_ref, cum_row_ref, linear_buffer)
-    linear_copy.start()
-    softmax_copy.wait()
-    linear_copy.wait()
+        raw = intra_ref[:, mine] + inter * jnp.exp(cum_row_ref[:, mine])
+        square = jnp.sum(raw * raw, axis=0, keepdims=True) * (1.0 / width)
+        put(0, mine, raw * lax.rsqrt(square + TINY))
+        put(1, mine, summed * (1.0 / sum_ref[:, mine]))
+    for copy in copies:
+        copy.wait()
 
 
 def early_kernel(step, axis, cores, near_count, *refs):
@@ -264,7 +262,7 @@
     def _():
         write_out(
             step, scaled, [side_by_side(ref, rows, width) for ref in values[:near_count]], probs_ref, sum_ref,
-            lambda: carried_state(position, cores, near_states, (), width),
+            carried_state(position, cores, near_states, (), width),
             (lin_qt_ref, intra_ref, cum_row_ref), (linear_ref, softmax_ref), scratch, sems,
         )
 
@@ -283,7 +281,7 @@
     def _():
         write_out(
             step, lambda mine: sofar_ref[:, mine], [jnp.transpose(ref[...]) for ref in values],
-            probs_ref, sum_ref, lambda: carried_state(position, cores, near_states, shares, width),
+            probs_ref, sum_ref, carried_state(position, cores, near_states, shares, width),
             (lin_qt_ref, intra_ref, cum_row_ref), (linear_ref, softmax_ref), scratch, sems,
         )
 
@@ -309,7 +307,7 @@
     inside, outside = pl.BlockSpec(memory_space=VMEM), pl.BlockSpec(memory_space=pl.ANY)
     hbm = (*given, *resumed)
     scratch = [VMEM(x.shape, x.dtype) for x in (*scratch, *written)]
-    moved = len(given) + len(written)
+    moved = len(given) + sum(x.shape[0] // math.gcd(x.shape[0], STEP) for x in written)
     return pl.pallas_call(
         body,
         out_shape=(*map(kept_in_hbm, written), *map(kept_in_vmem, outs)),
@@ -344,7 +342,7 @@
         return near(lax.optimization_barrier((block, after))[0] for block in blocks)
 
     def one_head(lq, lk, lv, decay, sq, sk, sv):
-        step = math.gcd(rows, 256)
+        step = math.gcd(rows, STEP)
         scale = math.log2(math.e) / math.sqrt(width)
 
         def shape(*dims, dtype=F32):

time: 12.5 us -> 12.5 us (level)
  no operation moved by 1% of the time
where the time goes in v15:
time: 12.5 us; the launch traced here: 12.3 us
  starting transfers between devices  6.65 us (53%)
  Pallas kernels  4.07 us (33%)
  waiting for transfers between devices  0.89 us (7%)
  between operations  0.72 us (6%)
    ppermute x3, starting transfers between devices, across(): lax.ppermute(x, axis, [(i, (i + apart * cores) % count) for i in range(co...  5.09 us
    pallas_call x8, Pallas kernels, call(): pl.pallas_call(body, out_shape=(*map(kept_in_hbm, written), *map(kept_in_...  4.07 us
    ppermute x6, starting transfers between devices, swapped(): return lax.ppermute(x, axis, [(i, i ^ 1) for i in range(count)])  1.57 us
    ppermute x6, waiting for transfers between devices, swapped(): return lax.ppermute(x, axis, [(i, i ^ 1) for i in range(count)])  0.88 us
  transfers between devices with their start and end apart: 9, of which 1 were waited for; matrix products, arithmetic and copies ran while one was open for 0% of the time, Pallas kernels for 33%

profile of v15, /device:TPU:0, one launch (start us, length us, event | category | flops | bytes accessed | tf_op | source)
XLA Modules:
  0.0 12.3 jit_solution(10523354593720410923)
XLA Ops:
  0.6 3.0 %collective-permute-start.1 = (bf16[512,128]{1,0:T(8,128)(2,1)}, bf16[512,128]{1,0:T(8,128)(2,1)S(1)}, u32[]{:S(2)}, u32[]{:S(2)}) collective-permute-start(bf16[512,128]{1,0:T(8,128)(2,1)} %bitcast.14), channel_id=1, source_target_pairs={{0,16},{8,24},{16,0},{24,8},{1,17},{9,25},{17,1},{25,9},{2,18},{10... | collective-permute-start | bytes 393224 | tf_op jit(solution)/shard_map/ppermute | solution.py:330
  3.6 0.0 collective-permute-start
  3.6 0.2 %collective-permute-start.3 = (bf16[512,128]{1,0:T(8,128)(2,1)}, bf16[512,128]{1,0:T(8,128)(2,1)S(1)}, u32[]{:S(2)}, u32[]{:S(2)}) collective-permute-start(bf16[512,128]{1,0:T(8,128)(2,1)} %bitcast.17), channel_id=1, source_target_pairs={{0,16},{8,24},{16,0},{24,8},{1,17},{9,25},{17,1},{25,9},{2,18},{10... | collective-permute-start | bytes 393224 | tf_op jit(solution)/shard_map/ppermute | solution.py:330
  3.8 1.3 %shard_map.86 = (bf16[512,128]{1,0:T(8,128)(2,1)S(1)}, bf16[144,128]{1,0:T(8,128)(2,1)S(1)}, f32[1,512]{1,0:T(1,128)S(1)}, f32[512,128]{1,0:T(8,128)S(1)}, bf16[...) custom-call(f32[1,512]{1,0:T(1,128)} %decay_hbm.1, ...), custom_call_target="tpu_custom_call" | custom-call | bytes 1875968 | tf_op jit(solution)/shard_map/pallas_call | solution.py:311
  5.1 0.4 %collective-permute-start.4 = (bf16[144,128]{1,0:T(8,128)(2,1)S(1)}, bf16[144,128]{1,0:T(8,128)(2,1)S(1)}, u32[]{:S(2)}, u32[]{:S(2)}) collective-permute-start(bf16[144,128]{1,0:T(8,128)(2,1)S(1)} %get-tuple-element.54.refs_0_), channel_id=1, source_target_pairs={{0,8},{8,0},{16,24},{24,16},{1,9},{9,1},{17,25},{25,17},{2,10},{10... | collective-permute-start | bytes 110600 | tf_op jit(solution)/shard_map/ppermute | solution.py:333
  5.6 0.9 %collective-permute-done.4.refs_8_.refs_1_ = bf16[144,128]{1,0:T(8,128)(2,1)S(1)} collective-permute-done((bf16[144,128]{1,0:T(8,128)(2,1)S(1)}, bf16[144,128]{1,0:T(8,128)(2,1)S(1)}, u32[]{:S(2)}, u32[]{:S(2)}) %collective-permute-start.4) | collective-permute-done | bytes 36896 | tf_op jit(solution)/shard_map/ppermute | solution.py:333
  6.5 1.9 %collective-permute-start.6 = (bf16[64,128]{1,0:T(8,128)(2,1)S(1)}, bf16[64,128]{1,0:T(8,128)(2,1)S(1)}, u32[]{:S(2)}, u32[]{:S(2)}) collective-permute-start(bf16[64,128]{1,0:T(8,128)(2,1)S(1)} %shard_map.92), channel_id=1, source_target_pairs={{0,16},{8,24},{16,0},{24,8},{1,17},{9,25},{17,1},{25,9},{2,18},{10... | collective-permute-start | bytes 49160 | tf_op jit(solution)/shard_map/ppermute | solution.py:330
  8.4 0.6 %shard_map.88 = (bf16[128,512]{1,0:T(8,128)(2,1)S(1)}, f32[1,512]{1,0:T(1,128)S(1)}, f32[1,512]{1,0:T(1,128)S(1)}, f32[128,512]{1,0:T(8,128)S(1)}) custom-call(bf16[512,128]{1,0:T(8,128)(2,1)S(1)} %get-tuple-element.40.q_ref, bf16[512,128]{1,0:T(8,128)(2,1)S(1)} %get-tuple-element.41.k_ref, bf16[512,128]{1,0:T(8,128)(2,1)S(1)} %get-tuple-element.42.pack_ref), custom_call_target="tpu_custom_call" | custom-call | bytes 790528 | tf_op jit(solution)/shard_map/pallas_call | solution.py:311
  9.0 0.5 %shard_map.87 = (bf16[128,512]{1,0:T(8,128)(2,1)S(1)}, f32[128,512]{1,0:T(8,128)S(1)}) custom-call(bf16[512,128]{1,0:T(8,128)(2,1)S(1)} %get-tuple-element.33.q_ref, bf16[512,128]{1,0:T(8,128)(2,1)S(1)} %get-tuple-element.34.k_ref, bf16[128,512]{1,0:T(8,128)(2,1)S(1)} %get-tuple-element.35.value_t_ref, ...), custom_call_target="tpu_custom_call" | custom-call | bytes 1050624 | tf_op jit(solution)/shard_map/pallas_call | solution.py:311
  9.5 0.0 collective-permute-done.1.refs_1_
  9.5 0.1 collective-permute-start.2
  9.6 0.5 %collective-permute-start.5 = (bf16[512,128]{1,0:T(8,128)(2,1)S(1)}, bf16[512,128]{1,0:T(8,128)(2,1)S(1)}, u32[]{:S(2)}, u32[]{:S(2)}) collective-permute-start(bf16[512,128]{1,0:T(8,128)(2,1)S(1)} %get-tuple-element.42.pack_ref), channel_id=1, source_target_pairs={{0,8},{8,0},{16,24},{24,16},{1,9},{9,1},{17,25},{25,17},{2,10},{10... | collective-permute-start | bytes 393224 | tf_op jit(solution)/shard_map/ppermute | solution.py:333
  10.1 0.0 collective-permute-done.refs_0_
  10.1 0.5 %shard_map.89 = (bf16[1024,512]{1,0:T(8,128)(2,1)S(1)}, f32[1,512]{1,0:T(1,128)S(1)}, f32[1,512]{1,0:T(1,128)S(1)}, f32[1,512]{1,0:T(1,128)S(1)}) custom-call(bf16[128,512]{1,0:T(8,128)(2,1)S(1)} %get-tuple-element.44.qt_ref, f32[1,512]{1,0:T(1,128)S(1)} %get-tuple-element.45.top_ref, f32[1,512]{1,0:T(1,128)S(1)} %get-tuple-element.46.total_ref, ...), custom_call_target="tpu_custom_call" | custom-call | bytes 1452032 | tf_op jit(solution)/shard_map/pallas_call | solution.py:311
  10.6 0.0 collective-permute-done.6.refs_9_
  10.6 0.0 collective-permute-done.3.refs_10_
  10.6 0.1 %collective-permute-start.8 = (bf16[512,128]{1,0:T(8,128)(2,1)S(1)}, bf16[512,128]{1,0:T(8,128)(2,1)S(1)}, u32[]{:S(2)}, u32[]{:S(2)}) collective-permute-start(bf16[512,128]{1,0:T(8,128)(2,1)S(1)} %collective-permute-done.3.refs_10_), channel_id=1, source_target_pairs={{0,8},{8,0},{16,24},{24,16},{1,9},{9,1},{17,25},{25,17},{2,10},{10... | collective-permute-start | bytes 393224 | tf_op jit(solution)/shard_map/ppermute | solution.py:333
  10.7 0.4 %collective-permute-start.7 = (bf16[64,128]{1,0:T(8,128)(2,1)S(1)}, bf16[64,128]{1,0:T(8,128)(2,1)S(1)}, u32[]{:S(2)}, u32[]{:S(2)}) collective-permute-start(bf16[64,128]{1,0:T(8,128)(2,1)S(1)} %collective-permute-done.6.refs_9_), channel_id=1, source_target_pairs={{0,8},{8,0},{16,24},{24,16},{1,9},{9,1},{17,25},{25,17},{2,10},{10... | collective-permute-start | bytes 49160 | tf_op jit(solution)/shard_map/ppermute | solution.py:333
  11.2 0.0 collective-permute-done.2.refs_0_
  11.2 0.0 collective-permute-done.5.refs_9_
  11.2 1.0 %shard_map.91 = (bf16[512,128]{1,0:T(8,128)(2,1)}, bf16[512,128]{1,0:T(8,128)(2,1)}, f32[128,512]{1,0:T(8,128)S(1)}) custom-call(bf16[128,512]{1,0:T(8,128)(2,1)S(1)} %get-tuple-element.38.refs_0_.refs_2_, f32[128,512]{1,0:T(8,128)S(1)} %get-tuple-element.39.refs_1_.refs_3_, f32[1,512]{1,0:T(1,128)S(1)} %get-tuple-element.36.cum_row_ref.refs_2_.refs_4_, ...), custom_call_target="tpu_custom_call" | custom-call | bytes 2273280 | tf_op jit(solution)/shard_map/pallas_call | solution.py:311
  12.3 0.0 collective-permute-done.7.refs_10_
  12.3 0.0 collective-permute-done.8.refs_11_
  12.3 0.1 shard_map.93
  (2 shorter events, 0.0 us)
Async XLA Ops:
  0.6 8.9 %collective-permute-start.1 = (bf16[512,128]{1,0:T(8,128)(2,1)}, bf16[512,128]{1,0:T(8,128)(2,1)S(1)}, u32[]{:S(2)}, u32[]{:S(2)}) collective-permute-start(bf16[512,128]{1,0:T(8,128)(2,1)} %bitcast.14), channel_id=1, source_target_pairs={{0,16},{8,24},{16,0},{24,8},{1,17},{9,25},{17,1},{25,9},{2,18},{10... | collective-permute-start | bytes 393224 | tf_op jit(solution)/shard_map/ppermute | solution.py:330
  3.6 6.4 %collective-permute-start = (bf16[512,128]{1,0:T(8,128)(2,1)}, bf16[512,128]{1,0:T(8,128)(2,1)S(1)}, u32[]{:S(2)}, u32[]{:S(2)}) collective-permute-start(bf16[512,128]{1,0:T(8,128)(2,1)} %bitcast.15), channel_id=1, source_target_pairs={{0,8},{8,0},{16,24},{24,16},{1,9},{9,1},{17,25},{25,17},{2,10},{10... | collective-permute-start | bytes 393224 | tf_op jit(solution)/shard_map/ppermute | solution.py:333
  3.6 7.0 %collective-permute-start.3 = (bf16[512,128]{1,0:T(8,128)(2,1)}, bf16[512,128]{1,0:T(8,128)(2,1)S(1)}, u32[]{:S(2)}, u32[]{:S(2)}) collective-permute-start(bf16[512,128]{1,0:T(8,128)(2,1)} %bitcast.17), channel_id=1, source_target_pairs={{0,16},{8,24},{16,0},{24,8},{1,17},{9,25},{17,1},{25,9},{2,18},{10... | collective-permute-start | bytes 393224 | tf_op jit(solution)/shard_map/ppermute | solution.py:330
  5.1 1.3 %collective-permute-start.4 = (bf16[144,128]{1,0:T(8,128)(2,1)S(1)}, bf16[144,128]{1,0:T(8,128)(2,1)S(1)}, u32[]{:S(2)}, u32[]{:S(2)}) collective-permute-start(bf16[144,128]{1,0:T(8,128)(2,1)S(1)} %get-tuple-element.54.refs_0_), channel_id=1, source_target_pairs={{0,8},{8,0},{16,24},{24,16},{1,9},{9,1},{17,25},{25,17},{2,10},{10... | collective-permute-start | bytes 110600 | tf_op jit(solution)/shard_map/ppermute | solution.py:333
  6.5 4.1 %collective-permute-start.6 = (bf16[64,128]{1,0:T(8,128)(2,1)S(1)}, bf16[64,128]{1,0:T(8,128)(2,1)S(1)}, u32[]{:S(2)}, u32[]{:S(2)}) collective-permute-start(bf16[64,128]{1,0:T(8,128)(2,1)S(1)} %shard_map.92), channel_id=1, source_target_pairs={{0,16},{8,24},{16,0},{24,8},{1,17},{9,25},{17,1},{25,9},{2,18},{10... | collective-permute-start | bytes 49160 | tf_op jit(solution)/shard_map/ppermute | solution.py:330
  9.5 1.7 %collective-permute-start.2 = (bf16[512,128]{1,0:T(8,128)(2,1)S(1)}, bf16[512,128]{1,0:T(8,128)(2,1)S(1)}, u32[]{:S(2)}, u32[]{:S(2)}) collective-permute-start(bf16[512,128]{1,0:T(8,128)(2,1)S(1)} %collective-permute-done.1.refs_1_), channel_id=1, source_target_pairs={{0,8},{8,0},{16,24},{24,16},{1,9},{9,1},{17,25},{25,17},{2,10},{10... | collective-permute-start | bytes 393224 | tf_op jit(solution)/shard_map/ppermute | solution.py:333
  9.6 1.6 %collective-permute-start.5 = (bf16[512,128]{1,0:T(8,128)(2,1)S(1)}, bf16[512,128]{1,0:T(8,128)(2,1)S(1)}, u32[]{:S(2)}, u32[]{:S(2)}) collective-permute-start(bf16[512,128]{1,0:T(8,128)(2,1)S(1)} %get-tuple-element.42.pack_ref), channel_id=1, source_target_pairs={{0,8},{8,0},{16,24},{24,16},{1,9},{9,1},{17,25},{25,17},{2,10},{10... | collective-permute-start | bytes 393224 | tf_op jit(solution)/shard_map/ppermute | solution.py:333
  10.6 1.7 %collective-permute-start.8 = (bf16[512,128]{1,0:T(8,128)(2,1)S(1)}, bf16[512,128]{1,0:T(8,128)(2,1)S(1)}, u32[]{:S(2)}, u32[]{:S(2)}) collective-permute-start(bf16[512,128]{1,0:T(8,128)(2,1)S(1)} %collective-permute-done.3.refs_10_), channel_id=1, source_target_pairs={{0,8},{8,0},{16,24},{24,16},{1,9},{9,1},{17,25},{25,17},{2,10},{10... | collective-permute-start | bytes 393224 | tf_op jit(solution)/shard_map/ppermute | solution.py:333
  10.7 1.5 %collective-permute-start.7 = (bf16[64,128]{1,0:T(8,128)(2,1)S(1)}, bf16[64,128]{1,0:T(8,128)(2,1)S(1)}, u32[]{:S(2)}, u32[]{:S(2)}) collective-permute-start(bf16[64,128]{1,0:T(8,128)(2,1)S(1)} %collective-permute-done.6.refs_9_), channel_id=1, source_target_pairs={{0,8},{8,0},{16,24},{24,16},{1,9},{9,1},{17,25},{25,17},{2,10},{10... | collective-permute-start | bytes 49160 | tf_op jit(solution)/shard_map/ppermute | solution.py:333

commit v16 on v15

--- a/solution.py
+++ b/solution.py
@@ -364,6 +364,7 @@
         qt, top, total, summed = call(
             functools.partial(soft_kernel, scale, step), (sq, own_keys, soft_vt), (flat16, row, row, flat)
         )
+        near_states, _ = lax.optimization_barrier((near_states, summed))
         (share,) = call(
             functools.partial(combine_kernel, axis, cores),
             (state, *near_states),

time: 12.5 us -> 12.4 us (level)
    ppermute x6, waiting for transfers between devices: 0.88 us -> 0.27 us  [swapped(): return lax.ppermute(x, axis, [(i, i ^ 1) for i in range(count)])]
    ppermute x3, waiting for transfers between devices: 0.01 us -> 0.53 us  [across(): lax.ppermute(x, axis, [(i, (i + apart * cores) % count) for i in range(co...]
  transfers between devices with their start and end apart: 9 -> 9, of which waited for: 1 -> 2; matrix products, arithmetic and copies ran while one was open for 0% -> 0% of each run, Pallas kernels for 33% -> 33%
where the time goes in v16:
time: 12.4 us; the launch traced here: 12.2 us
  starting transfers between devices  6.59 us (53%)
  Pallas kernels  4.07 us (33%)
  waiting for transfers between devices  0.81 us (7%)
  between operations  0.71 us (6%)
    ppermute x3, starting transfers between devices, across(): lax.ppermute(x, axis, [(i, (i + apart * cores) % count) for i in range(co...  5.09 us
    pallas_call x8, Pallas kernels, call(): pl.pallas_call(body, out_shape=(*map(kept_in_hbm, written), *map(kept_in_...  4.07 us
    ppermute x6, starting transfers between devices, swapped(): return lax.ppermute(x, axis, [(i, i ^ 1) for i in range(count)])  1.5 us
    ppermute x3, waiting for transfers between devices, across(): lax.ppermute(x, axis, [(i, (i + apart * cores) % count) for i in range(co...  0.53 us
    ppermute x6, waiting for transfers between devices, swapped(): return lax.ppermute(x, axis, [(i, i ^ 1) for i in range(count)])  0.27 us
  transfers between devices with their start and end apart: 9, of which 2 were waited for; matrix products, arithmetic and copies ran while one was open for 0% of the time, Pallas kernels for 33%

profile of v16, /device:TPU:0, one launch (start us, length us, event | category | flops | bytes accessed | tf_op | source)
XLA Modules:
  0.0 12.2 jit_solution(4668207419270311771)
XLA Ops:
  0.6 3.0 %collective-permute-start.1 = (bf16[512,128]{1,0:T(8,128)(2,1)}, bf16[512,128]{1,0:T(8,128)(2,1)S(1)}, u32[]{:S(2)}, u32[]{:S(2)}) collective-permute-start(bf16[512,128]{1,0:T(8,128)(2,1)} %bitcast.14), channel_id=1, source_target_pairs={{0,16},{8,24},{16,0},{24,8},{1,17},{9,25},{17,1},{25,9},{2,18},{10... | collective-permute-start | bytes 393224 | tf_op jit(solution)/shard_map/ppermute | solution.py:330
  3.6 0.0 collective-permute-start
  3.6 0.2 %collective-permute-start.3 = (bf16[512,128]{1,0:T(8,128)(2,1)}, bf16[512,128]{1,0:T(8,128)(2,1)S(1)}, u32[]{:S(2)}, u32[]{:S(2)}) collective-permute-start(bf16[512,128]{1,0:T(8,128)(2,1)} %bitcast.17), channel_id=1, source_target_pairs={{0,16},{8,24},{16,0},{24,8},{1,17},{9,25},{17,1},{25,9},{2,18},{10... | collective-permute-start | bytes 393224 | tf_op jit(solution)/shard_map/ppermute | solution.py:330
  3.8 1.3 %shard_map.86 = (bf16[512,128]{1,0:T(8,128)(2,1)S(1)}, bf16[144,128]{1,0:T(8,128)(2,1)S(1)}, f32[1,512]{1,0:T(1,128)S(1)}, f32[512,128]{1,0:T(8,128)S(1)}, bf16[...) custom-call(f32[1,512]{1,0:T(1,128)} %decay_hbm.1, ...), custom_call_target="tpu_custom_call" | custom-call | bytes 1875968 | tf_op jit(solution)/shard_map/pallas_call | solution.py:311
  5.1 0.4 %collective-permute-start.4 = (bf16[144,128]{1,0:T(8,128)(2,1)S(1)}, bf16[144,128]{1,0:T(8,128)(2,1)S(1)}, u32[]{:S(2)}, u32[]{:S(2)}) collective-permute-start(bf16[144,128]{1,0:T(8,128)(2,1)S(1)} %get-tuple-element.55.refs_0_), channel_id=1, source_target_pairs={{0,8},{8,0},{16,24},{24,16},{1,9},{9,1},{17,25},{25,17},{2,10},{10... | collective-permute-start | bytes 110600 | tf_op jit(solution)/shard_map/ppermute | solution.py:333
  5.6 0.6 %shard_map.88 = (bf16[128,512]{1,0:T(8,128)(2,1)S(1)}, f32[1,512]{1,0:T(1,128)S(1)}, f32[1,512]{1,0:T(1,128)S(1)}, f32[128,512]{1,0:T(8,128)S(1)}) custom-call(bf16[512,128]{1,0:T(8,128)(2,1)S(1)} %get-tuple-element.41.q_ref, bf16[512,128]{1,0:T(8,128)(2,1)S(1)} %get-tuple-element.42.k_ref, bf16[512,128]{1,0:T(8,128)(2,1)S(1)} %get-tuple-element.43.pack_ref), custom_call_target="tpu_custom_call" | custom-call | bytes 790528 | tf_op jit(solution)/shard_map/pallas_call | solution.py:311
  6.2 0.3 %collective-permute-done.4.refs_8_.refs_1_ = bf16[144,128]{1,0:T(8,128)(2,1)S(1)} collective-permute-done((bf16[144,128]{1,0:T(8,128)(2,1)S(1)}, bf16[144,128]{1,0:T(8,128)(2,1)S(1)}, u32[]{:S(2)}, u32[]{:S(2)}) %collective-permute-start.4) | collective-permute-done | bytes 36896 | tf_op jit(solution)/shard_map/ppermute | solution.py:333
  6.5 1.9 %collective-permute-start.6 = (bf16[64,128]{1,0:T(8,128)(2,1)S(1)}, bf16[64,128]{1,0:T(8,128)(2,1)S(1)}, u32[]{:S(2)}, u32[]{:S(2)}) collective-permute-start(bf16[64,128]{1,0:T(8,128)(2,1)S(1)} %shard_map.92), channel_id=1, source_target_pairs={{0,16},{8,24},{16,0},{24,8},{1,17},{9,25},{17,1},{25,9},{2,18},{10... | collective-permute-start | bytes 49160 | tf_op jit(solution)/shard_map/ppermute | solution.py:330
  8.4 0.5 %shard_map.87 = (bf16[128,512]{1,0:T(8,128)(2,1)S(1)}, f32[128,512]{1,0:T(8,128)S(1)}) custom-call(bf16[512,128]{1,0:T(8,128)(2,1)S(1)} %get-tuple-element.34.q_ref, bf16[512,128]{1,0:T(8,128)(2,1)S(1)} %get-tuple-element.35.k_ref, bf16[128,512]{1,0:T(8,128)(2,1)S(1)} %get-tuple-element.36.value_t_ref, ...), custom_call_target="tpu_custom_call" | custom-call | bytes 1050624 | tf_op jit(solution)/shard_map/pallas_call | solution.py:311
  8.9 0.0 collective-permute-done.1.refs_1_
  8.9 0.1 collective-permute-start.2
  9.0 0.5 %collective-permute-start.5 = (bf16[512,128]{1,0:T(8,128)(2,1)S(1)}, bf16[512,128]{1,0:T(8,128)(2,1)S(1)}, u32[]{:S(2)}, u32[]{:S(2)}) collective-permute-start(bf16[512,128]{1,0:T(8,128)(2,1)S(1)} %get-tuple-element.43.pack_ref), channel_id=1, source_target_pairs={{0,8},{8,0},{16,24},{24,16},{1,9},{9,1},{17,25},{25,17},{2,10},{10... | collective-permute-start | bytes 393224 | tf_op jit(solution)/shard_map/ppermute | solution.py:333
  9.5 0.0 collective-permute-done.refs_0_
  9.5 0.5 %shard_map.89 = (bf16[1024,512]{1,0:T(8,128)(2,1)S(1)}, f32[1,512]{1,0:T(1,128)S(1)}, f32[1,512]{1,0:T(1,128)S(1)}, f32[1,512]{1,0:T(1,128)S(1)}) custom-call(bf16[128,512]{1,0:T(8,128)(2,1)S(1)} %get-tuple-element.45.qt_ref, f32[1,512]{1,0:T(1,128)S(1)} %get-tuple-element.46.top_ref, f32[1,512]{1,0:T(1,128)S(1)} %get-tuple-element.47.total_ref, ...), custom_call_target="tpu_custom_call" | custom-call | bytes 1452032 | tf_op jit(solution)/shard_map/pallas_call | solution.py:311
  10.0 0.5 %collective-permute-done.6.refs_9_ = bf16[64,128]{1,0:T(8,128)(2,1)S(1)} collective-permute-done((bf16[64,128]{1,0:T(8,128)(2,1)S(1)}, bf16[64,128]{1,0:T(8,128)(2,1)S(1)}, u32[]{:S(2)}, u32[]{:S(2)}) %collective-permute-start.6) | collective-permute-done | bytes 16416 | tf_op jit(solution)/shard_map/ppermute | solution.py:330
  10.5 0.0 collective-permute-done.3.refs_10_
  10.5 0.0 collective-permute-start.8
  10.5 0.5 %collective-permute-start.7 = (bf16[64,128]{1,0:T(8,128)(2,1)S(1)}, bf16[64,128]{1,0:T(8,128)(2,1)S(1)}, u32[]{:S(2)}, u32[]{:S(2)}) collective-permute-start(bf16[64,128]{1,0:T(8,128)(2,1)S(1)} %collective-permute-done.6.refs_9_), channel_id=1, source_target_pairs={{0,8},{8,0},{16,24},{24,16},{1,9},{9,1},{17,25},{25,17},{2,10},{10... | collective-permute-start | bytes 49160 | tf_op jit(solution)/shard_map/ppermute | solution.py:333
  11.0 0.0 collective-permute-done.2.refs_0_
  11.0 0.0 collective-permute-done.5.refs_9_
  11.0 1.0 %shard_map.91 = (bf16[512,128]{1,0:T(8,128)(2,1)}, bf16[512,128]{1,0:T(8,128)(2,1)}, f32[128,512]{1,0:T(8,128)S(1)}) custom-call(bf16[128,512]{1,0:T(8,128)(2,1)S(1)} %get-tuple-element.39.refs_0_.refs_2_, f32[128,512]{1,0:T(8,128)S(1)} %get-tuple-element.40.refs_1_.refs_3_, f32[1,512]{1,0:T(1,128)S(1)} %get-tuple-element.37.cum_row_ref.refs_2_.refs_4_, ...), custom_call_target="tpu_custom_call" | custom-call | bytes 2273280 | tf_op jit(solution)/shard_map/pallas_call | solution.py:311
  12.1 0.0 collective-permute-done.7.refs_10_
  12.1 0.0 collective-permute-done.8.refs_11_
  12.1 0.1 shard_map.93
  (2 shorter events, 0.0 us)
Async XLA Ops:
  0.6 8.3 %collective-permute-start.1 = (bf16[512,128]{1,0:T(8,128)(2,1)}, bf16[512,128]{1,0:T(8,128)(2,1)S(1)}, u32[]{:S(2)}, u32[]{:S(2)}) collective-permute-start(bf16[512,128]{1,0:T(8,128)(2,1)} %bitcast.14), channel_id=1, source_target_pairs={{0,16},{8,24},{16,0},{24,8},{1,17},{9,25},{17,1},{25,9},{2,18},{10... | collective-permute-start | bytes 393224 | tf_op jit(solution)/shard_map/ppermute | solution.py:330
  3.6 5.8 %collective-permute-start = (bf16[512,128]{1,0:T(8,128)(2,1)}, bf16[512,128]{1,0:T(8,128)(2,1)S(1)}, u32[]{:S(2)}, u32[]{:S(2)}) collective-permute-start(bf16[512,128]{1,0:T(8,128)(2,1)} %bitcast.15), channel_id=1, source_target_pairs={{0,8},{8,0},{16,24},{24,16},{1,9},{9,1},{17,25},{25,17},{2,10},{10... | collective-permute-start | bytes 393224 | tf_op jit(solution)/shard_map/ppermute | solution.py:333
  3.6 6.9 %collective-permute-start.3 = (bf16[512,128]{1,0:T(8,128)(2,1)}, bf16[512,128]{1,0:T(8,128)(2,1)S(1)}, u32[]{:S(2)}, u32[]{:S(2)}) collective-permute-start(bf16[512,128]{1,0:T(8,128)(2,1)} %bitcast.17), channel_id=1, source_target_pairs={{0,16},{8,24},{16,0},{24,8},{1,17},{9,25},{17,1},{25,9},{2,18},{10... | collective-permute-start | bytes 393224 | tf_op jit(solution)/shard_map/ppermute | solution.py:330
  5.1 1.3 %collective-permute-start.4 = (bf16[144,128]{1,0:T(8,128)(2,1)S(1)}, bf16[144,128]{1,0:T(8,128)(2,1)S(1)}, u32[]{:S(2)}, u32[]{:S(2)}) collective-permute-start(bf16[144,128]{1,0:T(8,128)(2,1)S(1)} %get-tuple-element.55.refs_0_), channel_id=1, source_target_pairs={{0,8},{8,0},{16,24},{24,16},{1,9},{9,1},{17,25},{25,17},{2,10},{10... | collective-permute-start | bytes 110600 | tf_op jit(solution)/shard_map/ppermute | solution.py:333
  6.5 4.0 %collective-permute-start.6 = (bf16[64,128]{1,0:T(8,128)(2,1)S(1)}, bf16[64,128]{1,0:T(8,128)(2,1)S(1)}, u32[]{:S(2)}, u32[]{:S(2)}) collective-permute-start(bf16[64,128]{1,0:T(8,128)(2,1)S(1)} %shard_map.92), channel_id=1, source_target_pairs={{0,16},{8,24},{16,0},{24,8},{1,17},{9,25},{17,1},{25,9},{2,18},{10... | collective-permute-start | bytes 49160 | tf_op jit(solution)/shard_map/ppermute | solution.py:330
  8.9 2.1 %collective-permute-start.2 = (bf16[512,128]{1,0:T(8,128)(2,1)S(1)}, bf16[512,128]{1,0:T(8,128)(2,1)S(1)}, u32[]{:S(2)}, u32[]{:S(2)}) collective-permute-start(bf16[512,128]{1,0:T(8,128)(2,1)S(1)} %collective-permute-done.1.refs_1_), channel_id=1, source_target_pairs={{0,8},{8,0},{16,24},{24,16},{1,9},{9,1},{17,25},{25,17},{2,10},{10... | collective-permute-start | bytes 393224 | tf_op jit(solution)/shard_map/ppermute | solution.py:333
  9.0 2.1 %collective-permute-start.5 = (bf16[512,128]{1,0:T(8,128)(2,1)S(1)}, bf16[512,128]{1,0:T(8,128)(2,1)S(1)}, u32[]{:S(2)}, u32[]{:S(2)}) collective-permute-start(bf16[512,128]{1,0:T(8,128)(2,1)S(1)} %get-tuple-element.43.pack_ref), channel_id=1, source_target_pairs={{0,8},{8,0},{16,24},{24,16},{1,9},{9,1},{17,25},{25,17},{2,10},{10... | collective-permute-start | bytes 393224 | tf_op jit(solution)/shard_map/ppermute | solution.py:333
  10.5 1.6 %collective-permute-start.8 = (bf16[512,128]{1,0:T(8,128)(2,1)S(1)}, bf16[512,128]{1,0:T(8,128)(2,1)S(1)}, u32[]{:S(2)}, u32[]{:S(2)}) collective-permute-start(bf16[512,128]{1,0:T(8,128)(2,1)S(1)} %collective-permute-done.3.refs_10_), channel_id=1, source_target_pairs={{0,8},{8,0},{16,24},{24,16},{1,9},{9,1},{17,25},{25,17},{2,10},{10... | collective-permute-start | bytes 393224 | tf_op jit(solution)/shard_map/ppermute | solution.py:333
  10.5 1.6 %collective-permute-start.7 = (bf16[64,128]{1,0:T(8,128)(2,1)S(1)}, bf16[64,128]{1,0:T(8,128)(2,1)S(1)}, u32[]{:S(2)}, u32[]{:S(2)}) collective-permute-start(bf16[64,128]{1,0:T(8,128)(2,1)S(1)} %collective-permute-done.6.refs_9_), channel_id=1, source_target_pairs={{0,8},{8,0},{16,24},{24,16},{1,9},{9,1},{17,25},{25,17},{2,10},{10... | collective-permute-start | bytes 49160 | tf_op jit(solution)/shard_map/ppermute | solution.py:333

commit v17 on v16

--- a/solution.py
+++ b/solution.py
@@ -1,4 +1,5 @@
 import functools
+import itertools
 import math
 
 import jax
@@ -12,6 +13,7 @@
 TINY = 1e-6
 PAD = 16
 STEP = 256
+PARTS = 4
 KERNEL_VMEM = 16 * 2**20
 F32 = jnp.float32
 BF16 = jnp.bfloat16
@@ -47,37 +49,42 @@
     return pieces[0] if len(pieces) == 1 else jnp.concatenate(pieces, axis=1)
 
 
+def copies_of(source, target, sems, first):
+    rows = source.shape[0]
+    part = rows // PARTS if rows % (PARTS * 16) == 0 else rows
+    return [
+        pltpu.make_async_copy(source.at[pl.ds(start, part)], target.at[pl.ds(start, part)], sems.at[first + place])
+        for place, start in enumerate(range(0, rows, part))
+    ]
+
+
 def state_kernel(
     decay_hbm, key_hbm, value_hbm, soft_value_hbm, query_hbm, soft_query_hbm, soft_key_hbm,
     soft_vt_ref, state_ref, cum_row_ref, cum_col_ref, value_t_ref, key_ref, query_ref, soft_query_ref, soft_key_ref,
     decay_ref, value_ref, soft_value_ref, sems,
 ):
-    copies = [
-        pltpu.make_async_copy(source, target, sems.at[place])
-        for place, (source, target) in enumerate(
-            (
-                (decay_hbm, decay_ref),
-                (key_hbm, key_ref),
-                (value_hbm, value_ref),
-                (soft_value_hbm, soft_value_ref),
-                (soft_query_hbm, soft_query_ref),
-                (soft_key_hbm, soft_key_ref),
-                (query_hbm, query_ref),
-            )
-        )
-    ]
-    for copy in copies:
+    rows, width = key_ref.shape
+    pairs = (
+        (decay_hbm, decay_ref),
+        (key_hbm, key_ref),
+        (value_hbm, value_ref),
+        (soft_value_hbm, soft_value_ref),
+        (soft_query_hbm, soft_query_ref),
+        (soft_key_hbm, soft_key_ref),
+        (query_hbm, query_ref),
+    )
+    copies = [copies_of(*pair, sems, place * PARTS) for place, pair in enumerate(pairs)]
+    for copy in itertools.chain(*copies):
         copy.start()
-    rows, width = key_ref.shape
     upto = (iota((rows, rows), 0) <= iota((rows, rows), 1)).astype(F32).astype(BF16)
-    copies[0].wait()
+    copies[0][0].wait()
     parts = select_rows(three_parts(decay_ref[...]), PAD, rows)
     cum_row = jnp.sum(dot(parts, upto), axis=0, keepdims=True)
     cum_row_ref[...] = cum_row
     cum_col = jnp.transpose(jnp.broadcast_to(cum_row, (width, rows)))
     cum_col_ref[...] = cum_col
     total = cum_col[rows - 1 :, :]
-    for copy in copies[1:4]:
+    for copy in itertools.chain(*copies[1:4]):
         copy.wait()
     decayed = (key_ref[...].astype(F32) * jnp.exp(total - cum_col)).astype(BF16)
     value_t = jnp.transpose(value_ref[...])
@@ -86,7 +93,7 @@
     state_ref[width:, :] = select_rows(three_parts(total), PAD, width)
     for left in range(0, rows, width):
         soft_vt_ref[left : left + width, :] = jnp.transpose(soft_value_ref[left : left + width, :])
-    for copy in copies[4:]:
+    for copy in itertools.chain(*copies[4:]):
         copy.wait()
 
 
@@ -221,9 +228,9 @@
     def put(place, mine, block):
         buffers[place][mine, :] = jnp.transpose(block.astype(BF16))
         span = pl.ds(mine.start, step)
-        copy = pltpu.make_async_copy(buffers[place].at[span], outs[place].at[span], sems.at[len(copies)])
-        copy.start()
-        copies.append(copy)
+        for copy in copies_of(buffers[place].at[span], outs[place].at[span], sems, len(copies)):
+            copy.start()
+            copies.append(copy)
 
     for start in range(0, rows, step):
         mine = slice(start, start + step)
@@ -307,7 +314,7 @@
     inside, outside = pl.BlockSpec(memory_space=VMEM), pl.BlockSpec(memory_space=pl.ANY)
     hbm = (*given, *resumed)
     scratch = [VMEM(x.shape, x.dtype) for x in (*scratch, *written)]
-    moved = len(given) + sum(x.shape[0] // math.gcd(x.shape[0], STEP) for x in written)
+    moved = PARTS * (len(given) + sum(x.shape[0] // math.gcd(x.shape[0], STEP) for x in written))
     return pl.pallas_call(
         body,
         out_shape=(*map(kept_in_hbm, written), *map(kept_in_vmem, outs)),

time: 12.4 us -> 12.6 us (1.016)
  Pallas kernels: 4.07 us -> 4.42 us
  waiting for transfers between devices: 0.81 us -> 0.66 us
    pallas_call x8, Pallas kernels: 4.07 us -> 4.42 us  [call(): pl.pallas_call(body, out_shape=(*map(kept_in_hbm, written), *map(kept_in_...]
    ppermute x3, waiting for transfers between devices: 0.53 us -> 0.38 us  [across(): lax.ppermute(x, axis, [(i, (i + apart * cores) % count) for i in range(co...]
  transfers between devices with their start and end apart: 9 -> 9, of which waited for: 2 -> 2; matrix products, arithmetic and copies ran while one was open for 0% -> 0% of each run, Pallas kernels for 33% -> 34%
where the time goes in v17:
time: 12.6 us; the launch traced here: 12.4 us
  starting transfers between devices  6.59 us (52%)
  Pallas kernels  4.42 us (35%)
  between operations  0.71 us (6%)
  waiting for transfers between devices  0.66 us (5%)
    ppermute x3, starting transfers between devices, across(): lax.ppermute(x, axis, [(i, (i + apart * cores) % count) for i in range(co...  5.09 us
    pallas_call x8, Pallas kernels, call(): pl.pallas_call(body, out_shape=(*map(kept_in_hbm, written), *map(kept_in_...  4.42 us
    ppermute x6, starting transfers between devices, swapped(): return lax.ppermute(x, axis, [(i, i ^ 1) for i in range(count)])  1.5 us
    ppermute x3, waiting for transfers between devices, across(): lax.ppermute(x, axis, [(i, (i + apart * cores) % count) for i in range(co...  0.38 us
    ppermute x6, waiting for transfers between devices, swapped(): return lax.ppermute(x, axis, [(i, i ^ 1) for i in range(count)])  0.28 us
  transfers between devices with their start and end apart: 9, of which 2 were waited for; matrix products, arithmetic and copies ran while one was open for 0% of the time, Pallas kernels for 34%

profile of v17, /device:TPU:0, one launch (start us, length us, event | category | flops | bytes accessed | tf_op | source)
XLA Modules:
  0.0 12.4 jit_solution(11822840849930502595)
XLA Ops:
  0.6 3.0 %collective-permute-start.1 = (bf16[512,128]{1,0:T(8,128)(2,1)}, bf16[512,128]{1,0:T(8,128)(2,1)S(1)}, u32[]{:S(2)}, u32[]{:S(2)}) collective-permute-start(bf16[512,128]{1,0:T(8,128)(2,1)} %bitcast.14), channel_id=1, source_target_pairs={{0,16},{8,24},{16,0},{24,8},{1,17},{9,25},{17,1},{25,9},{2,18},{10... | collective-permute-start | bytes 393224 | tf_op jit(solution)/shard_map/ppermute | solution.py:337
  3.6 0.0 collective-permute-start
  3.6 0.2 %collective-permute-start.3 = (bf16[512,128]{1,0:T(8,128)(2,1)}, bf16[512,128]{1,0:T(8,128)(2,1)S(1)}, u32[]{:S(2)}, u32[]{:S(2)}) collective-permute-start(bf16[512,128]{1,0:T(8,128)(2,1)} %bitcast.17), channel_id=1, source_target_pairs={{0,16},{8,24},{16,0},{24,8},{1,17},{9,25},{17,1},{25,9},{2,18},{10... | collective-permute-start | bytes 393224 | tf_op jit(solution)/shard_map/ppermute | solution.py:337
  3.8 1.5 %shard_map.86 = (bf16[512,128]{1,0:T(8,128)(2,1)S(1)}, bf16[144,128]{1,0:T(8,128)(2,1)S(1)}, f32[1,512]{1,0:T(1,128)S(1)}, f32[512,128]{1,0:T(8,128)S(1)}, bf16[...) custom-call(f32[1,512]{1,0:T(1,128)} %decay_hbm.1, ...), custom_call_target="tpu_custom_call" | custom-call | bytes 1875968 | tf_op jit(solution)/shard_map/pallas_call | solution.py:318
  5.3 0.4 %collective-permute-start.4 = (bf16[144,128]{1,0:T(8,128)(2,1)S(1)}, bf16[144,128]{1,0:T(8,128)(2,1)S(1)}, u32[]{:S(2)}, u32[]{:S(2)}) collective-permute-start(bf16[144,128]{1,0:T(8,128)(2,1)S(1)} %get-tuple-element.55.refs_0_), channel_id=1, source_target_pairs={{0,8},{8,0},{16,24},{24,16},{1,9},{9,1},{17,25},{25,17},{2,10},{10... | collective-permute-start | bytes 110600 | tf_op jit(solution)/shard_map/ppermute | solution.py:340
  5.7 0.6 %shard_map.88 = (bf16[128,512]{1,0:T(8,128)(2,1)S(1)}, f32[1,512]{1,0:T(1,128)S(1)}, f32[1,512]{1,0:T(1,128)S(1)}, f32[128,512]{1,0:T(8,128)S(1)}) custom-call(bf16[512,128]{1,0:T(8,128)(2,1)S(1)} %get-tuple-element.41.q_ref, bf16[512,128]{1,0:T(8,128)(2,1)S(1)} %get-tuple-element.42.k_ref, bf16[512,128]{1,0:T(8,128)(2,1)S(1)} %get-tuple-element.43.pack_ref), custom_call_target="tpu_custom_call" | custom-call | bytes 790528 | tf_op jit(solution)/shard_map/pallas_call | solution.py:318
  6.3 0.3 %collective-permute-done.4.refs_8_.refs_1_ = bf16[144,128]{1,0:T(8,128)(2,1)S(1)} collective-permute-done((bf16[144,128]{1,0:T(8,128)(2,1)S(1)}, bf16[144,128]{1,0:T(8,128)(2,1)S(1)}, u32[]{:S(2)}, u32[]{:S(2)}) %collective-permute-start.4) | collective-permute-done | bytes 36896 | tf_op jit(solution)/shard_map/ppermute | solution.py:340
  6.6 1.9 %collective-permute-start.6 = (bf16[64,128]{1,0:T(8,128)(2,1)S(1)}, bf16[64,128]{1,0:T(8,128)(2,1)S(1)}, u32[]{:S(2)}, u32[]{:S(2)}) collective-permute-start(bf16[64,128]{1,0:T(8,128)(2,1)S(1)} %shard_map.92), channel_id=1, source_target_pairs={{0,16},{8,24},{16,0},{24,8},{1,17},{9,25},{17,1},{25,9},{2,18},{10... | collective-permute-start | bytes 49160 | tf_op jit(solution)/shard_map/ppermute | solution.py:337
  8.5 0.5 %shard_map.87 = (bf16[128,512]{1,0:T(8,128)(2,1)S(1)}, f32[128,512]{1,0:T(8,128)S(1)}) custom-call(bf16[512,128]{1,0:T(8,128)(2,1)S(1)} %get-tuple-element.34.q_ref, bf16[512,128]{1,0:T(8,128)(2,1)S(1)} %get-tuple-element.35.k_ref, bf16[128,512]{1,0:T(8,128)(2,1)S(1)} %get-tuple-element.36.value_t_ref, ...), custom_call_target="tpu_custom_call" | custom-call | bytes 1050624 | tf_op jit(solution)/shard_map/pallas_call | solution.py:318
  9.0 0.0 collective-permute-done.1.refs_1_
  9.0 0.1 collective-permute-start.2
  9.1 0.5 %collective-permute-start.5 = (bf16[512,128]{1,0:T(8,128)(2,1)S(1)}, bf16[512,128]{1,0:T(8,128)(2,1)S(1)}, u32[]{:S(2)}, u32[]{:S(2)}) collective-permute-start(bf16[512,128]{1,0:T(8,128)(2,1)S(1)} %get-tuple-element.43.pack_ref), channel_id=1, source_target_pairs={{0,8},{8,0},{16,24},{24,16},{1,9},{9,1},{17,25},{25,17},{2,10},{10... | collective-permute-start | bytes 393224 | tf_op jit(solution)/shard_map/ppermute | solution.py:340
  9.6 0.0 collective-permute-done.refs_0_
  9.6 0.5 %shard_map.89 = (bf16[1024,512]{1,0:T(8,128)(2,1)S(1)}, f32[1,512]{1,0:T(1,128)S(1)}, f32[1,512]{1,0:T(1,128)S(1)}, f32[1,512]{1,0:T(1,128)S(1)}) custom-call(bf16[128,512]{1,0:T(8,128)(2,1)S(1)} %get-tuple-element.45.qt_ref, f32[1,512]{1,0:T(1,128)S(1)} %get-tuple-element.46.top_ref, f32[1,512]{1,0:T(1,128)S(1)} %get-tuple-element.47.total_ref, ...), custom_call_target="tpu_custom_call" | custom-call | bytes 1452032 | tf_op jit(solution)/shard_map/pallas_call | solution.py:318
  10.1 0.4 %collective-permute-done.6.refs_9_ = bf16[64,128]{1,0:T(8,128)(2,1)S(1)} collective-permute-done((bf16[64,128]{1,0:T(8,128)(2,1)S(1)}, bf16[64,128]{1,0:T(8,128)(2,1)S(1)}, u32[]{:S(2)}, u32[]{:S(2)}) %collective-permute-start.6) | collective-permute-done | bytes 16416 | tf_op jit(solution)/shard_map/ppermute | solution.py:337
  10.5 0.0 collective-permute-done.3.refs_10_
  10.5 0.0 collective-permute-start.8
  10.5 0.5 %collective-permute-start.7 = (bf16[64,128]{1,0:T(8,128)(2,1)S(1)}, bf16[64,128]{1,0:T(8,128)(2,1)S(1)}, u32[]{:S(2)}, u32[]{:S(2)}) collective-permute-start(bf16[64,128]{1,0:T(8,128)(2,1)S(1)} %collective-permute-done.6.refs_9_), channel_id=1, source_target_pairs={{0,8},{8,0},{16,24},{24,16},{1,9},{9,1},{17,25},{25,17},{2,10},{10... | collective-permute-start | bytes 49160 | tf_op jit(solution)/shard_map/ppermute | solution.py:340
  11.0 0.0 collective-permute-done.2.refs_0_
  11.0 0.0 collective-permute-done.5.refs_9_
  11.0 1.1 %shard_map.91 = (bf16[512,128]{1,0:T(8,128)(2,1)}, bf16[512,128]{1,0:T(8,128)(2,1)}, f32[128,512]{1,0:T(8,128)S(1)}) custom-call(bf16[128,512]{1,0:T(8,128)(2,1)S(1)} %get-tuple-element.39.refs_0_.refs_2_, f32[128,512]{1,0:T(8,128)S(1)} %get-tuple-element.40.refs_1_.refs_3_, f32[1,512]{1,0:T(1,128)S(1)} %get-tuple-element.37.cum_row_ref.refs_2_.refs_4_, ...), custom_call_target="tpu_custom_call" | custom-call | bytes 2273280 | tf_op jit(solution)/shard_map/pallas_call | solution.py:318
  12.2 0.0 collective-permute-done.7.refs_10_
  12.2 0.0 collective-permute-done.8.refs_11_
  12.2 0.2 %shard_map.93 = (bf16[512,128]{1,0:T(8,128)(2,1)}, bf16[512,128]{1,0:T(8,128)(2,1)}) custom-call(bf16[512,128]{1,0:T(8,128)(2,1)} %get-tuple-element.57.refs_0_, bf16[512,128]{1,0:T(8,128)(2,1)} %get-tuple-element.58.refs_1_, bf16[128,512]{1,0:T(8,128)(2,1)S(1)} %get-tuple-element.39.refs_0_.refs_2_, ...), custom_call_target="tpu_custom_call", output_to_operand_aliasing={{0}: (0, {}), {1}: (1, {})} | custom-call | bytes 1384448 | tf_op jit(solution)/shard_map/pallas_call | solution.py:318
  (2 shorter events, 0.0 us)
Async XLA Ops:
  0.6 8.4 %collective-permute-start.1 = (bf16[512,128]{1,0:T(8,128)(2,1)}, bf16[512,128]{1,0:T(8,128)(2,1)S(1)}, u32[]{:S(2)}, u32[]{:S(2)}) collective-permute-start(bf16[512,128]{1,0:T(8,128)(2,1)} %bitcast.14), channel_id=1, source_target_pairs={{0,16},{8,24},{16,0},{24,8},{1,17},{9,25},{17,1},{25,9},{2,18},{10... | collective-permute-start | bytes 393224 | tf_op jit(solution)/shard_map/ppermute | solution.py:337
  3.6 6.0 %collective-permute-start = (bf16[512,128]{1,0:T(8,128)(2,1)}, bf16[512,128]{1,0:T(8,128)(2,1)S(1)}, u32[]{:S(2)}, u32[]{:S(2)}) collective-permute-start(bf16[512,128]{1,0:T(8,128)(2,1)} %bitcast.15), channel_id=1, source_target_pairs={{0,8},{8,0},{16,24},{24,16},{1,9},{9,1},{17,25},{25,17},{2,10},{10... | collective-permute-start | bytes 393224 | tf_op jit(solution)/shard_map/ppermute | solution.py:340
  3.6 6.9 %collective-permute-start.3 = (bf16[512,128]{1,0:T(8,128)(2,1)}, bf16[512,128]{1,0:T(8,128)(2,1)S(1)}, u32[]{:S(2)}, u32[]{:S(2)}) collective-permute-start(bf16[512,128]{1,0:T(8,128)(2,1)} %bitcast.17), channel_id=1, source_target_pairs={{0,16},{8,24},{16,0},{24,8},{1,17},{9,25},{17,1},{25,9},{2,18},{10... | collective-permute-start | bytes 393224 | tf_op jit(solution)/shard_map/ppermute | solution.py:337
  5.3 1.3 %collective-permute-start.4 = (bf16[144,128]{1,0:T(8,128)(2,1)S(1)}, bf16[144,128]{1,0:T(8,128)(2,1)S(1)}, u32[]{:S(2)}, u32[]{:S(2)}) collective-permute-start(bf16[144,128]{1,0:T(8,128)(2,1)S(1)} %get-tuple-element.55.refs_0_), channel_id=1, source_target_pairs={{0,8},{8,0},{16,24},{24,16},{1,9},{9,1},{17,25},{25,17},{2,10},{10... | collective-permute-start | bytes 110600 | tf_op jit(solution)/shard_map/ppermute | solution.py:340
  6.6 3.9 %collective-permute-start.6 = (bf16[64,128]{1,0:T(8,128)(2,1)S(1)}, bf16[64,128]{1,0:T(8,128)(2,1)S(1)}, u32[]{:S(2)}, u32[]{:S(2)}) collective-permute-start(bf16[64,128]{1,0:T(8,128)(2,1)S(1)} %shard_map.92), channel_id=1, source_target_pairs={{0,16},{8,24},{16,0},{24,8},{1,17},{9,25},{17,1},{25,9},{2,18},{10... | collective-permute-start | bytes 49160 | tf_op jit(solution)/shard_map/ppermute | solution.py:337
  9.0 2.0 %collective-permute-start.2 = (bf16[512,128]{1,0:T(8,128)(2,1)S(1)}, bf16[512,128]{1,0:T(8,128)(2,1)S(1)}, u32[]{:S(2)}, u32[]{:S(2)}) collective-permute-start(bf16[512,128]{1,0:T(8,128)(2,1)S(1)} %collective-permute-done.1.refs_1_), channel_id=1, source_target_pairs={{0,8},{8,0},{16,24},{24,16},{1,9},{9,1},{17,25},{25,17},{2,10},{10... | collective-permute-start | bytes 393224 | tf_op jit(solution)/shard_map/ppermute | solution.py:340
  9.1 1.9 %collective-permute-start.5 = (bf16[512,128]{1,0:T(8,128)(2,1)S(1)}, bf16[512,128]{1,0:T(8,128)(2,1)S(1)}, u32[]{:S(2)}, u32[]{:S(2)}) collective-permute-start(bf16[512,128]{1,0:T(8,128)(2,1)S(1)} %get-tuple-element.43.pack_ref), channel_id=1, source_target_pairs={{0,8},{8,0},{16,24},{24,16},{1,9},{9,1},{17,25},{25,17},{2,10},{10... | collective-permute-start | bytes 393224 | tf_op jit(solution)/shard_map/ppermute | solution.py:340
  10.5 1.7 %collective-permute-start.8 = (bf16[512,128]{1,0:T(8,128)(2,1)S(1)}, bf16[512,128]{1,0:T(8,128)(2,1)S(1)}, u32[]{:S(2)}, u32[]{:S(2)}) collective-permute-start(bf16[512,128]{1,0:T(8,128)(2,1)S(1)} %collective-permute-done.3.refs_10_), channel_id=1, source_target_pairs={{0,8},{8,0},{16,24},{24,16},{1,9},{9,1},{17,25},{25,17},{2,10},{10... | collective-permute-start | bytes 393224 | tf_op jit(solution)/shard_map/ppermute | solution.py:340
  10.5 1.7 %collective-permute-start.7 = (bf16[64,128]{1,0:T(8,128)(2,1)S(1)}, bf16[64,128]{1,0:T(8,128)(2,1)S(1)}, u32[]{:S(2)}, u32[]{:S(2)}) collective-permute-start(bf16[64,128]{1,0:T(8,128)(2,1)S(1)} %collective-permute-done.6.refs_9_), channel_id=1, source_target_pairs={{0,8},{8,0},{16,24},{24,16},{1,9},{9,1},{17,25},{25,17},{2,10},{10... | collective-permute-start | bytes 49160 | tf_op jit(solution)/shard_map/ppermute | solution.py:340

commit v18 on v16

--- a/solution.py
+++ b/solution.py
@@ -261,7 +261,7 @@
     @pl.when(position < cores)
     def _():
         write_out(
-            step, scaled, [side_by_side(ref, rows, width) for ref in values[:near_count]], probs_ref, sum_ref,
+            rows, scaled, [side_by_side(ref, rows, width) for ref in values[:near_count]], probs_ref, sum_ref,
             carried_state(position, cores, near_states, (), width),
             (lin_qt_ref, intra_ref, cum_row_ref), (linear_ref, softmax_ref), scratch, sems,
         )
@@ -280,7 +280,7 @@
     @pl.when(position >= cores)
     def _():
         write_out(
-            step, lambda mine: sofar_ref[:, mine], [jnp.transpose(ref[...]) for ref in values],
+            rows, lambda mine: sofar_ref[:, mine], [jnp.transpose(ref[...]) for ref in values],
             probs_ref, sum_ref, carried_state(position, cores, near_states, shares, width),
             (lin_qt_ref, intra_ref, cum_row_ref), (linear_ref, softmax_ref), scratch, sems,
         )

time: 12.4 us -> 12.4 us (level)
  no operation moved by 1% of the time
where the time goes in v18:
time: 12.4 us; the launch traced here: 12.2 us
  starting transfers between devices  6.59 us (53%)
  Pallas kernels  4.08 us (33%)
  waiting for transfers between devices  0.81 us (7%)
  between operations  0.71 us (6%)
    ppermute x3, starting transfers between devices, across(): lax.ppermute(x, axis, [(i, (i + apart * cores) % count) for i in range(co...  5.09 us
    pallas_call x8, Pallas kernels, call(): pl.pallas_call(body, out_shape=(*map(kept_in_hbm, written), *map(kept_in_...  4.08 us
    ppermute x6, starting transfers between devices, swapped(): return lax.ppermute(x, axis, [(i, i ^ 1) for i in range(count)])  1.5 us
    ppermute x3, waiting for transfers between devices, across(): lax.ppermute(x, axis, [(i, (i + apart * cores) % count) for i in range(co...  0.53 us
    ppermute x6, waiting for transfers between devices, swapped(): return lax.ppermute(x, axis, [(i, i ^ 1) for i in range(count)])  0.27 us
  transfers between devices with their start and end apart: 9, of which 2 were waited for; matrix products, arithmetic and copies ran while one was open for 0% of the time, Pallas kernels for 33%

profile of v18, /device:TPU:0, one launch (start us, length us, event | category | flops | bytes accessed | tf_op | source)
XLA Modules:
  0.0 12.2 jit_solution(12530188211051760768)
XLA Ops:
  0.6 3.0 %collective-permute-start.1 = (bf16[512,128]{1,0:T(8,128)(2,1)}, bf16[512,128]{1,0:T(8,128)(2,1)S(1)}, u32[]{:S(2)}, u32[]{:S(2)}) collective-permute-start(bf16[512,128]{1,0:T(8,128)(2,1)} %bitcast.14), channel_id=1, source_target_pairs={{0,16},{8,24},{16,0},{24,8},{1,17},{9,25},{17,1},{25,9},{2,18},{10... | collective-permute-start | bytes 393224 | tf_op jit(solution)/shard_map/ppermute | solution.py:330
  3.6 0.0 collective-permute-start
  3.6 0.2 %collective-permute-start.3 = (bf16[512,128]{1,0:T(8,128)(2,1)}, bf16[512,128]{1,0:T(8,128)(2,1)S(1)}, u32[]{:S(2)}, u32[]{:S(2)}) collective-permute-start(bf16[512,128]{1,0:T(8,128)(2,1)} %bitcast.17), channel_id=1, source_target_pairs={{0,16},{8,24},{16,0},{24,8},{1,17},{9,25},{17,1},{25,9},{2,18},{10... | collective-permute-start | bytes 393224 | tf_op jit(solution)/shard_map/ppermute | solution.py:330
  3.8 1.3 %shard_map.86 = (bf16[512,128]{1,0:T(8,128)(2,1)S(1)}, bf16[144,128]{1,0:T(8,128)(2,1)S(1)}, f32[1,512]{1,0:T(1,128)S(1)}, f32[512,128]{1,0:T(8,128)S(1)}, bf16[...) custom-call(f32[1,512]{1,0:T(1,128)} %decay_hbm.1, ...), custom_call_target="tpu_custom_call" | custom-call | bytes 1875968 | tf_op jit(solution)/shard_map/pallas_call | solution.py:311
  5.1 0.4 %collective-permute-start.4 = (bf16[144,128]{1,0:T(8,128)(2,1)S(1)}, bf16[144,128]{1,0:T(8,128)(2,1)S(1)}, u32[]{:S(2)}, u32[]{:S(2)}) collective-permute-start(bf16[144,128]{1,0:T(8,128)(2,1)S(1)} %get-tuple-element.55.refs_0_), channel_id=1, source_target_pairs={{0,8},{8,0},{16,24},{24,16},{1,9},{9,1},{17,25},{25,17},{2,10},{10... | collective-permute-start | bytes 110600 | tf_op jit(solution)/shard_map/ppermute | solution.py:333
  5.6 0.6 %shard_map.88 = (bf16[128,512]{1,0:T(8,128)(2,1)S(1)}, f32[1,512]{1,0:T(1,128)S(1)}, f32[1,512]{1,0:T(1,128)S(1)}, f32[128,512]{1,0:T(8,128)S(1)}) custom-call(bf16[512,128]{1,0:T(8,128)(2,1)S(1)} %get-tuple-element.41.q_ref, bf16[512,128]{1,0:T(8,128)(2,1)S(1)} %get-tuple-element.42.k_ref, bf16[512,128]{1,0:T(8,128)(2,1)S(1)} %get-tuple-element.43.pack_ref), custom_call_target="tpu_custom_call" | custom-call | bytes 790528 | tf_op jit(solution)/shard_map/pallas_call | solution.py:311
  6.2 0.3 %collective-permute-done.4.refs_8_.refs_1_ = bf16[144,128]{1,0:T(8,128)(2,1)S(1)} collective-permute-done((bf16[144,128]{1,0:T(8,128)(2,1)S(1)}, bf16[144,128]{1,0:T(8,128)(2,1)S(1)}, u32[]{:S(2)}, u32[]{:S(2)}) %collective-permute-start.4) | collective-permute-done | bytes 36896 | tf_op jit(solution)/shard_map/ppermute | solution.py:333
  6.5 1.9 %collective-permute-start.6 = (bf16[64,128]{1,0:T(8,128)(2,1)S(1)}, bf16[64,128]{1,0:T(8,128)(2,1)S(1)}, u32[]{:S(2)}, u32[]{:S(2)}) collective-permute-start(bf16[64,128]{1,0:T(8,128)(2,1)S(1)} %shard_map.92), channel_id=1, source_target_pairs={{0,16},{8,24},{16,0},{24,8},{1,17},{9,25},{17,1},{25,9},{2,18},{10... | collective-permute-start | bytes 49160 | tf_op jit(solution)/shard_map/ppermute | solution.py:330
  8.4 0.5 %shard_map.87 = (bf16[128,512]{1,0:T(8,128)(2,1)S(1)}, f32[128,512]{1,0:T(8,128)S(1)}) custom-call(bf16[512,128]{1,0:T(8,128)(2,1)S(1)} %get-tuple-element.34.q_ref, bf16[512,128]{1,0:T(8,128)(2,1)S(1)} %get-tuple-element.35.k_ref, bf16[128,512]{1,0:T(8,128)(2,1)S(1)} %get-tuple-element.36.value_t_ref, ...), custom_call_target="tpu_custom_call" | custom-call | bytes 1050624 | tf_op jit(solution)/shard_map/pallas_call | solution.py:311
  8.9 0.0 collective-permute-done.1.refs_1_
  8.9 0.1 collective-permute-start.2
  9.0 0.5 %collective-permute-start.5 = (bf16[512,128]{1,0:T(8,128)(2,1)S(1)}, bf16[512,128]{1,0:T(8,128)(2,1)S(1)}, u32[]{:S(2)}, u32[]{:S(2)}) collective-permute-start(bf16[512,128]{1,0:T(8,128)(2,1)S(1)} %get-tuple-element.43.pack_ref), channel_id=1, source_target_pairs={{0,8},{8,0},{16,24},{24,16},{1,9},{9,1},{17,25},{25,17},{2,10},{10... | collective-permute-start | bytes 393224 | tf_op jit(solution)/shard_map/ppermute | solution.py:333
  9.5 0.0 collective-permute-done.refs_0_
  9.5 0.5 %shard_map.89 = (bf16[1024,512]{1,0:T(8,128)(2,1)S(1)}, f32[1,512]{1,0:T(1,128)S(1)}, f32[1,512]{1,0:T(1,128)S(1)}, f32[1,512]{1,0:T(1,128)S(1)}) custom-call(bf16[128,512]{1,0:T(8,128)(2,1)S(1)} %get-tuple-element.45.qt_ref, f32[1,512]{1,0:T(1,128)S(1)} %get-tuple-element.46.top_ref, f32[1,512]{1,0:T(1,128)S(1)} %get-tuple-element.47.total_ref, ...), custom_call_target="tpu_custom_call" | custom-call | bytes 1452032 | tf_op jit(solution)/shard_map/pallas_call | solution.py:311
  10.0 0.5 %collective-permute-done.6.refs_9_ = bf16[64,128]{1,0:T(8,128)(2,1)S(1)} collective-permute-done((bf16[64,128]{1,0:T(8,128)(2,1)S(1)}, bf16[64,128]{1,0:T(8,128)(2,1)S(1)}, u32[]{:S(2)}, u32[]{:S(2)}) %collective-permute-start.6) | collective-permute-done | bytes 16416 | tf_op jit(solution)/shard_map/ppermute | solution.py:330
  10.5 0.0 collective-permute-done.3.refs_10_
  10.5 0.0 collective-permute-start.8
  10.5 0.5 %collective-permute-start.7 = (bf16[64,128]{1,0:T(8,128)(2,1)S(1)}, bf16[64,128]{1,0:T(8,128)(2,1)S(1)}, u32[]{:S(2)}, u32[]{:S(2)}) collective-permute-start(bf16[64,128]{1,0:T(8,128)(2,1)S(1)} %collective-permute-done.6.refs_9_), channel_id=1, source_target_pairs={{0,8},{8,0},{16,24},{24,16},{1,9},{9,1},{17,25},{25,17},{2,10},{10... | collective-permute-start | bytes 49160 | tf_op jit(solution)/shard_map/ppermute | solution.py:333
  11.0 0.0 collective-permute-done.2.refs_0_
  11.0 0.0 collective-permute-done.5.refs_9_
  11.0 1.1 %shard_map.91 = (bf16[512,128]{1,0:T(8,128)(2,1)}, bf16[512,128]{1,0:T(8,128)(2,1)}, f32[128,512]{1,0:T(8,128)S(1)}) custom-call(bf16[128,512]{1,0:T(8,128)(2,1)S(1)} %get-tuple-element.39.refs_0_.refs_2_, f32[128,512]{1,0:T(8,128)S(1)} %get-tuple-element.40.refs_1_.refs_3_, f32[1,512]{1,0:T(1,128)S(1)} %get-tuple-element.37.cum_row_ref.refs_2_.refs_4_, ...), custom_call_target="tpu_custom_call" | custom-call | bytes 2273280 | tf_op jit(solution)/shard_map/pallas_call | solution.py:311
  12.1 0.0 collective-permute-done.7.refs_10_
  12.1 0.0 collective-permute-done.8.refs_11_
  12.1 0.1 shard_map.93
  (2 shorter events, 0.0 us)
Async XLA Ops:
  0.6 8.3 %collective-permute-start.1 = (bf16[512,128]{1,0:T(8,128)(2,1)}, bf16[512,128]{1,0:T(8,128)(2,1)S(1)}, u32[]{:S(2)}, u32[]{:S(2)}) collective-permute-start(bf16[512,128]{1,0:T(8,128)(2,1)} %bitcast.14), channel_id=1, source_target_pairs={{0,16},{8,24},{16,0},{24,8},{1,17},{9,25},{17,1},{25,9},{2,18},{10... | collective-permute-start | bytes 393224 | tf_op jit(solution)/shard_map/ppermute | solution.py:330
  3.6 5.8 %collective-permute-start = (bf16[512,128]{1,0:T(8,128)(2,1)}, bf16[512,128]{1,0:T(8,128)(2,1)S(1)}, u32[]{:S(2)}, u32[]{:S(2)}) collective-permute-start(bf16[512,128]{1,0:T(8,128)(2,1)} %bitcast.15), channel_id=1, source_target_pairs={{0,8},{8,0},{16,24},{24,16},{1,9},{9,1},{17,25},{25,17},{2,10},{10... | collective-permute-start | bytes 393224 | tf_op jit(solution)/shard_map/ppermute | solution.py:333
  3.6 6.9 %collective-permute-start.3 = (bf16[512,128]{1,0:T(8,128)(2,1)}, bf16[512,128]{1,0:T(8,128)(2,1)S(1)}, u32[]{:S(2)}, u32[]{:S(2)}) collective-permute-start(bf16[512,128]{1,0:T(8,128)(2,1)} %bitcast.17), channel_id=1, source_target_pairs={{0,16},{8,24},{16,0},{24,8},{1,17},{9,25},{17,1},{25,9},{2,18},{10... | collective-permute-start | bytes 393224 | tf_op jit(solution)/shard_map/ppermute | solution.py:330
  5.1 1.3 %collective-permute-start.4 = (bf16[144,128]{1,0:T(8,128)(2,1)S(1)}, bf16[144,128]{1,0:T(8,128)(2,1)S(1)}, u32[]{:S(2)}, u32[]{:S(2)}) collective-permute-start(bf16[144,128]{1,0:T(8,128)(2,1)S(1)} %get-tuple-element.55.refs_0_), channel_id=1, source_target_pairs={{0,8},{8,0},{16,24},{24,16},{1,9},{9,1},{17,25},{25,17},{2,10},{10... | collective-permute-start | bytes 110600 | tf_op jit(solution)/shard_map/ppermute | solution.py:333
  6.5 4.0 %collective-permute-start.6 = (bf16[64,128]{1,0:T(8,128)(2,1)S(1)}, bf16[64,128]{1,0:T(8,128)(2,1)S(1)}, u32[]{:S(2)}, u32[]{:S(2)}) collective-permute-start(bf16[64,128]{1,0:T(8,128)(2,1)S(1)} %shard_map.92), channel_id=1, source_target_pairs={{0,16},{8,24},{16,0},{24,8},{1,17},{9,25},{17,1},{25,9},{2,18},{10... | collective-permute-start | bytes 49160 | tf_op jit(solution)/shard_map/ppermute | solution.py:330
  8.9 2.1 %collective-permute-start.2 = (bf16[512,128]{1,0:T(8,128)(2,1)S(1)}, bf16[512,128]{1,0:T(8,128)(2,1)S(1)}, u32[]{:S(2)}, u32[]{:S(2)}) collective-permute-start(bf16[512,128]{1,0:T(8,128)(2,1)S(1)} %collective-permute-done.1.refs_1_), channel_id=1, source_target_pairs={{0,8},{8,0},{16,24},{24,16},{1,9},{9,1},{17,25},{25,17},{2,10},{10... | collective-permute-start | bytes 393224 | tf_op jit(solution)/shard_map/ppermute | solution.py:333
  9.0 2.1 %collective-permute-start.5 = (bf16[512,128]{1,0:T(8,128)(2,1)S(1)}, bf16[512,128]{1,0:T(8,128)(2,1)S(1)}, u32[]{:S(2)}, u32[]{:S(2)}) collective-permute-start(bf16[512,128]{1,0:T(8,128)(2,1)S(1)} %get-tuple-element.43.pack_ref), channel_id=1, source_target_pairs={{0,8},{8,0},{16,24},{24,16},{1,9},{9,1},{17,25},{25,17},{2,10},{10... | collective-permute-start | bytes 393224 | tf_op jit(solution)/shard_map/ppermute | solution.py:333
  10.5 1.6 %collective-permute-start.8 = (bf16[512,128]{1,0:T(8,128)(2,1)S(1)}, bf16[512,128]{1,0:T(8,128)(2,1)S(1)}, u32[]{:S(2)}, u32[]{:S(2)}) collective-permute-start(bf16[512,128]{1,0:T(8,128)(2,1)S(1)} %collective-permute-done.3.refs_10_), channel_id=1, source_target_pairs={{0,8},{8,0},{16,24},{24,16},{1,9},{9,1},{17,25},{25,17},{2,10},{10... | collective-permute-start | bytes 393224 | tf_op jit(solution)/shard_map/ppermute | solution.py:333
  10.5 1.6 %collective-permute-start.7 = (bf16[64,128]{1,0:T(8,128)(2,1)S(1)}, bf16[64,128]{1,0:T(8,128)(2,1)S(1)}, u32[]{:S(2)}, u32[]{:S(2)}) collective-permute-start(bf16[64,128]{1,0:T(8,128)(2,1)S(1)} %collective-permute-done.6.refs_9_), channel_id=1, source_target_pairs={{0,8},{8,0},{16,24},{24,16},{1,9},{9,1},{17,25},{25,17},{2,10},{10... | collective-permute-start | bytes 49160 | tf_op jit(solution)/shard_map/ppermute | solution.py:333

commit v19 on v18

--- a/solution.py
+++ b/solution.py
@@ -49,8 +49,8 @@
 
 def state_kernel(
     decay_hbm, key_hbm, value_hbm, soft_value_hbm, query_hbm, soft_query_hbm, soft_key_hbm,
-    soft_vt_ref, state_ref, cum_row_ref, cum_col_ref, value_t_ref, key_ref, query_ref, soft_query_ref, soft_key_ref,
-    decay_ref, value_ref, soft_value_ref, sems,
+    soft_value_ref, state_ref, cum_row_ref, cum_col_ref, value_t_ref, key_ref, query_ref, soft_query_ref, soft_key_ref,
+    decay_ref, value_ref, sems,
 ):
     copies = [
         pltpu.make_async_copy(source, target, sems.at[place])
@@ -77,16 +77,14 @@
     cum_col = jnp.transpose(jnp.broadcast_to(cum_row, (width, rows)))
     cum_col_ref[...] = cum_col
     total = cum_col[rows - 1 :, :]
-    for copy in copies[1:4]:
+    for copy in copies[1:3]:
         copy.wait()
     decayed = (key_ref[...].astype(F32) * jnp.exp(total - cum_col)).astype(BF16)
     value_t = jnp.transpose(value_ref[...])
     value_t_ref[...] = value_t
     state_ref[:width, :] = dot(value_t, decayed).astype(BF16)
     state_ref[width:, :] = select_rows(three_parts(total), PAD, width)
-    for left in range(0, rows, width):
-        soft_vt_ref[left : left + width, :] = jnp.transpose(soft_value_ref[left : left + width, :])
-    for copy in copies[4:]:
+    for copy in copies[3:]:
         copy.wait()
 
 
@@ -113,10 +111,12 @@
         share_ref[share:, :] = select_rows(three_parts(total), PAD, width)
 
 
-def soft_kernel(scale, step, q_ref, k_ref, pack_ref, qt_ref, top_ref, total_ref, summed_ref):
+def soft_kernel(scale, step, q_ref, k_ref, v_ref, soft_vt_ref, qt_ref, top_ref, total_ref, summed_ref):
     rows, width = q_ref.shape
     qt_ref[...] = jnp.transpose(q_ref[...])
-    value_t = side_by_side(pack_ref, rows, width)
+    value_t = jnp.transpose(v_ref[...])
+    for left in range(0, rows, width):
+        soft_vt_ref[left : left + width, :] = value_t[:, left : left + width]
     keep = iota((step, step), 0) <= iota((step, step), 1)
     for start in range(0, rows, step):
         stop = start + step
@@ -353,17 +353,18 @@
 
         row, flat, flat16, block = shape(1, rows), shape(width, rows), half(width, rows), half(rows, width)
         keys, values = far(sk), far(sv)
-        soft_vt, state, cum_row, cum_col, lin_vt, lk, lq, sq, own_keys = call(
+        own_values, state, cum_row, cum_col, lin_vt, lk, lq, sq, own_keys = call(
             state_kernel,
             (),
             (block, half(width + PAD, width), row, shape(rows, width), flat16, block, block, block, block),
             given=(decay, lk, lv, sv, lq, sq, sk),
-            scratch=(row, block, block),
-        )
-        near_states, near_values = near([state]), near([soft_vt])
-        qt, top, total, summed = call(
-            functools.partial(soft_kernel, scale, step), (sq, own_keys, soft_vt), (flat16, row, row, flat)
-        )
+            scratch=(row, block),
+        )
+        near_states = near([state])
+        soft_vt, qt, top, total, summed = call(
+            functools.partial(soft_kernel, scale, step), (sq, own_keys, own_values), (block, flat16, row, row, flat)
+        )
+        near_values = near([soft_vt])
         near_states, _ = lax.optimization_barrier((near_states, summed))
         (share,) = call(
             functools.partial(combine_kernel, axis, cores),

time: 12.4 us -> 12.4 us (level)
  transfers between devices with their start and end apart: 9 -> 9, of which waited for: 2 -> 2; matrix products, arithmetic and copies ran while one was open for 0% -> 0% of each run, Pallas kernels for 33% -> 32%
where the time goes in v19:
time: 12.4 us; the launch traced here: 12.2 us
  starting transfers between devices  6.59 us (53%)
  Pallas kernels  4 us (32%)
  waiting for transfers between devices  0.88 us (7%)
  between operations  0.71 us (6%)
    ppermute x3, starting transfers between devices, across(): lax.ppermute(x, axis, [(i, (i + apart * cores) % count) for i in range(co...  5.09 us
    pallas_call x8, Pallas kernels, call(): pl.pallas_call(body, out_shape=(*map(kept_in_hbm, written), *map(kept_in_...  4 us
    ppermute x6, starting transfers between devices, swapped(): return lax.ppermute(x, axis, [(i, i ^ 1) for i in range(count)])  1.5 us
    ppermute x3, waiting for transfers between devices, across(): lax.ppermute(x, axis, [(i, (i + apart * cores) % count) for i in range(co...  0.61 us
    ppermute x6, waiting for transfers between devices, swapped(): return lax.ppermute(x, axis, [(i, i ^ 1) for i in range(count)])  0.27 us
  transfers between devices with their start and end apart: 9, of which 2 were waited for; matrix products, arithmetic and copies ran while one was open for 0% of the time, Pallas kernels for 32%

profile of v19, /device:TPU:0, one launch (start us, length us, event | category | flops | bytes accessed | tf_op | source)
XLA Modules:
  0.0 12.2 jit_solution(9797268072145279866)
XLA Ops:
  0.6 3.0 %collective-permute-start.1 = (bf16[512,128]{1,0:T(8,128)(2,1)}, bf16[512,128]{1,0:T(8,128)(2,1)S(1)}, u32[]{:S(2)}, u32[]{:S(2)}) collective-permute-start(bf16[512,128]{1,0:T(8,128)(2,1)} %bitcast.14), channel_id=1, source_target_pairs={{0,16},{8,24},{16,0},{24,8},{1,17},{9,25},{17,1},{25,9},{2,18},{10... | collective-permute-start | bytes 393224 | tf_op jit(solution)/shard_map/ppermute | solution.py:330
  3.6 0.0 collective-permute-start
  3.6 0.2 %collective-permute-start.3 = (bf16[512,128]{1,0:T(8,128)(2,1)}, bf16[512,128]{1,0:T(8,128)(2,1)S(1)}, u32[]{:S(2)}, u32[]{:S(2)}) collective-permute-start(bf16[512,128]{1,0:T(8,128)(2,1)} %bitcast.17), channel_id=1, source_target_pairs={{0,16},{8,24},{16,0},{24,8},{1,17},{9,25},{17,1},{25,9},{2,18},{10... | collective-permute-start | bytes 393224 | tf_op jit(solution)/shard_map/ppermute | solution.py:330
  3.8 1.3 %shard_map.86 = (bf16[512,128]{1,0:T(8,128)(2,1)S(1)}, bf16[144,128]{1,0:T(8,128)(2,1)S(1)}, f32[1,512]{1,0:T(1,128)S(1)}, f32[512,128]{1,0:T(8,128)S(1)}, bf16[...) custom-call(f32[1,512]{1,0:T(1,128)} %decay_hbm.1, ...), custom_call_target="tpu_custom_call" | custom-call | bytes 1875968 | tf_op jit(solution)/shard_map/pallas_call | solution.py:311
  5.1 0.4 %collective-permute-start.4 = (bf16[144,128]{1,0:T(8,128)(2,1)S(1)}, bf16[144,128]{1,0:T(8,128)(2,1)S(1)}, u32[]{:S(2)}, u32[]{:S(2)}) collective-permute-start(bf16[144,128]{1,0:T(8,128)(2,1)S(1)} %get-tuple-element.56.refs_0_), channel_id=1, source_target_pairs={{0,8},{8,0},{16,24},{24,16},{1,9},{9,1},{17,25},{25,17},{2,10},{10... | collective-permute-start | bytes 110600 | tf_op jit(solution)/shard_map/ppermute | solution.py:333
  5.5 0.6 %shard_map.88 = (bf16[512,128]{1,0:T(8,128)(2,1)S(1)}, bf16[128,512]{1,0:T(8,128)(2,1)S(1)}, f32[1,512]{1,0:T(1,128)S(1)}, f32[1,512]{1,0:T(1,128)S(1)}, f32[128,512]{1,0:T(8,128)S(1)}) custom-call(bf16[512,128]{1,0:T(8,128)(2,1)S(1)} %get-tuple-element.42.q_ref, bf16[512,128]{1,0:T(8,128)(2,1)S(1)} %get-tuple-element.43.k_ref, ...), custom_call_target="tpu_custom_call" | custom-call | bytes 921600 | tf_op jit(solution)/shard_map/pallas_call | solution.py:311
  6.1 0.3 %collective-permute-done.4.refs_8_.refs_1_ = bf16[144,128]{1,0:T(8,128)(2,1)S(1)} collective-permute-done((bf16[144,128]{1,0:T(8,128)(2,1)S(1)}, bf16[144,128]{1,0:T(8,128)(2,1)S(1)}, u32[]{:S(2)}, u32[]{:S(2)}) %collective-permute-start.4) | collective-permute-done | bytes 36896 | tf_op jit(solution)/shard_map/ppermute | solution.py:333
  6.4 1.9 %collective-permute-start.6 = (bf16[64,128]{1,0:T(8,128)(2,1)S(1)}, bf16[64,128]{1,0:T(8,128)(2,1)S(1)}, u32[]{:S(2)}, u32[]{:S(2)}) collective-permute-start(bf16[64,128]{1,0:T(8,128)(2,1)S(1)} %shard_map.92), channel_id=1, source_target_pairs={{0,16},{8,24},{16,0},{24,8},{1,17},{9,25},{17,1},{25,9},{2,18},{10... | collective-permute-start | bytes 49160 | tf_op jit(solution)/shard_map/ppermute | solution.py:330
  8.3 0.5 %shard_map.87 = (bf16[128,512]{1,0:T(8,128)(2,1)S(1)}, f32[128,512]{1,0:T(8,128)S(1)}) custom-call(bf16[512,128]{1,0:T(8,128)(2,1)S(1)} %get-tuple-element.35.q_ref, bf16[512,128]{1,0:T(8,128)(2,1)S(1)} %get-tuple-element.36.k_ref, bf16[128,512]{1,0:T(8,128)(2,1)S(1)} %get-tuple-element.37.value_t_ref, ...), custom_call_target="tpu_custom_call" | custom-call | bytes 1050624 | tf_op jit(solution)/shard_map/pallas_call | solution.py:311
  8.8 0.0 collective-permute-done.1.refs_1_
  8.8 0.1 collective-permute-start.2
  8.9 0.5 %collective-permute-start.5 = (bf16[512,128]{1,0:T(8,128)(2,1)S(1)}, bf16[512,128]{1,0:T(8,128)(2,1)S(1)}, u32[]{:S(2)}, u32[]{:S(2)}) collective-permute-start(bf16[512,128]{1,0:T(8,128)(2,1)S(1)} %get-tuple-element.58), channel_id=1, source_target_pairs={{0,8},{8,0},{16,24},{24,16},{1,9},{9,1},{17,25},{25,17},{2,10},{10... | collective-permute-start | bytes 393224 | tf_op jit(solution)/shard_map/ppermute | solution.py:333
  9.4 0.0 collective-permute-done.refs_0_
  9.4 0.5 %shard_map.89 = (bf16[1024,512]{1,0:T(8,128)(2,1)S(1)}, f32[1,512]{1,0:T(1,128)S(1)}, f32[1,512]{1,0:T(1,128)S(1)}, f32[1,512]{1,0:T(1,128)S(1)}) custom-call(bf16[128,512]{1,0:T(8,128)(2,1)S(1)} %get-tuple-element.46.qt_ref, f32[1,512]{1,0:T(1,128)S(1)} %get-tuple-element.47.top_ref, f32[1,512]{1,0:T(1,128)S(1)} %get-tuple-element.48.total_ref, ...), custom_call_target="tpu_custom_call" | custom-call | bytes 1452032 | tf_op jit(solution)/shard_map/pallas_call | solution.py:311
  9.9 0.6 %collective-permute-done.6.refs_9_ = bf16[64,128]{1,0:T(8,128)(2,1)S(1)} collective-permute-done((bf16[64,128]{1,0:T(8,128)(2,1)S(1)}, bf16[64,128]{1,0:T(8,128)(2,1)S(1)}, u32[]{:S(2)}, u32[]{:S(2)}) %collective-permute-start.6) | collective-permute-done | bytes 16416 | tf_op jit(solution)/shard_map/ppermute | solution.py:330
  10.5 0.0 collective-permute-done.3.refs_10_
  10.5 0.0 collective-permute-start.8
  10.5 0.5 %collective-permute-start.7 = (bf16[64,128]{1,0:T(8,128)(2,1)S(1)}, bf16[64,128]{1,0:T(8,128)(2,1)S(1)}, u32[]{:S(2)}, u32[]{:S(2)}) collective-permute-start(bf16[64,128]{1,0:T(8,128)(2,1)S(1)} %collective-permute-done.6.refs_9_), channel_id=1, source_target_pairs={{0,8},{8,0},{16,24},{24,16},{1,9},{9,1},{17,25},{25,17},{2,10},{10... | collective-permute-start | bytes 49160 | tf_op jit(solution)/shard_map/ppermute | solution.py:333
  11.0 0.0 collective-permute-done.2.refs_0_
  11.0 0.0 collective-permute-done.5.refs_9_
  11.0 1.1 %shard_map.91 = (bf16[512,128]{1,0:T(8,128)(2,1)}, bf16[512,128]{1,0:T(8,128)(2,1)}, f32[128,512]{1,0:T(8,128)S(1)}) custom-call(bf16[128,512]{1,0:T(8,128)(2,1)S(1)} %get-tuple-element.40.refs_0_.refs_2_, f32[128,512]{1,0:T(8,128)S(1)} %get-tuple-element.41.refs_1_.refs_3_, f32[1,512]{1,0:T(1,128)S(1)} %get-tuple-element.38.cum_row_ref.refs_2_.refs_4_, ...), custom_call_target="tpu_custom_call" | custom-call | bytes 2273280 | tf_op jit(solution)/shard_map/pallas_call | solution.py:311
  12.1 0.0 collective-permute-done.7.refs_10_
  12.1 0.0 collective-permute-done.8.refs_11_
  12.1 0.1 shard_map.93
  (2 shorter events, 0.0 us)
Async XLA Ops:
  0.6 8.2 %collective-permute-start.1 = (bf16[512,128]{1,0:T(8,128)(2,1)}, bf16[512,128]{1,0:T(8,128)(2,1)S(1)}, u32[]{:S(2)}, u32[]{:S(2)}) collective-permute-start(bf16[512,128]{1,0:T(8,128)(2,1)} %bitcast.14), channel_id=1, source_target_pairs={{0,16},{8,24},{16,0},{24,8},{1,17},{9,25},{17,1},{25,9},{2,18},{10... | collective-permute-start | bytes 393224 | tf_op jit(solution)/shard_map/ppermute | solution.py:330
  3.6 5.8 %collective-permute-start = (bf16[512,128]{1,0:T(8,128)(2,1)}, bf16[512,128]{1,0:T(8,128)(2,1)S(1)}, u32[]{:S(2)}, u32[]{:S(2)}) collective-permute-start(bf16[512,128]{1,0:T(8,128)(2,1)} %bitcast.15), channel_id=1, source_target_pairs={{0,8},{8,0},{16,24},{24,16},{1,9},{9,1},{17,25},{25,17},{2,10},{10... | collective-permute-start | bytes 393224 | tf_op jit(solution)/shard_map/ppermute | solution.py:333
  3.6 6.9 %collective-permute-start.3 = (bf16[512,128]{1,0:T(8,128)(2,1)}, bf16[512,128]{1,0:T(8,128)(2,1)S(1)}, u32[]{:S(2)}, u32[]{:S(2)}) collective-permute-start(bf16[512,128]{1,0:T(8,128)(2,1)} %bitcast.17), channel_id=1, source_target_pairs={{0,16},{8,24},{16,0},{24,8},{1,17},{9,25},{17,1},{25,9},{2,18},{10... | collective-permute-start | bytes 393224 | tf_op jit(solution)/shard_map/ppermute | solution.py:330
  5.1 1.3 %collective-permute-start.4 = (bf16[144,128]{1,0:T(8,128)(2,1)S(1)}, bf16[144,128]{1,0:T(8,128)(2,1)S(1)}, u32[]{:S(2)}, u32[]{:S(2)}) collective-permute-start(bf16[144,128]{1,0:T(8,128)(2,1)S(1)} %get-tuple-element.56.refs_0_), channel_id=1, source_target_pairs={{0,8},{8,0},{16,24},{24,16},{1,9},{9,1},{17,25},{25,17},{2,10},{10... | collective-permute-start | bytes 110600 | tf_op jit(solution)/shard_map/ppermute | solution.py:333
  6.4 4.1 %collective-permute-start.6 = (bf16[64,128]{1,0:T(8,128)(2,1)S(1)}, bf16[64,128]{1,0:T(8,128)(2,1)S(1)}, u32[]{:S(2)}, u32[]{:S(2)}) collective-permute-start(bf16[64,128]{1,0:T(8,128)(2,1)S(1)} %shard_map.92), channel_id=1, source_target_pairs={{0,16},{8,24},{16,0},{24,8},{1,17},{9,25},{17,1},{25,9},{2,18},{10... | collective-permute-start | bytes 49160 | tf_op jit(solution)/shard_map/ppermute | solution.py:330
  8.8 2.2 %collective-permute-start.2 = (bf16[512,128]{1,0:T(8,128)(2,1)S(1)}, bf16[512,128]{1,0:T(8,128)(2,1)S(1)}, u32[]{:S(2)}, u32[]{:S(2)}) collective-permute-start(bf16[512,128]{1,0:T(8,128)(2,1)S(1)} %collective-permute-done.1.refs_1_), channel_id=1, source_target_pairs={{0,8},{8,0},{16,24},{24,16},{1,9},{9,1},{17,25},{25,17},{2,10},{10... | collective-permute-start | bytes 393224 | tf_op jit(solution)/shard_map/ppermute | solution.py:333
  8.9 2.1 %collective-permute-start.5 = (bf16[512,128]{1,0:T(8,128)(2,1)S(1)}, bf16[512,128]{1,0:T(8,128)(2,1)S(1)}, u32[]{:S(2)}, u32[]{:S(2)}) collective-permute-start(bf16[512,128]{1,0:T(8,128)(2,1)S(1)} %get-tuple-element.58), channel_id=1, source_target_pairs={{0,8},{8,0},{16,24},{24,16},{1,9},{9,1},{17,25},{25,17},{2,10},{10... | collective-permute-start | bytes 393224 | tf_op jit(solution)/shard_map/ppermute | solution.py:333
  10.5 1.6 %collective-permute-start.8 = (bf16[512,128]{1,0:T(8,128)(2,1)S(1)}, bf16[512,128]{1,0:T(8,128)(2,1)S(1)}, u32[]{:S(2)}, u32[]{:S(2)}) collective-permute-start(bf16[512,128]{1,0:T(8,128)(2,1)S(1)} %collective-permute-done.3.refs_10_), channel_id=1, source_target_pairs={{0,8},{8,0},{16,24},{24,16},{1,9},{9,1},{17,25},{25,17},{2,10},{10... | collective-permute-start | bytes 393224 | tf_op jit(solution)/shard_map/ppermute | solution.py:333
  10.5 1.6 %collective-permute-start.7 = (bf16[64,128]{1,0:T(8,128)(2,1)S(1)}, bf16[64,128]{1,0:T(8,128)(2,1)S(1)}, u32[]{:S(2)}, u32[]{:S(2)}) collective-permute-start(bf16[64,128]{1,0:T(8,128)(2,1)S(1)} %collective-permute-done.6.refs_9_), channel_id=1, source_target_pairs={{0,8},{8,0},{16,24},{24,16},{1,9},{9,1},{17,25},{25,17},{2,10},{10... | collective-permute-start | bytes 49160 | tf_op jit(solution)/shard_map/ppermute | solution.py:333

commit v20 on v19

--- a/solution.py
+++ b/solution.py
@@ -261,7 +261,7 @@
     @pl.when(position < cores)
     def _():
         write_out(
-            rows, scaled, [side_by_side(ref, rows, width) for ref in values[:near_count]], probs_ref, sum_ref,
+            step, scaled, [side_by_side(ref, rows, width) for ref in values[:near_count]], probs_ref, sum_ref,
             carried_state(position, cores, near_states, (), width),
             (lin_qt_ref, intra_ref, cum_row_ref), (linear_ref, softmax_ref), scratch, sems,
         )
@@ -280,7 +280,7 @@
     @pl.when(position >= cores)
     def _():
         write_out(
-            rows, lambda mine: sofar_ref[:, mine], [jnp.transpose(ref[...]) for ref in values],
+            step, lambda mine: sofar_ref[:, mine], [jnp.transpose(ref[...]) for ref in values],
             probs_ref, sum_ref, carried_state(position, cores, near_states, shares, width),
             (lin_qt_ref, intra_ref, cum_row_ref), (linear_ref, softmax_ref), scratch, sems,
         )

time: 12.4 us -> 12.4 us (level)
  no operation moved by 1% of the time
where the time goes in v20:
time: 12.4 us; the launch traced here: 12.2 us
  starting transfers between devices  6.59 us (53%)
  Pallas kernels  3.99 us (32%)
  waiting for transfers between devices  0.88 us (7%)
  between operations  0.71 us (6%)
    ppermute x3, starting transfers between devices, across(): lax.ppermute(x, axis, [(i, (i + apart * cores) % count) for i in range(co...  5.09 us
    pallas_call x8, Pallas kernels, call(): pl.pallas_call(body, out_shape=(*map(kept_in_hbm, written), *map(kept_in_...  3.99 us
    ppermute x6, starting transfers between devices, swapped(): return lax.ppermute(x, axis, [(i, i ^ 1) for i in range(count)])  1.5 us
    ppermute x3, waiting for transfers between devices, across(): lax.ppermute(x, axis, [(i, (i + apart * cores) % count) for i in range(co...  0.61 us
    ppermute x6, waiting for transfers between devices, swapped(): return lax.ppermute(x, axis, [(i, i ^ 1) for i in range(count)])  0.27 us
  transfers between devices with their start and end apart: 9, of which 2 were waited for; matrix products, arithmetic and copies ran while one was open for 0% of the time, Pallas kernels for 32%

profile of v20, /device:TPU:0, one launch (start us, length us, event | category | flops | bytes accessed | tf_op | source)
XLA Modules:
  0.0 12.2 jit_solution(597888061715963404)
XLA Ops:
  0.6 3.0 %collective-permute-start.1 = (bf16[512,128]{1,0:T(8,128)(2,1)}, bf16[512,128]{1,0:T(8,128)(2,1)S(1)}, u32[]{:S(2)}, u32[]{:S(2)}) collective-permute-start(bf16[512,128]{1,0:T(8,128)(2,1)} %bitcast.14), channel_id=1, source_target_pairs={{0,16},{8,24},{16,0},{24,8},{1,17},{9,25},{17,1},{25,9},{2,18},{10... | collective-permute-start | bytes 393224 | tf_op jit(solution)/shard_map/ppermute | solution.py:330
  3.6 0.0 collective-permute-start
  3.6 0.2 %collective-permute-start.3 = (bf16[512,128]{1,0:T(8,128)(2,1)}, bf16[512,128]{1,0:T(8,128)(2,1)S(1)}, u32[]{:S(2)}, u32[]{:S(2)}) collective-permute-start(bf16[512,128]{1,0:T(8,128)(2,1)} %bitcast.17), channel_id=1, source_target_pairs={{0,16},{8,24},{16,0},{24,8},{1,17},{9,25},{17,1},{25,9},{2,18},{10... | collective-permute-start | bytes 393224 | tf_op jit(solution)/shard_map/ppermute | solution.py:330
  3.8 1.3 %shard_map.86 = (bf16[512,128]{1,0:T(8,128)(2,1)S(1)}, bf16[144,128]{1,0:T(8,128)(2,1)S(1)}, f32[1,512]{1,0:T(1,128)S(1)}, f32[512,128]{1,0:T(8,128)S(1)}, bf16[...) custom-call(f32[1,512]{1,0:T(1,128)} %decay_hbm.1, ...), custom_call_target="tpu_custom_call" | custom-call | bytes 1875968 | tf_op jit(solution)/shard_map/pallas_call | solution.py:311
  5.1 0.4 %collective-permute-start.4 = (bf16[144,128]{1,0:T(8,128)(2,1)S(1)}, bf16[144,128]{1,0:T(8,128)(2,1)S(1)}, u32[]{:S(2)}, u32[]{:S(2)}) collective-permute-start(bf16[144,128]{1,0:T(8,128)(2,1)S(1)} %get-tuple-element.56.refs_0_), channel_id=1, source_target_pairs={{0,8},{8,0},{16,24},{24,16},{1,9},{9,1},{17,25},{25,17},{2,10},{10... | collective-permute-start | bytes 110600 | tf_op jit(solution)/shard_map/ppermute | solution.py:333
  5.5 0.6 %shard_map.88 = (bf16[512,128]{1,0:T(8,128)(2,1)S(1)}, bf16[128,512]{1,0:T(8,128)(2,1)S(1)}, f32[1,512]{1,0:T(1,128)S(1)}, f32[1,512]{1,0:T(1,128)S(1)}, f32[128,512]{1,0:T(8,128)S(1)}) custom-call(bf16[512,128]{1,0:T(8,128)(2,1)S(1)} %get-tuple-element.42.q_ref, bf16[512,128]{1,0:T(8,128)(2,1)S(1)} %get-tuple-element.43.k_ref, ...), custom_call_target="tpu_custom_call" | custom-call | bytes 921600 | tf_op jit(solution)/shard_map/pallas_call | solution.py:311
  6.1 0.3 %collective-permute-done.4.refs_8_.refs_1_ = bf16[144,128]{1,0:T(8,128)(2,1)S(1)} collective-permute-done((bf16[144,128]{1,0:T(8,128)(2,1)S(1)}, bf16[144,128]{1,0:T(8,128)(2,1)S(1)}, u32[]{:S(2)}, u32[]{:S(2)}) %collective-permute-start.4) | collective-permute-done | bytes 36896 | tf_op jit(solution)/shard_map/ppermute | solution.py:333
  6.4 1.9 %collective-permute-start.6 = (bf16[64,128]{1,0:T(8,128)(2,1)S(1)}, bf16[64,128]{1,0:T(8,128)(2,1)S(1)}, u32[]{:S(2)}, u32[]{:S(2)}) collective-permute-start(bf16[64,128]{1,0:T(8,128)(2,1)S(1)} %shard_map.92), channel_id=1, source_target_pairs={{0,16},{8,24},{16,0},{24,8},{1,17},{9,25},{17,1},{25,9},{2,18},{10... | collective-permute-start | bytes 49160 | tf_op jit(solution)/shard_map/ppermute | solution.py:330
  8.3 0.5 %shard_map.87 = (bf16[128,512]{1,0:T(8,128)(2,1)S(1)}, f32[128,512]{1,0:T(8,128)S(1)}) custom-call(bf16[512,128]{1,0:T(8,128)(2,1)S(1)} %get-tuple-element.35.q_ref, bf16[512,128]{1,0:T(8,128)(2,1)S(1)} %get-tuple-element.36.k_ref, bf16[128,512]{1,0:T(8,128)(2,1)S(1)} %get-tuple-element.37.value_t_ref, ...), custom_call_target="tpu_custom_call" | custom-call | bytes 1050624 | tf_op jit(solution)/shard_map/pallas_call | solution.py:311
  8.8 0.0 collective-permute-done.1.refs_1_
  8.8 0.1 collective-permute-start.2
  8.9 0.5 %collective-permute-start.5 = (bf16[512,128]{1,0:T(8,128)(2,1)S(1)}, bf16[512,128]{1,0:T(8,128)(2,1)S(1)}, u32[]{:S(2)}, u32[]{:S(2)}) collective-permute-start(bf16[512,128]{1,0:T(8,128)(2,1)S(1)} %get-tuple-element.58), channel_id=1, source_target_pairs={{0,8},{8,0},{16,24},{24,16},{1,9},{9,1},{17,25},{25,17},{2,10},{10... | collective-permute-start | bytes 393224 | tf_op jit(solution)/shard_map/ppermute | solution.py:333
  9.4 0.0 collective-permute-done.refs_0_
  9.4 0.5 %shard_map.89 = (bf16[1024,512]{1,0:T(8,128)(2,1)S(1)}, f32[1,512]{1,0:T(1,128)S(1)}, f32[1,512]{1,0:T(1,128)S(1)}, f32[1,512]{1,0:T(1,128)S(1)}) custom-call(bf16[128,512]{1,0:T(8,128)(2,1)S(1)} %get-tuple-element.46.qt_ref, f32[1,512]{1,0:T(1,128)S(1)} %get-tuple-element.47.top_ref, f32[1,512]{1,0:T(1,128)S(1)} %get-tuple-element.48.total_ref, ...), custom_call_target="tpu_custom_call" | custom-call | bytes 1452032 | tf_op jit(solution)/shard_map/pallas_call | solution.py:311
  9.9 0.6 %collective-permute-done.6.refs_9_ = bf16[64,128]{1,0:T(8,128)(2,1)S(1)} collective-permute-done((bf16[64,128]{1,0:T(8,128)(2,1)S(1)}, bf16[64,128]{1,0:T(8,128)(2,1)S(1)}, u32[]{:S(2)}, u32[]{:S(2)}) %collective-permute-start.6) | collective-permute-done | bytes 16416 | tf_op jit(solution)/shard_map/ppermute | solution.py:330
  10.5 0.0 collective-permute-done.3.refs_10_
  10.5 0.0 collective-permute-start.8
  10.5 0.5 %collective-permute-start.7 = (bf16[64,128]{1,0:T(8,128)(2,1)S(1)}, bf16[64,128]{1,0:T(8,128)(2,1)S(1)}, u32[]{:S(2)}, u32[]{:S(2)}) collective-permute-start(bf16[64,128]{1,0:T(8,128)(2,1)S(1)} %collective-permute-done.6.refs_9_), channel_id=1, source_target_pairs={{0,8},{8,0},{16,24},{24,16},{1,9},{9,1},{17,25},{25,17},{2,10},{10... | collective-permute-start | bytes 49160 | tf_op jit(solution)/shard_map/ppermute | solution.py:333
  11.0 0.0 collective-permute-done.2.refs_0_
  11.0 0.0 collective-permute-done.5.refs_9_
  11.0 1.0 %shard_map.91 = (bf16[512,128]{1,0:T(8,128)(2,1)}, bf16[512,128]{1,0:T(8,128)(2,1)}, f32[128,512]{1,0:T(8,128)S(1)}) custom-call(bf16[128,512]{1,0:T(8,128)(2,1)S(1)} %get-tuple-element.40.refs_0_.refs_2_, f32[128,512]{1,0:T(8,128)S(1)} %get-tuple-element.41.refs_1_.refs_3_, f32[1,512]{1,0:T(1,128)S(1)} %get-tuple-element.38.cum_row_ref.refs_2_.refs_4_, ...), custom_call_target="tpu_custom_call" | custom-call | bytes 2273280 | tf_op jit(solution)/shard_map/pallas_call | solution.py:311
  12.1 0.0 collective-permute-done.7.refs_10_
  12.1 0.0 collective-permute-done.8.refs_11_
  12.1 0.1 shard_map.93
  (2 shorter events, 0.0 us)
Async XLA Ops:
  0.6 8.2 %collective-permute-start.1 = (bf16[512,128]{1,0:T(8,128)(2,1)}, bf16[512,128]{1,0:T(8,128)(2,1)S(1)}, u32[]{:S(2)}, u32[]{:S(2)}) collective-permute-start(bf16[512,128]{1,0:T(8,128)(2,1)} %bitcast.14), channel_id=1, source_target_pairs={{0,16},{8,24},{16,0},{24,8},{1,17},{9,25},{17,1},{25,9},{2,18},{10... | collective-permute-start | bytes 393224 | tf_op jit(solution)/shard_map/ppermute | solution.py:330
  3.6 5.8 %collective-permute-start = (bf16[512,128]{1,0:T(8,128)(2,1)}, bf16[512,128]{1,0:T(8,128)(2,1)S(1)}, u32[]{:S(2)}, u32[]{:S(2)}) collective-permute-start(bf16[512,128]{1,0:T(8,128)(2,1)} %bitcast.15), channel_id=1, source_target_pairs={{0,8},{8,0},{16,24},{24,16},{1,9},{9,1},{17,25},{25,17},{2,10},{10... | collective-permute-start | bytes 393224 | tf_op jit(solution)/shard_map/ppermute | solution.py:333
  3.6 6.9 %collective-permute-start.3 = (bf16[512,128]{1,0:T(8,128)(2,1)}, bf16[512,128]{1,0:T(8,128)(2,1)S(1)}, u32[]{:S(2)}, u32[]{:S(2)}) collective-permute-start(bf16[512,128]{1,0:T(8,128)(2,1)} %bitcast.17), channel_id=1, source_target_pairs={{0,16},{8,24},{16,0},{24,8},{1,17},{9,25},{17,1},{25,9},{2,18},{10... | collective-permute-start | bytes 393224 | tf_op jit(solution)/shard_map/ppermute | solution.py:330
  5.1 1.3 %collective-permute-start.4 = (bf16[144,128]{1,0:T(8,128)(2,1)S(1)}, bf16[144,128]{1,0:T(8,128)(2,1)S(1)}, u32[]{:S(2)}, u32[]{:S(2)}) collective-permute-start(bf16[144,128]{1,0:T(8,128)(2,1)S(1)} %get-tuple-element.56.refs_0_), channel_id=1, source_target_pairs={{0,8},{8,0},{16,24},{24,16},{1,9},{9,1},{17,25},{25,17},{2,10},{10... | collective-permute-start | bytes 110600 | tf_op jit(solution)/shard_map/ppermute | solution.py:333
  6.4 4.1 %collective-permute-start.6 = (bf16[64,128]{1,0:T(8,128)(2,1)S(1)}, bf16[64,128]{1,0:T(8,128)(2,1)S(1)}, u32[]{:S(2)}, u32[]{:S(2)}) collective-permute-start(bf16[64,128]{1,0:T(8,128)(2,1)S(1)} %shard_map.92), channel_id=1, source_target_pairs={{0,16},{8,24},{16,0},{24,8},{1,17},{9,25},{17,1},{25,9},{2,18},{10... | collective-permute-start | bytes 49160 | tf_op jit(solution)/shard_map/ppermute | solution.py:330
  8.8 2.2 %collective-permute-start.2 = (bf16[512,128]{1,0:T(8,128)(2,1)S(1)}, bf16[512,128]{1,0:T(8,128)(2,1)S(1)}, u32[]{:S(2)}, u32[]{:S(2)}) collective-permute-start(bf16[512,128]{1,0:T(8,128)(2,1)S(1)} %collective-permute-done.1.refs_1_), channel_id=1, source_target_pairs={{0,8},{8,0},{16,24},{24,16},{1,9},{9,1},{17,25},{25,17},{2,10},{10... | collective-permute-start | bytes 393224 | tf_op jit(solution)/shard_map/ppermute | solution.py:333
  8.9 2.1 %collective-permute-start.5 = (bf16[512,128]{1,0:T(8,128)(2,1)S(1)}, bf16[512,128]{1,0:T(8,128)(2,1)S(1)}, u32[]{:S(2)}, u32[]{:S(2)}) collective-permute-start(bf16[512,128]{1,0:T(8,128)(2,1)S(1)} %get-tuple-element.58), channel_id=1, source_target_pairs={{0,8},{8,0},{16,24},{24,16},{1,9},{9,1},{17,25},{25,17},{2,10},{10... | collective-permute-start | bytes 393224 | tf_op jit(solution)/shard_map/ppermute | solution.py:333
  10.5 1.6 %collective-permute-start.8 = (bf16[512,128]{1,0:T(8,128)(2,1)S(1)}, bf16[512,128]{1,0:T(8,128)(2,1)S(1)}, u32[]{:S(2)}, u32[]{:S(2)}) collective-permute-start(bf16[512,128]{1,0:T(8,128)(2,1)S(1)} %collective-permute-done.3.refs_10_), channel_id=1, source_target_pairs={{0,8},{8,0},{16,24},{24,16},{1,9},{9,1},{17,25},{25,17},{2,10},{10... | collective-permute-start | bytes 393224 | tf_op jit(solution)/shard_map/ppermute | solution.py:333
  10.5 1.6 %collective-permute-start.7 = (bf16[64,128]{1,0:T(8,128)(2,1)S(1)}, bf16[64,128]{1,0:T(8,128)(2,1)S(1)}, u32[]{:S(2)}, u32[]{:S(2)}) collective-permute-start(bf16[64,128]{1,0:T(8,128)(2,1)S(1)} %collective-permute-done.6.refs_9_), channel_id=1, source_target_pairs={{0,8},{8,0},{16,24},{24,16},{1,9},{9,1},{17,25},{25,17},{2,10},{10... | collective-permute-start | bytes 49160 | tf_op jit(solution)/shard_map/ppermute | solution.py:333
